TPU v7x, 32 devices: a whole 2x2x4 slice. The times are simulated.
32 devices in a mesh: seq: 4 (over z), fsdp: 8 (over y, x, core).
Axes of the slice: x: 2, y: 2, z: 4, core: 2. Of those that a mesh axis runs over, the one named last changes fastest.
Arguments:
- tokens: bfloat16 [8, 512, 1024], P('fsdp', 'seq'), may hold values from -6 to 6
- scene_ids: int32 [8, 512], P('fsdp', 'seq'), may hold values from 0 to 1, as said below
- token_kind: int32 [8, 512], P('fsdp', 'seq'), may hold values from 0 to 1, as said below
- out_grad: bfloat16 [8, 512, 1024], P('fsdp', 'seq'), may hold values from -6 to 6
- first_gain: bfloat16 [2, 1024], P(None, 'fsdp'), may hold values from 0.5 to 1.5
- first_shift: bfloat16 [2, 1024], P(None, 'fsdp'), may hold values from -1.796875 to 1.796875
- qkv_weight: bfloat16 [2, 1024, 3072], P(None, 'fsdp'), may hold values from -0.1875 to 0.1875
- qv_bias: bfloat16 [2, 2048], P(None, 'fsdp'), may hold values from -3 to 3
- proj_weight: bfloat16 [2, 1024, 1024], P(None, 'fsdp'), may hold values from -1.5 to 1.5
- proj_bias: bfloat16 [2, 1024], P(None, 'fsdp'), may hold values from -3 to 3
- second_gain: bfloat16 [2, 1024], P(None, 'fsdp'), may hold values from 0.5 to 1.5
- second_shift: bfloat16 [2, 1024], P(None, 'fsdp'), may hold values from -1.796875 to 1.796875
- up_weight: bfloat16 [2, 1024, 4096], P(None, 'fsdp'), may hold values from -0.1875 to 0.1875
- up_bias: bfloat16 [2, 4096], P(None, 'fsdp'), may hold values from -3 to 3
- down_weight: bfloat16 [2, 4096, 1024], P(None, 'fsdp'), may hold values from -0.09375 to 0.09375
- down_bias: bfloat16 [2, 1024], P(None, 'fsdp'), may hold values from -3 to 3
Outputs:
- block_out: float32 [8, 512, 1024], P('fsdp', 'seq')
- input_grad: float32 [8, 512, 1024], P('fsdp', 'seq')
- first_gain_grad: float32 [2, 1024], P(None, 'fsdp')
- first_shift_grad: float32 [2, 1024], P(None, 'fsdp')
- qkv_weight_grad: float32 [2, 1024, 3072], P(None, 'fsdp')
- qv_bias_grad: float32 [2, 2048], P(None, 'fsdp')
- proj_weight_grad: float32 [2, 1024, 1024], P(None, 'fsdp')
- proj_bias_grad: float32 [2, 1024], P(None, 'fsdp')
- second_gain_grad: float32 [2, 1024], P(None, 'fsdp')
- second_shift_grad: float32 [2, 1024], P(None, 'fsdp')
- up_weight_grad: float32 [2, 1024, 4096], P(None, 'fsdp')
- up_bias_grad: float32 [2, 4096], P(None, 'fsdp')
- down_weight_grad: float32 [2, 4096, 1024], P(None, 'fsdp')
- down_bias_grad: float32 [2, 1024], P(None, 'fsdp')
Inputs may be any that keep to these rules, and one draw needn't show every extreme that they name: `scene_ids`: within each group the positions hold in order: image tokens of one scene, image tokens of the other, triplane tokens of the other, triplane tokens of the first; all four runs are nonempty. `token_kind`: the image tokens of a group come before its triplane tokens, as described for scene_ids.
All inputs are finite; a program needn't handle non-finite values.
Results may differ from a plain program's by a relative error of at most 0.015.
Values may be sent and summed in bfloat16 or wider, within the bound.
No kernel may reach another device: no remote copies, remote signals or barrier semaphores. Data moves between devices by JAX's collectives and lax.ppermute only.
A program may use at most 256 MiB of HBM per device.

v0:
```python
from functools import partial

import jax
import jax.numpy as jnp
from jax import lax
from jax.sharding import PartitionSpec as P

D = 1024
HEADS = 16
HEAD_DIM = 64


EPS = 1e-05
NEG = -1e30
SCALE = 0.125


def normalize(hidden):
    centred = hidden - jnp.mean(hidden, axis=-1, keepdims=True)
    spread = jnp.mean(centred * centred, axis=-1, keepdims=True)
    inverse = lax.rsqrt(spread + EPS)
    return (centred * inverse, inverse)


def norm_back(gradient, normed, inverse, norm_gain):
    scaled = gradient * norm_gain.astype(jnp.float32)
    mean_one = jnp.mean(scaled, axis=-1, keepdims=True)
    mean_two = jnp.mean(scaled * normed, axis=-1, keepdims=True)
    input_part = inverse * (scaled - mean_one - normed * mean_two)
    return (input_part, jnp.sum(gradient * normed, axis=0), jnp.sum(gradient, axis=0))


def outer_product(left_side, right_side):
    return lax.dot_general(
        left_side, right_side, (((0,), (0,)), ((), ())), preferred_element_type=jnp.float32
    )


def back_product(gradient, weight):
    return lax.dot_general(
        gradient, weight, (((1,), (1,)), ((), ())), preferred_element_type=jnp.float32
    )


def allowed_pairs(query_labels, key_labels):
    query_code = query_labels.astype(jnp.int32)
    key_code = key_labels.astype(jnp.int32)
    same_scene = query_code[:, None] // 2 == key_code[None, :] // 2
    visible = (key_code[None, :] % 2 == 0) | (query_code[:, None] % 2 == 1)
    return same_scene & visible


def score_block(query_part, key_part, allowed):
    raw_scores = (
        jnp.einsum("the,she->hts", query_part, key_part, preferred_element_type=jnp.float32) * SCALE
    )
    return jnp.where(allowed[None], raw_scores, NEG)


def attend_forward(queries, keys, values, allowed):
    row_count = queries.shape[0]
    key_count = keys.shape[0]
    head_span = min(4, HEADS) * HEAD_DIM
    outputs = []
    log_totals = []
    for offset in range(0, D, head_span):
        query_part = queries[:, offset : offset + head_span].reshape(row_count, -1, HEAD_DIM)
        key_part = keys[:, offset : offset + head_span].reshape(key_count, -1, HEAD_DIM)
        value_part = values[:, offset : offset + head_span].reshape(key_count, -1, HEAD_DIM)
        scores = score_block(query_part, key_part, allowed)
        largest = jnp.max(scores, axis=-1, keepdims=True)
        exp_scores = jnp.exp(scores - largest)
        row_total = jnp.sum(exp_scores, axis=-1, keepdims=True)
        probabilities = exp_scores / row_total
        attended = jnp.einsum(
            "hts,she->the",
            probabilities.astype(jnp.bfloat16),
            value_part,
            preferred_element_type=jnp.float32,
        )
        outputs.append(attended.reshape(row_count, head_span))
        log_totals.append(largest + jnp.log(row_total))
    return (jnp.concatenate(outputs, axis=1).astype(jnp.bfloat16), log_totals)


def attend_backward(queries, keys, values, allowed, log_totals, out_low):
    row_count = queries.shape[0]
    key_count = keys.shape[0]
    head_span = min(4, HEADS) * HEAD_DIM
    query_grads = []
    key_grads = []
    value_grads = []
    for part_index, offset in enumerate(range(0, D, head_span)):
        query_part = queries[:, offset : offset + head_span].reshape(row_count, -1, HEAD_DIM)
        key_part = keys[:, offset : offset + head_span].reshape(key_count, -1, HEAD_DIM)
        value_part = values[:, offset : offset + head_span].reshape(key_count, -1, HEAD_DIM)
        out_part = out_low[:, offset : offset + head_span].reshape(row_count, -1, HEAD_DIM)
        scores = score_block(query_part, key_part, allowed)
        probabilities = jnp.exp(scores - log_totals[part_index])
        value_grad = jnp.einsum(
            "hts,the->she",
            probabilities.astype(jnp.bfloat16),
            out_part,
            preferred_element_type=jnp.float32,
        )
        prob_grad = jnp.einsum(
            "the,she->hts", out_part, value_part, preferred_element_type=jnp.float32
        )
        score_grad = probabilities * (
            prob_grad - jnp.sum(probabilities * prob_grad, axis=-1, keepdims=True)
        )
        score_low = score_grad.astype(jnp.bfloat16)
        query_grad = (
            jnp.einsum("hts,she->the", score_low, key_part, preferred_element_type=jnp.float32)
            * SCALE
        )
        key_grad = (
            jnp.einsum("hts,the->she", score_low, query_part, preferred_element_type=jnp.float32)
            * SCALE
        )
        query_grads.append(query_grad.reshape(row_count, head_span))
        key_grads.append(key_grad.reshape(key_count, head_span))
        value_grads.append(value_grad.reshape(key_count, head_span))
    return (
        jnp.concatenate(query_grads, axis=1),
        jnp.concatenate(key_grads, axis=1),
        jnp.concatenate(value_grads, axis=1),
    )


def fetch_forward(shards, layer_index):
    pieces = [member[layer_index] for member in shards]
    return (
        lax.all_gather(pieces[0], "fsdp", axis=0, tiled=True),
        lax.all_gather(pieces[1], "fsdp", axis=0, tiled=True),
        lax.all_gather(pieces[2], "fsdp", axis=0, tiled=True),
        lax.all_gather(pieces[3], "fsdp", axis=0, tiled=True),
        lax.all_gather(pieces[4], "fsdp", axis=0, tiled=True),
        lax.all_gather(pieces[5], "fsdp", axis=0, tiled=True),
        lax.all_gather(pieces[6], "fsdp", axis=0, tiled=True),
        lax.all_gather(pieces[7], "fsdp", axis=0, tiled=True),
        lax.all_gather(pieces[8], "fsdp", axis=0, tiled=True),
        lax.all_gather(pieces[9], "fsdp", axis=0, tiled=True),
        lax.all_gather(pieces[10], "fsdp", axis=0, tiled=True),
        lax.all_gather(pieces[11], "fsdp", axis=0, tiled=True),
    )


def fetch_backward(shards, layer_index):
    pieces = [member[layer_index] for member in shards]
    return (
        lax.all_gather(pieces[0], "fsdp", axis=0, tiled=True),
        lax.all_gather(pieces[1], "fsdp", axis=0, tiled=True),
        lax.all_gather(pieces[2], "fsdp", axis=0, tiled=True),
        lax.all_gather(pieces[3], "fsdp", axis=0, tiled=True),
        lax.all_gather(pieces[4], "fsdp", axis=0, tiled=True),
        lax.all_gather(pieces[5], "fsdp", axis=0, tiled=True),
        lax.all_gather(pieces[6], "fsdp", axis=0, tiled=True),
        lax.all_gather(pieces[7], "fsdp", axis=0, tiled=True),
        lax.all_gather(pieces[8], "fsdp", axis=0, tiled=True),
        lax.all_gather(pieces[9], "fsdp", axis=0, tiled=True),
        lax.all_gather(pieces[10], "fsdp", axis=0, tiled=True),
        lax.all_gather(pieces[11], "fsdp", axis=0, tiled=True),
    )


def forward_layer(hidden, labels, params):
    (
        gain_one,
        shift_one,
        qkv_full,
        qv_full,
        proj_full,
        proj_add,
        gain_two,
        shift_two,
        up_full,
        up_add,
        down_full,
        down_add,
    ) = params
    normed_one, inverse_one = normalize(hidden)
    input_one = (normed_one * gain_one.astype(jnp.float32) + shift_one.astype(jnp.float32)).astype(
        jnp.bfloat16
    )
    qkv_add = jnp.concatenate([qv_full[:D], jnp.zeros((D,), jnp.bfloat16), qv_full[D:]]).astype(
        jnp.float32
    )
    projected = (jnp.dot(input_one, qkv_full, preferred_element_type=jnp.float32) + qkv_add).astype(
        jnp.bfloat16
    )
    queries = projected[:, :D]
    keys, values, key_labels = (
        lax.all_gather(projected[:, D : 2 * D], "seq", axis=0, tiled=True),
        lax.all_gather(projected[:, 2 * D :], "seq", axis=0, tiled=True),
        lax.all_gather(labels, "seq", axis=0, tiled=True),
    )
    allowed = allowed_pairs(labels, key_labels)
    attended, log_totals = attend_forward(queries, keys, values, allowed)
    middle = (
        hidden
        + jnp.dot(attended, proj_full, preferred_element_type=jnp.float32)
        + proj_add.astype(jnp.float32)
    )
    normed_two, inverse_two = normalize(middle)
    input_two = (normed_two * gain_two.astype(jnp.float32) + shift_two.astype(jnp.float32)).astype(
        jnp.bfloat16
    )
    pre_act = jnp.dot(input_two, up_full, preferred_element_type=jnp.float32) + up_add.astype(
        jnp.float32
    )
    activated = jax.nn.gelu(pre_act, approximate=False).astype(jnp.bfloat16)
    result = (
        middle
        + jnp.dot(activated, down_full, preferred_element_type=jnp.float32)
        + down_add.astype(jnp.float32)
    )
    kept = (
        normed_one,
        inverse_one,
        input_one,
        queries,
        keys,
        values,
        allowed,
        log_totals,
        attended,
        normed_two,
        inverse_two,
        input_two,
        pre_act,
        activated,
    )
    return (result, kept)


def backward_layer(gradient, params, kept):
    (
        gain_one,
        shift_one,
        qkv_full,
        qv_full,
        proj_full,
        proj_add,
        gain_two,
        shift_two,
        up_full,
        up_add,
        down_full,
        down_add,
    ) = params
    (
        normed_one,
        inverse_one,
        input_one,
        queries,
        keys,
        values,
        allowed,
        log_totals,
        attended,
        normed_two,
        inverse_two,
        input_two,
        pre_act,
        activated,
    ) = kept
    branch_low = gradient.astype(jnp.bfloat16)
    down_grad = outer_product(activated, branch_low)
    down_add_grad = jnp.sum(branch_low.astype(jnp.float32), axis=0)
    hidden_grad = back_product(branch_low, down_full)
    gelu_back = jax.vjp(partial(jax.nn.gelu, approximate=False), pre_act)[1]
    pre_low = gelu_back(hidden_grad)[0].astype(jnp.bfloat16)
    up_grad = outer_product(input_two, pre_low)
    up_add_grad = jnp.sum(pre_low.astype(jnp.float32), axis=0)
    input_two_grad = back_product(pre_low, up_full)
    middle_part, gain_two_grad, shift_two_grad = norm_back(
        input_two_grad, normed_two, inverse_two, gain_two
    )
    middle_grad = gradient + middle_part
    attn_low = middle_grad.astype(jnp.bfloat16)
    proj_grad = outer_product(attended, attn_low)
    proj_add_grad = jnp.sum(attn_low.astype(jnp.float32), axis=0)
    out_low = back_product(attn_low, proj_full).astype(jnp.bfloat16)
    query_grad, key_terms, value_terms = attend_backward(
        queries, keys, values, allowed, log_totals, out_low
    )
    key_grad, value_grad = (
        lax.psum_scatter(
            key_terms.astype(jnp.bfloat16), "seq", scatter_dimension=0, tiled=True
        ).astype(jnp.float32),
        lax.psum_scatter(
            value_terms.astype(jnp.bfloat16), "seq", scatter_dimension=0, tiled=True
        ).astype(jnp.float32),
    )
    qkv_low = jnp.concatenate([query_grad, key_grad, value_grad], axis=1).astype(jnp.bfloat16)
    qkv_grad = outer_product(input_one, qkv_low)
    column_sums = jnp.sum(qkv_low.astype(jnp.float32), axis=0)
    qv_grad = jnp.concatenate([column_sums[:D], column_sums[2 * D :]])
    input_one_grad = back_product(qkv_low, qkv_full)
    input_part, gain_one_grad, shift_one_grad = norm_back(
        input_one_grad, normed_one, inverse_one, gain_one
    )
    terms = (
        gain_one_grad,
        shift_one_grad,
        qkv_grad,
        qv_grad,
        proj_grad,
        proj_add_grad,
        gain_two_grad,
        shift_two_grad,
        up_grad,
        up_add_grad,
        down_grad,
        down_add_grad,
    )
    return (middle_grad + input_part, terms)


def reduce_terms(terms):
    shares = (
        lax.psum_scatter(
            terms[0].astype(jnp.bfloat16), "fsdp", scatter_dimension=0, tiled=True
        ).astype(jnp.float32),
        lax.psum_scatter(
            terms[1].astype(jnp.bfloat16), "fsdp", scatter_dimension=0, tiled=True
        ).astype(jnp.float32),
        lax.psum_scatter(
            terms[2].astype(jnp.bfloat16), "fsdp", scatter_dimension=0, tiled=True
        ).astype(jnp.float32),
        lax.psum_scatter(
            terms[3].astype(jnp.bfloat16), "fsdp", scatter_dimension=0, tiled=True
        ).astype(jnp.float32),
        lax.psum_scatter(
            terms[4].astype(jnp.bfloat16), "fsdp", scatter_dimension=0, tiled=True
        ).astype(jnp.float32),
        lax.psum_scatter(
            terms[5].astype(jnp.bfloat16), "fsdp", scatter_dimension=0, tiled=True
        ).astype(jnp.float32),
        lax.psum_scatter(
            terms[6].astype(jnp.bfloat16), "fsdp", scatter_dimension=0, tiled=True
        ).astype(jnp.float32),
        lax.psum_scatter(
            terms[7].astype(jnp.bfloat16), "fsdp", scatter_dimension=0, tiled=True
        ).astype(jnp.float32),
        lax.psum_scatter(
            terms[8].astype(jnp.bfloat16), "fsdp", scatter_dimension=0, tiled=True
        ).astype(jnp.float32),
        lax.psum_scatter(
            terms[9].astype(jnp.bfloat16), "fsdp", scatter_dimension=0, tiled=True
        ).astype(jnp.float32),
        lax.psum_scatter(
            terms[10].astype(jnp.bfloat16), "fsdp", scatter_dimension=0, tiled=True
        ).astype(jnp.float32),
        lax.psum_scatter(
            terms[11].astype(jnp.bfloat16), "fsdp", scatter_dimension=0, tiled=True
        ).astype(jnp.float32),
    )
    summed = (
        lax.psum(shares[0].astype(jnp.bfloat16), "seq").astype(jnp.float32),
        lax.psum(shares[1].astype(jnp.bfloat16), "seq").astype(jnp.float32),
        lax.psum(shares[2].astype(jnp.bfloat16), "seq").astype(jnp.float32),
        lax.psum(shares[3].astype(jnp.bfloat16), "seq").astype(jnp.float32),
        lax.psum(shares[4].astype(jnp.bfloat16), "seq").astype(jnp.float32),
        lax.psum(shares[5].astype(jnp.bfloat16), "seq").astype(jnp.float32),
        lax.psum(shares[6].astype(jnp.bfloat16), "seq").astype(jnp.float32),
        lax.psum(shares[7].astype(jnp.bfloat16), "seq").astype(jnp.float32),
        lax.psum(shares[8].astype(jnp.bfloat16), "seq").astype(jnp.float32),
        lax.psum(shares[9].astype(jnp.bfloat16), "seq").astype(jnp.float32),
        lax.psum(shares[10].astype(jnp.bfloat16), "seq").astype(jnp.float32),
        lax.psum(shares[11].astype(jnp.bfloat16), "seq").astype(jnp.float32),
    )
    return summed


def on_device(
    tokens,
    scene_ids,
    token_kind,
    out_grad,
    first_gain,
    first_shift,
    qkv_weight,
    qv_bias,
    proj_weight,
    proj_bias,
    second_gain,
    second_shift,
    up_weight,
    up_bias,
    down_weight,
    down_bias,
):
    shards = (
        first_gain,
        first_shift,
        qkv_weight,
        qv_bias,
        proj_weight,
        proj_bias,
        second_gain,
        second_shift,
        up_weight,
        up_bias,
        down_weight,
        down_bias,
    )
    layer_count = qkv_weight.shape[0]
    hidden = tokens[0].astype(jnp.float32)
    labels = (scene_ids[0] * 2 + token_kind[0]).astype(jnp.bfloat16)
    saved = []
    gathered_all = []
    for layer_index in range(layer_count):
        params = fetch_forward(shards, layer_index)
        hidden, kept = forward_layer(hidden, labels, params)
        saved.append(kept)
        gathered_all.append(params)
    gradient = out_grad[0].astype(jnp.float32)
    reduced = [None] * layer_count
    for layer_index in reversed(range(layer_count)):
        params = fetch_backward(shards, layer_index)
        gradient, terms = backward_layer(gradient, params, saved[layer_index])
        reduced[layer_index] = reduce_terms(terms)
    stacked = tuple(
        (
            jnp.stack([reduced[layer_index][member] for layer_index in range(layer_count)])
            for member in range(12)
        )
    )
    return (
        hidden[None],
        gradient[None],
        stacked[0],
        stacked[1],
        stacked[2],
        stacked[3],
        stacked[4],
        stacked[5],
        stacked[6],
        stacked[7],
        stacked[8],
        stacked[9],
        stacked[10],
        stacked[11],
    )


def solution(mesh):
    placed = (
        P("fsdp", "seq", None),
        P("fsdp", "seq"),
        P("fsdp", "seq"),
        P("fsdp", "seq", None),
        P(None, "fsdp"),
        P(None, "fsdp"),
        P(None, "fsdp", None),
        P(None, "fsdp"),
        P(None, "fsdp", None),
        P(None, "fsdp"),
        P(None, "fsdp"),
        P(None, "fsdp"),
        P(None, "fsdp", None),
        P(None, "fsdp"),
        P(None, "fsdp", None),
        P(None, "fsdp"),
    )
    return jax.shard_map(
        on_device,
        mesh=mesh,
        in_specs=placed,
        out_specs=(
            P("fsdp", "seq", None),
            P("fsdp", "seq", None),
            P(None, "fsdp"),
            P(None, "fsdp"),
            P(None, "fsdp", None),
            P(None, "fsdp"),
            P(None, "fsdp", None),
            P(None, "fsdp"),
            P(None, "fsdp"),
            P(None, "fsdp"),
            P(None, "fsdp", None),
            P(None, "fsdp"),
            P(None, "fsdp", None),
            P(None, "fsdp"),
        ),
        check_vma=False,
    )
```

profile of v0, /device:TPU:10, one launch (start us, length us, event | category | flops | bytes accessed | tf_op | source)
XLA Modules:
  0.0 1469.7 jit_solution(3910276345997859821)
XLA Ops:
  7.3 2.6 fusion.194
  10.0 8.8 all-gather.1
  18.8 7.8 all-gather
  26.6 8.9 all-gather.16
  35.5 7.9 all-gather.3
  44.4 12.8 all-gather.46.cloned.1.call-done
  57.2 3.9 fusion.39
  63.8 3.1 fusion.193
  67.0 3.0 fusion.192
  70.9 8.1 all-gather.4
  79.0 7.8 all-gather.14
  86.8 8.7 all-gather.13
  96.0 7.8 all-gather.12
  104.9 8.7 all-gather.8
  114.1 7.8 all-gather.7
  122.4 8.7 all-gather.6
  132.3 8.1 all-gather.10
  158.3 47.4 %all-gather.50.cloned.1.call-done = bf16[1,1024,4096]{2,1,0:T(8,128)(2,1)} async-done(((bf16[1,128,4096]{2,1,0:T(8,128)(2,1)}), bf16[1,1024,4096]{2,1,0:T(8,128)(2,1)}) %all-gather.50.cloned.1.call-update) | async-done | bytes 8388624 | tf_op jit(solution)/shard_map/all_gather | solution.py:142
  205.7 9.3 multiply_convert_fusion.1
  215.0 47.4 %all-gather.52.cloned.1.call-done = bf16[1,4096,1024]{2,1,0:T(8,128)(2,1)} async-done(((bf16[1,512,1024]{2,1,0:T(8,128)(2,1)}), bf16[1,4096,1024]{2,1,0:T(8,128)(2,1)}) %all-gather.52.cloned.1.call-update) | async-done | bytes 8388624 | tf_op jit(solution)/shard_map/all_gather | solution.py:144
  262.4 5.0 fusion.221
  267.7 42.2 %all-gather.54.cloned.1.call-done = bf16[1,1024,3072]{2,1,0:T(8,128)(2,1)} async-done(((bf16[1,128,3072]{2,1,0:T(8,128)(2,1)}), bf16[1,1024,3072]{2,1,0:T(8,128)(2,1)}) %all-gather.54.cloned.1.call-update) | async-done | bytes 6291472 | tf_op jit(solution)/shard_map/all_gather | solution.py:136
  309.9 3.9 fusion.36
  318.2 8.2 all-gather.20
  327.0 8.7 all-gather.19
  335.7 7.8 all-gather.18
  344.1 8.8 all-gather.22
  359.6 13.0 all-gather.42.cloned.1.call-done
  394.4 8.0 all-gather.56.cloned.1.call-done
  407.3 52.0 %all-gather.58.cloned.1.call-done = bf16[1,1024,4096]{2,1,0:T(8,128)(2,1)} async-done(((bf16[1,128,4096]{2,1,0:T(8,128)(2,1)}), bf16[1,1024,4096]{2,1,0:T(8,128)(2,1)}) %all-gather.58.cloned.1.call-update) | async-done | bytes 8388624 | tf_op jit(solution)/shard_map/all_gather | solution.py:142
  459.3 9.2 multiply_convert_fusion
  468.5 46.9 %all-gather.60.cloned.1.call-done = bf16[1,4096,1024]{2,1,0:T(8,128)(2,1)} async-done(((bf16[1,512,1024]{2,1,0:T(8,128)(2,1)}), bf16[1,4096,1024]{2,1,0:T(8,128)(2,1)}) %all-gather.60.cloned.1.call-update) | async-done | bytes 8388624 | tf_op jit(solution)/shard_map/all_gather | solution.py:144
  515.4 10.7 fusion.227
  526.2 3.6 multiply_reduce_fusion.8
  567.6 6.8 reduce-scatter.37.cloned.1.call-done
  577.9 24.6 %reduce-scatter.39.cloned.1.call-done = bf16[128,1024]{1,0:T(8,128)(2,1)} async-done(((bf16[512,1024]{1,0:T(8,128)(2,1)}), bf16[128,1024]{1,0:T(8,128)(2,1)}) %reduce-scatter.39.cloned.1.call-update) | async-done | bytes 262160
  606.0 6.0 multiply_reduce_fusion.10
  613.7 10.5 fusion.228
  624.2 3.6 multiply_reduce_fusion.9
  631.9 2.4 convolution_convert_fusion.8
  634.3 2.9 multiply_reduce_fusion
  640.5 2.9 multiply_reduce_fusion.1
  659.2 2.9 convolution_convert_fusion.6
  664.3 5.7 convolution_convert_fusion.4
  671.3 5.8 convolution_convert_fusion.2
  678.3 5.7 convolution_convert_fusion
  689.8 15.9 %reduce-scatter.41.cloned.1.call-done = bf16[128,1024]{1,0:T(8,128)(2,1)} async-done(((bf16[512,1024]{1,0:T(8,128)(2,1)}), bf16[128,1024]{1,0:T(8,128)(2,1)}) %reduce-scatter.41.cloned.1.call-update) | async-done | bytes 262160
  708.5 4.6 convolution_convert_fusion.5
  714.1 6.9 convolution_convert_fusion.3
  722.4 6.7 convolution_convert_fusion.1
  729.2 22.1 %reduce-scatter.27.cloned.1.call-done = bf16[128,1024]{1,0:T(8,128)(2,1)} async-done(((bf16[1024,1024]{1,0:T(8,128)(2,1)}), bf16[128,1024]{1,0:T(8,128)(2,1)}) %reduce-scatter.27.cloned.1.call-update) | async-done | bytes 262160 | tf_op jit(solution)/shard_map/reduce_scatter | solution.py:335
  751.3 45.3 %reduce-scatter.25.cloned.1.call-done = bf16[128,1024]{1,0:T(8,128)(2,1)} async-done(((bf16[1024,1024]{1,0:T(8,128)(2,1)}), bf16[128,1024]{1,0:T(8,128)(2,1)}) %reduce-scatter.25.cloned.1.call-update) | async-done | bytes 262160 | tf_op jit(solution)/shard_map/reduce_scatter | solution.py:335
  796.7 65.1 %reduce-scatter.23.cloned.1.call-done = bf16[128,3072]{1,0:T(8,128)(2,1)} async-done(((bf16[1024,3072]{1,0:T(8,128)(2,1)}), bf16[128,3072]{1,0:T(8,128)(2,1)}) %reduce-scatter.23.cloned.1.call-update) | async-done | bytes 786448 | tf_op jit(solution)/shard_map/reduce_scatter | solution.py:329
  861.8 75.0 %reduce-scatter.31.cloned.1.call-done = bf16[128,4096]{1,0:T(8,128)(2,1)} async-done(((bf16[1024,4096]{1,0:T(8,128)(2,1)}), bf16[128,4096]{1,0:T(8,128)(2,1)}) %reduce-scatter.31.cloned.1.call-update) | async-done | bytes 1048592 | tf_op jit(solution)/shard_map/reduce_scatter | solution.py:347
  936.8 74.8 %reduce-scatter.35.cloned.1.call-done = bf16[512,1024]{1,0:T(8,128)(2,1)} async-done(((bf16[4096,1024]{1,0:T(8,128)(2,1)}), bf16[512,1024]{1,0:T(8,128)(2,1)}) %reduce-scatter.35.cloned.1.call-update) | async-done | bytes 1048592 | tf_op jit(solution)/shard_map/reduce_scatter | solution.py:353
  1011.5 65.6 %reduce-scatter.21.cloned.1.call-done = bf16[128,3072]{1,0:T(8,128)(2,1)} async-done(((bf16[1024,3072]{1,0:T(8,128)(2,1)}), bf16[128,3072]{1,0:T(8,128)(2,1)}) %reduce-scatter.21.cloned.1.call-update) | async-done | bytes 786448 | tf_op jit(solution)/shard_map/reduce_scatter | solution.py:329
  1077.1 74.7 %reduce-scatter.29.cloned.1.call-done = bf16[128,4096]{1,0:T(8,128)(2,1)} async-done(((bf16[1024,4096]{1,0:T(8,128)(2,1)}), bf16[128,4096]{1,0:T(8,128)(2,1)}) %reduce-scatter.29.cloned.1.call-update) | async-done | bytes 1048592 | tf_op jit(solution)/shard_map/reduce_scatter | solution.py:347
  1151.8 75.0 %reduce-scatter.33.cloned.1.call-done = bf16[512,1024]{1,0:T(8,128)(2,1)} async-done(((bf16[4096,1024]{1,0:T(8,128)(2,1)}), bf16[512,1024]{1,0:T(8,128)(2,1)}) %reduce-scatter.33.cloned.1.call-update) | async-done | bytes 1048592 | tf_op jit(solution)/shard_map/reduce_scatter | solution.py:353
  1230.4 7.9 all-gather.24
  1238.3 5.5 fusion.98
  1245.6 5.3 fusion.153
  1251.0 23.6 %all-reduce.16 = (bf16[1024]{0:T(1024)(128)(2,1)S(1)}, bf16[1024]{0:T(1024)(128)(2,1)S(1)}, bf16[1024]{0:T(1024)(128)(2,1)S(1)}, bf16[1024]{0:T(1024)(128)(2,1)S...) all-reduce(bf16[1024]{0:T(1024)(128)(2,1)S(1)} %copy-done.191, ...), channel_id=32, replica_groups=mesh['seq'=4,'fsdp'=8] {'fsdp'}, use_global_device_ids=true, to_apply=%region_48.49.clone | all-reduce | flops 24576 | bytes 98304
  1275.9 21.2 %all-reduce.17 = (bf16[1,128]{1,0:T(2,128)(2,1)S(1)}, bf16[1,128]{1,0:T(2,128)(2,1)S(1)}, bf16[1,128]{1,0:T(2,128)(2,1)S(1)}, bf16[1,128]{1,0:T(2,128)(2,1)S(1)}...) all-reduce(bf16[1,128]{1,0:T(2,128)(2,1)S(1)} %dynamic-slice_bitcas, ...), channel_id=1, replica_groups=mesh['seq'=4,'fsdp'=8] {'seq'}, use_global_device_ids=true, to_apply=%region_49.50 | all-reduce | flops 3072 | bytes 12288 | tf_op jit(solution)/shard_map/psum | solution.py:361
  1302.7 150.8 %all-reduce.21.cloned.1.call-done = (bf16[1,128,3072]{2,1,0:T(8,128)(2,1)}, bf16[1,128,3072]{2,1,0:T(8,128)(2,1)}, bf16[1,128,1024]{2,1,0:T(8,128)(2,1)}, bf16[1...) async-done(((bf16[1,128,3072]{2,1,0:T(8,128)(2,1)}, ...) | async-done | bytes 6291472 | tf_op jit(solution)/shard_map/psum | solution.py:363
  (713 shorter events, 168.5 us)
Async XLA Ops:
  7.2 11.6 copy-start.195
  7.2 19.4 %copy-start.193 = (bf16[2,256]{1,0:T(2,128)(2,1)S(1)}, bf16[2,256]{1,0:T(2,128)(2,1)}, u32[]{:S(2)}) copy-start(bf16[2,256]{1,0:T(2,128)(2,1)} %param.23) | copy-start | bytes 3076
  7.2 36.9 %copy-start.19 = (bf16[1,128,1024]{2,1,0:T(8,128)(2,1)S(1)}, bf16[1,128,1024]{2,1,0:T(8,128)(2,1)}, u32[]{:S(2)}) copy-start(bf16[1,128,1024]{2,1,0:T(8,128)(2,1)} %param.16) | copy-start | bytes 786436
  7.2 50.0 %all-gather.46.cloned.1.call-start = ((), (), s32[]{:S(2)}) async-start(), calls=%async_computation.24 | async-start | bytes 7077888 | tf_op jit(solution)/shard_map/all_gather | solution.py:136
  9.9 131.8 %all-gather.40.cloned.1.call-start = ((), (), s32[]{:S(2)}) async-start(), calls=%async_computation.13 | async-start | bytes 1310720 | tf_op jit(solution)/shard_map/all_gather | solution.py:194
  18.8 42.4 %copy-start.104 = (f32[1,1024]{1,0:T(1,128)}, f32[1,1024]{1,0:T(1,128)S(1)}, u32[]{:S(2)}) copy-start(f32[1,1024]{1,0:T(1,128)S(1)} %convert_element_type.448) | copy-start | bytes 12292
  26.6 34.6 %copy-start.102 = (f32[1,1024]{1,0:T(1,128)}, f32[1,1024]{1,0:T(1,128)S(1)}, u32[]{:S(2)}) copy-start(f32[1,1024]{1,0:T(1,128)S(1)} %convert_element_type.447) | copy-start | bytes 12292
  44.2 17.0 %copy-start.128 = (f32[128]{0:T(128)}, f32[128]{0:T(128)S(1)}, u32[]{:S(2)}) copy-start(f32[128]{0:T(128)S(1)} %broadcast_multiply_fusion.11) | copy-start | bytes 1540
  44.4 16.8 %copy-start.130 = (f32[128]{0:T(128)}, f32[128]{0:T(128)S(1)}, u32[]{:S(2)}) copy-start(f32[128]{0:T(128)S(1)} %add_rsqrt_fusion.3) | copy-start | bytes 1540
  62.1 81.1 %all-gather.38.cloned.1.call-start = ((), (), s32[]{:S(2)}) async-start(), calls=%async_computation.12 | async-start | bytes 1310720 | tf_op jit(solution)/shard_map/all_gather | solution.py:195
  62.8 92.7 %all-gather.48.cloned.1.call-start = ((), (), s32[]{:S(2)}) async-start(), calls=%async_computation.25 | async-start | bytes 2359296 | tf_op jit(solution)/shard_map/all_gather | solution.py:138
  63.7 142.0 %all-gather.50.cloned.1.call-start = ((), (), s32[]{:S(2)}) async-start(), calls=%async_computation.26 | async-start | bytes 9437184 | tf_op jit(solution)/shard_map/all_gather | solution.py:142
  66.9 28.6 %copy-start.196 = (bf16[2,128]{1,0:T(2,128)(2,1)S(1)}, bf16[2,128]{1,0:T(2,128)(2,1)}, u32[]{:S(2)}) copy-start(bf16[2,128]{1,0:T(2,128)(2,1)} %param.31) | copy-start | bytes 1540
  66.9 37.5 %copy-start.197 = (bf16[2,128]{1,0:T(2,128)(2,1)S(1)}, bf16[2,128]{1,0:T(2,128)(2,1)}, u32[]{:S(2)}) copy-start(bf16[2,128]{1,0:T(2,128)(2,1)} %param.27) | copy-start | bytes 1540
  66.9 46.7 %copy-start.198 = (bf16[2,128]{1,0:T(2,128)(2,1)S(1)}, bf16[2,128]{1,0:T(2,128)(2,1)}, u32[]{:S(2)}) copy-start(bf16[2,128]{1,0:T(2,128)(2,1)} %param.26) | copy-start | bytes 1540
  66.9 55.0 %copy-start.199 = (bf16[2,128]{1,0:T(2,128)(2,1)S(1)}, bf16[2,128]{1,0:T(2,128)(2,1)}, u32[]{:S(2)}) copy-start(bf16[2,128]{1,0:T(2,128)(2,1)} %param.25) | copy-start | bytes 1540
  66.9 64.8 %copy-start.182 = (bf16[2,512]{1,0:T(2,128)(2,1)S(1)}, bf16[2,512]{1,0:T(2,128)(2,1)}, u32[]{:S(2)}) copy-start(bf16[2,512]{1,0:T(2,128)(2,1)} %param.29) | copy-start | bytes 6148
  67.0 195.5 %all-gather.52.cloned.1.call-start = ((), (), s32[]{:S(2)}) async-start(), calls=%async_computation.27 | async-start | bytes 9437184 | tf_op jit(solution)/shard_map/all_gather | solution.py:144
  70.1 239.8 %all-gather.54.cloned.1.call-start = ((), (), s32[]{:S(2)}) async-start(), calls=%async_computation.28 | async-start | bytes 7077888 | tf_op jit(solution)/shard_map/all_gather | solution.py:136
  70.8 286.6 %all-gather.44.cloned.1.call-start = ((), (), s32[]{:S(2)}) async-start(), calls=%async_computation.15 | async-start | bytes 1310720 | tf_op jit(solution)/shard_map/all_gather | solution.py:194
  113.6 92.1 %copy-start.117 = (f32[1,1024]{1,0:T(1,128)}, f32[1,1024]{1,0:T(1,128)S(1)}, u32[]{:S(2)}) copy-start(f32[1,1024]{1,0:T(1,128)S(1)} %convert_element_type.453) | copy-start | bytes 12292
  141.5 8.6 copy-start.83
  155.5 59.5 %copy-start.115 = (bf16[4,64,128]{2,1,0:T(8,128)(2,1)}, bf16[4,64,128]{2,1,0:T(8,128)(2,1)S(1)}, u32[]{:S(2)}) copy-start(bf16[4,64,128]{2,1,0:T(8,128)(2,1)S(1)} %convolution_convert_fusion.23) | copy-start | bytes 196612
  155.5 50.2 %copy-start.150 = (f32[1,4096]{1,0:T(1,128)S(1)}, f32[1,4096]{1,0:T(1,128)}, u32[]{:S(2)}) copy-start(f32[1,4096]{1,0:T(1,128)} %convert_element_type.454) | copy-start | bytes 49156
  158.1 104.4 %copy-start.16 = (f32[128,1024]{1,0:T(8,128)}, f32[128,1024]{1,0:T(8,128)S(1)}, u32[]{:S(2)}) copy-start(f32[128,1024]{1,0:T(8,128)S(1)} %get-tuple-element.157) | copy-start | bytes 1572868
  158.1 56.9 %copy-start.153 = (f32[128]{0:T(128)}, f32[128]{0:T(128)S(1)}, u32[]{:S(2)}) copy-start(f32[128]{0:T(128)S(1)} %broadcast_multiply_fusion.10) | copy-start | bytes 1540
  158.3 56.7 %copy-start.188 = (f32[128]{0:T(128)}, f32[128]{0:T(128)S(1)}, u32[]{:S(2)}) copy-start(f32[128]{0:T(128)S(1)} %add_rsqrt_fusion.2) | copy-start | bytes 1540
  267.5 46.3 %copy-start.147 = (f32[128]{0:T(128)}, f32[128]{0:T(128)S(1)}, u32[]{:S(2)}) copy-start(f32[128]{0:T(128)S(1)} %broadcast_multiply_fusion.9) | copy-start | bytes 1540
  267.7 46.1 %copy-start.156 = (f32[128]{0:T(128)}, f32[128]{0:T(128)S(1)}, u32[]{:S(2)}) copy-start(f32[128]{0:T(128)S(1)} %add_rsqrt_fusion.1) | copy-start | bytes 1540
  314.6 12.3 copy-start.202
  314.6 21.0 %copy-start.203 = (bf16[1,128]{1,0:T(2,128)(2,1)S(1)}, bf16[1,128]{1,0:T(2,128)(2,1)}, u32[]{:S(2)}) copy-start(bf16[1,128]{1,0:T(2,128)(2,1)} %get-tuple-element.146) | copy-start | bytes 772
  314.6 29.4 %copy-start.183 = (bf16[1,512]{1,0:T(2,128)(2,1)S(1)}, bf16[1,512]{1,0:T(2,128)(2,1)}, u32[]{:S(2)}) copy-start(bf16[1,512]{1,0:T(2,128)(2,1)} %get-tuple-element.130) | copy-start | bytes 3076
  315.5 57.1 %all-gather.42.cloned.1.call-start = ((), (), s32[]{:S(2)}) async-start(), calls=%async_computation.14 | async-start | bytes 1310720 | tf_op jit(solution)/shard_map/all_gather | solution.py:195
  316.2 86.1 %all-gather.56.cloned.1.call-start = ((), (), s32[]{:S(2)}) async-start(), calls=%async_computation.29 | async-start | bytes 2359296 | tf_op jit(solution)/shard_map/all_gather | solution.py:138
  316.8 142.4 %all-gather.58.cloned.1.call-start = ((), (), s32[]{:S(2)}) async-start(), calls=%async_computation.30 | async-start | bytes 9437184 | tf_op jit(solution)/shard_map/all_gather | solution.py:142
  317.6 197.9 %all-gather.60.cloned.1.call-start = ((), (), s32[]{:S(2)}) async-start(), calls=%async_computation.31 | async-start | bytes 9437184 | tf_op jit(solution)/shard_map/all_gather | solution.py:144
  318.1 256.3 %reduce-scatter.37.cloned.1.call-start = ((), (), s32[]{:S(2)}) async-start(), calls=%async_computation.32 | async-start | bytes 1310720
  359.6 29.6 %copy-start.53 = (bf16[512,256]{0,1:T(8,128)(2,1)}, bf16[512,256]{0,1:T(8,128)(2,1)S(1)}, u32[]{:S(2)}) copy-start(bf16[512,256]{0,1:T(8,128)(2,1)S(1)} %copy.140) | copy-start | bytes 786436
  390.6 11.8 copy-start.106
  404.7 125.1 %copy-start.151 = (f32[128]{0:T(128)}, f32[128]{0:T(128)S(1)}, u32[]{:S(2)}) copy-start(f32[128]{0:T(128)S(1)} %broadcast_multiply_fusion.8) | copy-start | bytes 1540
  404.9 124.8 %copy-start.160 = (f32[128]{0:T(128)}, f32[128]{0:T(128)S(1)}, u32[]{:S(2)}) copy-start(f32[128]{0:T(128)S(1)} %add_rsqrt_fusion) | copy-start | bytes 1540
  515.4 10.7 copy-start.22
  549.2 53.3 %reduce-scatter.39.cloned.1.call-start = ((), (), s32[]{:S(2)}) async-start(), calls=%async_computation.33 | async-start | bytes 1310720
  558.6 130.0 %reduce-scatter.43.cloned.1.call-start = ((), (), s32[]{:S(2)}) async-start(), calls=%async_computation.35 | async-start | bytes 1310720
  606.0 18.1 %slice-start = ((s8[8388608]{0:T(1024)(128)(4,1)}), s8[4194304]{0:T(1024)(128)(4,1)S(1)}, s32[]{:S(2)}) async-start(s8[8388608]{0:T(1024)(128)(4,1)} %bitcast.436), calls=%async_computation.37 | async-start | bytes 8388608
  613.0 14.8 %copy-start.41 = (f32[128,1024]{1,0:T(8,128)}, f32[128,1024]{1,0:T(8,128)S(1)}, u32[]{:S(2)}) copy-start(f32[128,1024]{1,0:T(8,128)S(1)} %get-tuple-element.75) | copy-start | bytes 1572868
  613.7 10.5 copy-start.17
  613.7 10.5 slice-start.1
  613.7 10.5 copy-start.154
  613.7 10.5 copy-start.189
  651.6 54.0 %reduce-scatter.41.cloned.1.call-start = ((), (), s32[]{:S(2)}) async-start(), calls=%async_computation.34 | async-start | bytes 1310720
  658.7 92.6 %reduce-scatter.27.cloned.1.call-start = ((), (), s32[]{:S(2)}) async-start(), calls=%async_computation.19 | async-start | bytes 2359296 | tf_op jit(solution)/shard_map/reduce_scatter | solution.py:335
  662.1 134.5 %reduce-scatter.25.cloned.1.call-start = ((), (), s32[]{:S(2)}) async-start(), calls=%async_computation.18 | async-start | bytes 2359296 | tf_op jit(solution)/shard_map/reduce_scatter | solution.py:335
  664.3 197.5 %reduce-scatter.23.cloned.1.call-start = ((), (), s32[]{:S(2)}) async-start(), calls=%async_computation.17 | async-start | bytes 7077888 | tf_op jit(solution)/shard_map/reduce_scatter | solution.py:329
  670.1 266.7 %reduce-scatter.31.cloned.1.call-start = ((), (), s32[]{:S(2)}) async-start(), calls=%async_computation.21 | async-start | bytes 9437184 | tf_op jit(solution)/shard_map/reduce_scatter | solution.py:347
  677.1 334.4 %reduce-scatter.35.cloned.1.call-start = ((), (), s32[]{:S(2)}) async-start(), calls=%async_computation.23 | async-start | bytes 9437184 | tf_op jit(solution)/shard_map/reduce_scatter | solution.py:353
  684.1 393.0 %reduce-scatter.21.cloned.1.call-start = ((), (), s32[]{:S(2)}) async-start(), calls=%async_computation.16 | async-start | bytes 7077888 | tf_op jit(solution)/shard_map/reduce_scatter | solution.py:329
  686.7 21.7 %copy-start.103 = (f32[1,1024]{1,0:T(1,128)S(1)}, f32[1,1024]{1,0:T(1,128)}, u32[]{:S(2)}) copy-start(f32[1,1024]{1,0:T(1,128)} %copy-done.102) | copy-start | bytes 12292
  686.8 21.7 %copy-start.105 = (f32[1,1024]{1,0:T(1,128)S(1)}, f32[1,1024]{1,0:T(1,128)}, u32[]{:S(2)}) copy-start(f32[1,1024]{1,0:T(1,128)} %copy-done.104) | copy-start | bytes 12292
  686.8 21.7 %copy-start.129 = (f32[128]{0:T(128)S(1)}, f32[128]{0:T(128)}, u32[]{:S(2)}) copy-start(f32[128]{0:T(128)} %copy-done.128) | copy-start | bytes 1540
  686.8 21.7 %copy-start.131 = (f32[128]{0:T(128)S(1)}, f32[128]{0:T(128)}, u32[]{:S(2)}) copy-start(f32[128]{0:T(128)} %copy-done.130) | copy-start | bytes 1540
  713.1 438.7 %reduce-scatter.29.cloned.1.call-start = ((), (), s32[]{:S(2)}) async-start(), calls=%async_computation.20 | async-start | bytes 9437184 | tf_op jit(solution)/shard_map/reduce_scatter | solution.py:347
  721.1 505.7 %reduce-scatter.33.cloned.1.call-start = ((), (), s32[]{:S(2)}) async-start(), calls=%async_computation.22 | async-start | bytes 9437184 | tf_op jit(solution)/shard_map/reduce_scatter | solution.py:353
  729.2 724.4 %all-reduce.21.cloned.1.call-start = ((), (), s32[]{:S(2)}) async-start(), calls=%async_computation.36 | async-start | bytes 12582912 | tf_op jit(solution)/shard_map/psum | solution.py:363
  (171 other events, 465.7 us)
Sparse Core Ops, SparseCore 0:
  10.5 46.6 all-gather.45
  62.2 27.9 all-gather.39
  91.7 27.4 all-gather.37
  121.5 27.4 all-gather.47
  151.3 54.3 all-gather.49
  208.0 54.3 all-gather.51
  264.3 45.5 all-gather.53
  315.6 27.8 all-gather.43
  345.1 27.4 all-gather.41
  374.9 27.4 all-gather.55
  404.8 54.3 all-gather.57
  461.0 54.3 all-gather.59
  549.4 25.0 reduce-scatter.36
  576.7 25.8 reduce-scatter.38
  651.7 25.7 reduce-scatter.42
  679.8 25.7 reduce-scatter.40
  709.4 41.9 reduce-scatter.26
  755.4 41.2 reduce-scatter.24
  800.0 61.7 reduce-scatter.22
  865.5 71.2 reduce-scatter.30
  940.2 71.2 reduce-scatter.34
  1015.3 61.7 reduce-scatter.20
  1080.5 71.2 reduce-scatter.28
  1155.5 71.2 reduce-scatter.32
  1229.8 223.7 all-reduce.20
where the time goes:
time: 1480 us; the launch traced here: 1470 us
  waiting for transfers between devices  970 us (66%)
  blocking collectives  185 us (12%)
  matrix products  166 us (11%)
  local copies, waits for them, and re-layouts  89.4 us (6%)
  other arithmetic  39.2 us (3%)
  between operations  18.9 us (1%)
    psum x1, waiting for transfers between devices, reduce_terms(): lax.psum(shares[2].astype(jnp.bfloat16), 'seq').astype(jnp.float32)  151 us
    reduce_scatter x2, waiting for transfers between devices, reduce_terms(): lax.psum_scatter(terms[10].astype(jnp.bfloat16), 'fsdp', scatter_dimensio...  150 us
    reduce_scatter x2, waiting for transfers between devices, reduce_terms(): lax.psum_scatter(terms[8].astype(jnp.bfloat16), 'fsdp', scatter_dimension...  150 us
    reduce_scatter x2, waiting for transfers between devices, reduce_terms(): lax.psum_scatter(terms[2].astype(jnp.bfloat16), 'fsdp', scatter_dimension...  131 us
    all_gather x2, waiting for transfers between devices, fetch_forward(): lax.all_gather(pieces[8], 'fsdp', axis=0, tiled=True)  99.4 us
    all_gather x2, waiting for transfers between devices, fetch_forward(): lax.all_gather(pieces[10], 'fsdp', axis=0, tiled=True)  94.4 us
    reduce_scatter x2, waiting for transfers between devices, reduce_terms(): lax.psum_scatter(terms[4].astype(jnp.bfloat16), 'fsdp', scatter_dimension...  67.5 us
    all_gather x2, waiting for transfers between devices, fetch_forward(): lax.all_gather(pieces[2], 'fsdp', axis=0, tiled=True)  55 us
  transfers between devices with their start and end apart: 25, of which 20 were waited for; matrix products, arithmetic and copies ran while one was open for 12% of the time, Pallas kernels for 0%

commit v1 on v0

v1 whole, which is shorter than its diff:
```python
from functools import partial

import jax
import jax.numpy as jnp
from jax import lax
from jax.sharding import PartitionSpec as P

D = 1024
HEADS = 16
HEAD_DIM = 64
FF = 4096
EPS = 1e-05
NEG = -1e30
SCALE = 0.125
BF = jnp.bfloat16
F32 = jnp.float32


def xor_pairs(count, mask):
    return [(i, i ^ mask) for i in range(count)]


class Net:
    def __init__(self):
        self.n_s = lax.axis_size("seq")
        self.n_f = lax.axis_size("fsdp")
        self.n_p = self.n_f // 2
        self.s = lax.axis_index("seq")
        self.f = lax.axis_index("fsdp")
        self.p = self.f // 2
        self.c = self.f % 2

    def transpose(self, v):
        pairs = []
        for s in range(self.n_s):
            for f in range(self.n_f):
                pairs.append((s * self.n_f + f, (f // 2) * self.n_f + 2 * s + f % 2))
        return lax.ppermute(v, ("seq", "fsdp"), pairs)

    def chip(self, v, j):
        return lax.ppermute(v, "fsdp", xor_pairs(self.n_f, 2 * j))

    def core(self, v):
        return lax.ppermute(v, "fsdp", xor_pairs(self.n_f, 1))

    def gather(self, v):
        return [v] + [self.chip(v, j) for j in range(1, self.n_p)]

    def exchange(self, blocks):
        return [blocks[0]] + [self.chip(blocks[j], j) for j in range(1, self.n_p)]

    def scatter(self, blocks):
        parts = self.exchange(blocks)
        total = parts[0].astype(F32)
        for part in parts[1:]:
            total = total + part.astype(F32)
        return total

    def natural(self, blocks):
        bit = 1
        while bit < self.n_p:
            on = (self.p & bit) != 0
            blocks = [jnp.where(on, blocks[i ^ bit], blocks[i]) for i in range(self.n_p)]
            bit *= 2
        return blocks

    def by_core(self, own, other):
        on = self.c == 0
        return jnp.where(on, own, other), jnp.where(on, other, own)

    def z_sum(self, v):
        n = self.n_s
        half = n // 2
        total = v
        for k in range(1, half):
            got = lax.ppermute(total, "seq", [(k - 1, k), (n - k, n - k - 1)])
            here = (self.s == k) | (self.s == n - 1 - k)
            total = jnp.where(here, (v.astype(F32) + got.astype(F32)).astype(BF), total)
        got = lax.ppermute(total, "seq", [(half - 1, half), (half, half - 1)])
        total = (total.astype(F32) + got.astype(F32)).astype(BF)
        for k in range(half - 1, 0, -1):
            got = lax.ppermute(total, "seq", [(k, k - 1), (n - 1 - k, n - k)])
            here = (self.s == k - 1) | (self.s == n - k)
            total = jnp.where(here, got, total)
        return total


def normalize(hidden):
    centred = hidden - jnp.mean(hidden, axis=-1, keepdims=True)
    spread = jnp.mean(centred * centred, axis=-1, keepdims=True)
    inverse = lax.rsqrt(spread + EPS)
    return (centred * inverse, inverse)


def norm_back(gradient, normed, inverse, norm_gain):
    scaled = gradient * norm_gain
    mean_one = jnp.mean(scaled, axis=-1, keepdims=True)
    mean_two = jnp.mean(scaled * normed, axis=-1, keepdims=True)
    input_part = inverse * (scaled - mean_one - normed * mean_two)
    return (input_part, jnp.sum(gradient * normed, axis=0), jnp.sum(gradient, axis=0))


def dot(a, b):
    return jnp.dot(a, b, preferred_element_type=F32)


def dot_tn(a, b):
    return lax.dot_general(a, b, (((0,), (0,)), ((), ())), preferred_element_type=F32)


def dot_nt(a, b):
    return lax.dot_general(a, b, (((1,), (1,)), ((), ())), preferred_element_type=F32)


def scores_of(q, k, allowed):
    raw = jnp.einsum("the,she->hts", q, k, preferred_element_type=F32) * SCALE
    return jnp.where(allowed[None], raw, NEG)


def attend(qkv, allowed, width):
    rows = qkv.shape[0]
    q, k, v = [qkv[:, i * width : (i + 1) * width].reshape(rows, -1, HEAD_DIM) for i in range(3)]
    scores = scores_of(q, k, allowed)
    largest = jnp.max(scores, axis=-1, keepdims=True)
    powers = jnp.exp(scores - largest)
    total = jnp.sum(powers, axis=-1, keepdims=True)
    probs = (powers / total).astype(BF)
    out = jnp.einsum("hts,she->the", probs, v, preferred_element_type=F32)
    return out.reshape(rows, width).astype(BF), largest + jnp.log(total)


def attend_back(qkv, allowed, log_total, do, width):
    rows = qkv.shape[0]
    q, k, v = [qkv[:, i * width : (i + 1) * width].reshape(rows, -1, HEAD_DIM) for i in range(3)]
    do = do.reshape(rows, -1, HEAD_DIM)
    probs = jnp.exp(scores_of(q, k, allowed) - log_total)
    dv = jnp.einsum("hts,the->she", probs.astype(BF), do, preferred_element_type=F32)
    dp = jnp.einsum("the,she->hts", do, v, preferred_element_type=F32)
    ds = (probs * (dp - jnp.sum(probs * dp, axis=-1, keepdims=True))).astype(BF)
    dq = jnp.einsum("hts,she->the", ds, k, preferred_element_type=F32) * SCALE
    dk = jnp.einsum("hts,the->she", ds, q, preferred_element_type=F32) * SCALE
    return jnp.concatenate([t.reshape(rows, width) for t in (dq, dk, dv)], axis=1).astype(BF)


def quarter(v, index, width):
    return lax.dynamic_slice_in_dim(v, index * width, width, axis=1)


def fetch_rows(net, payload_of):
    got = net.exchange([payload_of(net.p ^ j) for j in range(net.n_p)])
    own = jnp.stack(net.natural(got))
    other = net.core(own)
    first, second = net.by_core(own, other)
    return jnp.stack([first, second], axis=1).reshape(-1, own.shape[-1])


def return_rows(net, partial_rows):
    n = partial_rows.shape[1]
    by_owner = partial_rows.astype(BF).reshape(net.n_p, 2, -1, n)
    keep = lax.dynamic_index_in_dim(by_owner, net.c, axis=1, keepdims=False)
    send = lax.dynamic_index_in_dim(by_owner, 1 - net.c, axis=1, keepdims=False)
    summed = (keep.astype(F32) + net.core(send).astype(F32)).astype(BF)
    blocks = [
        lax.dynamic_index_in_dim(summed, net.p ^ j, axis=0, keepdims=False) for j in range(net.n_p)
    ]
    return net.exchange(blocks)


def on_device(
    tokens,
    scene_ids,
    token_kind,
    out_grad,
    first_gain,
    first_shift,
    qkv_weight,
    qv_bias,
    proj_weight,
    proj_bias,
    second_gain,
    second_shift,
    up_weight,
    up_bias,
    down_weight,
    down_bias,
):
    net = Net()
    n_p = net.n_p
    layers = qkv_weight.shape[0]
    cw = D // n_p
    fw = FF // n_p
    rows = tokens.shape[1]

    small = jnp.concatenate(
        [first_gain, first_shift, qv_bias, proj_bias, second_gain, second_shift, up_bias, down_bias],
        axis=1,
    )
    small = lax.all_gather(small, "fsdp", axis=0).astype(F32)
    d8 = first_gain.shape[1]
    widths = [d8, d8, 2 * d8, d8, d8, d8, 4 * d8, d8]
    starts = [sum(widths[:i]) for i in range(8)]

    def vector(layer, which):
        return small[:, layer, starts[which] : starts[which] + widths[which]].reshape(-1)

    hidden = net.transpose(tokens[0]).astype(F32)
    code = net.transpose((scene_ids[0] * 2 + token_kind[0]).reshape(1, -1))
    codes = jnp.concatenate(net.gather(code), axis=1)
    same = codes.reshape(-1, 1) // 2 == codes.reshape(1, -1) // 2
    seen = (codes.reshape(1, -1) % 2 == 0) | (codes.reshape(-1, 1) % 2 == 1)
    allowed = same & seen
    dm_first = net.transpose(out_grad[0])

    def qkv_payload(layer):
        w = qkv_weight[layer].reshape(-1, 3, D)

        def of(i):
            return lax.dynamic_slice_in_dim(w, i * cw, cw, axis=2).reshape(-1, 3 * cw)

        return of

    weights = []
    for layer in range(layers):
        qkv_w = fetch_rows(net, qkv_payload(layer))
        rest = fetch_rows(
            net,
            lambda i, layer=layer: jnp.concatenate(
                [proj_weight[layer], quarter(up_weight[layer], i, fw)], axis=1
            ),
        )
        first, second = net.by_core(down_weight[layer], net.core(down_weight[layer]))
        down_w = jnp.concatenate([first, second], axis=0)
        qv = vector(layer, 2)
        qkv_b = jnp.concatenate(
            [
                lax.dynamic_slice_in_dim(qv, net.p * cw, cw),
                jnp.zeros((cw,), F32),
                lax.dynamic_slice_in_dim(qv, D + net.p * cw, cw),
            ]
        )
        up_b = lax.dynamic_slice_in_dim(vector(layer, 6), net.p * fw, fw)
        weights.append((qkv_w, qkv_b, rest[:, :D], rest[:, D:], up_b, down_w))

    kept = []
    for layer in range(layers):
        qkv_w, qkv_b, proj_w, up_w, up_b, down_w = weights[layer]
        n1, r1 = normalize(hidden)
        a1 = (n1 * vector(layer, 0) + vector(layer, 1)).astype(BF)
        a1g = jnp.concatenate(net.gather(a1), axis=0)
        qkv = (dot(a1g, qkv_w) + qkv_b).astype(BF)
        og, log_total = attend(qkv, allowed, cw)
        o = net.exchange([og[j * rows : (j + 1) * rows] for j in range(n_p)])
        o = jnp.concatenate(net.natural(o), axis=1)
        h2 = hidden + dot(o, proj_w) + vector(layer, 3)
        n2, r2 = normalize(h2)
        a2 = (n2 * vector(layer, 4) + vector(layer, 5)).astype(BF)
        a2g = jnp.concatenate(net.gather(a2), axis=0)
        u = dot(a2g, up_w) + up_b
        z = jax.nn.gelu(u, approximate=False).astype(BF)
        y = dot(z, down_w).astype(BF)
        h3 = h2 + net.scatter([y[j * rows : (j + 1) * rows] for j in range(n_p)]) + vector(layer, 7)
        kept.append((n1, r1, a1g, qkv, log_total, o, n2, r2, a2g, u, z))
        hidden = h3
    block_out = net.transpose(hidden.astype(BF)).astype(F32)

    grads = [None] * layers
    grad = None
    dm = dm_first
    for layer in reversed(range(layers)):
        qkv_w, qkv_b, proj_w, up_w, up_b, down_w = weights[layer]
        n1, r1, a1g, qkv, log_total, o, n2, r2, a2g, u, z = kept[layer]
        if grad is None:
            grad = dm.astype(F32)
        else:
            dm = grad.astype(BF)
        dmg = jnp.concatenate(net.gather(dm), axis=0)
        down_b_grad = jnp.sum(dm.astype(F32), axis=0)
        down_q = dot_tn(z, dmg).astype(BF).reshape(2, -1, D)
        keep = lax.dynamic_index_in_dim(down_q, net.c, axis=0, keepdims=False)
        send = lax.dynamic_index_in_dim(down_q, 1 - net.c, axis=0, keepdims=False)
        down_g = (keep.astype(F32) + net.core(send).astype(F32)).astype(BF)
        dz = dot_nt(dmg, down_w)
        du = jax.vjp(partial(jax.nn.gelu, approximate=False), u)[1](dz)[0].astype(BF)
        up_b_grad = jnp.sum(du.astype(F32), axis=0)
        up_g = jnp.concatenate(net.natural(return_rows(net, dot_tn(a2g, du))), axis=1)
        da2 = dot_nt(du, up_w).astype(BF)
        da2 = net.scatter([da2[j * rows : (j + 1) * rows] for j in range(n_p)])
        part, gain2_grad, shift2_grad = norm_back(da2, n2, r2, vector(layer, 4))
        dh2 = grad + part
        dy = dh2.astype(BF)
        proj_b_grad = jnp.sum(dy.astype(F32), axis=0)
        proj_parts = return_rows(net, dot_tn(o, dy))
        proj_g = sum(t.astype(F32) for t in proj_parts).astype(BF)
        do = dot_nt(dy, proj_w).astype(BF)
        dog = net.exchange([quarter(do, net.p ^ j, cw) for j in range(n_p)])
        dog = jnp.concatenate(dog, axis=0)
        dqkv = attend_back(qkv, allowed, log_total, dog, cw)
        qkv_b_grad = jnp.sum(dqkv.astype(F32), axis=0)
        da1 = dot_nt(dqkv, qkv_w).astype(BF)
        da1 = net.scatter([da1[j * rows : (j + 1) * rows] for j in range(n_p)])
        part, gain1_grad, shift1_grad = norm_back(da1, n1, r1, vector(layer, 0))
        grad = dh2 + part
        qkv_parts = net.natural(return_rows(net, dot_tn(a1g, dqkv)))
        qkv_g = jnp.stack([t.reshape(-1, 3, cw) for t in qkv_parts], axis=2).reshape(-1, 3 * D)
        qv_grad = jnp.zeros((2 * D,), F32)
        qv_grad = lax.dynamic_update_slice(qv_grad, qkv_b_grad[:cw], (net.p * cw,))
        qv_grad = lax.dynamic_update_slice(qv_grad, qkv_b_grad[2 * cw :], (D + net.p * cw,))
        up_b_grad = lax.dynamic_update_slice(jnp.zeros((FF,), F32), up_b_grad, (net.p * fw,))
        vectors = (
            gain1_grad,
            shift1_grad,
            qv_grad,
            proj_b_grad,
            gain2_grad,
            shift2_grad,
            up_b_grad,
            down_b_grad,
        )
        grads[layer] = (
            net.z_sum(qkv_g),
            net.z_sum(proj_g),
            net.z_sum(up_g),
            net.z_sum(down_g),
            jnp.concatenate([t.reshape(net.n_f, -1) for t in vectors], axis=1),
        )
    input_grad = net.transpose(grad.astype(BF)).astype(F32)

    small_g = jnp.stack([g[4] for g in grads], axis=1).astype(BF)
    small_g = lax.psum_scatter(small_g, "fsdp", scatter_dimension=0, tiled=True)[0]
    small_g = lax.psum(small_g, "seq").astype(F32)
    small_out = [small_g[:, starts[i] : starts[i] + widths[i]] for i in range(8)]
    big = [jnp.stack([g[i] for g in grads]).astype(F32) for i in range(4)]
    return (
        block_out[None],
        input_grad[None],
        small_out[0],
        small_out[1],
        big[0],
        small_out[2],
        big[1],
        small_out[3],
        small_out[4],
        small_out[5],
        big[2],
        small_out[6],
        big[3],
        small_out[7],
    )


def solution(mesh):
    tok = P("fsdp", "seq", None)
    lab = P("fsdp", "seq")
    vec = P(None, "fsdp")
    mat = P(None, "fsdp", None)
    return jax.shard_map(
        on_device,
        mesh=mesh,
        in_specs=(tok, lab, lab, tok, vec, vec, mat, vec, mat, vec, vec, vec, mat, vec, mat, vec),
        out_specs=(tok, tok, vec, vec, mat, vec, mat, vec, vec, vec, mat, vec, mat, vec),
        check_vma=False,
    )
```

time: 1480 us -> 785 us (0.53)
  waiting for transfers between devices: 970 us -> 330 us
  starting transfers between devices: 1.6 us -> 159 us
  blocking collectives: 185 us -> 43.4 us
  matrix products: 166 us -> 65.3 us
  other arithmetic: 39.2 us -> 87.8 us
    reduce_scatter x8 -> x0, waiting for transfers between devices: 498 us -> none  [the longest x2 150 us: reduce_terms(): lax.psum_scatter(terms[10].astype(jnp.bfloat16), 'fsdp', scatter_dimensio...]
    ppermute x0 -> x124, waiting for transfers between devices: none -> 330 us  [the longest x81 158 us: chip(): return lax.ppermute(v, 'fsdp', xor_pairs(self.n_f, 2 * j))]
    all_gather x12 -> x0, waiting for transfers between devices: 270 us -> none  [the longest x2 99.4 us: fetch_forward(): lax.all_gather(pieces[8], 'fsdp', axis=0, tiled=True)]
    ppermute x0 -> x124, starting transfers between devices: none -> 159 us  [the longest x81 101 us: chip(): return lax.ppermute(v, 'fsdp', xor_pairs(self.n_f, 2 * j))]
    psum x1 -> x0, waiting for transfers between devices: 151 us -> none  [reduce_terms(): lax.psum(shares[2].astype(jnp.bfloat16), 'seq').astype(jnp.float32)]
    all_gather x17 -> x1, blocking collectives: 140 us -> 9.22 us  [on_device(): small = lax.all_gather(small, 'fsdp', axis=0).astype(F32)]
    dot_general x72 -> x36, matrix products: 166 us -> 65.3 us  [the longest x8 21.8 us: dot(): return jnp.dot(a, b, preferred_element_type=F32)]
    unnamed x29 -> x0, waiting for transfers between devices: 51.5 us -> none
  transfers between devices with their start and end apart: 25 -> 124, of which waited for: 20 -> 60; matrix products, arithmetic and copies ran while one was open for 12% -> 25% of each run, Pallas kernels for 0% -> 0%
where the time goes in v1:
time: 785 us; the launch traced here: 770 us
  waiting for transfers between devices  330 us (42%)
  starting transfers between devices  159 us (20%)
  other arithmetic  87.8 us (11%)
  local copies, waits for them, and re-layouts  80.8 us (10%)
  matrix products  65.3 us (8%)
  blocking collectives  43.4 us (6%)
    ppermute x81, waiting for transfers between devices, chip(): return lax.ppermute(v, 'fsdp', xor_pairs(self.n_f, 2 * j))  158 us
    ppermute x81, starting transfers between devices, chip(): return lax.ppermute(v, 'fsdp', xor_pairs(self.n_f, 2 * j))  101 us
    ppermute x8, waiting for transfers between devices, z_sum(): got = lax.ppermute(total, 'seq', [(k, k - 1), (n - 1 - k, n - k)])  60.9 us
    ppermute x8, waiting for transfers between devices, z_sum(): got = lax.ppermute(total, 'seq', [(k - 1, k), (n - k, n - k - 1)])  56.7 us
    ppermute x8, waiting for transfers between devices, z_sum(): got = lax.ppermute(total, 'seq', [(half - 1, half), (half, half - 1)])  54 us
    dot_general x8, matrix products, dot(): return jnp.dot(a, b, preferred_element_type=F32)  21.8 us
    unnamed x1, blocking collectives  21.4 us
    ppermute x8, starting transfers between devices, z_sum(): got = lax.ppermute(total, 'seq', [(half - 1, half), (half, half - 1)])  20 us
  transfers between devices with their start and end apart: 124, of which 60 were waited for; matrix products, arithmetic and copies ran while one was open for 25% of the time, Pallas kernels for 0%

profile of v1, /device:TPU:10, one launch (start us, length us, event | category | flops | bytes accessed | tf_op | source)
XLA Modules:
  0.0 770.5 jit_solution(6544546770645130315)
XLA Ops:
  4.9 3.2 collective-permute-start.31
  8.1 2.6 collective-permute-start.30
  10.8 9.2 %all-gather.1 = bf16[8,2,1536]{2,1,0:T(2,128)(2,1)S(1)} all-gather(bf16[1,2,1536]{2,1,0:T(2,128)(2,1)S(1)} %bitcast.538), channel_id=2, replica_groups=mesh['seq'=4,'fsdp'=8] {'fsdp'}, dimensions={0}, use_global_device_ids=true | all-gather | bytes 55296 | tf_op jit(solution)/shard_map/all_gather | solution.py:198
  22.1 3.2 fusion.148
  26.9 2.5 dynamic-slice_bitcast_fusion.20
  46.4 3.6 collective-permute-start.48
  50.0 21.3 %collective-permute-done.6 = bf16[128,768]{0,1:T(8,128)(2,1)S(1)} collective-permute-done((bf16[128,768]{0,1:T(8,128)(2,1)}, bf16[128,768]{0,1:T(8,128)(2,1)S(1)}, u32[]{:S(2)}, u32[]{:S(2)}) %collective-permute-start.6) | collective-permute-done | bytes 196640 | tf_op jit(solution)/shard_map/ppermute | solution.py:41
  78.2 3.4 collective-permute-start.15
  86.6 11.3 %collective-permute-done.17 = bf16[128,2048]{1,0:T(8,128)(2,1)S(1)} collective-permute-done((bf16[128,2048]{1,0:T(8,128)(2,1)}, bf16[128,2048]{1,0:T(8,128)(2,1)S(1)}, u32[]{:S(2)}, u32[]{:S(2)}) %collective-permute-start.17) | collective-permute-done | bytes 524320 | tf_op jit(solution)/shard_map/ppermute | solution.py:41
  98.0 14.8 %collective-permute-done.16 = bf16[128,2048]{1,0:T(8,128)(2,1)S(1)} collective-permute-done((bf16[128,2048]{1,0:T(8,128)(2,1)}, bf16[128,2048]{1,0:T(8,128)(2,1)S(1)}, u32[]{:S(2)}, u32[]{:S(2)}) %collective-permute-start.16) | collective-permute-done | bytes 524320 | tf_op jit(solution)/shard_map/ppermute | solution.py:41
  115.5 8.8 %collective-permute-done.49 = bf16[128,1024]{1,0:T(8,128)(2,1)S(1)} collective-permute-done((bf16[128,1024]{1,0:T(8,128)(2,1)}, bf16[128,1024]{1,0:T(8,128)(2,1)S(1)}, u32[]{:S(2)}, u32[]{:S(2)}) %collective-permute-start.49) | collective-permute-done | bytes 262176 | tf_op jit(solution)/shard_map/ppermute | solution.py:41
  126.9 3.8 collective-permute-start.3
  134.0 2.8 collective-permute-start.51
  138.2 3.0 copy.124
  143.8 2.6 add_convert_fusion.15
  170.0 2.8 broadcast_select_fusion.1
  172.8 3.7 collective-permute-done.21
  176.5 5.2 collective-permute-done.20
  182.1 8.0 %multiply_convert_fusion.3 = (bf16[512,1024]{1,0:T(8,128)(2,1)S(1)}, f32[512,1024]{1,0:T(8,128)}, f32[512,1024]{1,0:T(8,128)}) fusion(f32[1024]{0:T(1024)S(1)} %dynamic_slice.245, bf16[1024,2048]{1,0:T(8,128)(2,1)S(1)} %bitcast.432, bf16[128,1024]{1,0:T(8,128)(2,1)S(1)} %collective-permute-done.21, bf16[128,1024]{1,0:T(8,128)(2,1)S(1)} %collective-permute-done.20, ...), kind=kOutput, calls=%fused_computation.71 | convolution fusion | flops 1112539136 | bytes 8392704 | tf_op jit(solution)/shard_map/dot_general | solution.py:104
  197.8 4.0 collective-permute-done.23
  201.8 4.5 collective-permute-done.25
  213.5 2.9 select_bitcast_fusion.1
  216.5 3.2 collective-permute-done.28
  219.7 2.7 collective-permute-done.27
  246.9 6.6 collective-permute-done.42
  253.5 2.7 collective-permute-done.41
  256.2 5.5 multiply_convert_fusion.2
  264.1 3.1 convert_reduce_fusion
  272.8 3.3 fusion.55
  285.6 4.1 collective-permute-done.52
  289.8 4.7 collective-permute-done.54
  295.8 2.9 multiply_reduce_fusion.2
  305.8 4.0 collective-permute-start.47
  313.3 3.2 fusion.78
  342.8 4.3 collective-permute-done.63
  347.0 2.7 collective-permute-done.62
  349.9 3.7 convert_reduce_fusion.1
  359.0 2.7 convolution_convert_fusion.3
  371.9 2.6 fusion.10
  381.8 2.5 multiply_reduce_fusion.4
  396.9 3.1 fusion.81
  421.7 3.1 collective-permute-done.83
  431.9 5.3 collective-permute-done.72
  443.3 21.4 %all-reduce = bf16[8,2,1536]{2,1,0:T(2,128)(2,1)S(1)} all-reduce(bf16[8,2,1536]{2,1,0:T(2,128)(2,1)S(1)} %copy.145), channel_id=3, replica_groups=mesh['seq'=4,'fsdp'=8] {'fsdp'}, use_global_device_ids=true, to_apply=%region_38.39.clone | all-reduce | flops 24576 | bytes 98304
  465.4 12.8 %psum.7 = bf16[2,1536]{1,0:T(2,128)(2,1)S(1)} all-reduce(bf16[2,1536]{1,0:T(2,128)(2,1)S(1)} %dynamic-slice_bitcast_fusion.28), channel_id=1, replica_groups=mesh['seq'=4,'fsdp'=8] {'seq'}, use_global_device_ids=true, to_apply=%region_39.40 | all-reduce | flops 3072 | bytes 12288 | tf_op jit(solution)/shard_map/psum | solution.py:330
  486.3 28.9 %collective-permute-done.99 = bf16[128,1024]{1,0:T(8,128)(2,1)S(1)} collective-permute-done((bf16[128,1024]{1,0:T(8,128)(2,1)S(1)}, bf16[128,1024]{1,0:T(8,128)(2,1)S(1)}, u32[]{:S(2)}, u32[]{:S(2)}) %collective-permute-start.99) | collective-permute-done | bytes 262176 | tf_op jit(solution)/shard_map/ppermute | solution.py:76
  532.5 5.4 collective-permute-done.85
  549.1 3.1 collective-permute-done.76
  555.6 2.8 collective-permute-done.105
  560.8 5.4 collective-permute-done.104
  571.1 3.8 collective-permute-done.91
  579.3 4.0 collective-permute-start.101
  588.9 5.1 collective-permute-done.92
  595.3 16.1 %collective-permute-done.86 = bf16[128,3072]{0,1:T(8,128)(2,1)S(1)} collective-permute-done((bf16[128,3072]{0,1:T(8,128)(2,1)S(1)}, bf16[128,3072]{0,1:T(8,128)(2,1)S(1)}, u32[]{:S(2)}, u32[]{:S(2)}) %collective-permute-start.86) | collective-permute-done | bytes 786464 | tf_op jit(solution)/shard_map/ppermute | solution.py:79
  613.8 17.4 %collective-permute-done.78 = bf16[128,3072]{0,1:T(8,128)(2,1)S(1)} collective-permute-done((bf16[128,3072]{0,1:T(8,128)(2,1)S(1)}, bf16[128,3072]{0,1:T(8,128)(2,1)S(1)}, u32[]{:S(2)}, u32[]{:S(2)}) %collective-permute-start.78) | collective-permute-done | bytes 786464 | tf_op jit(solution)/shard_map/ppermute | solution.py:76
  635.5 6.4 collective-permute-done.93
  645.9 10.0 %collective-permute-done.94 = bf16[128,1024]{1,0:T(8,128)(2,1)S(1)} collective-permute-done((bf16[128,1024]{1,0:T(8,128)(2,1)S(1)}, bf16[128,1024]{1,0:T(8,128)(2,1)S(1)}, u32[]{:S(2)}, u32[]{:S(2)}) %collective-permute-start.94) | collective-permute-done | bytes 262176 | tf_op jit(solution)/shard_map/ppermute | solution.py:82
  655.9 3.6 collective-permute-start.79
  662.5 3.6 collective-permute-start.107
  667.9 18.8 %collective-permute-done.79 = bf16[128,3072]{0,1:T(8,128)(2,1)S(1)} collective-permute-done((bf16[128,3072]{0,1:T(8,128)(2,1)S(1)}, bf16[128,3072]{0,1:T(8,128)(2,1)S(1)}, u32[]{:S(2)}, u32[]{:S(2)}) %collective-permute-start.79) | collective-permute-done | bytes 786464 | tf_op jit(solution)/shard_map/ppermute | solution.py:79
  693.1 12.7 %collective-permute-done.107 = bf16[128,4096]{1,0:T(8,128)(2,1)S(1)} collective-permute-done((bf16[128,4096]{1,0:T(8,128)(2,1)S(1)}, bf16[128,4096]{1,0:T(8,128)(2,1)S(1)}, u32[]{:S(2)}, u32[]{:S(2)}) %collective-permute-start.107) | collective-permute-done | bytes 1048608 | tf_op jit(solution)/shard_map/ppermute | solution.py:79
  710.4 14.6 %collective-permute-done.80 = bf16[128,3072]{0,1:T(8,128)(2,1)S(1)} collective-permute-done((bf16[128,3072]{0,1:T(8,128)(2,1)S(1)}, bf16[128,3072]{0,1:T(8,128)(2,1)S(1)}, u32[]{:S(2)}, u32[]{:S(2)}) %collective-permute-start.80) | collective-permute-done | bytes 786464 | tf_op jit(solution)/shard_map/ppermute | solution.py:82
  727.7 19.9 %collective-permute-done.119 = bf16[512,1024]{1,0:T(8,128)(2,1)} collective-permute-done((bf16[512,1024]{1,0:T(8,128)(2,1)}, bf16[512,1024]{1,0:T(8,128)(2,1)}, u32[]{:S(2)}, u32[]{:S(2)}) %collective-permute-start.119) | collective-permute-done | bytes 1048608 | tf_op jit(solution)/shard_map/ppermute | solution.py:82
  751.2 15.2 %collective-permute-done.108 = bf16[128,4096]{1,0:T(8,128)(2,1)} collective-permute-done((bf16[128,4096]{1,0:T(8,128)(2,1)}, bf16[128,4096]{1,0:T(8,128)(2,1)}, u32[]{:S(2)}, u32[]{:S(2)}) %collective-permute-start.108) | collective-permute-done | bytes 1048608 | tf_op jit(solution)/shard_map/ppermute | solution.py:82
  (876 shorter events, 331.4 us)
Async XLA Ops:
  1.3 31.9 %collective-permute-start.8 = (s32[1,128]{1,0:T(1,128)S(1)}, s32[1,128]{1,0:T(1,128)S(1)}, u32[]{:S(2)}, u32[]{:S(2)}) collective-permute-start(s32[1,128]{1,0:T(1,128)S(1)} %multiply_add_fusion.3), channel_id=1, source_target_pairs={{0,0},{1,1},{2,8},{3,9},{4,16},{5,17},{6,24},{7,25},{8,2},{9,3},{1... | collective-permute-start | bytes 1544 | tf_op jit(solution)/shard_map/ppermute | solution.py:38
  4.9 36.3 %collective-permute-start.31 = (bf16[128,768]{0,1:T(8,128)(2,1)}, bf16[128,768]{0,1:T(8,128)(2,1)}, u32[]{:S(2)}, u32[]{:S(2)}) collective-permute-start(bf16[128,768]{0,1:T(8,128)(2,1)} %bitcast.54), channel_id=1, source_target_pairs={{0,2},{1,3},{2,0},{3,1},{4,6},{5,7},{6,4},{7,5},{8,10},{9,11},{10,... | collective-permute-start | bytes 589832 | tf_op jit(solution)/shard_map/ppermute | solution.py:41
  8.1 35.7 %collective-permute-start.30 = (bf16[128,768]{0,1:T(8,128)(2,1)}, bf16[128,768]{0,1:T(8,128)(2,1)}, u32[]{:S(2)}, u32[]{:S(2)}) collective-permute-start(bf16[128,768]{0,1:T(8,128)(2,1)} %bitcast.53), channel_id=1, source_target_pairs={{0,4},{1,5},{2,6},{3,7},{4,0},{5,1},{6,2},{7,3},{8,12},{9,13},{10,... | collective-permute-start | bytes 589832 | tf_op jit(solution)/shard_map/ppermute | solution.py:41
  39.1 32.1 %collective-permute-start.6 = (bf16[128,768]{0,1:T(8,128)(2,1)}, bf16[128,768]{0,1:T(8,128)(2,1)S(1)}, u32[]{:S(2)}, u32[]{:S(2)}) collective-permute-start(bf16[128,768]{0,1:T(8,128)(2,1)} %bitcast.7), channel_id=1, source_target_pairs={{0,2},{1,3},{2,0},{3,1},{4,6},{5,7},{6,4},{7,5},{8,10},{9,11},{10,... | collective-permute-start | bytes 589832 | tf_op jit(solution)/shard_map/ppermute | solution.py:41
  40.5 33.2 %collective-permute-start.5 = (bf16[128,768]{0,1:T(8,128)(2,1)}, bf16[128,768]{0,1:T(8,128)(2,1)S(1)}, u32[]{:S(2)}, u32[]{:S(2)}) collective-permute-start(bf16[128,768]{0,1:T(8,128)(2,1)} %bitcast.6), channel_id=1, source_target_pairs={{0,4},{1,5},{2,6},{3,7},{4,0},{5,1},{6,2},{7,3},{8,12},{9,13},{10,... | collective-permute-start | bytes 589832 | tf_op jit(solution)/shard_map/ppermute | solution.py:41
  41.2 34.2 %collective-permute-start.4 = (bf16[128,768]{0,1:T(8,128)(2,1)S(1)}, bf16[128,768]{0,1:T(8,128)(2,1)S(1)}, u32[]{:S(2)}, u32[]{:S(2)}) collective-permute-start(bf16[128,768]{0,1:T(8,128)(2,1)S(1)} %bitcast.501), channel_id=1, source_target_pairs={{0,6},{1,7},{2,4},{3,5},{4,2},{5,3},{6,0},{7,1},{8,14},{9,15},{10,... | collective-permute-start | bytes 589832 | tf_op jit(solution)/shard_map/ppermute | solution.py:41
  43.7 34.2 %collective-permute-start = (bf16[128,1024]{1,0:T(8,128)(2,1)}, bf16[128,1024]{1,0:T(8,128)(2,1)S(1)}, u32[]{:S(2)}, u32[]{:S(2)}) collective-permute-start(bf16[128,1024]{1,0:T(8,128)(2,1)} %bitcast.549), channel_id=1, source_target_pairs={{0,0},{1,1},{2,8},{3,9},{4,16},{5,17},{6,24},{7,25},{8,2},{9,3},{1... | collective-permute-start | bytes 786440 | tf_op jit(solution)/shard_map/ppermute | solution.py:38
  46.4 35.6 %collective-permute-start.48 = (bf16[128,1024]{1,0:T(8,128)(2,1)}, bf16[128,1024]{1,0:T(8,128)(2,1)}, u32[]{:S(2)}, u32[]{:S(2)}) collective-permute-start(bf16[128,1024]{1,0:T(8,128)(2,1)} %bitcast.550), channel_id=1, source_target_pairs={{0,0},{1,1},{2,8},{3,9},{4,16},{5,17},{6,24},{7,25},{8,2},{9,3},{1... | collective-permute-start | bytes 786440 | tf_op jit(solution)/shard_map/ppermute | solution.py:38
  71.3 55.6 %collective-permute-start.38 = (bf16[128,2048]{1,0:T(8,128)(2,1)}, bf16[128,2048]{1,0:T(8,128)(2,1)S(1)}, u32[]{:S(2)}, u32[]{:S(2)}) collective-permute-start(bf16[128,2048]{1,0:T(8,128)(2,1)} %get-tuple-element.208), channel_id=1, source_target_pairs={{0,2},{1,3},{2,0},{3,1},{4,6},{5,7},{6,4},{7,5},{8,10},{9,11},{10,... | collective-permute-start | bytes 1572872 | tf_op jit(solution)/shard_map/ppermute | solution.py:41
  73.7 24.3 %collective-permute-start.17 = (bf16[128,2048]{1,0:T(8,128)(2,1)}, bf16[128,2048]{1,0:T(8,128)(2,1)S(1)}, u32[]{:S(2)}, u32[]{:S(2)}) collective-permute-start(bf16[128,2048]{1,0:T(8,128)(2,1)} %get-tuple-element.219), channel_id=1, source_target_pairs={{0,2},{1,3},{2,0},{3,1},{4,6},{5,7},{6,4},{7,5},{8,10},{9,11},{10,... | collective-permute-start | bytes 1572872 | tf_op jit(solution)/shard_map/ppermute | solution.py:41
  75.4 37.3 %collective-permute-start.16 = (bf16[128,2048]{1,0:T(8,128)(2,1)}, bf16[128,2048]{1,0:T(8,128)(2,1)S(1)}, u32[]{:S(2)}, u32[]{:S(2)}) collective-permute-start(bf16[128,2048]{1,0:T(8,128)(2,1)} %get-tuple-element.220), channel_id=1, source_target_pairs={{0,4},{1,5},{2,6},{3,7},{4,0},{5,1},{6,2},{7,3},{8,12},{9,13},{10,... | collective-permute-start | bytes 1572872 | tf_op jit(solution)/shard_map/ppermute | solution.py:41
  78.2 34.7 %collective-permute-start.15 = (bf16[128,2048]{1,0:T(8,128)(2,1)S(1)}, bf16[128,2048]{1,0:T(8,128)(2,1)S(1)}, u32[]{:S(2)}, u32[]{:S(2)}) collective-permute-start(bf16[128,2048]{1,0:T(8,128)(2,1)S(1)} %copy-done.92), channel_id=1, source_target_pairs={{0,6},{1,7},{2,4},{3,5},{4,2},{5,3},{6,0},{7,1},{8,14},{9,15},{10,... | collective-permute-start | bytes 1572872 | tf_op jit(solution)/shard_map/ppermute | solution.py:41
  82.0 48.7 %collective-permute-start.37 = (bf16[128,2048]{1,0:T(8,128)(2,1)S(1)}, bf16[128,2048]{1,0:T(8,128)(2,1)S(1)}, u32[]{:S(2)}, u32[]{:S(2)}) collective-permute-start(bf16[128,2048]{1,0:T(8,128)(2,1)S(1)} %copy-done.91), channel_id=1, source_target_pairs={{0,4},{1,5},{2,6},{3,7},{4,0},{5,1},{6,2},{7,3},{8,12},{9,13},{10,... | collective-permute-start | bytes 1572872 | tf_op jit(solution)/shard_map/ppermute | solution.py:41
  98.0 32.8 %collective-permute-start.36 = (bf16[128,2048]{1,0:T(8,128)(2,1)S(1)}, bf16[128,2048]{1,0:T(8,128)(2,1)S(1)}, u32[]{:S(2)}, u32[]{:S(2)}) collective-permute-start(bf16[128,2048]{1,0:T(8,128)(2,1)S(1)} %copy-done.90), channel_id=1, source_target_pairs={{0,6},{1,7},{2,4},{3,5},{4,2},{5,3},{6,0},{7,1},{8,14},{9,15},{10,... | collective-permute-start | bytes 1572872 | tf_op jit(solution)/shard_map/ppermute | solution.py:41
  124.2 43.6 %collective-permute-start.43 = (bf16[512,1024]{1,0:T(8,128)(2,1)}, bf16[512,1024]{1,0:T(8,128)(2,1)}, u32[]{:S(2)}, u32[]{:S(2)}) collective-permute-start(bf16[512,1024]{1,0:T(8,128)(2,1)} %get-tuple-element.85), channel_id=1, source_target_pairs={{0,1},{1,0},{2,3},{3,2},{4,5},{5,4},{6,7},{7,6},{8,9},{9,8},{10,11... | collective-permute-start | bytes 3145736 | tf_op jit(solution)/shard_map/ppermute | solution.py:44
  126.9 14.4 %collective-permute-start.3 = (bf16[128,1024]{1,0:T(8,128)(2,1)}, bf16[128,1024]{1,0:T(8,128)(2,1)S(1)}, u32[]{:S(2)}, u32[]{:S(2)}) collective-permute-start(bf16[128,1024]{1,0:T(8,128)(2,1)} %fusion.101), channel_id=1, source_target_pairs={{0,6},{1,7},{2,4},{3,5},{4,2},{5,3},{6,0},{7,1},{8,14},{9,15},{10,... | collective-permute-start | bytes 786440 | tf_op jit(solution)/shard_map/ppermute | solution.py:41
  134.0 23.7 %collective-permute-start.51 = (bf16[128,1024]{1,0:T(8,128)(2,1)}, bf16[128,1024]{1,0:T(8,128)(2,1)}, u32[]{:S(2)}, u32[]{:S(2)}) collective-permute-start(bf16[128,1024]{1,0:T(8,128)(2,1)} %collective-permute-done.48), channel_id=1, source_target_pairs={{0,6},{1,7},{2,4},{3,5},{4,2},{5,3},{6,0},{7,1},{8,14},{9,15},{10,... | collective-permute-start | bytes 786440 | tf_op jit(solution)/shard_map/ppermute | solution.py:41
  141.3 21.6 %collective-permute-start.18 = (bf16[4,128,2048]{2,1,0:T(8,128)(2,1)}, bf16[4,128,2048]{2,1,0:T(8,128)(2,1)}, u32[]{:S(2)}, u32[]{:S(2)}) collective-permute-start(bf16[4,128,2048]{2,1,0:T(8,128)(2,1)} %pad_maximum_fusion.2), channel_id=1, source_target_pairs={{0,1},{1,0},{2,3},{3,2},{4,5},{5,4},{6,7},{7,6},{8,9},{9,8},{10,11... | collective-permute-start | bytes 6291464 | tf_op jit(solution)/shard_map/ppermute | solution.py:44
  161.7 34.1 %collective-permute-start.32 = (bf16[4,128,768]{1,2,0:T(8,128)(2,1)S(1)}, bf16[4,128,768]{1,2,0:T(8,128)(2,1)S(1)}, u32[]{:S(2)}, u32[]{:S(2)}) collective-permute-start(bf16[4,128,768]{1,2,0:T(8,128)(2,1)S(1)} %copy-done.87), channel_id=1, source_target_pairs={{0,1},{1,0},{2,3},{3,2},{4,5},{5,4},{6,7},{7,6},{8,9},{9,8},{10,11... | collective-permute-start | bytes 2359304 | tf_op jit(solution)/shard_map/ppermute | solution.py:44
  162.8 50.6 %collective-permute-start.39 = (bf16[4,128,2048]{2,1,0:T(8,128)(2,1)}, bf16[4,128,2048]{2,1,0:T(8,128)(2,1)}, u32[]{:S(2)}, u32[]{:S(2)}) collective-permute-start(bf16[4,128,2048]{2,1,0:T(8,128)(2,1)} %pad_maximum_fusion.4), channel_id=1, source_target_pairs={{0,1},{1,0},{2,3},{3,2},{4,5},{5,4},{6,7},{7,6},{8,9},{9,8},{10,11... | collective-permute-start | bytes 6291464 | tf_op jit(solution)/shard_map/ppermute | solution.py:44
  167.8 13.9 %collective-permute-start.20 = (bf16[128,1024]{1,0:T(8,128)(2,1)S(1)}, bf16[128,1024]{1,0:T(8,128)(2,1)S(1)}, u32[]{:S(2)}, u32[]{:S(2)}) collective-permute-start(bf16[128,1024]{1,0:T(8,128)(2,1)S(1)} %add_convert_fusion.23), channel_id=1, source_target_pairs={{0,4},{1,5},{2,6},{3,7},{4,0},{5,1},{6,2},{7,3},{8,12},{9,13},{10,... | collective-permute-start | bytes 786440 | tf_op jit(solution)/shard_map/ppermute | solution.py:41
  168.4 13.7 %collective-permute-start.19 = (bf16[128,1024]{1,0:T(8,128)(2,1)S(1)}, bf16[128,1024]{1,0:T(8,128)(2,1)S(1)}, u32[]{:S(2)}, u32[]{:S(2)}) collective-permute-start(bf16[128,1024]{1,0:T(8,128)(2,1)S(1)} %add_convert_fusion.23), channel_id=1, source_target_pairs={{0,2},{1,3},{2,0},{3,1},{4,6},{5,7},{6,4},{7,5},{8,10},{9,11},{10,... | collective-permute-start | bytes 786440 | tf_op jit(solution)/shard_map/ppermute | solution.py:41
  192.7 13.7 %collective-permute-start.25 = (bf16[128,1024]{1,0:T(8,128)(2,1)}, bf16[128,1024]{1,0:T(8,128)(2,1)S(1)}, u32[]{:S(2)}, u32[]{:S(2)}) collective-permute-start(bf16[128,1024]{1,0:T(8,128)(2,1)} %get-tuple-element.143), channel_id=1, source_target_pairs={{0,6},{1,7},{2,4},{3,5},{4,2},{5,3},{6,0},{7,1},{8,14},{9,15},{10,... | collective-permute-start | bytes 786440 | tf_op jit(solution)/shard_map/ppermute | solution.py:41
  270.3 14.4 %collective-permute-start.46 = (bf16[128,1024]{1,0:T(8,128)(2,1)S(1)}, bf16[128,1024]{1,0:T(8,128)(2,1)S(1)}, u32[]{:S(2)}, u32[]{:S(2)}) collective-permute-start(bf16[128,1024]{1,0:T(8,128)(2,1)S(1)} %get-tuple-element.136), channel_id=1, source_target_pairs={{0,6},{1,7},{2,4},{3,5},{4,2},{5,3},{6,0},{7,1},{8,14},{9,15},{10,... | collective-permute-start | bytes 786440 | tf_op jit(solution)/shard_map/ppermute | solution.py:41
  271.8 13.8 %collective-permute-start.45 = (bf16[128,1024]{1,0:T(8,128)(2,1)S(1)}, bf16[128,1024]{1,0:T(8,128)(2,1)S(1)}, u32[]{:S(2)}, u32[]{:S(2)}) collective-permute-start(bf16[128,1024]{1,0:T(8,128)(2,1)S(1)} %get-tuple-element.137), channel_id=1, source_target_pairs={{0,4},{1,5},{2,6},{3,7},{4,0},{5,1},{6,2},{7,3},{8,12},{9,13},{10,... | collective-permute-start | bytes 786440 | tf_op jit(solution)/shard_map/ppermute | solution.py:41
  277.2 17.2 %collective-permute-start.54 = (bf16[128,1024]{1,0:T(8,128)(2,1)S(1)}, bf16[128,1024]{1,0:T(8,128)(2,1)S(1)}, u32[]{:S(2)}, u32[]{:S(2)}) collective-permute-start(bf16[128,1024]{1,0:T(8,128)(2,1)S(1)} %get-tuple-element.133), channel_id=1, source_target_pairs={{0,6},{1,7},{2,4},{3,5},{4,2},{5,3},{6,0},{7,1},{8,14},{9,15},{10,... | collective-permute-start | bytes 786440 | tf_op jit(solution)/shard_map/ppermute | solution.py:41
  281.4 14.3 %collective-permute-start.53 = (bf16[128,1024]{1,0:T(8,128)(2,1)S(1)}, bf16[128,1024]{1,0:T(8,128)(2,1)S(1)}, u32[]{:S(2)}, u32[]{:S(2)}) collective-permute-start(bf16[128,1024]{1,0:T(8,128)(2,1)S(1)} %get-tuple-element.134), channel_id=1, source_target_pairs={{0,4},{1,5},{2,6},{3,7},{4,0},{5,1},{6,2},{7,3},{8,12},{9,13},{10,... | collective-permute-start | bytes 786440 | tf_op jit(solution)/shard_map/ppermute | solution.py:41
  284.6 86.2 %collective-permute-start.120 = (bf16[512,1024]{1,0:T(8,128)(2,1)}, bf16[512,1024]{1,0:T(8,128)(2,1)}, u32[]{:S(2)}, u32[]{:S(2)}) collective-permute-start(bf16[512,1024]{1,0:T(8,128)(2,1)} %dynamic-slice_bitcast_fusion), channel_id=1, source_target_pairs={{0,1},{1,0},{2,3},{3,2},{4,5},{5,4},{6,7},{7,6},{8,9},{9,8},{10,11... | collective-permute-start | bytes 3145736 | tf_op jit(solution)/shard_map/ppermute | solution.py:44
  305.8 23.9 %collective-permute-start.47 = (bf16[128,1024]{1,0:T(8,128)(2,1)}, bf16[128,1024]{1,0:T(8,128)(2,1)}, u32[]{:S(2)}, u32[]{:S(2)}) collective-permute-start(bf16[128,1024]{1,0:T(8,128)(2,1)} %get-tuple-element.187), channel_id=1, source_target_pairs={{0,0},{1,1},{2,8},{3,9},{4,16},{5,17},{6,24},{7,25},{8,2},{9,3},{1... | collective-permute-start | bytes 786440 | tf_op jit(solution)/shard_map/ppermute | solution.py:38
  329.7 36.8 %collective-permute-start.109 = (bf16[4,128,1024]{2,1,0:T(8,128)(2,1)}, bf16[4,128,1024]{2,1,0:T(8,128)(2,1)}, u32[]{:S(2)}, u32[]{:S(2)}) collective-permute-start(bf16[4,128,1024]{2,1,0:T(8,128)(2,1)} %dynamic-slice_bitcast_fusion.2), channel_id=1, source_target_pairs={{0,1},{1,0},{2,3},{3,2},{4,5},{5,4},{6,7},{7,6},{8,9},{9,8},{10,11... | collective-permute-start | bytes 3145736 | tf_op jit(solution)/shard_map/ppermute | solution.py:44
  347.0 70.1 %collective-permute-start.95 = (bf16[4,128,1024]{2,1,0:T(8,128)(2,1)}, bf16[4,128,1024]{2,1,0:T(8,128)(2,1)}, u32[]{:S(2)}, u32[]{:S(2)}) collective-permute-start(bf16[4,128,1024]{2,1,0:T(8,128)(2,1)} %dynamic-slice_bitcast_fusion.4), channel_id=1, source_target_pairs={{0,1},{1,0},{2,3},{3,2},{4,5},{5,4},{6,7},{7,6},{8,9},{9,8},{10,11... | collective-permute-start | bytes 3145736 | tf_op jit(solution)/shard_map/ppermute | solution.py:44
  349.7 24.8 %collective-permute-start.81 = (bf16[4,128,768]{2,1,0:T(8,128)(2,1)}, bf16[4,128,768]{2,1,0:T(8,128)(2,1)}, u32[]{:S(2)}, u32[]{:S(2)}) collective-permute-start(bf16[4,128,768]{2,1,0:T(8,128)(2,1)} %dynamic-slice_bitcast_fusion.6), channel_id=1, source_target_pairs={{0,1},{1,0},{2,3},{3,2},{4,5},{5,4},{6,7},{7,6},{8,9},{9,8},{10,11... | collective-permute-start | bytes 2359304 | tf_op jit(solution)/shard_map/ppermute | solution.py:44
  357.9 22.9 %collective-permute-start.64 = (bf16[128,1024]{1,0:T(8,128)(2,1)}, bf16[128,1024]{1,0:T(8,128)(2,1)}, u32[]{:S(2)}, u32[]{:S(2)}) collective-permute-start(bf16[128,1024]{1,0:T(8,128)(2,1)} %get-tuple-element.126), channel_id=1, source_target_pairs={{0,2},{1,3},{2,0},{3,1},{4,6},{5,7},{6,4},{7,5},{8,10},{9,11},{10,... | collective-permute-start | bytes 786440 | tf_op jit(solution)/shard_map/ppermute | solution.py:41
  366.5 14.3 %collective-permute-start.66 = (bf16[128,1024]{1,0:T(8,128)(2,1)}, bf16[128,1024]{1,0:T(8,128)(2,1)}, u32[]{:S(2)}, u32[]{:S(2)}) collective-permute-start(bf16[128,1024]{1,0:T(8,128)(2,1)} %get-tuple-element.127), channel_id=1, source_target_pairs={{0,6},{1,7},{2,4},{3,5},{4,2},{5,3},{6,0},{7,1},{8,14},{9,15},{10,... | collective-permute-start | bytes 786440 | tf_op jit(solution)/shard_map/ppermute | solution.py:41
  374.5 145.1 %collective-permute-start.116 = (bf16[512,1024]{1,0:T(8,128)(2,1)}, bf16[512,1024]{1,0:T(8,128)(2,1)}, u32[]{:S(2)}, u32[]{:S(2)}) collective-permute-start(bf16[512,1024]{1,0:T(8,128)(2,1)} %dynamic-slice_bitcast_fusion.1), channel_id=1, source_target_pairs={{0,1},{1,0},{2,3},{3,2},{4,5},{5,4},{6,7},{7,6},{8,9},{9,8},{10,11... | collective-permute-start | bytes 3145736 | tf_op jit(solution)/shard_map/ppermute | solution.py:44
  393.2 18.9 %collective-permute-start.112 = (bf16[128,1024]{1,0:T(8,128)(2,1)}, bf16[128,1024]{1,0:T(8,128)(2,1)}, u32[]{:S(2)}, u32[]{:S(2)}) collective-permute-start(bf16[128,1024]{1,0:T(8,128)(2,1)} %get-tuple-element.114), channel_id=1, source_target_pairs={{0,2},{1,3},{2,0},{3,1},{4,6},{5,7},{6,4},{7,5},{8,10},{9,11},{10,... | collective-permute-start | bytes 786440 | tf_op jit(solution)/shard_map/ppermute | solution.py:41
  394.2 18.0 %collective-permute-start.111 = (bf16[128,1024]{1,0:T(8,128)(2,1)}, bf16[128,1024]{1,0:T(8,128)(2,1)}, u32[]{:S(2)}, u32[]{:S(2)}) collective-permute-start(bf16[128,1024]{1,0:T(8,128)(2,1)} %get-tuple-element.115), channel_id=1, source_target_pairs={{0,4},{1,5},{2,6},{3,7},{4,0},{5,1},{6,2},{7,3},{8,12},{9,13},{10,... | collective-permute-start | bytes 786440 | tf_op jit(solution)/shard_map/ppermute | solution.py:41
  395.7 18.5 %collective-permute-start.110 = (bf16[128,1024]{1,0:T(8,128)(2,1)}, bf16[128,1024]{1,0:T(8,128)(2,1)}, u32[]{:S(2)}, u32[]{:S(2)}) collective-permute-start(bf16[128,1024]{1,0:T(8,128)(2,1)} %get-tuple-element.116), channel_id=1, source_target_pairs={{0,6},{1,7},{2,4},{3,5},{4,2},{5,3},{6,0},{7,1},{8,14},{9,15},{10,... | collective-permute-start | bytes 786440 | tf_op jit(solution)/shard_map/ppermute | solution.py:41
  412.1 103.2 %collective-permute-start.102 = (bf16[4,128,1024]{2,1,0:T(8,128)(2,1)}, bf16[4,128,1024]{2,1,0:T(8,128)(2,1)}, u32[]{:S(2)}, u32[]{:S(2)}) collective-permute-start(bf16[4,128,1024]{2,1,0:T(8,128)(2,1)} %dynamic-slice_bitcast_fusion.3), channel_id=1, source_target_pairs={{0,1},{1,0},{2,3},{3,2},{4,5},{5,4},{6,7},{7,6},{8,9},{9,8},{10,11... | collective-permute-start | bytes 3145736 | tf_op jit(solution)/shard_map/ppermute | solution.py:44
  430.8 47.4 %collective-permute-start.96 = (bf16[128,1024]{1,0:T(8,128)(2,1)}, bf16[128,1024]{1,0:T(8,128)(2,1)S(1)}, u32[]{:S(2)}, u32[]{:S(2)}) collective-permute-start(bf16[128,1024]{1,0:T(8,128)(2,1)} %get-tuple-element.120), channel_id=1, source_target_pairs={{0,2},{1,3},{2,0},{3,1},{4,6},{5,7},{6,4},{7,5},{8,10},{9,11},{10,... | collective-permute-start | bytes 786440 | tf_op jit(solution)/shard_map/ppermute | solution.py:41
  437.3 42.3 %collective-permute-start.98 = (bf16[128,1024]{1,0:T(8,128)(2,1)S(1)}, bf16[128,1024]{1,0:T(8,128)(2,1)S(1)}, u32[]{:S(2)}, u32[]{:S(2)}) collective-permute-start(bf16[128,1024]{1,0:T(8,128)(2,1)S(1)} %get-tuple-element.121), channel_id=1, source_target_pairs={{0,6},{1,7},{2,4},{3,5},{4,2},{5,3},{6,0},{7,1},{8,14},{9,15},{10,... | collective-permute-start | bytes 786440 | tf_op jit(solution)/shard_map/ppermute | solution.py:41
  440.0 41.2 %collective-permute-start.97 = (bf16[128,1024]{1,0:T(8,128)(2,1)S(1)}, bf16[128,1024]{1,0:T(8,128)(2,1)}, u32[]{:S(2)}, u32[]{:S(2)}) collective-permute-start(bf16[128,1024]{1,0:T(8,128)(2,1)S(1)} %get-tuple-element.122), channel_id=1, source_target_pairs={{0,4},{1,5},{2,6},{3,7},{4,0},{5,1},{6,2},{7,3},{8,12},{9,13},{10,... | collective-permute-start | bytes 786440 | tf_op jit(solution)/shard_map/ppermute | solution.py:41
  478.2 62.7 %collective-permute-start.121 = (bf16[512,1024]{1,0:T(8,128)(2,1)S(1)}, bf16[512,1024]{1,0:T(8,128)(2,1)}, u32[]{:S(2)}, u32[]{:S(2)}) collective-permute-start(bf16[512,1024]{1,0:T(8,128)(2,1)S(1)} %copy-done.31), channel_id=1, source_target_pairs={{0,8},{24,16},{1,9},{25,17},{2,10},{26,18},{3,11},{27,19},{4,12},{... | collective-permute-start | bytes 3145736 | tf_op jit(solution)/shard_map/ppermute | solution.py:76
  482.4 32.8 %collective-permute-start.99 = (bf16[128,1024]{1,0:T(8,128)(2,1)S(1)}, bf16[128,1024]{1,0:T(8,128)(2,1)S(1)}, u32[]{:S(2)}, u32[]{:S(2)}) collective-permute-start(bf16[128,1024]{1,0:T(8,128)(2,1)S(1)} %fusion.111), channel_id=1, source_target_pairs={{0,8},{24,16},{1,9},{25,17},{2,10},{26,18},{3,11},{27,19},{4,12},{... | collective-permute-start | bytes 786440 | tf_op jit(solution)/shard_map/ppermute | solution.py:76
  485.4 59.7 %collective-permute-start.88 = (bf16[4,128,1024]{2,1,0:T(8,128)(2,1)}, bf16[4,128,1024]{2,1,0:T(8,128)(2,1)}, u32[]{:S(2)}, u32[]{:S(2)}) collective-permute-start(bf16[4,128,1024]{2,1,0:T(8,128)(2,1)} %dynamic-slice_bitcast_fusion.5), channel_id=1, source_target_pairs={{0,1},{1,0},{2,3},{3,2},{4,5},{5,4},{6,7},{7,6},{8,9},{9,8},{10,11... | collective-permute-start | bytes 3145736 | tf_op jit(solution)/shard_map/ppermute | solution.py:44
  515.3 22.7 %collective-permute-start.85 = (bf16[128,3072]{0,1:T(8,128)(2,1)}, bf16[128,3072]{0,1:T(8,128)(2,1)}, u32[]{:S(2)}, u32[]{:S(2)}) collective-permute-start(bf16[128,3072]{0,1:T(8,128)(2,1)} %bitcast.146), channel_id=1, source_target_pairs={{0,8},{24,16},{1,9},{25,17},{2,10},{26,18},{3,11},{27,19},{4,12},{... | collective-permute-start | bytes 2359304 | tf_op jit(solution)/shard_map/ppermute | solution.py:76
  519.6 63.9 %collective-permute-start.113 = (bf16[128,4096]{1,0:T(8,128)(2,1)}, bf16[128,4096]{1,0:T(8,128)(2,1)}, u32[]{:S(2)}, u32[]{:S(2)}) collective-permute-start(bf16[128,4096]{1,0:T(8,128)(2,1)} %pad_maximum_fusion.22), channel_id=1, source_target_pairs={{0,8},{24,16},{1,9},{25,17},{2,10},{26,18},{3,11},{27,19},{4,12},{... | collective-permute-start | bytes 3145736 | tf_op jit(solution)/shard_map/ppermute | solution.py:76
  522.5 20.8 %collective-permute-start.100 = (bf16[128,1024]{1,0:T(8,128)(2,1)S(1)}, bf16[128,1024]{1,0:T(8,128)(2,1)}, u32[]{:S(2)}, u32[]{:S(2)}) collective-permute-start(bf16[128,1024]{1,0:T(8,128)(2,1)S(1)} %fusion.116), channel_id=1, source_target_pairs={{8,16},{16,8},{9,17},{17,9},{10,18},{18,10},{11,19},{19,11},{12,20... | collective-permute-start | bytes 786440 | tf_op jit(solution)/shard_map/ppermute | solution.py:79
  537.9 95.8 %collective-permute-start.117 = (bf16[512,1024]{1,0:T(8,128)(2,1)S(1)}, bf16[512,1024]{1,0:T(8,128)(2,1)S(1)}, u32[]{:S(2)}, u32[]{:S(2)}) collective-permute-start(bf16[512,1024]{1,0:T(8,128)(2,1)S(1)} %fusion.11), channel_id=1, source_target_pairs={{0,8},{24,16},{1,9},{25,17},{2,10},{26,18},{3,11},{27,19},{4,12},{... | collective-permute-start | bytes 3145736 | tf_op jit(solution)/shard_map/ppermute | solution.py:76
  552.2 14.0 %collective-permute-start.104 = (bf16[128,1024]{1,0:T(8,128)(2,1)S(1)}, bf16[128,1024]{1,0:T(8,128)(2,1)S(1)}, u32[]{:S(2)}, u32[]{:S(2)}) collective-permute-start(bf16[128,1024]{1,0:T(8,128)(2,1)S(1)} %copy-done.95), channel_id=1, source_target_pairs={{0,4},{1,5},{2,6},{3,7},{4,0},{5,1},{6,2},{7,3},{8,12},{9,13},{10,... | collective-permute-start | bytes 786440 | tf_op jit(solution)/shard_map/ppermute | solution.py:41
  568.8 75.4 %collective-permute-start.122 = (bf16[512,1024]{1,0:T(8,128)(2,1)S(1)}, bf16[512,1024]{1,0:T(8,128)(2,1)S(1)}, u32[]{:S(2)}, u32[]{:S(2)}) collective-permute-start(bf16[512,1024]{1,0:T(8,128)(2,1)S(1)} %fusion.49), channel_id=1, source_target_pairs={{8,16},{16,8},{9,17},{17,9},{10,18},{18,10},{11,19},{19,11},{12,20... | collective-permute-start | bytes 3145736 | tf_op jit(solution)/shard_map/ppermute | solution.py:79
  574.9 36.5 %collective-permute-start.86 = (bf16[128,3072]{0,1:T(8,128)(2,1)S(1)}, bf16[128,3072]{0,1:T(8,128)(2,1)S(1)}, u32[]{:S(2)}, u32[]{:S(2)}) collective-permute-start(bf16[128,3072]{0,1:T(8,128)(2,1)S(1)} %fusion.91), channel_id=1, source_target_pairs={{8,16},{16,8},{9,17},{17,9},{10,18},{18,10},{11,19},{19,11},{12,20... | collective-permute-start | bytes 2359304 | tf_op jit(solution)/shard_map/ppermute | solution.py:79
  587.6 73.1 %collective-permute-start.106 = (bf16[128,4096]{1,0:T(8,128)(2,1)S(1)}, bf16[128,4096]{1,0:T(8,128)(2,1)S(1)}, u32[]{:S(2)}, u32[]{:S(2)}) collective-permute-start(bf16[128,4096]{1,0:T(8,128)(2,1)S(1)} %pad_maximum_fusion.21), channel_id=1, source_target_pairs={{0,8},{24,16},{1,9},{25,17},{2,10},{26,18},{3,11},{27,19},{4,12},{... | collective-permute-start | bytes 3145736 | tf_op jit(solution)/shard_map/ppermute | solution.py:76
  594.0 37.3 %collective-permute-start.78 = (bf16[128,3072]{0,1:T(8,128)(2,1)S(1)}, bf16[128,3072]{0,1:T(8,128)(2,1)S(1)}, u32[]{:S(2)}, u32[]{:S(2)}) collective-permute-start(bf16[128,3072]{0,1:T(8,128)(2,1)S(1)} %bitcast.439), channel_id=1, source_target_pairs={{0,8},{24,16},{1,9},{25,17},{2,10},{26,18},{3,11},{27,19},{4,12},{... | collective-permute-start | bytes 2359304 | tf_op jit(solution)/shard_map/ppermute | solution.py:76
  611.4 51.1 %collective-permute-start.114 = (bf16[128,4096]{1,0:T(8,128)(2,1)S(1)}, bf16[128,4096]{1,0:T(8,128)(2,1)S(1)}, u32[]{:S(2)}, u32[]{:S(2)}) collective-permute-start(bf16[128,4096]{1,0:T(8,128)(2,1)S(1)} %fusion.47), channel_id=1, source_target_pairs={{8,16},{16,8},{9,17},{17,9},{10,18},{18,10},{11,19},{19,11},{12,20... | collective-permute-start | bytes 3145736 | tf_op jit(solution)/shard_map/ppermute | solution.py:79
  633.7 32.7 %collective-permute-start.87 = (bf16[128,3072]{0,1:T(8,128)(2,1)S(1)}, bf16[128,3072]{0,1:T(8,128)(2,1)S(1)}, u32[]{:S(2)}, u32[]{:S(2)}) collective-permute-start(bf16[128,3072]{0,1:T(8,128)(2,1)S(1)} %add_convert_fusion.10), channel_id=1, source_target_pairs={{8,0},{16,24},{9,1},{17,25},{10,2},{18,26},{11,3},{19,27},{12,4},{... | collective-permute-start | bytes 2359304 | tf_op jit(solution)/shard_map/ppermute | solution.py:82
  641.9 46.4 %collective-permute-start.118 = (bf16[512,1024]{1,0:T(8,128)(2,1)S(1)}, bf16[512,1024]{1,0:T(8,128)(2,1)S(1)}, u32[]{:S(2)}, u32[]{:S(2)}) collective-permute-start(bf16[512,1024]{1,0:T(8,128)(2,1)S(1)} %fusion.48), channel_id=1, source_target_pairs={{8,16},{16,8},{9,17},{17,9},{10,18},{18,10},{11,19},{19,11},{12,20... | collective-permute-start | bytes 3145736 | tf_op jit(solution)/shard_map/ppermute | solution.py:79
  655.9 30.8 %collective-permute-start.79 = (bf16[128,3072]{0,1:T(8,128)(2,1)S(1)}, bf16[128,3072]{0,1:T(8,128)(2,1)S(1)}, u32[]{:S(2)}, u32[]{:S(2)}) collective-permute-start(bf16[128,3072]{0,1:T(8,128)(2,1)S(1)} %fusion.90), channel_id=1, source_target_pairs={{8,16},{16,8},{9,17},{17,9},{10,18},{18,10},{11,19},{19,11},{12,20... | collective-permute-start | bytes 2359304 | tf_op jit(solution)/shard_map/ppermute | solution.py:79
  660.6 31.4 %collective-permute-start.123 = (bf16[512,1024]{1,0:T(8,128)(2,1)S(1)}, bf16[512,1024]{1,0:T(8,128)(2,1)S(1)}, u32[]{:S(2)}, u32[]{:S(2)}) collective-permute-start(bf16[512,1024]{1,0:T(8,128)(2,1)S(1)} %add_convert_fusion), channel_id=1, source_target_pairs={{8,0},{16,24},{9,1},{17,25},{10,2},{18,26},{11,3},{19,27},{12,4},{... | collective-permute-start | bytes 3145736 | tf_op jit(solution)/shard_map/ppermute | solution.py:82
  662.5 43.3 %collective-permute-start.107 = (bf16[128,4096]{1,0:T(8,128)(2,1)S(1)}, bf16[128,4096]{1,0:T(8,128)(2,1)S(1)}, u32[]{:S(2)}, u32[]{:S(2)}) collective-permute-start(bf16[128,4096]{1,0:T(8,128)(2,1)S(1)} %fusion.46), channel_id=1, source_target_pairs={{8,16},{16,8},{9,17},{17,9},{10,18},{18,10},{11,19},{19,11},{12,20... | collective-permute-start | bytes 3145736 | tf_op jit(solution)/shard_map/ppermute | solution.py:79
  666.5 42.9 %collective-permute-start.115 = (bf16[128,4096]{1,0:T(8,128)(2,1)S(1)}, bf16[128,4096]{1,0:T(8,128)(2,1)S(1)}, u32[]{:S(2)}, u32[]{:S(2)}) collective-permute-start(bf16[128,4096]{1,0:T(8,128)(2,1)S(1)} %add_convert_fusion.4), channel_id=1, source_target_pairs={{8,0},{16,24},{9,1},{17,25},{10,2},{18,26},{11,3},{19,27},{12,4},{... | collective-permute-start | bytes 3145736 | tf_op jit(solution)/shard_map/ppermute | solution.py:82
  687.0 38.1 %collective-permute-start.80 = (bf16[128,3072]{0,1:T(8,128)(2,1)S(1)}, bf16[128,3072]{0,1:T(8,128)(2,1)S(1)}, u32[]{:S(2)}, u32[]{:S(2)}) collective-permute-start(bf16[128,3072]{0,1:T(8,128)(2,1)S(1)} %add_convert_fusion.12), channel_id=1, source_target_pairs={{8,0},{16,24},{9,1},{17,25},{10,2},{18,26},{11,3},{19,27},{12,4},{... | collective-permute-start | bytes 2359304 | tf_op jit(solution)/shard_map/ppermute | solution.py:82
  689.7 57.9 %collective-permute-start.119 = (bf16[512,1024]{1,0:T(8,128)(2,1)}, bf16[512,1024]{1,0:T(8,128)(2,1)}, u32[]{:S(2)}, u32[]{:S(2)}) collective-permute-start(bf16[512,1024]{1,0:T(8,128)(2,1)} %add_convert_fusion.2), channel_id=1, source_target_pairs={{8,0},{16,24},{9,1},{17,25},{10,2},{18,26},{11,3},{19,27},{12,4},{... | collective-permute-start | bytes 3145736 | tf_op jit(solution)/shard_map/ppermute | solution.py:82
  707.1 59.4 %collective-permute-start.108 = (bf16[128,4096]{1,0:T(8,128)(2,1)}, bf16[128,4096]{1,0:T(8,128)(2,1)}, u32[]{:S(2)}, u32[]{:S(2)}) collective-permute-start(bf16[128,4096]{1,0:T(8,128)(2,1)} %add_convert_fusion.6), channel_id=1, source_target_pairs={{8,0},{16,24},{9,1},{17,25},{10,2},{18,26},{11,3},{19,27},{12,4},{... | collective-permute-start | bytes 3145736 | tf_op jit(solution)/shard_map/ppermute | solution.py:82
  (270 other events, 2711.4 us)

commit v2 on v1

v2 whole, which is shorter than its diff:
```python
import jax
import jax.numpy as jnp
from jax import lax
from jax.experimental import pallas as pl
from jax.experimental.pallas import tpu as pltpu
from jax.sharding import PartitionSpec as P

D = 1024
HEAD_DIM = 64
FF = 4096
EPS = 1e-05
NEG = -1e30
SCALE = 0.125
BF = jnp.bfloat16
F32 = jnp.float32
LANES = 128


def xor_pairs(count, mask):
    return [(i, i ^ mask) for i in range(count)]


class Net:
    def __init__(self):
        self.n_s = lax.axis_size("seq")
        self.n_f = lax.axis_size("fsdp")
        self.n_p = self.n_f // 2
        self.s = lax.axis_index("seq")
        self.f = lax.axis_index("fsdp")
        self.p = self.f // 2
        self.c = self.f % 2
        self.place = jnp.stack([self.p, self.c]).astype(jnp.int32)

    def pairs(self):
        n = self.n_f
        return [
            (s * n + f, (f // 2) * n + 2 * ((f // 2) ^ s) + f % 2) for s in range(self.n_s) for f in range(n)
        ]

    def to_planes(self, v):
        return lax.ppermute(v, ("seq", "fsdp"), self.pairs())

    def from_planes(self, v):
        return lax.ppermute(v, ("seq", "fsdp"), [(b, a) for a, b in self.pairs()])

    def chip(self, v, j):
        return lax.ppermute(v, "fsdp", xor_pairs(self.n_f, 2 * j))

    def core(self, v):
        return lax.ppermute(v, "fsdp", xor_pairs(self.n_f, 1))

    def gather(self, v):
        return [v] + [self.chip(v, j) for j in range(1, self.n_p)]

    def exchange(self, blocks):
        return [blocks[0]] + [self.chip(blocks[j], j) for j in range(1, self.n_p)]


def fence(values):
    return lax.optimization_barrier(values)


def block(v, index, size, axis):
    return lax.dynamic_slice_in_dim(v, index * size, size, axis=axis)


IN_VMEM = pl.BlockSpec(memory_space=pltpu.VMEM)
IN_SMEM = pl.BlockSpec(memory_space=pltpu.SMEM)
IN_ANY = pl.BlockSpec(memory_space=pl.ANY)


def run(name, body, outs, ins, place=None, scratch=(), flops=0, ins_at=IN_VMEM):
    specs = [ins_at] * len(ins)
    if place is not None:
        specs = [IN_SMEM] + specs
        ins = [place, *ins]
    moved = sum(v.size * v.dtype.itemsize for v in ins)
    return pl.pallas_call(
        body,
        out_shape=[jax.ShapeDtypeStruct(shape, dtype) for shape, dtype in outs],
        in_specs=specs,
        out_specs=[IN_VMEM] * len(outs),
        scratch_shapes=list(scratch),
        compiler_params=pltpu.CompilerParams(vmem_limit_bytes=16 << 20),
        cost_estimate=pl.CostEstimate(flops=flops, bytes_accessed=moved, transcendentals=0),
        name=name,
    )(*ins)


def dot(a, b):
    return jnp.dot(a, b, preferred_element_type=F32)


def dot_nt(a, b):
    return lax.dot_general(a, b, (((1,), (1,)), ((), ())), preferred_element_type=F32)


def dot_tn(a, b):
    return lax.dot_general(a, b, (((0,), (0,)), ((), ())), preferred_element_type=F32)


def tile(i, size):
    return pl.ds(pl.multiple_of(i * size, size), size)


def join_weights(net, own, other, own_pair, other_pair):
    n_p = net.n_p
    rows, width = D // net.n_f, own[0].shape[1]
    half, depth = own_pair.shape
    count = 2 * n_p + 2

    def body(place, *refs):
        p, c = place[0], place[1]
        whole, pair, sems = refs[count:]
        copies = []
        for j in range(n_p):
            at = (p ^ j) * 2
            copies.append((refs[j].at[0:rows], whole.at[tile(at + c, rows)]))
            copies.append((refs[n_p + j].at[0:rows], whole.at[tile(at + 1 - c, rows)]))
        copies.append((refs[2 * n_p], pair.at[tile(c, half)]))
        copies.append((refs[2 * n_p + 1], pair.at[tile(1 - c, half)]))
        copies = [pltpu.make_async_copy(src, dst, sems.at[k]) for k, (src, dst) in enumerate(copies)]
        for copy in copies:
            copy.start()
        for copy in copies:
            copy.wait()

    outs = [((2 * n_p * rows, width), BF), ((2 * half, depth), BF)]
    ins = [*own, *other, own_pair, other_pair]
    return run("join_weights", body, outs, ins, net.place, [pltpu.SemaphoreType.DMA((count,))], ins_at=IN_ANY)


def cut_columns(net, weight, layer, more):
    n_p = net.n_p
    cw = D // n_p
    rows = weight.shape[1]
    extra = 0 if more is None else more.shape[0]
    count = n_p * (3 + (extra > 0))

    def body(place, weight_ref, *refs):
        p = place[0]
        outs, sems = refs[-n_p - 1 : -1], refs[-1]
        copies = []
        for j in range(n_p):
            for i in range(3):
                cols = tile(i * n_p + (p ^ j), cw)
                to = outs[j].at[0:rows, i * cw : (i + 1) * cw]
                copies.append((weight_ref.at[layer, :, cols], to))
            if extra:
                copies.append((refs[0], outs[j].at[rows : rows + extra]))
        copies = [pltpu.make_async_copy(src, dst, sems.at[k]) for k, (src, dst) in enumerate(copies)]
        for copy in copies:
            copy.start()
        for copy in copies:
            copy.wait()

    outs = [((rows + extra, 3 * cw), BF)] * n_p
    ins = [weight] + ([more] if extra else [])
    scratch = [pltpu.SemaphoreType.DMA((count,))]
    return run("cut_columns", body, outs, ins, net.place, scratch, ins_at=IN_ANY)


def join_vectors(net, layers, pieces, sizes):
    n_p = net.n_p
    width = pieces[0].shape[1]
    starts = [sum(sizes[:i]) for i in range(len(sizes))]
    first_row = D // net.n_f

    def body(place, *refs):
        p, c = place[0], place[1]
        ins, outs = refs[:n_p], refs[n_p:]
        for j in range(n_p):
            low = ins[j][first_row : first_row + 16, :].astype(F32)
            for layer in range(layers):
                for half in range(2):
                    row = layer * 2 + half
                    own = low[row : row + 1, :]
                    other = low[2 * layers + row : 2 * layers + row + 1, :]
                    first = jnp.where(c == 0, own, other)
                    second = jnp.where(c == 0, other, own)
                    for k, (at, size) in enumerate(zip(starts, sizes)):
                        if at // width != half:
                            continue
                        cols = slice(at - half * width, at - half * width + size)
                        both = jnp.concatenate([first[:, cols], second[:, cols]], axis=1)
                        outs[k][layer : layer + 1, tile(p ^ j, 2 * size)] = both

    outs = [((layers, 2 * n_p * size), F32) for size in sizes]
    return run("join_vectors", body, outs, pieces, net.place)


def first_norm(tokens, more, gain, shift):
    rows = tokens.shape[0] - more

    def body(token_ref, gain_ref, shift_ref, out, low):
        hidden = token_ref[0:rows, :].astype(F32)
        normed, _ = norm_rows(hidden)
        out[...] = hidden
        low[0:rows, :] = (normed * gain_ref[0:1, :] + shift_ref[0:1, :]).astype(BF)
        low[rows:, :] = token_ref[rows:, :]

    outs = [((rows, D), F32), (tokens.shape, BF)]
    return run("first_norm", body, outs, [tokens, gain, shift])


def norm_rows(hidden):
    centred = hidden - jnp.mean(hidden, axis=-1, keepdims=True)
    spread = jnp.mean(centred * centred, axis=-1, keepdims=True)
    inverse = lax.rsqrt(spread + EPS)
    return centred * inverse, inverse


def add_and_norm(layer, hidden, parts, bias, norm):
    rows = hidden.shape[0]
    count = len(parts)

    def body(*refs):
        total = refs[0][...].astype(F32)
        for part in refs[1 : 1 + count]:
            total = total + part[...].astype(F32)
        at = 1 + count
        if bias is not None:
            total = total + refs[at][layer : layer + 1, :]
            at += 1
        if norm is None:
            refs[at][...] = total.astype(BF)
            return
        gain, shift, out, low = refs[at : at + 4]
        normed, _ = norm_rows(total)
        row = slice(norm[0], norm[0] + 1)
        out[...] = total
        low[...] = (normed * gain[row, :] + shift[row, :]).astype(BF)

    ins = [hidden, *parts] + ([] if bias is None else [bias]) + ([] if norm is None else list(norm[1:]))
    outs = [((rows, D), BF)] if norm is None else [((rows, D), F32), ((rows, D), BF)]
    return run("add_and_norm", body, outs, ins)


def norm_back(layer, grad, hidden, parts, gain):
    rows = hidden.shape[0]
    count = len(parts)

    def body(grad_ref, hidden_ref, gain_ref, *refs):
        total = refs[0][...].astype(F32)
        for part in refs[1:count]:
            total = total + part[...].astype(F32)
        out, low, sums = refs[count:]
        normed, inverse = norm_rows(hidden_ref[...])
        scaled = total * gain_ref[layer : layer + 1, :]
        one = jnp.mean(scaled, axis=-1, keepdims=True)
        two = jnp.mean(scaled * normed, axis=-1, keepdims=True)
        result = grad_ref[...].astype(F32) + inverse * (scaled - one - normed * two)
        rounded = result.astype(BF)
        out[...] = result
        low[...] = rounded
        sums[0:1, :] = jnp.sum(total * normed, axis=0, keepdims=True)
        sums[1:2, :] = jnp.sum(total, axis=0, keepdims=True)
        sums[2:3, :] = jnp.sum(rounded.astype(F32), axis=0, keepdims=True)

    outs = [((rows, D), F32), ((rows, D), BF), ((3, D), F32)]
    return run("norm_back", body, outs, [grad, hidden, gain, *parts])


def gather_rows(blocks, scratch):
    rows = scratch.shape[0] // len(blocks)
    for j, ref in enumerate(blocks):
        scratch[j * rows : (j + 1) * rows, :] = ref[0:rows, :]


def allowed_pairs(code_col, code_row):
    same = (code_col >> 1) == (code_row >> 1)
    return same & (((code_col & 1) == 0) | ((code_row & 1) == 1))


def head_lanes(shape, head, axis):
    lane = lax.broadcasted_iota(jnp.int32, shape, axis)
    return (lane < HEAD_DIM) if head == 0 else (lane >= HEAD_DIM)


def keep_head(v, head, axis):
    return jnp.where(head_lanes(v.shape, head, axis), v, jnp.zeros_like(v))


def probs_by_key(k2, q2, allowed, head):
    scores = dot_nt(keep_head(k2, head, 1), q2) * SCALE
    scores = jnp.where(allowed, scores, NEG)
    powers = jnp.exp(scores - jnp.max(scores, axis=0, keepdims=True))
    return powers * (1.0 / jnp.sum(powers, axis=0, keepdims=True))


Q_TILE = 256


def attend(net, layer, rows, blocks, weight, bias, codes, proj):
    n_p = net.n_p
    tokens = n_p * rows
    cw = D // n_p
    n_codes = 0 if codes is None else 2

    def body(place, *refs):
        weight_ref, bias_ref, proj_ref = refs[n_p : n_p + 3]
        row_ref, col_ref = refs[n_p + 3 : n_p + 5]
        outs = refs[n_p + 5 : 2 * n_p + 5]
        qkv, attended, a, vt = refs[2 * n_p + 5 :]
        p = place[0]
        gather_rows(refs[:n_p], a)
        if codes is None:
            eye = lax.broadcasted_iota(jnp.int32, (rows, rows), 0) == lax.broadcasted_iota(
                jnp.int32, (rows, rows), 1
            )
            for j in range(n_p):
                line = refs[j][rows : rows + 1, 0:rows].astype(F32)
                row_ref[:, j * rows : (j + 1) * rows] = line.astype(jnp.int32)
                column = jnp.sum(jnp.where(eye, line, 0.0), axis=1, keepdims=True)
                col_ref[j * rows : (j + 1) * rows, :] = column.astype(jnp.int32)
        for i in range(3):
            out = dot(a[...], weight_ref[:, i * cw : (i + 1) * cw])
            if i == 0:
                out = out + bias_ref[layer : layer + 1, tile(p, cw)]
            if i == 2:
                out = out + bias_ref[layer : layer + 1, tile(p + n_p, cw)]
            qkv[:, i * cw : (i + 1) * cw] = out.astype(BF)
        vt[...] = jnp.transpose(qkv[:, 2 * cw : 3 * cw].astype(F32)).astype(BF)

        @pl.loop(0, tokens // Q_TILE)
        def _(t):
            here = tile(t, Q_TILE)
            allowed = allowed_pairs(col_ref[...], row_ref[:, here])
            for pair in range(cw // LANES):
                lanes = slice(pair * LANES, (pair + 1) * LANES)
                q2 = qkv[here, lanes]
                k2 = qkv[:, cw + pair * LANES : cw + (pair + 1) * LANES]
                total = None
                for head in range(2):
                    probs = probs_by_key(k2, q2, allowed, head).astype(BF)
                    part = dot(keep_head(vt[lanes, :], head, 0), probs)
                    total = part if total is None else total + part
                attended[here, lanes] = jnp.transpose(total).astype(BF)

        for j in range(n_p):
            outs[j][...] = dot(attended[j * rows : (j + 1) * rows, :], proj_ref[...]).astype(BF)

    outs = [((rows, D), BF)] * n_p + [((tokens, 3 * cw), BF), ((tokens, cw), BF)]
    scratch = [pltpu.VMEM((tokens, D), BF), pltpu.VMEM((cw, tokens), BF)]
    ins = [*blocks, weight, bias, proj] + ([] if codes is None else list(codes))
    if codes is None:
        outs = [((1, tokens), jnp.int32), ((tokens, 1), jnp.int32)] + outs
    got = run("attend", body, outs, ins, net.place, scratch, flops=2 * tokens * D * 4 * cw)
    if codes is None:
        codes, got = got[:2], got[2:]
    return got[:n_p], got[n_p], got[n_p + 1], codes


def attend_back(net, blocks, proj, qkv, codes, weight):
    n_p = net.n_p
    rows = blocks[0].shape[0]
    tokens = n_p * rows
    cw = D // n_p

    def body(*refs):
        proj_ref, qkv_ref, row_ref, col_ref, weight_ref = refs[n_p : n_p + 5]
        outs = refs[n_p + 5 : 2 * n_p + 5]
        dqkv, sums, do, kt, dk, dv = refs[2 * n_p + 5 :]
        for j in range(n_p):
            do[j * rows : (j + 1) * rows, :] = dot_nt(refs[j][...], proj_ref[...]).astype(BF)
        kt[...] = jnp.transpose(qkv_ref[:, cw : 2 * cw].astype(F32)).astype(BF)
        dk[...] = jnp.zeros_like(dk)
        dv[...] = jnp.zeros_like(dv)

        @pl.loop(0, tokens // Q_TILE)
        def _(t):
            here = tile(t, Q_TILE)
            allowed = allowed_pairs(col_ref[...], row_ref[:, here])
            for pair in range(cw // LANES):
                lanes = slice(pair * LANES, (pair + 1) * LANES)
                q2 = qkv_ref[here, lanes]
                k2 = qkv_ref[:, cw + pair * LANES : cw + (pair + 1) * LANES]
                v2 = qkv_ref[:, 2 * cw + pair * LANES : 2 * cw + (pair + 1) * LANES]
                do2 = do[here, lanes]
                total = None
                for head in range(2):
                    probs = probs_by_key(k2, q2, allowed, head)
                    dp = dot_nt(keep_head(v2, head, 1), do2)
                    mean = jnp.sum(probs * dp, axis=0, keepdims=True)
                    ds = (probs * (dp - mean)).astype(BF)
                    dv[:, lanes] += dot(probs.astype(BF), keep_head(do2, head, 1))
                    dk[:, lanes] += dot(ds, keep_head(q2, head, 1))
                    part = dot(keep_head(kt[lanes, :], head, 0), ds)
                    total = part if total is None else total + part
                dqkv[here, lanes] = (jnp.transpose(total) * SCALE).astype(BF)

        dqkv[:, cw : 2 * cw] = (dk[...] * SCALE).astype(BF)
        dqkv[:, 2 * cw :] = dv[...].astype(BF)
        sums[...] = jnp.sum(dqkv[...].astype(F32), axis=0, keepdims=True)
        for j in range(n_p):
            outs[j][...] = dot_nt(dqkv[j * rows : (j + 1) * rows, :], weight_ref[...]).astype(BF)

    outs = [((rows, D), BF)] * n_p + [((tokens, 3 * cw), BF), ((1, 3 * cw), F32)]
    scratch = [
        pltpu.VMEM((tokens, cw), BF),
        pltpu.VMEM((cw, tokens), BF),
        pltpu.VMEM((tokens, cw), F32),
        pltpu.VMEM((tokens, cw), F32),
    ]
    ins = [*blocks, proj, qkv, *codes, weight]
    got = run("attend_back", body, outs, ins, None, scratch, flops=2 * tokens * D * 8 * cw)
    return got[:n_p], got[n_p], got[n_p + 1]


F_TILE = 256


def feed_forward(net, layer, blocks, up, bias, down):
    n_p = net.n_p
    rows = blocks[0].shape[0]
    tokens = n_p * rows
    fw = FF // n_p

    def body(place, *refs):
        up_ref, bias_ref, down_ref = refs[n_p : n_p + 3]
        outs = refs[n_p + 3 : 2 * n_p + 3]
        z_ref, slope_ref, a_ref = refs[2 * n_p + 3 :]
        p = place[0]
        gather_rows(refs[:n_p], a_ref)

        @pl.loop(0, fw // F_TILE)
        def _(t):
            cols = tile(t, F_TILE)
            there = pl.ds(pl.multiple_of(p * fw + t * F_TILE, F_TILE), F_TILE)
            u = dot(a_ref[...], up_ref[:, cols]) + bias_ref[layer : layer + 1, there]
            phi = 0.5 * (1.0 + lax.erf(u * 0.7071067811865476))
            z_ref[:, cols] = (u * phi).astype(BF)
            slope_ref[:, cols] = phi + u * (jnp.exp(-0.5 * u * u) * 0.3989422804014327)

        for j in range(n_p):
            outs[j][...] = dot(z_ref[j * rows : (j + 1) * rows, :], down_ref[...]).astype(BF)

    outs = [((rows, D), BF)] * n_p + [((tokens, fw), BF), ((tokens, fw), F32)]
    scratch = [pltpu.VMEM((tokens, D), BF)]
    ins = [*blocks, up, bias, down]
    got = run("feed_forward", body, outs, ins, net.place, scratch, flops=4 * tokens * D * fw)
    return got[:n_p], got[n_p], got[n_p + 1]


def feed_back(net, blocks, down, slope, up):
    n_p = net.n_p
    rows = blocks[0].shape[0]
    tokens = n_p * rows
    fw = FF // n_p

    def body(*refs):
        down_ref, slope_ref, up_ref = refs[n_p : n_p + 3]
        outs = refs[n_p + 3 : 2 * n_p + 3]
        du_ref, sums, dm = refs[2 * n_p + 3 :]
        gather_rows(refs[:n_p], dm)

        @pl.loop(0, fw // F_TILE)
        def _(t):
            cols = tile(t, F_TILE)
            dz = dot_nt(dm[...], down_ref[cols, :])
            du = (dz * slope_ref[:, cols]).astype(BF)
            du_ref[:, cols] = du
            sums[:, cols] = jnp.sum(du.astype(F32), axis=0, keepdims=True)

        for j in range(n_p):
            outs[j][...] = dot_nt(du_ref[j * rows : (j + 1) * rows, :], up_ref[...]).astype(BF)

    outs = [((rows, D), BF)] * n_p + [((tokens, fw), BF), ((1, fw), F32)]
    scratch = [pltpu.VMEM((tokens, D), BF)]
    ins = [*blocks, down, slope, up]
    got = run("feed_back", body, outs, ins, None, scratch, flops=4 * tokens * D * fw)
    return got[:n_p], got[n_p], got[n_p + 1]


def by_turns(a, b, parts, c, keep, send, cols):
    rows = a.shape[1] // (2 * parts)
    for i in range(parts):
        both = dot_tn(a[:, i * 2 * rows : (i + 1) * 2 * rows], b).astype(BF)
        first, second = both[:rows], both[rows:]
        here = slice(i * rows, (i + 1) * rows)
        keep[here, cols] = jnp.where(c == 0, first, second)
        send[here, cols] = jnp.where(c == 0, second, first)


def weight_grad(net, left, right, parts):
    n_l, n_r = len(left), len(right)
    tokens = sum(v.shape[0] for v in right)
    m, n = left[0].shape[1], right[0].shape[1]

    def body(place, *refs):
        keep, send, a, b = refs[n_l + n_r :]
        gather_rows(refs[:n_l], a)
        gather_rows(refs[n_l : n_l + n_r], b)
        by_turns(a[...], b[...], parts, place[1], keep, send, slice(0, n))

    outs = [((m // 2, n), BF)] * 2
    scratch = [pltpu.VMEM((tokens, m), BF), pltpu.VMEM((tokens, n), BF)]
    return run("weight_grad", body, outs, [*left, *right], net.place, scratch, flops=2 * tokens * m * n)


def attend_weight_grad(net, a1, dqkv, attended, dy):
    n_p = net.n_p
    tokens, width = dqkv.shape
    cw = D // n_p
    rows = D // net.n_f

    def body(place, *refs):
        dqkv_ref, attended_ref = refs[n_p : n_p + 2]
        keep, send, a, b, low = refs[2 * n_p + 2 :]
        c = place[1]
        gather_rows(refs[:n_p], a)
        by_turns(a[...], dqkv_ref[...], n_p, c, keep, send, slice(0, width))
        gather_rows(refs[n_p + 2 : 2 * n_p + 2], b)
        low[...] = dot_tn(attended_ref[...], b[...]).astype(BF)
        for i in range(n_p):
            first = low[0:rows, i * cw : (i + 1) * cw]
            second = low[rows : 2 * rows, i * cw : (i + 1) * cw]
            keep[i * rows : (i + 1) * rows, width:] = jnp.where(c == 0, first, second)
            send[i * rows : (i + 1) * rows, width:] = jnp.where(c == 0, second, first)

    outs = [((D // 2, width + cw), BF)] * 2
    scratch = [pltpu.VMEM((tokens, D), BF), pltpu.VMEM((tokens, D), BF), pltpu.VMEM((cw, D), BF)]
    flops = 2 * tokens * D * (width + cw)
    ins = [*a1, dqkv, attended, *dy]
    return run("attend_weight_grad", body, outs, ins, net.place, scratch, flops=flops)


def add_low(a, b):
    def body(a_ref, b_ref, out):
        out[...] = (a_ref[...].astype(F32) + b_ref[...].astype(F32)).astype(BF)

    return run("add_low", body, [(a.shape, BF)], [a, b])[0]


def take_if(here, a, b):
    def body(flag, a_ref, b_ref, out):
        @pl.when(flag[0] != 0)
        def _():
            out[...] = a_ref[...]

        @pl.when(flag[0] == 0)
        def _():
            out[...] = b_ref[...]

    return run("take_if", body, [(a.shape, BF)], [a, b], here.astype(jnp.int32).reshape(1))[0]


class Chunk:
    def __init__(self, net, value):
        self.net = net
        self.value = value
        self.got = None
        self.step = 0

    @property
    def done(self):
        return self.step == self.net.n_s - 1

    def start(self):
        if self.done:
            return
        n, k = self.net.n_s, self.step + 1
        half = n // 2
        if k < half:
            pairs = [(k - 1, k), (n - k, n - k - 1)]
        elif k == half:
            pairs = [(half - 1, half), (half, half - 1)]
        else:
            k = n - 1 - k
            pairs = [(k + 1, k), (n - 2 - k, n - 1 - k)]
        self.got = lax.ppermute(self.value, "seq", pairs)

    def finish(self):
        if self.done:
            return
        n, k = self.net.n_s, self.step + 1
        if k <= n // 2:
            self.value = add_low(self.value, self.got)
        else:
            k = n - 1 - k
            here = (self.net.s == k) | (self.net.s == n - 1 - k)
            self.value = take_if(here, self.got, self.value)
        self.got = None
        self.step += 1


def start(*chunks):
    for chunk in chunks:
        chunk.start()


def finish(values, *chunks):
    values, side = fence((values, [(c.value, c.got) for c in chunks]))
    for c, (value, got) in zip(chunks, side):
        c.value, c.got = value, got
        c.finish()
    return values


def pack_vectors(net, layers, vectors, sizes, singles):
    n_p = net.n_p
    starts = [sum(sizes[:i]) for i in range(len(sizes))]
    flat = [v for of_layer in vectors for v in of_layer]
    count = len(sizes)

    def body(place, *refs):
        p, c = place[0], place[1]
        keep, send = refs[-2], refs[-1]
        keep[...] = jnp.zeros_like(keep)
        send[...] = jnp.zeros_like(send)
        for layer in range(layers):
            for k, (at, size) in enumerate(zip(starts, sizes)):
                ref = refs[layer * count + k]
                cols = slice(at, at + size)
                if singles[k] == "chip":
                    first, second = ref[:, :size], ref[:, size:]
                    keep[p, layer : layer + 1, cols] = jnp.where(c == 0, first, second)
                    send[p, layer : layer + 1, cols] = jnp.where(c == 0, second, first)
                elif singles[k] == "heads":
                    mine = (p % 2) == c
                    for turn, value in enumerate((ref[:, :size], ref[:, 2 * size :])):
                        to = p // 2 + turn * (n_p // 2)
                        keep[to, layer : layer + 1, cols] = jnp.where(mine, value, 0.0)
                        send[to, layer : layer + 1, cols] = jnp.where(mine, 0.0, value)
                else:
                    for i in range(n_p):
                        first = ref[:, 2 * i * size : (2 * i + 1) * size]
                        second = ref[:, (2 * i + 1) * size : (2 * i + 2) * size]
                        keep[i, layer : layer + 1, cols] = jnp.where(c == 0, first, second)
                        send[i, layer : layer + 1, cols] = jnp.where(c == 0, second, first)

    outs = [((n_p, layers, sum(sizes)), F32)] * 2
    return run("pack_vectors", body, outs, flat, net.place)


def write_layer(net, layer, layers, before, down, proj, up, qkv):
    n_p = net.n_p
    rows = up[0].shape[0]
    cw, fw = D // n_p, FF // n_p
    n_in = 1 + 3 * n_p
    skip = 0 if before is None else 4
    steps = rows // 16
    while steps > 4:
        steps //= 2
    part = rows // steps
    down_part = down.shape[0] // steps

    def body(place, *refs):
        p = place[0]
        down_ref = refs[0]
        projs, ups, qkvs = refs[1 : 1 + n_p], refs[1 + n_p : 1 + 2 * n_p], refs[1 + 2 * n_p : n_in]
        qkv_out, proj_out, up_out, down_out = refs[n_in + skip :]
        down_out[0] = down_ref[...].astype(F32)
        for j in range(n_p):
            proj_out[0, :, j * cw : (j + 1) * cw] = projs[j][...].astype(F32)
            up_out[0, :, tile(p ^ j, fw)] = ups[j][...].astype(F32)
            for i in range(3):
                to = i * n_p + (p ^ j)
                qkv_out[0, :, tile(to, cw)] = qkvs[j][:, i * cw : (i + 1) * cw].astype(F32)

    def of_rows(v, size):
        return pl.BlockSpec((size, v.shape[1]), lambda i: (i, 0))

    def of_piece(j):
        return pl.BlockSpec((part, cw), lambda i: (j * steps + i, 0))

    ins = [down, *[proj] * n_p, *up, *qkv]
    specs = [IN_SMEM, of_rows(down, down_part)] + [of_piece(j) for j in range(n_p)]
    specs += [of_rows(v, part) for v in [*up, *qkv]]
    aliases = {}
    if before is not None:
        aliases = {1 + n_in + k: k for k in range(4)}
        specs += [IN_ANY] * 4
        ins = ins + list(before)
    shapes = [(rows, 3 * D), (rows, D), (rows, FF), down.shape]
    sizes = [part, part, part, down_part]
    return pl.pallas_call(
        body,
        grid=(steps,),
        out_shape=[jax.ShapeDtypeStruct((layers, *shape), F32) for shape in shapes],
        in_specs=specs,
        out_specs=[
            pl.BlockSpec((1, size, shape[1]), lambda i: (layer, i, 0)) for size, shape in zip(sizes, shapes)
        ],
        input_output_aliases=aliases,
        compiler_params=pltpu.CompilerParams(vmem_limit_bytes=16 << 20),
        name="write_layer",
    )(net.place, *ins)


def on_device(
    tokens,
    scene_ids,
    token_kind,
    out_grad,
    first_gain,
    first_shift,
    qkv_weight,
    qv_bias,
    proj_weight,
    proj_bias,
    second_gain,
    second_shift,
    up_weight,
    up_bias,
    down_weight,
    down_bias,
):
    net = Net()
    n_p = net.n_p
    layers = qkv_weight.shape[0]
    rows = tokens.shape[1]
    cw = D // n_p
    fw = FF // n_p

    def up_send(weight, layer):
        shape = (1, weight.shape[1], fw)
        return net.exchange(
            [lax.dynamic_slice(weight, (layer, 0, (net.p ^ j) * fw), shape)[0] for j in range(n_p)]
        )

    def core_all(values):
        return [net.core(v) for v in values]

    def by_chip(v, size):
        return [block(v, net.p ^ j, size, 0) for j in range(n_p)]

    code = (scene_ids[0] * 2 + token_kind[0]).astype(BF).reshape(1, -1)
    code = jnp.pad(code, ((0, 15), (0, D - code.shape[1])))
    tok = net.to_planes(jnp.concatenate([tokens[0], code], axis=0))
    small_in = [first_gain, first_shift, qv_bias, proj_bias, second_gain, second_shift, up_bias, down_bias]
    sizes = [v.shape[1] for v in small_in]
    small = jnp.concatenate(small_in, axis=1)
    small = jnp.concatenate([small, net.core(small)], axis=0).reshape(-1, 3 * cw)
    small = jnp.pad(small, ((0, 16 - small.shape[0]), (0, 0)))
    qkv_own = net.exchange(cut_columns(net, qkv_weight, 0, small))
    tok, qkv_own, later = fence((tok, qkv_own, (qkv_weight, proj_weight, up_weight, down_weight, out_grad)))
    qkv_weight, proj_weight, up_weight, down_weight, out_grad = later
    vectors = join_vectors(net, layers, qkv_own, sizes)
    gain1, shift1, qv_b, proj_b, gain2, shift2, up_b, down_b = vectors

    weights = []
    kept = []
    dm = None
    codes = None
    proj_own = proj_weight[0]
    hidden, a1 = first_norm(tok, 16, gain1, shift1)
    qkv_other, proj_other = core_all(qkv_own), net.core(proj_own)
    for layer in range(layers):
        last = layer == layers - 1
        a1g = net.gather(a1)
        qkv_w, proj_w = join_weights(net, qkv_own, qkv_other, proj_own, proj_other)
        a1g, qkv_w, proj_w = fence((a1g, qkv_w, proj_w))
        y, qkv, og, codes = attend(net, layer, rows, a1g, qkv_w, qv_b, codes, proj_w)
        up_own = up_send(up_weight, layer)
        y, up_own = fence((y, up_own))
        parts = net.exchange(y)
        down_own = down_weight[layer]
        up_other, down_other = core_all(up_own), net.core(down_own)
        parts, up_other, down_other = fence((parts, up_other, down_other))
        h2, a2 = add_and_norm(layer, hidden, parts, proj_b, (layer, gain2, shift2))
        a2g = net.gather(a2)
        up_w, down_w = join_weights(net, up_own, up_other, down_own, down_other)
        if last:
            dmg = net.gather(dm)
            a2g, up_w, down_w, dmg = fence((a2g, up_w, down_w, dmg))
        else:
            a2g, up_w, down_w = fence((a2g, up_w, down_w))
        y, z, slope = feed_forward(net, layer, a2g, up_w, up_b, down_w)
        kept.append((hidden, a1g, qkv, og, h2, a2g, z, slope))
        weights.append((qkv_w, proj_w, up_w, down_w))
        if last:
            last_y = y
            break
        qkv_own = net.exchange(cut_columns(net, qkv_weight, layer + 1, None))
        y, qkv_own = fence((y, qkv_own))
        parts = net.exchange(y)
        proj_own = proj_weight[layer + 1]
        qkv_other, proj_other = core_all(qkv_own), net.core(proj_own)
        if layer == layers - 2:
            dm = net.to_planes(out_grad[0])
            parts, qkv_other, proj_other, dm = fence((parts, qkv_other, proj_other, dm))
        else:
            parts, qkv_other, proj_other = fence((parts, qkv_other, proj_other))
        hidden, a1 = add_and_norm(layer, h2, parts, down_b, (layer + 1, gain1, shift1))

    sums = [None] * layers
    small_grads = [None] * layers
    grad = dm
    down_b_grad = jnp.sum(dm.astype(F32), axis=0, keepdims=True)
    running = []
    waiting = []

    def run_on():
        running.extend(waiting)
        waiting.clear()
        running[:] = [c for c in running if not c.done]
        start(*running)
        return list(running)

    for layer in reversed(range(layers)):
        last = layer == layers - 1
        qkv_w, proj_w, up_w, down_w = weights[layer]
        h1, a1g, qkv, og, h2, a2g, z, slope = kept[layer]
        down_k, down_s = weight_grad(net, [z], dmg, 1)
        da2, du, up_b_grad = feed_back(net, dmg, down_w, slope, up_w)
        down_s = net.core(down_s)
        da2, du, down_k, down_s = finish((da2, du, down_k, down_s), *([] if last else moved))
        down_g = Chunk(net, add_low(down_k, down_s))
        waiting.append(down_g)
        moved = run_on()
        parts = net.exchange(da2)
        up_k, up_s = weight_grad(net, a2g, [du], n_p)
        up_s = net.core(up_s)
        parts, up_k, up_s = fence((parts, up_k, up_s))
        dh2, dy, sums2 = norm_back(layer, grad, h2, parts, gain2)
        dyg = net.gather(dy)
        up_g = Chunk(net, add_low(up_k, up_s))
        dyg = finish(dyg, *moved)
        waiting.append(up_g)
        moved = run_on()
        da1, dqkv, qkv_b_grad = attend_back(net, dyg, proj_w, qkv, codes, qkv_w)
        if last:
            da1, dqkv = fence((da1, dqkv))
        else:
            last_parts = net.exchange(last_y)
            da1, dqkv, last_parts = fence((da1, dqkv, last_parts))
        parts = net.exchange(da1)
        qkv_k, qkv_s = attend_weight_grad(net, a1g, dqkv, og, dyg)
        qkv_s = net.core(qkv_s)
        parts, qkv_k, qkv_s = finish((parts, qkv_k, qkv_s), *moved)
        grad, dm, sums1 = norm_back(layer, dh2, h1, parts, gain1)
        qkv_g = add_low(qkv_k, qkv_s)
        small_grads[layer] = [
            sums1[0:1],
            sums1[1:2],
            qkv_b_grad,
            sums2[2:3],
            sums2[0:1],
            sums2[1:2],
            up_b_grad,
            down_b_grad,
        ]
        sums[layer] = (down_g, up_g)
        if not last:
            break
        attend_g = Chunk(net, qkv_g)
        sums[layer] += (attend_g,)
        waiting.append(attend_g)
        moved = run_on()
        dmg = net.gather(dm)
        down_b_grad = sums1[2:3]
        dmg, grad = fence((dmg, grad))

    moved = run_on()
    (sent_out,) = add_and_norm(layers - 1, kept[-1][4], last_parts, down_b, None)
    input_grad = net.from_planes(dm)
    kinds = [None, None, "heads", None, None, None, "chip", None]
    keep, send = pack_vectors(net, layers, small_grads, sizes, kinds)
    small = keep + net.core(send)
    pieces = net.exchange(by_chip(qkv_g[:, : 3 * cw], D // net.n_f))
    pieces.append(qkv_g[:, 3 * cw :])
    input_grad, small, pieces, sent_out = finish((input_grad, small, pieces, sent_out), *moved)
    pieces = [Chunk(net, v) for v in pieces]
    sent_out = net.from_planes(sent_out)
    got = net.exchange([v[0] for v in by_chip(small, 1)])
    small = got[0]
    for part in got[1:]:
        small = small + part

    queue = [c for c in running if not c.done] + [pieces[0], pieces[-1], *pieces[1:-1]]
    bit = 1
    while not all(c.done for c in queue):
        moved = []
        for c in queue:
            if not c.done and c.step not in [m.step for m in moved]:
                moved.append(c)
        start(*moved)
        if bit < net.n_s:
            small = small + lax.ppermute(small, "seq", xor_pairs(net.n_s, bit))
            bit *= 2
        sent_out, small = finish((sent_out, small), *moved)

    out = None
    for layer in reversed(range(layers)):
        down_g, up_g = sums[layer][:2]
        up_pieces = net.exchange(by_chip(up_g.value, D // net.n_f))
        if len(sums[layer]) > 2:
            whole = sums[layer][2].value
            qkv_pieces = net.exchange(by_chip(whole[:, : 3 * cw], D // net.n_f))
            proj_g = whole[:, 3 * cw :]
        else:
            qkv_pieces = [c.value for c in pieces[:-1]]
            proj_g = pieces[-1].value
        out = write_layer(net, layer, layers, out, down_g.value, proj_g, up_pieces, qkv_pieces)
    small_out = []
    at = 0
    for size in sizes:
        small_out.append(small[:, at : at + size])
        at += size
    return (
        sent_out.astype(F32)[None],
        input_grad.astype(F32)[None],
        small_out[0],
        small_out[1],
        out[0],
        small_out[2],
        out[1],
        small_out[3],
        small_out[4],
        small_out[5],
        out[2],
        small_out[6],
        out[3],
        small_out[7],
    )


def solution(mesh):
    tok = P("fsdp", "seq", None)
    lab = P("fsdp", "seq")
    vec = P(None, "fsdp")
    mat = P(None, "fsdp", None)
    return jax.shard_map(
        on_device,
        mesh=mesh,
        in_specs=(tok, lab, lab, tok, vec, vec, mat, vec, mat, vec, vec, vec, mat, vec, mat, vec),
        out_specs=(tok, tok, vec, vec, mat, vec, mat, vec, vec, vec, mat, vec, mat, vec),
        check_vma=False,
    )
```

time: 785 us -> 568 us (0.72)
  waiting for transfers between devices: 330 us -> 222 us
  Pallas kernels: 0 us -> 102 us
  other arithmetic: 87.8 us -> 3.6 us
  matrix products: 65.3 us -> 0 us
  local copies, waits for them, and re-layouts: 80.8 us -> 19.9 us
  starting transfers between devices: 159 us -> 210 us
  blocking collectives: 43.4 us -> 0 us
    ppermute x29 -> x36, waiting for transfers between devices: 172 us -> 57.9 us  [the longest x30 37.8 us: start(): self.got = lax.ppermute(self.value, 'seq', pairs)]
    pallas_call x0 -> x69, Pallas kernels: none -> 102 us  [the longest x67 94.9 us: run(): pl.pallas_call(body, out_shape=[jax.ShapeDtypeStruct(shape, dtype) for sh...]
    dot_general x36 -> x0, matrix products: 65.3 us -> none  [the longest x8 21.8 us: dot(): return jnp.dot(a, b, preferred_element_type=F32)]
    ppermute x29 -> x36, starting transfers between devices: 57.2 us -> 93.7 us  [the longest x30 79.3 us: start(): self.got = lax.ppermute(self.value, 'seq', pairs)]
    convert_element_type x29 -> x1, other arithmetic: 29.5 us -> 0.74 us  [on_device(): code = (scene_ids[0] * 2 + token_kind[0]).astype(BF).reshape(1, -1)]
    unnamed x1 -> x0, blocking collectives: 21.4 us -> none
    slice x24 -> x11, local copies, waits for them, and re-layouts: 22.7 us -> 2.01 us  [the longest x3 1.76 us: on_device(): small_out.append(small[:, at:at + size])]
    another operation x28 -> x1, other arithmetic: 19.5 us -> 0.07 us  [__init__(): self.place = jnp.stack([self.p, self.c]).astype(jnp.int32)]
  transfers between devices with their start and end apart: 124 -> 139, of which waited for: 60 -> 58; matrix products, arithmetic and copies ran while one was open for 25% -> 2% of each run, Pallas kernels for 0% -> 15%
where the time goes in v2:
time: 568 us; the launch traced here: 561 us
  waiting for transfers between devices  222 us (39%)
  starting transfers between devices  210 us (37%)
  Pallas kernels  102 us (18%)
  local copies, waits for them, and re-layouts  19.9 us (4%)
    ppermute x75, waiting for transfers between devices, chip(): return lax.ppermute(v, 'fsdp', xor_pairs(self.n_f, 2 * j))  157 us
    ppermute x75, starting transfers between devices, chip(): return lax.ppermute(v, 'fsdp', xor_pairs(self.n_f, 2 * j))  112 us
    pallas_call x67, Pallas kernels, run(): pl.pallas_call(body, out_shape=[jax.ShapeDtypeStruct(shape, dtype) for sh...  94.9 us
    ppermute x30, starting transfers between devices, start(): self.got = lax.ppermute(self.value, 'seq', pairs)  79.3 us
    ppermute x30, waiting for transfers between devices, start(): self.got = lax.ppermute(self.value, 'seq', pairs)  37.8 us
    ppermute x2, waiting for transfers between devices, on_device(): small = small + lax.ppermute(small, 'seq', xor_pairs(net.n_s, bit))  15.2 us
    unnamed x127, local copies, waits for them, and re-layouts  14.3 us
  transfers between devices with their start and end apart: 139, of which 58 were waited for; matrix products, arithmetic and copies ran while one was open for 2% of the time, Pallas kernels for 15%

profile of v2, /device:TPU:10, one launch (start us, length us, event | category | flops | bytes accessed | tf_op | source)
XLA Modules:
  0.0 560.5 jit_solution(11022979077146639604)
XLA Ops:
  18.9 4.4 collective-permute-done.2.refs_1_
  23.3 5.5 collective-permute-done.3.refs_2_
  43.3 6.7 %collective-permute-start.15 = (bf16[128,1024]{1,0:T(8,128)(2,1)S(1)}, bf16[128,1024]{1,0:T(8,128)(2,1)S(1)}, u32[]{:S(2)}, u32[]{:S(2)}) collective-permute-start(bf16[128,1024]{1,0:T(8,128)(2,1)S(1)} %get-tuple-element.724), channel_id=1, source_target_pairs={{0,6},{1,7},{2,4},{3,5},{4,2},{5,3},{6,0},{7,1},{8,14},{9,15},{10,... | collective-permute-start | bytes 786440 | tf_op jit(solution)/shard_map/ppermute | solution.py:47
  50.0 3.3 join_weights.4
  53.4 5.9 %attend.2 = (s32[1,512]{1,0:T(1,128)S(1)}, s32[512,1]{1,0:T(8,128)S(1)}, bf16[128,1024]{1,0:T(8,128)(2,1)S(1)}, bf16[128,1024]{1,0:T(8,128)(2,1)S(1)}, bf16[128,...) custom-call(s32[2]{0:T(128)S(1)} %pad_add_fusion.place, ...), custom_call_target="tpu_custom_call" | custom-call | flops 1073741824 | bytes 3293192 | tf_op jit(solution)/shard_map/attend/pallas_call | solution.py:78
  63.1 5.7 %collective-permute-done.16.refs_2_ = bf16[128,1024]{1,0:T(8,128)(2,1)S(1)} collective-permute-done((bf16[128,1024]{1,0:T(8,128)(2,1)S(1)}, bf16[128,1024]{1,0:T(8,128)(2,1)S(1)}, u32[]{:S(2)}, u32[]{:S(2)}) %collective-permute-start.16) | collective-permute-done | bytes 262176 | tf_op jit(solution)/shard_map/ppermute | solution.py:47
  68.8 5.8 %collective-permute-done.17.refs_3_ = bf16[128,1024]{1,0:T(8,128)(2,1)S(1)} collective-permute-done((bf16[128,1024]{1,0:T(8,128)(2,1)S(1)}, bf16[128,1024]{1,0:T(8,128)(2,1)S(1)}, u32[]{:S(2)}, u32[]{:S(2)}) %collective-permute-start.17) | collective-permute-done | bytes 262176 | tf_op jit(solution)/shard_map/ppermute | solution.py:47
  87.0 4.7 collective-permute-done.25.refs_2_
  91.9 4.3 collective-permute-start.38
  96.2 4.2 feed_forward.2
  104.1 4.9 collective-permute-done.38.refs_0_.refs_1_.grad_ref
  109.0 4.4 collective-permute-start.31
  113.4 4.1 collective-permute-start.32
  120.4 5.1 collective-permute-done.31.refs_3_
  125.9 4.1 collective-permute-start.39
  133.5 3.7 collective-permute-done.39.refs_1_
  137.5 6.9 %collective-permute-done.40.refs_2_ = bf16[128,1024]{1,0:T(8,128)(2,1)S(1)} collective-permute-done((bf16[128,1024]{1,0:T(8,128)(2,1)S(1)}, bf16[128,1024]{1,0:T(8,128)(2,1)S(1)}, u32[]{:S(2)}, u32[]{:S(2)}) %collective-permute-start.40) | collective-permute-done | bytes 262176 | tf_op jit(solution)/shard_map/ppermute | solution.py:47
  147.2 5.2 attend.3
  157.8 3.7 collective-permute-done.45.refs_2_
  161.5 4.3 collective-permute-done.46.refs_3_
  171.9 3.1 collective-permute-done.56.refs_1_.refs_2_
  177.4 4.5 collective-permute-done.57.refs_2_.refs_3_
  182.0 4.3 collective-permute-done.53.refs_1_
  186.3 6.3 %collective-permute-done.54.refs_2_ = bf16[128,1024]{1,0:T(8,128)(2,1)S(1)} collective-permute-done((bf16[128,1024]{1,0:T(8,128)(2,1)S(1)}, bf16[128,1024]{1,0:T(8,128)(2,1)S(1)}, u32[]{:S(2)}, u32[]{:S(2)}) %collective-permute-start.54) | collective-permute-done | bytes 262176 | tf_op jit(solution)/shard_map/ppermute | solution.py:47
  192.5 4.2 feed_forward.3
  198.6 5.1 feed_back.2
  211.2 5.7 %collective-permute-done.60.refs_1_ = bf16[128,1024]{1,0:T(8,128)(2,1)S(1)} collective-permute-done((bf16[128,1024]{1,0:T(8,128)(2,1)S(1)}, bf16[128,1024]{1,0:T(8,128)(2,1)S(1)}, u32[]{:S(2)}, u32[]{:S(2)}) %collective-permute-start.60) | collective-permute-done | bytes 262176 | tf_op jit(solution)/shard_map/ppermute | solution.py:47
  216.9 5.1 collective-permute-done.61.refs_2_
  227.7 6.5 %collective-permute-done.67.b_ref = bf16[512,1024]{1,0:T(8,128)(2,1)S(1)} collective-permute-done((bf16[512,1024]{1,0:T(8,128)(2,1)S(1)}, bf16[512,1024]{1,0:T(8,128)(2,1)S(1)}, u32[]{:S(2)}, u32[]{:S(2)}) %collective-permute-start.67) | collective-permute-done | bytes 1048608 | tf_op jit(solution)/shard_map/ppermute | solution.py:571
  236.6 8.5 %attend_back.2 = (bf16[128,1024]{1,0:T(8,128)(2,1)S(1)}, bf16[128,1024]{1,0:T(8,128)(2,1)S(1)}, bf16[128,1024]{1,0:T(8,128)(2,1)S(1)}, bf16[128,1024]{1,0:T(8,12...) custom-call(bf16[128,1024]{1,0:T(8,128)(2,1)S(1)} %get-tuple-element.526.refs_0_.refs_6_, ...), custom_call_target="tpu_custom_call" | custom-call | flops 2147483648 | bytes 3936256 | tf_op jit(solution)/shard_map/attend_back/pallas_call | solution.py:78
  247.3 3.6 collective-permute-start.72
  253.1 6.2 %collective-permute-done.68.refs_1_ = bf16[128,1024]{1,0:T(8,128)(2,1)S(1)} collective-permute-done((bf16[128,1024]{1,0:T(8,128)(2,1)S(1)}, bf16[128,1024]{1,0:T(8,128)(2,1)S(1)}, u32[]{:S(2)}, u32[]{:S(2)}) %collective-permute-start.68) | collective-permute-done | bytes 262176 | tf_op jit(solution)/shard_map/ppermute | solution.py:47
  261.0 6.8 %collective-permute-done.70.refs_3_ = bf16[128,1024]{1,0:T(8,128)(2,1)S(1)} collective-permute-done((bf16[128,1024]{1,0:T(8,128)(2,1)S(1)}, bf16[128,1024]{1,0:T(8,128)(2,1)S(1)}, u32[]{:S(2)}, u32[]{:S(2)}) %collective-permute-start.70) | collective-permute-done | bytes 262176 | tf_op jit(solution)/shard_map/ppermute | solution.py:47
  267.8 6.9 %collective-permute-done.72.b_ref = bf16[512,1024]{1,0:T(8,128)(2,1)S(1)} collective-permute-done((bf16[512,1024]{1,0:T(8,128)(2,1)S(1)}, bf16[512,1024]{1,0:T(8,128)(2,1)S(1)}, u32[]{:S(2)}, u32[]{:S(2)}) %collective-permute-start.72) | collective-permute-done | bytes 1048608 | tf_op jit(solution)/shard_map/ppermute | solution.py:571
  281.0 3.6 collective-permute-start.79
  286.1 3.9 collective-permute-done.75.refs_2_.refs_3_
  291.9 4.9 feed_back.3
  296.8 5.3 collective-permute-done.78.a_ref
  302.1 4.6 collective-permute-done.79.b_ref
  306.8 3.5 collective-permute-done.80.b_ref
  323.8 6.5 %collective-permute-done.82.refs_2_ = bf16[128,1024]{1,0:T(8,128)(2,1)S(1)} collective-permute-done((bf16[128,1024]{1,0:T(8,128)(2,1)S(1)}, bf16[128,1024]{1,0:T(8,128)(2,1)S(1)}, u32[]{:S(2)}, u32[]{:S(2)}) %collective-permute-start.82) | collective-permute-done | bytes 262176 | tf_op jit(solution)/shard_map/ppermute | solution.py:47
  332.0 6.1 %collective-permute-done.83.refs_3_ = bf16[128,1024]{1,0:T(8,128)(2,1)S(1)} collective-permute-done((bf16[128,1024]{1,0:T(8,128)(2,1)S(1)}, bf16[128,1024]{1,0:T(8,128)(2,1)S(1)}, u32[]{:S(2)}, u32[]{:S(2)}) %collective-permute-start.83) | collective-permute-done | bytes 262176 | tf_op jit(solution)/shard_map/ppermute | solution.py:47
  354.4 9.0 %attend_back.3 = (bf16[128,1024]{1,0:T(8,128)(2,1)S(1)}, bf16[128,1024]{1,0:T(8,128)(2,1)S(1)}, bf16[128,1024]{1,0:T(8,128)(2,1)}, bf16[128,1024]{1,0:T(8,128)(2...) custom-call(bf16[128,1024]{1,0:T(8,128)(2,1)S(1)} %get-tuple-element.593.refs_0_.refs_6_, ...), custom_call_target="tpu_custom_call" | custom-call | flops 2147483648 | bytes 3936256 | tf_op jit(solution)/shard_map/attend_back/pallas_call | solution.py:78
  363.4 3.8 attend_weight_grad.3
  368.6 4.6 collective-permute-start.98
  376.2 7.7 %collective-permute-done.94.refs_1_ = bf16[128,1024]{1,0:T(8,128)(2,1)S(1)} collective-permute-done((bf16[128,1024]{1,0:T(8,128)(2,1)S(1)}, bf16[128,1024]{1,0:T(8,128)(2,1)S(1)}, u32[]{:S(2)}, u32[]{:S(2)}) %collective-permute-start.94) | collective-permute-done | bytes 262176 | tf_op jit(solution)/shard_map/ppermute | solution.py:47
  386.0 6.5 %collective-permute-done.95.refs_2_ = bf16[128,1024]{1,0:T(8,128)(2,1)} collective-permute-done((bf16[128,1024]{1,0:T(8,128)(2,1)}, bf16[128,1024]{1,0:T(8,128)(2,1)}, u32[]{:S(2)}, u32[]{:S(2)}) %collective-permute-start.95) | collective-permute-done | bytes 262176 | tf_op jit(solution)/shard_map/ppermute | solution.py:47
  393.9 6.4 %collective-permute-done.96.refs_3_ = bf16[128,1024]{1,0:T(8,128)(2,1)S(1)} collective-permute-done((bf16[128,1024]{1,0:T(8,128)(2,1)}, bf16[128,1024]{1,0:T(8,128)(2,1)S(1)}, u32[]{:S(2)}, u32[]{:S(2)}) %collective-permute-start.96) | collective-permute-done | bytes 262176 | tf_op jit(solution)/shard_map/ppermute | solution.py:47
  419.4 4.2 collective-permute-done.103.a_ref
  426.9 4.8 collective-permute-done.105.a_ref
  432.9 5.3 collective-permute-start.113
  438.2 11.6 %collective-permute-start.111 = (f32[2,1536]{1,0:T(2,128)S(1)}, f32[2,1536]{1,0:T(2,128)S(1)}, u32[]{:S(2)}, u32[]{:S(2)}) collective-permute-start(f32[2,1536]{1,0:T(2,128)S(1)} %get-tuple-element.747), channel_id=1, source_target_pairs={{0,6},{1,7},{2,4},{3,5},{4,2},{5,3},{6,0},{7,1},{8,14},{9,15},{10,... | collective-permute-start | bytes 36872 | tf_op jit(solution)/shard_map/ppermute | solution.py:47
  457.9 11.3 %collective-permute-done.112 = f32[2,1536]{1,0:T(2,128)S(1)} collective-permute-done((f32[2,1536]{1,0:T(2,128)S(1)}, f32[2,1536]{1,0:T(2,128)S(1)}, u32[]{:S(2)}, u32[]{:S(2)}) %collective-permute-start.112) | collective-permute-done | bytes 12320 | tf_op jit(solution)/shard_map/ppermute | solution.py:880
  471.0 8.4 %collective-permute-start.116 = (bf16[128,768]{1,0:T(8,128)(2,1)S(1)}, bf16[128,768]{1,0:T(8,128)(2,1)S(1)}, u32[]{:S(2)}, u32[]{:S(2)}) collective-permute-start(bf16[128,768]{1,0:T(8,128)(2,1)S(1)} %add_low.42.a_ref), channel_id=1, source_target_pairs={{8,16},{16,8},{9,17},{17,9},{10,18},{18,10},{11,19},{19,11},{12,20... | collective-permute-start | bytes 589832 | tf_op jit(solution)/shard_map/ppermute | solution.py:571
  480.1 3.9 collective-permute-done.115
  488.5 4.6 collective-permute-start.118
  497.2 5.1 collective-permute-start.121
  504.3 3.2 collective-permute-start.122
  515.7 4.6 collective-permute-start.124
  526.3 4.7 collective-permute-done.125.b_ref
  533.3 3.1 collective-permute-start.128
  538.7 3.6 write_layer.2
  553.3 3.2 collective-permute-done.131.refs_7_
  556.5 3.5 write_layer.3
  (443 shorter events, 222.8 us)
Async XLA Ops:
  2.4 26.8 %collective-permute-start = (bf16[144,1024]{1,0:T(8,128)(2,1)S(1)}, bf16[144,1024]{1,0:T(8,128)(2,1)S(1)}, u32[]{:S(2)}, u32[]{:S(2)}) collective-permute-start(bf16[144,1024]{1,0:T(8,128)(2,1)S(1)} %fusion.1), channel_id=1, source_target_pairs={{0,0},{1,1},{2,10},{3,11},{4,20},{5,21},{6,30},{7,31},{8,2},{9,3},... | collective-permute-start | bytes 884744 | tf_op jit(solution)/shard_map/ppermute | solution.py:41
  15.2 13.5 %collective-permute-start.3 = (bf16[144,768]{1,0:T(8,128)(2,1)S(1)}, bf16[144,768]{1,0:T(8,128)(2,1)S(1)}, u32[]{:S(2)}, u32[]{:S(2)}) collective-permute-start(bf16[144,768]{1,0:T(8,128)(2,1)S(1)} %get-tuple-element.368), channel_id=1, source_target_pairs={{0,4},{1,5},{2,6},{3,7},{4,0},{5,1},{6,2},{7,3},{8,12},{9,13},{10,... | collective-permute-start | bytes 663560 | tf_op jit(solution)/shard_map/ppermute | solution.py:47
  37.7 38.8 %collective-permute-start.23 = (bf16[512,1024]{1,0:T(8,128)(2,1)S(1)}, bf16[512,1024]{1,0:T(8,128)(2,1)}, u32[]{:S(2)}, u32[]{:S(2)}) collective-permute-start(bf16[512,1024]{1,0:T(8,128)(2,1)S(1)} %get-tuple-element.719.refs_8_), channel_id=1, source_target_pairs={{0,1},{1,0},{2,3},{3,2},{4,5},{5,4},{6,7},{7,6},{8,9},{9,8},{10,11... | collective-permute-start | bytes 3145736 | tf_op jit(solution)/shard_map/ppermute | solution.py:50
  37.9 15.5 %collective-permute-start.7 = (bf16[144,1024]{1,0:T(8,128)(2,1)}, bf16[144,1024]{1,0:T(8,128)(2,1)S(1)}, u32[]{:S(2)}, u32[]{:S(2)}) collective-permute-start(bf16[144,1024]{1,0:T(8,128)(2,1)} %get-tuple-element.382.refs_0_), channel_id=1, source_target_pairs={{0,6},{1,7},{2,4},{3,5},{4,2},{5,3},{6,0},{7,1},{8,14},{9,15},{10,... | collective-permute-start | bytes 884744 | tf_op jit(solution)/shard_map/ppermute | solution.py:47
  41.0 18.2 %collective-permute-start.13 = (bf16[128,1024]{1,0:T(8,128)(2,1)S(1)}, bf16[128,1024]{1,0:T(8,128)(2,1)S(1)}, u32[]{:S(2)}, u32[]{:S(2)}) collective-permute-start(bf16[128,1024]{1,0:T(8,128)(2,1)S(1)} %get-tuple-element.726), channel_id=1, source_target_pairs={{0,2},{1,3},{2,0},{3,1},{4,6},{5,7},{6,4},{7,5},{8,10},{9,11},{10,... | collective-permute-start | bytes 786440 | tf_op jit(solution)/shard_map/ppermute | solution.py:47
  41.8 17.4 %collective-permute-start.14 = (bf16[128,1024]{1,0:T(8,128)(2,1)S(1)}, bf16[128,1024]{1,0:T(8,128)(2,1)S(1)}, u32[]{:S(2)}, u32[]{:S(2)}) collective-permute-start(bf16[128,1024]{1,0:T(8,128)(2,1)S(1)} %get-tuple-element.725), channel_id=1, source_target_pairs={{0,4},{1,5},{2,6},{3,7},{4,0},{5,1},{6,2},{7,3},{8,12},{9,13},{10,... | collective-permute-start | bytes 786440 | tf_op jit(solution)/shard_map/ppermute | solution.py:47
  43.3 16.3 %collective-permute-start.15 = (bf16[128,1024]{1,0:T(8,128)(2,1)S(1)}, bf16[128,1024]{1,0:T(8,128)(2,1)S(1)}, u32[]{:S(2)}, u32[]{:S(2)}) collective-permute-start(bf16[128,1024]{1,0:T(8,128)(2,1)S(1)} %get-tuple-element.724), channel_id=1, source_target_pairs={{0,6},{1,7},{2,4},{3,5},{4,2},{5,3},{6,0},{7,1},{8,14},{9,15},{10,... | collective-permute-start | bytes 786440 | tf_op jit(solution)/shard_map/ppermute | solution.py:47
  61.5 13.1 %collective-permute-start.17 = (bf16[128,1024]{1,0:T(8,128)(2,1)S(1)}, bf16[128,1024]{1,0:T(8,128)(2,1)S(1)}, u32[]{:S(2)}, u32[]{:S(2)}) collective-permute-start(bf16[128,1024]{1,0:T(8,128)(2,1)S(1)} %get-tuple-element.396), channel_id=1, source_target_pairs={{0,4},{1,5},{2,6},{3,7},{4,0},{5,1},{6,2},{7,3},{8,12},{9,13},{10,... | collective-permute-start | bytes 786440 | tf_op jit(solution)/shard_map/ppermute | solution.py:47
  77.0 14.7 %collective-permute-start.25 = (bf16[128,1024]{1,0:T(8,128)(2,1)S(1)}, bf16[128,1024]{1,0:T(8,128)(2,1)S(1)}, u32[]{:S(2)}, u32[]{:S(2)}) collective-permute-start(bf16[128,1024]{1,0:T(8,128)(2,1)S(1)} %get-tuple-element.418.refs_0_), channel_id=1, source_target_pairs={{0,4},{1,5},{2,6},{3,7},{4,0},{5,1},{6,2},{7,3},{8,12},{9,13},{10,... | collective-permute-start | bytes 786440 | tf_op jit(solution)/shard_map/ppermute | solution.py:47
  78.3 13.6 %collective-permute-start.26 = (bf16[128,1024]{1,0:T(8,128)(2,1)S(1)}, bf16[128,1024]{1,0:T(8,128)(2,1)S(1)}, u32[]{:S(2)}, u32[]{:S(2)}) collective-permute-start(bf16[128,1024]{1,0:T(8,128)(2,1)S(1)} %get-tuple-element.418.refs_0_), channel_id=1, source_target_pairs={{0,6},{1,7},{2,4},{3,5},{4,2},{5,3},{6,0},{7,1},{8,14},{9,15},{10,... | collective-permute-start | bytes 786440 | tf_op jit(solution)/shard_map/ppermute | solution.py:47
  81.2 19.1 %collective-permute-start.27 = (bf16[128,768]{1,0:T(8,128)(2,1)S(1)}, bf16[128,768]{1,0:T(8,128)(2,1)S(1)}, u32[]{:S(2)}, u32[]{:S(2)}) collective-permute-start(bf16[128,768]{1,0:T(8,128)(2,1)S(1)} %get-tuple-element.431), channel_id=1, source_target_pairs={{0,2},{1,3},{2,0},{3,1},{4,6},{5,7},{6,4},{7,5},{8,10},{9,11},{10,... | collective-permute-start | bytes 589832 | tf_op jit(solution)/shard_map/ppermute | solution.py:47
  81.4 19.0 %collective-permute-start.28 = (bf16[128,768]{1,0:T(8,128)(2,1)S(1)}, bf16[128,768]{1,0:T(8,128)(2,1)S(1)}, u32[]{:S(2)}, u32[]{:S(2)}) collective-permute-start(bf16[128,768]{1,0:T(8,128)(2,1)S(1)} %get-tuple-element.432), channel_id=1, source_target_pairs={{0,4},{1,5},{2,6},{3,7},{4,0},{5,1},{6,2},{7,3},{8,12},{9,13},{10,... | collective-permute-start | bytes 589832 | tf_op jit(solution)/shard_map/ppermute | solution.py:47
  86.1 14.3 %collective-permute-start.29 = (bf16[128,768]{1,0:T(8,128)(2,1)S(1)}, bf16[128,768]{1,0:T(8,128)(2,1)S(1)}, u32[]{:S(2)}, u32[]{:S(2)}) collective-permute-start(bf16[128,768]{1,0:T(8,128)(2,1)S(1)} %get-tuple-element.433), channel_id=1, source_target_pairs={{0,6},{1,7},{2,4},{3,5},{4,2},{5,3},{6,0},{7,1},{8,14},{9,15},{10,... | collective-permute-start | bytes 589832 | tf_op jit(solution)/shard_map/ppermute | solution.py:47
  91.9 17.1 %collective-permute-start.38 = (bf16[128,1024]{1,0:T(8,128)(2,1)S(1)}, bf16[128,1024]{1,0:T(8,128)(2,1)S(1)}, u32[]{:S(2)}, u32[]{:S(2)}) collective-permute-start(bf16[128,1024]{1,0:T(8,128)(2,1)S(1)} %bitcast.50), channel_id=1, source_target_pairs={{0,0},{1,1},{2,10},{3,11},{4,20},{5,21},{6,30},{7,31},{8,2},{9,3},... | collective-permute-start | bytes 786440 | tf_op jit(solution)/shard_map/ppermute | solution.py:41
  100.7 16.8 %collective-permute-start.34 = (bf16[128,768]{1,0:T(8,128)(2,1)S(1)}, bf16[128,768]{1,0:T(8,128)(2,1)S(1)}, u32[]{:S(2)}, u32[]{:S(2)}) collective-permute-start(bf16[128,768]{1,0:T(8,128)(2,1)S(1)} %collective-permute-done.27.refs_1_), channel_id=1, source_target_pairs={{0,1},{1,0},{2,3},{3,2},{4,5},{5,4},{6,7},{7,6},{8,9},{9,8},{10,11... | collective-permute-start | bytes 589832 | tf_op jit(solution)/shard_map/ppermute | solution.py:50
  101.0 16.5 %collective-permute-start.35 = (bf16[128,768]{1,0:T(8,128)(2,1)S(1)}, bf16[128,768]{1,0:T(8,128)(2,1)S(1)}, u32[]{:S(2)}, u32[]{:S(2)}) collective-permute-start(bf16[128,768]{1,0:T(8,128)(2,1)S(1)} %collective-permute-done.28.refs_2_), channel_id=1, source_target_pairs={{0,1},{1,0},{2,3},{3,2},{4,5},{5,4},{6,7},{7,6},{8,9},{9,8},{10,11... | collective-permute-start | bytes 589832 | tf_op jit(solution)/shard_map/ppermute | solution.py:50
  101.2 19.2 %collective-permute-start.30 = (bf16[128,1024]{1,0:T(8,128)(2,1)S(1)}, bf16[128,1024]{1,0:T(8,128)(2,1)S(1)}, u32[]{:S(2)}, u32[]{:S(2)}) collective-permute-start(bf16[128,1024]{1,0:T(8,128)(2,1)S(1)} %get-tuple-element.435), channel_id=1, source_target_pairs={{0,2},{1,3},{2,0},{3,1},{4,6},{5,7},{6,4},{7,5},{8,10},{9,11},{10,... | collective-permute-start | bytes 786440 | tf_op jit(solution)/shard_map/ppermute | solution.py:47
  109.0 16.5 %collective-permute-start.31 = (bf16[128,1024]{1,0:T(8,128)(2,1)S(1)}, bf16[128,1024]{1,0:T(8,128)(2,1)S(1)}, u32[]{:S(2)}, u32[]{:S(2)}) collective-permute-start(bf16[128,1024]{1,0:T(8,128)(2,1)S(1)} %get-tuple-element.436), channel_id=1, source_target_pairs={{0,4},{1,5},{2,6},{3,7},{4,0},{5,1},{6,2},{7,3},{8,12},{9,13},{10,... | collective-permute-start | bytes 786440 | tf_op jit(solution)/shard_map/ppermute | solution.py:47
  117.5 39.9 %collective-permute-start.52 = (bf16[512,1024]{1,0:T(8,128)(2,1)S(1)}, bf16[512,1024]{1,0:T(8,128)(2,1)S(1)}, u32[]{:S(2)}, u32[]{:S(2)}) collective-permute-start(bf16[512,1024]{1,0:T(8,128)(2,1)S(1)} %get-tuple-element.718.refs_8_), channel_id=1, source_target_pairs={{0,1},{1,0},{2,3},{3,2},{4,5},{5,4},{6,7},{7,6},{8,9},{9,8},{10,11... | collective-permute-start | bytes 3145736 | tf_op jit(solution)/shard_map/ppermute | solution.py:50
  130.0 14.4 %collective-permute-start.40 = (bf16[128,1024]{1,0:T(8,128)(2,1)S(1)}, bf16[128,1024]{1,0:T(8,128)(2,1)S(1)}, u32[]{:S(2)}, u32[]{:S(2)}) collective-permute-start(bf16[128,1024]{1,0:T(8,128)(2,1)S(1)} %get-tuple-element.459.refs_0_), channel_id=1, source_target_pairs={{0,4},{1,5},{2,6},{3,7},{4,0},{5,1},{6,2},{7,3},{8,12},{9,13},{10,... | collective-permute-start | bytes 786440 | tf_op jit(solution)/shard_map/ppermute | solution.py:47
  130.3 17.0 %collective-permute-start.41 = (bf16[128,1024]{1,0:T(8,128)(2,1)S(1)}, bf16[128,1024]{1,0:T(8,128)(2,1)S(1)}, u32[]{:S(2)}, u32[]{:S(2)}) collective-permute-start(bf16[128,1024]{1,0:T(8,128)(2,1)S(1)} %get-tuple-element.459.refs_0_), channel_id=1, source_target_pairs={{0,6},{1,7},{2,4},{3,5},{4,2},{5,3},{6,0},{7,1},{8,14},{9,15},{10,... | collective-permute-start | bytes 786440 | tf_op jit(solution)/shard_map/ppermute | solution.py:47
  131.5 20.9 %collective-permute-start.42 = (bf16[128,1024]{1,0:T(8,128)(2,1)S(1)}, bf16[128,1024]{1,0:T(8,128)(2,1)S(1)}, u32[]{:S(2)}, u32[]{:S(2)}) collective-permute-start(bf16[128,1024]{1,0:T(8,128)(2,1)S(1)} %get-tuple-element.722), channel_id=1, source_target_pairs={{0,2},{1,3},{2,0},{3,1},{4,6},{5,7},{6,4},{7,5},{8,10},{9,11},{10,... | collective-permute-start | bytes 786440 | tf_op jit(solution)/shard_map/ppermute | solution.py:47
  137.2 16.6 %collective-permute-start.43 = (bf16[128,1024]{1,0:T(8,128)(2,1)S(1)}, bf16[128,1024]{1,0:T(8,128)(2,1)S(1)}, u32[]{:S(2)}, u32[]{:S(2)}) collective-permute-start(bf16[128,1024]{1,0:T(8,128)(2,1)S(1)} %get-tuple-element.721), channel_id=1, source_target_pairs={{0,4},{1,5},{2,6},{3,7},{4,0},{5,1},{6,2},{7,3},{8,12},{9,13},{10,... | collective-permute-start | bytes 786440 | tf_op jit(solution)/shard_map/ppermute | solution.py:47
  167.2 14.8 %collective-permute-start.57 = (bf16[128,1024]{1,0:T(8,128)(2,1)S(1)}, bf16[128,1024]{1,0:T(8,128)(2,1)S(1)}, u32[]{:S(2)}, u32[]{:S(2)}) collective-permute-start(bf16[128,1024]{1,0:T(8,128)(2,1)S(1)} %collective-permute-done.38.refs_0_.refs_1_.grad_ref), channel_id=1, source_target_pairs={{0,4},{1,5},{2,6},{3,7},{4,0},{5,1},{6,2},{7,3},{8,12},{9,13},{10,... | collective-permute-start | bytes 786440 | tf_op jit(solution)/shard_map/ppermute | solution.py:47
  167.9 14.0 %collective-permute-start.58 = (bf16[128,1024]{1,0:T(8,128)(2,1)S(1)}, bf16[128,1024]{1,0:T(8,128)(2,1)S(1)}, u32[]{:S(2)}, u32[]{:S(2)}) collective-permute-start(bf16[128,1024]{1,0:T(8,128)(2,1)S(1)} %collective-permute-done.38.refs_0_.refs_1_.grad_ref), channel_id=1, source_target_pairs={{0,6},{1,7},{2,4},{3,5},{4,2},{5,3},{6,0},{7,1},{8,14},{9,15},{10,... | collective-permute-start | bytes 786440 | tf_op jit(solution)/shard_map/ppermute | solution.py:47
  169.8 16.5 %collective-permute-start.53 = (bf16[128,1024]{1,0:T(8,128)(2,1)S(1)}, bf16[128,1024]{1,0:T(8,128)(2,1)S(1)}, u32[]{:S(2)}, u32[]{:S(2)}) collective-permute-start(bf16[128,1024]{1,0:T(8,128)(2,1)S(1)} %get-tuple-element.497.refs_0_), channel_id=1, source_target_pairs={{0,2},{1,3},{2,0},{3,1},{4,6},{5,7},{6,4},{7,5},{8,10},{9,11},{10,... | collective-permute-start | bytes 786440 | tf_op jit(solution)/shard_map/ppermute | solution.py:47
  171.2 21.4 %collective-permute-start.54 = (bf16[128,1024]{1,0:T(8,128)(2,1)S(1)}, bf16[128,1024]{1,0:T(8,128)(2,1)S(1)}, u32[]{:S(2)}, u32[]{:S(2)}) collective-permute-start(bf16[128,1024]{1,0:T(8,128)(2,1)S(1)} %get-tuple-element.497.refs_0_), channel_id=1, source_target_pairs={{0,4},{1,5},{2,6},{3,7},{4,0},{5,1},{6,2},{7,3},{8,12},{9,13},{10,... | collective-permute-start | bytes 786440 | tf_op jit(solution)/shard_map/ppermute | solution.py:47
  175.0 17.5 %collective-permute-start.55 = (bf16[128,1024]{1,0:T(8,128)(2,1)S(1)}, bf16[128,1024]{1,0:T(8,128)(2,1)S(1)}, u32[]{:S(2)}, u32[]{:S(2)}) collective-permute-start(bf16[128,1024]{1,0:T(8,128)(2,1)S(1)} %get-tuple-element.497.refs_0_), channel_id=1, source_target_pairs={{0,6},{1,7},{2,4},{3,5},{4,2},{5,3},{6,0},{7,1},{8,14},{9,15},{10,... | collective-permute-start | bytes 786440 | tf_op jit(solution)/shard_map/ppermute | solution.py:47
  205.5 16.4 %collective-permute-start.63 = (bf16[512,1024]{1,0:T(8,128)(2,1)S(1)}, bf16[512,1024]{1,0:T(8,128)(2,1)S(1)}, u32[]{:S(2)}, u32[]{:S(2)}) collective-permute-start(bf16[512,1024]{1,0:T(8,128)(2,1)S(1)} %get-tuple-element.517), channel_id=1, source_target_pairs={{0,1},{1,0},{2,3},{3,2},{4,5},{5,4},{6,7},{7,6},{8,9},{9,8},{10,11... | collective-permute-start | bytes 3145736 | tf_op jit(solution)/shard_map/ppermute | solution.py:50
  206.3 27.9 %collective-permute-start.67 = (bf16[512,1024]{1,0:T(8,128)(2,1)S(1)}, bf16[512,1024]{1,0:T(8,128)(2,1)S(1)}, u32[]{:S(2)}, u32[]{:S(2)}) collective-permute-start(bf16[512,1024]{1,0:T(8,128)(2,1)S(1)} %add_low.26.a_ref), channel_id=1, source_target_pairs={{0,8},{24,16},{1,9},{25,17},{2,10},{26,18},{3,11},{27,19},{4,12},{... | collective-permute-start | bytes 3145736 | tf_op jit(solution)/shard_map/ppermute | solution.py:571
  208.4 13.6 %collective-permute-start.61 = (bf16[128,1024]{1,0:T(8,128)(2,1)S(1)}, bf16[128,1024]{1,0:T(8,128)(2,1)S(1)}, u32[]{:S(2)}, u32[]{:S(2)}) collective-permute-start(bf16[128,1024]{1,0:T(8,128)(2,1)S(1)} %get-tuple-element.513), channel_id=1, source_target_pairs={{0,4},{1,5},{2,6},{3,7},{4,0},{5,1},{6,2},{7,3},{8,12},{9,13},{10,... | collective-permute-start | bytes 786440 | tf_op jit(solution)/shard_map/ppermute | solution.py:47
  226.4 41.4 %collective-permute-start.73 = (bf16[512,1024]{1,0:T(8,128)(2,1)S(1)}, bf16[512,1024]{1,0:T(8,128)(2,1)S(1)}, u32[]{:S(2)}, u32[]{:S(2)}) collective-permute-start(bf16[512,1024]{1,0:T(8,128)(2,1)S(1)} %add_low.28.a_ref), channel_id=1, source_target_pairs={{0,8},{24,16},{1,9},{25,17},{2,10},{26,18},{3,11},{27,19},{4,12},{... | collective-permute-start | bytes 3145736 | tf_op jit(solution)/shard_map/ppermute | solution.py:571
  246.9 20.9 %collective-permute-start.71 = (bf16[512,1024]{1,0:T(8,128)(2,1)S(1)}, bf16[512,1024]{1,0:T(8,128)(2,1)S(1)}, u32[]{:S(2)}, u32[]{:S(2)}) collective-permute-start(bf16[512,1024]{1,0:T(8,128)(2,1)S(1)} %get-tuple-element.543), channel_id=1, source_target_pairs={{0,1},{1,0},{2,3},{3,2},{4,5},{5,4},{6,7},{7,6},{8,9},{9,8},{10,11... | collective-permute-start | bytes 3145736 | tf_op jit(solution)/shard_map/ppermute | solution.py:50
  247.3 27.4 %collective-permute-start.72 = (bf16[512,1024]{1,0:T(8,128)(2,1)S(1)}, bf16[512,1024]{1,0:T(8,128)(2,1)S(1)}, u32[]{:S(2)}, u32[]{:S(2)}) collective-permute-start(bf16[512,1024]{1,0:T(8,128)(2,1)S(1)} %add_low.27.a_ref), channel_id=1, source_target_pairs={{8,16},{16,8},{9,17},{17,9},{10,18},{18,10},{11,19},{19,11},{12,20... | collective-permute-start | bytes 3145736 | tf_op jit(solution)/shard_map/ppermute | solution.py:571
  276.5 13.5 %collective-permute-start.75 = (bf16[128,1024]{1,0:T(8,128)(2,1)S(1)}, bf16[128,1024]{1,0:T(8,128)(2,1)S(1)}, u32[]{:S(2)}, u32[]{:S(2)}) collective-permute-start(bf16[128,1024]{1,0:T(8,128)(2,1)S(1)} %get-tuple-element.555.refs_0_.refs_1_), channel_id=1, source_target_pairs={{0,4},{1,5},{2,6},{3,7},{4,0},{5,1},{6,2},{7,3},{8,12},{9,13},{10,... | collective-permute-start | bytes 786440 | tf_op jit(solution)/shard_map/ppermute | solution.py:47
  279.1 23.0 %collective-permute-start.78 = (bf16[512,1024]{1,0:T(8,128)(2,1)S(1)}, bf16[512,1024]{1,0:T(8,128)(2,1)S(1)}, u32[]{:S(2)}, u32[]{:S(2)}) collective-permute-start(bf16[512,1024]{1,0:T(8,128)(2,1)S(1)} %add_low.29.b_ref), channel_id=1, source_target_pairs={{8,0},{16,24},{9,1},{17,25},{10,2},{18,26},{11,3},{19,27},{12,4},{... | collective-permute-start | bytes 3145736 | tf_op jit(solution)/shard_map/ppermute | solution.py:571
  281.0 25.8 %collective-permute-start.79 = (bf16[512,1024]{1,0:T(8,128)(2,1)S(1)}, bf16[512,1024]{1,0:T(8,128)(2,1)S(1)}, u32[]{:S(2)}, u32[]{:S(2)}) collective-permute-start(bf16[512,1024]{1,0:T(8,128)(2,1)S(1)} %add_low.30.a_ref), channel_id=1, source_target_pairs={{8,16},{16,8},{9,17},{17,9},{10,18},{18,10},{11,19},{19,11},{12,20... | collective-permute-start | bytes 3145736 | tf_op jit(solution)/shard_map/ppermute | solution.py:571
  284.8 25.5 %collective-permute-start.80 = (bf16[512,1024]{1,0:T(8,128)(2,1)S(1)}, bf16[512,1024]{1,0:T(8,128)(2,1)S(1)}, u32[]{:S(2)}, u32[]{:S(2)}) collective-permute-start(bf16[512,1024]{1,0:T(8,128)(2,1)S(1)} %add_low.31.a_ref), channel_id=1, source_target_pairs={{0,8},{24,16},{1,9},{25,17},{2,10},{26,18},{3,11},{27,19},{4,12},{... | collective-permute-start | bytes 3145736 | tf_op jit(solution)/shard_map/ppermute | solution.py:571
  291.8 18.5 %collective-permute-start.77 = (bf16[512,1024]{1,0:T(8,128)(2,1)S(1)}, bf16[512,1024]{1,0:T(8,128)(2,1)S(1)}, u32[]{:S(2)}, u32[]{:S(2)}) collective-permute-start(bf16[512,1024]{1,0:T(8,128)(2,1)S(1)} %get-tuple-element.567), channel_id=1, source_target_pairs={{0,1},{1,0},{2,3},{3,2},{4,5},{5,4},{6,7},{7,6},{8,9},{9,8},{10,11... | collective-permute-start | bytes 3145736 | tf_op jit(solution)/shard_map/ppermute | solution.py:50
  312.2 25.9 %collective-permute-start.84 = (bf16[512,1024]{1,0:T(8,128)(2,1)S(1)}, bf16[512,1024]{1,0:T(8,128)(2,1)S(1)}, u32[]{:S(2)}, u32[]{:S(2)}) collective-permute-start(bf16[512,1024]{1,0:T(8,128)(2,1)S(1)} %get-tuple-element.580), channel_id=1, source_target_pairs={{0,1},{1,0},{2,3},{3,2},{4,5},{5,4},{6,7},{7,6},{8,9},{9,8},{10,11... | collective-permute-start | bytes 3145736 | tf_op jit(solution)/shard_map/ppermute | solution.py:50
  312.5 28.5 %collective-permute-start.88 = (bf16[512,1024]{1,0:T(8,128)(2,1)S(1)}, bf16[512,1024]{1,0:T(8,128)(2,1)S(1)}, u32[]{:S(2)}, u32[]{:S(2)}) collective-permute-start(bf16[512,1024]{1,0:T(8,128)(2,1)S(1)} %add_low.32.b_ref), channel_id=1, source_target_pairs={{8,0},{16,24},{9,1},{17,25},{10,2},{18,26},{11,3},{19,27},{12,4},{... | collective-permute-start | bytes 3145736 | tf_op jit(solution)/shard_map/ppermute | solution.py:571
  315.6 27.0 %collective-permute-start.89 = (bf16[512,1024]{1,0:T(8,128)(2,1)S(1)}, bf16[512,1024]{1,0:T(8,128)(2,1)S(1)}, u32[]{:S(2)}, u32[]{:S(2)}) collective-permute-start(bf16[512,1024]{1,0:T(8,128)(2,1)S(1)} %add_low.33.a_ref), channel_id=1, source_target_pairs={{8,16},{16,8},{9,17},{17,9},{10,18},{18,10},{11,19},{19,11},{12,20... | collective-permute-start | bytes 3145736 | tf_op jit(solution)/shard_map/ppermute | solution.py:571
  318.2 26.7 %collective-permute-start.90 = (bf16[512,1024]{1,0:T(8,128)(2,1)S(1)}, bf16[512,1024]{1,0:T(8,128)(2,1)S(1)}, u32[]{:S(2)}, u32[]{:S(2)}) collective-permute-start(bf16[512,1024]{1,0:T(8,128)(2,1)S(1)} %add_low.34.a_ref), channel_id=1, source_target_pairs={{0,8},{24,16},{1,9},{25,17},{2,10},{26,18},{3,11},{27,19},{4,12},{... | collective-permute-start | bytes 3145736 | tf_op jit(solution)/shard_map/ppermute | solution.py:571
  341.0 13.4 %collective-permute-start.87 = (bf16[128,1024]{1,0:T(8,128)(2,1)S(1)}, bf16[128,1024]{1,0:T(8,128)(2,1)S(1)}, u32[]{:S(2)}, u32[]{:S(2)}) collective-permute-start(bf16[128,1024]{1,0:T(8,128)(2,1)S(1)} %get-tuple-element.593.refs_0_.refs_6_), channel_id=1, source_target_pairs={{0,6},{1,7},{2,4},{3,5},{4,2},{5,3},{6,0},{7,1},{8,14},{9,15},{10,... | collective-permute-start | bytes 786440 | tf_op jit(solution)/shard_map/ppermute | solution.py:47
  342.6 20.8 %collective-permute-start.91 = (bf16[128,1024]{1,0:T(8,128)(2,1)S(1)}, bf16[128,1024]{1,0:T(8,128)(2,1)S(1)}, u32[]{:S(2)}, u32[]{:S(2)}) collective-permute-start(bf16[128,1024]{1,0:T(8,128)(2,1)S(1)} %get-tuple-element.604), channel_id=1, source_target_pairs={{0,2},{1,3},{2,0},{3,1},{4,6},{5,7},{6,4},{7,5},{8,10},{9,11},{10,... | collective-permute-start | bytes 786440 | tf_op jit(solution)/shard_map/ppermute | solution.py:47
  345.0 18.4 %collective-permute-start.92 = (bf16[128,1024]{1,0:T(8,128)(2,1)S(1)}, bf16[128,1024]{1,0:T(8,128)(2,1)S(1)}, u32[]{:S(2)}, u32[]{:S(2)}) collective-permute-start(bf16[128,1024]{1,0:T(8,128)(2,1)S(1)} %get-tuple-element.605), channel_id=1, source_target_pairs={{0,4},{1,5},{2,6},{3,7},{4,0},{5,1},{6,2},{7,3},{8,12},{9,13},{10,... | collective-permute-start | bytes 786440 | tf_op jit(solution)/shard_map/ppermute | solution.py:47
  348.0 15.4 %collective-permute-start.93 = (bf16[128,1024]{1,0:T(8,128)(2,1)S(1)}, bf16[128,1024]{1,0:T(8,128)(2,1)S(1)}, u32[]{:S(2)}, u32[]{:S(2)}) collective-permute-start(bf16[128,1024]{1,0:T(8,128)(2,1)S(1)} %get-tuple-element.606), channel_id=1, source_target_pairs={{0,6},{1,7},{2,4},{3,5},{4,2},{5,3},{6,0},{7,1},{8,14},{9,15},{10,... | collective-permute-start | bytes 786440 | tf_op jit(solution)/shard_map/ppermute | solution.py:47
  350.9 49.4 %collective-permute-start.100 = (bf16[512,1024]{1,0:T(8,128)(2,1)S(1)}, bf16[512,1024]{1,0:T(8,128)(2,1)}, u32[]{:S(2)}, u32[]{:S(2)}) collective-permute-start(bf16[512,1024]{1,0:T(8,128)(2,1)S(1)} %add_low.37.a_ref), channel_id=1, source_target_pairs={{0,8},{24,16},{1,9},{25,17},{2,10},{26,18},{3,11},{27,19},{4,12},{... | collective-permute-start | bytes 3145736 | tf_op jit(solution)/shard_map/ppermute | solution.py:571
  367.3 33.1 %collective-permute-start.97 = (bf16[512,1024]{1,0:T(8,128)(2,1)}, bf16[512,1024]{1,0:T(8,128)(2,1)}, u32[]{:S(2)}, u32[]{:S(2)}) collective-permute-start(bf16[512,1024]{1,0:T(8,128)(2,1)} %get-tuple-element.614), channel_id=1, source_target_pairs={{0,1},{1,0},{2,3},{3,2},{4,5},{5,4},{6,7},{7,6},{8,9},{9,8},{10,11... | collective-permute-start | bytes 3145736 | tf_op jit(solution)/shard_map/ppermute | solution.py:50
  368.6 31.7 %collective-permute-start.98 = (bf16[512,1024]{1,0:T(8,128)(2,1)}, bf16[512,1024]{1,0:T(8,128)(2,1)}, u32[]{:S(2)}, u32[]{:S(2)}) collective-permute-start(bf16[512,1024]{1,0:T(8,128)(2,1)} %add_low.35.b_ref), channel_id=1, source_target_pairs={{8,0},{16,24},{9,1},{17,25},{10,2},{18,26},{11,3},{19,27},{12,4},{... | collective-permute-start | bytes 3145736 | tf_op jit(solution)/shard_map/ppermute | solution.py:571
  373.5 27.2 %collective-permute-start.99 = (bf16[512,1024]{1,0:T(8,128)(2,1)S(1)}, bf16[512,1024]{1,0:T(8,128)(2,1)}, u32[]{:S(2)}, u32[]{:S(2)}) collective-permute-start(bf16[512,1024]{1,0:T(8,128)(2,1)S(1)} %add_low.36.a_ref), channel_id=1, source_target_pairs={{8,16},{16,8},{9,17},{17,9},{10,18},{18,10},{11,19},{19,11},{12,20... | collective-permute-start | bytes 3145736 | tf_op jit(solution)/shard_map/ppermute | solution.py:571
  402.2 29.5 %collective-permute-start.106 = (bf16[512,1024]{1,0:T(8,128)(2,1)S(1)}, bf16[512,1024]{1,0:T(8,128)(2,1)S(1)}, u32[]{:S(2)}, u32[]{:S(2)}) collective-permute-start(bf16[512,1024]{1,0:T(8,128)(2,1)S(1)} %add_low.39.b_ref), channel_id=1, source_target_pairs={{8,0},{16,24},{9,1},{17,25},{10,2},{18,26},{11,3},{19,27},{12,4},{... | collective-permute-start | bytes 3145736 | tf_op jit(solution)/shard_map/ppermute | solution.py:571
  405.3 26.4 %collective-permute-start.107 = (bf16[512,1024]{1,0:T(8,128)(2,1)S(1)}, bf16[512,1024]{1,0:T(8,128)(2,1)S(1)}, u32[]{:S(2)}, u32[]{:S(2)}) collective-permute-start(bf16[512,1024]{1,0:T(8,128)(2,1)S(1)} %add_low.40.a_ref), channel_id=1, source_target_pairs={{8,16},{16,8},{9,17},{17,9},{10,18},{18,10},{11,19},{19,11},{12,20... | collective-permute-start | bytes 3145736 | tf_op jit(solution)/shard_map/ppermute | solution.py:571
  410.4 21.3 %collective-permute-start.101 = (bf16[128,1024]{1,0:T(8,128)(2,1)S(1)}, bf16[128,1024]{1,0:T(8,128)(2,1)S(1)}, u32[]{:S(2)}, u32[]{:S(2)}) collective-permute-start(bf16[128,1024]{1,0:T(8,128)(2,1)S(1)} %get-tuple-element.625), channel_id=1, source_target_pairs={{0,0},{1,1},{10,2},{11,3},{20,4},{21,5},{30,6},{31,7},{2,8},{3,9},... | collective-permute-start | bytes 786440 | tf_op jit(solution)/shard_map/ppermute | solution.py:44
  432.9 37.1 %collective-permute-start.113 = (bf16[512,1024]{1,0:T(8,128)(2,1)S(1)}, bf16[512,1024]{1,0:T(8,128)(2,1)}, u32[]{:S(2)}, u32[]{:S(2)}) collective-permute-start(bf16[512,1024]{1,0:T(8,128)(2,1)S(1)} %add_low.41.b_ref), channel_id=1, source_target_pairs={{8,0},{16,24},{9,1},{17,25},{10,2},{18,26},{11,3},{19,27},{12,4},{... | collective-permute-start | bytes 3145736 | tf_op jit(solution)/shard_map/ppermute | solution.py:571
  438.2 14.1 %collective-permute-start.111 = (f32[2,1536]{1,0:T(2,128)S(1)}, f32[2,1536]{1,0:T(2,128)S(1)}, u32[]{:S(2)}, u32[]{:S(2)}) collective-permute-start(f32[2,1536]{1,0:T(2,128)S(1)} %get-tuple-element.747), channel_id=1, source_target_pairs={{0,6},{1,7},{2,4},{3,5},{4,2},{5,3},{6,0},{7,1},{8,14},{9,15},{10,... | collective-permute-start | bytes 36872 | tf_op jit(solution)/shard_map/ppermute | solution.py:47
  450.4 18.9 %collective-permute-start.108 = (bf16[128,1024]{1,0:T(8,128)(2,1)}, bf16[128,1024]{1,0:T(8,128)(2,1)S(1)}, u32[]{:S(2)}, u32[]{:S(2)}) collective-permute-start(bf16[128,1024]{1,0:T(8,128)(2,1)} %copy-done.35), channel_id=1, source_target_pairs={{0,0},{1,1},{10,2},{11,3},{20,4},{21,5},{30,6},{31,7},{2,8},{3,9},... | collective-permute-start | bytes 786440 | tf_op jit(solution)/shard_map/ppermute | solution.py:44
  452.3 16.9 %collective-permute-start.114 = (bf16[128,768]{1,0:T(8,128)(2,1)}, bf16[128,768]{1,0:T(8,128)(2,1)S(1)}, u32[]{:S(2)}, u32[]{:S(2)}) collective-permute-start(bf16[128,768]{1,0:T(8,128)(2,1)} %get-tuple-element.653.a_ref), channel_id=1, source_target_pairs={{0,8},{24,16},{1,9},{25,17},{2,10},{26,18},{3,11},{27,19},{4,12},{... | collective-permute-start | bytes 589832 | tf_op jit(solution)/shard_map/ppermute | solution.py:571
  453.6 30.4 %collective-permute-start.117 = (bf16[512,256]{1,0:T(8,128)(2,1)S(1)}, bf16[512,256]{1,0:T(8,128)(2,1)S(1)}, u32[]{:S(2)}, u32[]{:S(2)}) collective-permute-start(bf16[512,256]{1,0:T(8,128)(2,1)S(1)} %slice.109.a_ref), channel_id=1, source_target_pairs={{0,8},{24,16},{1,9},{25,17},{2,10},{26,18},{3,11},{27,19},{4,12},{... | collective-permute-start | bytes 786440 | tf_op jit(solution)/shard_map/ppermute | solution.py:571
  454.9 14.3 %collective-permute-start.112 = (f32[2,1536]{1,0:T(2,128)S(1)}, f32[2,1536]{1,0:T(2,128)S(1)}, u32[]{:S(2)}, u32[]{:S(2)}) collective-permute-start(f32[2,1536]{1,0:T(2,128)S(1)} %fusion.3), channel_id=1, source_target_pairs={{0,8},{8,0},{16,24},{24,16},{1,9},{9,1},{17,25},{25,17},{2,10},{10... | collective-permute-start | bytes 36872 | tf_op jit(solution)/shard_map/ppermute | solution.py:880
  497.2 17.4 %collective-permute-start.121 = (bf16[512,256]{1,0:T(8,128)(2,1)S(1)}, bf16[512,256]{1,0:T(8,128)(2,1)}, u32[]{:S(2)}, u32[]{:S(2)}) collective-permute-start(bf16[512,256]{1,0:T(8,128)(2,1)S(1)} %add_low.45.b_ref), channel_id=1, source_target_pairs={{8,0},{16,24},{9,1},{17,25},{10,2},{18,26},{11,3},{19,27},{12,4},{... | collective-permute-start | bytes 786440 | tf_op jit(solution)/shard_map/ppermute | solution.py:571
  511.1 19.9 %collective-permute-start.133 = (bf16[128,1024]{1,0:T(8,128)(2,1)S(1)}, bf16[128,1024]{1,0:T(8,128)(2,1)S(1)}, u32[]{:S(2)}, u32[]{:S(2)}) collective-permute-start(bf16[128,1024]{1,0:T(8,128)(2,1)S(1)} %get-tuple-element.730), channel_id=1, source_target_pairs={{0,2},{1,3},{2,0},{3,1},{4,6},{5,7},{6,4},{7,5},{8,10},{9,11},{10,... | collective-permute-start | bytes 786440 | tf_op jit(solution)/shard_map/ppermute | solution.py:47
  511.1 20.8 %collective-permute-start.134 = (bf16[128,1024]{1,0:T(8,128)(2,1)S(1)}, bf16[128,1024]{1,0:T(8,128)(2,1)S(1)}, u32[]{:S(2)}, u32[]{:S(2)}) collective-permute-start(bf16[128,1024]{1,0:T(8,128)(2,1)S(1)} %get-tuple-element.729), channel_id=1, source_target_pairs={{0,4},{1,5},{2,6},{3,7},{4,0},{5,1},{6,2},{7,3},{8,12},{9,13},{10,... | collective-permute-start | bytes 786440 | tf_op jit(solution)/shard_map/ppermute | solution.py:47
  512.4 20.9 %collective-permute-start.135 = (bf16[128,1024]{1,0:T(8,128)(2,1)S(1)}, bf16[128,1024]{1,0:T(8,128)(2,1)S(1)}, u32[]{:S(2)}, u32[]{:S(2)}) collective-permute-start(bf16[128,1024]{1,0:T(8,128)(2,1)S(1)} %get-tuple-element.728), channel_id=1, source_target_pairs={{0,6},{1,7},{2,4},{3,5},{4,2},{5,3},{6,0},{7,1},{8,14},{9,15},{10,... | collective-permute-start | bytes 786440 | tf_op jit(solution)/shard_map/ppermute | solution.py:47
  (135 other events, 1272.5 us)

commit v3 on v2

v3 whole, which is shorter than its diff:
```python
import jax
import jax.numpy as jnp
from jax import lax
from jax.experimental import pallas as pl
from jax.experimental.pallas import tpu as pltpu
from jax.sharding import PartitionSpec as P

D = 1024
HEAD_DIM = 64
FF = 4096
EPS = 1e-05
NEG = -1e30
SCALE = 0.125
BF = jnp.bfloat16
F32 = jnp.float32
LANES = 128


def xor_pairs(count, mask):
    return [(i, i ^ mask) for i in range(count)]


class Net:
    def __init__(self):
        self.n_s = lax.axis_size("seq")
        self.n_f = lax.axis_size("fsdp")
        self.n_p = self.n_f // 2
        self.s = lax.axis_index("seq")
        self.f = lax.axis_index("fsdp")
        self.p = self.f // 2
        self.c = self.f % 2
        self.place = jnp.stack([self.p, self.c]).astype(jnp.int32)

    def moves(self):
        n, n_p = self.n_f, self.n_p
        square = [[s ^ q for s in range(self.n_s)] for q in range(n_p)]
        if n_p == 4:
            square = [[0, 2, 1, 3], [1, 3, 2, 0], [2, 0, 3, 1], [3, 1, 0, 2]]
        pairs = []
        for s in range(self.n_s):
            for q in range(n_p):
                p = square[q][s]
                pairs += [(s * n + 2 * p + c, p * n + 2 * q + c) for c in range(2)]
        return pairs

    def to_planes(self, v):
        return lax.ppermute(v, ("seq", "fsdp"), self.moves())

    def from_planes(self, v):
        return lax.ppermute(v, ("seq", "fsdp"), [(b, a) for a, b in self.moves()])

    def chip(self, v, j):
        return lax.ppermute(v, "fsdp", xor_pairs(self.n_f, 2 * j))

    def core(self, v):
        return lax.ppermute(v, "fsdp", xor_pairs(self.n_f, 1))

    def gather(self, v):
        return [v] + [self.chip(v, j) for j in range(1, self.n_p)]

    def exchange(self, blocks):
        return [blocks[0]] + [self.chip(blocks[j], j) for j in range(1, self.n_p)]


def fence(values):
    return lax.optimization_barrier(values)


def block(v, index, size, axis):
    return lax.dynamic_slice_in_dim(v, index * size, size, axis=axis)


IN_VMEM = pl.BlockSpec(memory_space=pltpu.VMEM)
IN_SMEM = pl.BlockSpec(memory_space=pltpu.SMEM)
IN_ANY = pl.BlockSpec(memory_space=pl.ANY)
IN_HBM = pl.BlockSpec(memory_space=pltpu.HBM)


def run(name, body, outs, ins, place=None, scratch=(), flops=0, ins_at=None):
    specs = [IN_VMEM] * len(ins) if ins_at is None else ins_at
    if place is not None:
        specs = [IN_SMEM] + specs
        ins = [place, *ins]
    moved = sum(v.size * v.dtype.itemsize for v in ins)
    return pl.pallas_call(
        body,
        out_shape=[jax.ShapeDtypeStruct(shape, dtype) for shape, dtype in outs],
        in_specs=specs,
        out_specs=[IN_VMEM] * len(outs),
        scratch_shapes=list(scratch),
        compiler_params=pltpu.CompilerParams(vmem_limit_bytes=16 << 20),
        cost_estimate=pl.CostEstimate(flops=flops, bytes_accessed=moved, transcendentals=0),
        name=name,
    )(*ins)


def dot(a, b):
    return jnp.dot(a, b, preferred_element_type=F32)


def dot_nt(a, b):
    return lax.dot_general(a, b, (((1,), (1,)), ((), ())), preferred_element_type=F32)


def dot_tn(a, b):
    return lax.dot_general(a, b, (((0,), (0,)), ((), ())), preferred_element_type=F32)


def tile(i, size):
    return pl.ds(pl.multiple_of(i * size, size), size)


def copy_all(pairs, sems):
    copies = [pltpu.make_async_copy(src, dst, sems.at[k]) for k, (src, dst) in enumerate(pairs)]
    for copy in copies:
        copy.start()
    return copies


def own_first(v, parts, c):
    rows = v.shape[-1] // (2 * parts)
    own, other = [], []
    for i in range(parts):
        even = v[:, 2 * i * rows : (2 * i + 1) * rows]
        odd = v[:, (2 * i + 1) * rows : (2 * i + 2) * rows]
        own.append(jnp.where(c == 0, even, odd))
        other.append(jnp.where(c == 0, odd, even))
    return jnp.concatenate(own, axis=1), jnp.concatenate(other, axis=1)


def model_order(v, parts, c):
    half = v.shape[-1] // 2
    rows = half // parts
    out = []
    for i in range(parts):
        own = v[:, i * rows : (i + 1) * rows]
        other = v[:, half + i * rows : half + (i + 1) * rows]
        out += [jnp.where(c == 0, own, other), jnp.where(c == 0, other, own)]
    return jnp.concatenate(out, axis=1)


def stack_rows(net, pieces, weight, layer):
    n_p = net.n_p
    rows, width = D // net.n_f, pieces[0].shape[1]
    more, depth = weight.shape[1:]

    def body(place, *refs):
        p = place[0]
        own, rest, sems = refs[n_p + 1 :]
        pairs = [(refs[j].at[0:rows], own.at[tile(p ^ j, rows)]) for j in range(n_p)]
        for copy in copy_all([*pairs, (refs[n_p].at[layer], rest)], sems):
            copy.wait()

    outs = [((n_p * rows, width), BF), ((more, depth), BF)]
    specs = [IN_ANY] * n_p + [IN_HBM]
    scratch = [pltpu.SemaphoreType.DMA((n_p + 1,))]
    return run("stack_rows", body, outs, [*pieces, weight], net.place, scratch, ins_at=specs)


def pack_tokens(tokens, scene_ids, token_kind):
    rows = tokens.shape[1]
    code = (scene_ids * 2 + token_kind).astype(BF)
    return jnp.pad(tokens[0], ((0, 16), (0, 0))) + jnp.pad(code, ((rows, 15), (0, D - rows)))


def pack_small(vectors):
    sizes = [v.shape[1] for v in vectors]
    total = None
    for k, v in enumerate(vectors):
        at = sum(sizes[:k])
        put = jnp.pad(v, ((0, 0), (at, sum(sizes) - at - sizes[k])))
        total = put if total is None else total + put
    return total


def cut_columns(net, weight, layer, groups, small):
    n_p = net.n_p
    rows = weight.shape[1]
    width = weight.shape[2] // (groups * n_p)
    extra = 16 if small else 0

    def body(place, weight_ref, *refs):
        p = place[0]
        outs, sems = refs[len(small) : len(small) + n_p], refs[-1]
        pairs = []
        for j in range(n_p):
            for i in range(groups):
                cols = tile(i * n_p + (p ^ j), width)
                to = outs[j].at[0:rows, i * width : (i + 1) * width]
                pairs.append((weight_ref.at[layer, :, cols], to))
        copies = copy_all(pairs, sems)
        if extra:
            lines = refs[2 + n_p]
            lines[...] = jnp.zeros_like(lines)
            row = 0
            for ref in refs[:2]:
                low = ref[...].astype(F32)
                for k in range(ref.shape[0]):
                    for half in range(2):
                        cols = slice(half * groups * width, (half + 1) * groups * width)
                        lines[row : row + 1, :] = low[k : k + 1, cols]
                        row += 1
            for j in range(n_p):
                outs[j][rows : rows + extra, :] = lines[...].astype(BF)
        for copy in copies:
            copy.wait()

    outs = [((rows + extra, groups * width), BF)] * n_p
    specs = [IN_HBM] + [IN_VMEM] * len(small)
    scratch = [pltpu.VMEM((16, groups * width), F32)] if extra else []
    scratch.append(pltpu.SemaphoreType.DMA((groups * n_p,)))
    return list(run("cut_columns", body, outs, [weight, *small], net.place, scratch, ins_at=specs))


def join_vectors(net, layers, pieces, sizes):
    n_p = net.n_p
    width = pieces[0].shape[1]
    starts = [sum(sizes[:i]) for i in range(len(sizes))]
    first_row = D // net.n_f

    def body(place, *refs):
        p, c = place[0], place[1]
        ins, outs = refs[:n_p], refs[n_p:]
        for j in range(n_p):
            low = ins[j][first_row : first_row + 16, :].astype(F32)
            for layer in range(layers):
                for half in range(2):
                    row = layer * 2 + half
                    own = low[row : row + 1, :]
                    other = low[2 * layers + row : 2 * layers + row + 1, :]
                    first = jnp.where(c == 0, own, other)
                    second = jnp.where(c == 0, other, own)
                    for k, (at, size) in enumerate(zip(starts, sizes)):
                        if at // width != half:
                            continue
                        cols = slice(at - half * width, at - half * width + size)
                        both = jnp.concatenate([first[:, cols], second[:, cols]], axis=1)
                        outs[k][layer : layer + 1, tile(p ^ j, 2 * size)] = both

    outs = [((layers, 2 * n_p * size), F32) for size in sizes]
    return run("join_vectors", body, outs, pieces, net.place)


def norm_rows(hidden):
    centred = hidden - jnp.mean(hidden, axis=-1, keepdims=True)
    spread = jnp.mean(centred * centred, axis=-1, keepdims=True)
    inverse = lax.rsqrt(spread + EPS)
    return centred * inverse, inverse


def add_and_norm(net, layer, hidden, parts, bias, norm):
    rows = parts[0].shape[0]
    count = len(parts)

    def body(place, *refs):
        total = refs[0][0:rows, :].astype(F32) + refs[1 + count][layer : layer + 1, :]
        for part in refs[1 : 1 + count]:
            total = total + part[...].astype(F32)
        if norm is None:
            refs[2 + count][...] = total.astype(BF)
            return
        gain, shift, out, low = refs[2 + count : 6 + count]
        normed, _ = norm_rows(total)
        row = slice(norm[0], norm[0] + 1)
        out[...] = total
        own, other = own_first(normed * gain[row, :] + shift[row, :], net.n_p, place[1])
        low[:, : D // 2] = own.astype(BF)
        low[:, D // 2 :] = other.astype(BF)

    ins = [hidden, *parts, bias] + ([] if norm is None else list(norm[1:]))
    outs = [((rows, D), BF)] if norm is None else [((rows, D), F32), ((rows, D), BF)]
    return run("add_and_norm", body, outs, ins, net.place)


def norm_back(net, layer, grad, hidden, parts, gain):
    rows = parts[0].shape[0]
    count = len(parts)

    def body(place, grad_ref, hidden_ref, gain_ref, *refs):
        total = refs[0][...].astype(F32)
        for part in refs[1:count]:
            total = total + part[...].astype(F32)
        total = model_order(total, net.n_p, place[1])
        out, low, sums = refs[count:]
        normed, inverse = norm_rows(hidden_ref[0:rows, :].astype(F32))
        scaled = total * gain_ref[layer : layer + 1, :]
        one = jnp.mean(scaled, axis=-1, keepdims=True)
        two = jnp.mean(scaled * normed, axis=-1, keepdims=True)
        result = grad_ref[...].astype(F32) + inverse * (scaled - one - normed * two)
        rounded = result.astype(BF)
        out[...] = result
        low[...] = rounded
        sums[0:1, :] = jnp.sum(total * normed, axis=0, keepdims=True)
        sums[1:2, :] = jnp.sum(total, axis=0, keepdims=True)
        sums[2:3, :] = jnp.sum(rounded.astype(F32), axis=0, keepdims=True)

    outs = [((rows, D), F32), ((rows, D), BF), ((3, D), F32)]
    return run("norm_back", body, outs, [grad, hidden, gain, *parts], net.place)


def column_sums(v):
    def body(ref, out):
        out[...] = jnp.sum(ref[...].astype(F32), axis=0, keepdims=True)

    return run("column_sums", body, [((1, v.shape[1]), F32)], [v])[0]


def gather_rows(blocks, scratch):
    rows = scratch.shape[0] // len(blocks)
    for j, ref in enumerate(blocks):
        scratch[j * rows : (j + 1) * rows, :] = ref[0:rows, :]


def allowed_pairs(code_col, code_row):
    same = (code_col >> 1) == (code_row >> 1)
    return same & (((code_col & 1) == 0) | ((code_row & 1) == 1))


def head_lanes(shape, head, axis):
    lane = lax.broadcasted_iota(jnp.int32, shape, axis)
    return (lane < HEAD_DIM) if head == 0 else (lane >= HEAD_DIM)


def keep_head(v, head, axis):
    return jnp.where(head_lanes(v.shape, head, axis), v, jnp.zeros_like(v))


def probs_by_key(k2, q2, allowed, head):
    scores = dot_nt(keep_head(k2, head, 1), q2) * SCALE
    scores = jnp.where(allowed, scores, NEG)
    powers = jnp.exp(scores - jnp.max(scores, axis=0, keepdims=True))
    return powers * (1.0 / jnp.sum(powers, axis=0, keepdims=True))


Q_TILE = 256


def attend(net, layer, rows, blocks, norm, weight, bias, codes, proj):
    n_p = net.n_p
    tokens = n_p * rows
    cw = D // n_p
    first = norm is not None

    def body(place, *refs):
        bias_ref, w_own, w_other, p_own, p_other = refs[n_p : n_p + 5]
        if first:
            gain_ref, shift_ref = refs[n_p + 5 : n_p + 7]
            row_ref, col_ref, a = refs[n_p + 7 : n_p + 10]
            outs = refs[n_p + 10 : 2 * n_p + 10]
            qkv, attended, vt = refs[2 * n_p + 10 :]
        else:
            row_ref, col_ref = refs[n_p + 5 : n_p + 7]
            outs = refs[n_p + 7 : 2 * n_p + 7]
            qkv, attended, vt, a = refs[2 * n_p + 7 :]
        p, c = place[0], place[1]
        if first:
            eye = lax.broadcasted_iota(jnp.int32, (rows, rows), 0) == lax.broadcasted_iota(
                jnp.int32, (rows, rows), 1
            )
            for j in range(n_p):
                here = slice(j * rows, (j + 1) * rows)
                line = refs[j][rows : rows + 1, 0:rows].astype(F32)
                row_ref[:, here] = line.astype(jnp.int32)
                column = jnp.sum(jnp.where(eye, line, 0.0), axis=1, keepdims=True)
                col_ref[here, :] = column.astype(jnp.int32)
                normed, _ = norm_rows(refs[j][0:rows, :].astype(F32))
                own, other = own_first(normed * gain_ref[0:1, :] + shift_ref[0:1, :], n_p, c)
                a[here, : D // 2] = own.astype(BF)
                a[here, D // 2 :] = other.astype(BF)
        else:
            gather_rows(refs[:n_p], a)
        for i in range(3):
            cols = slice(i * cw, (i + 1) * cw)
            out = dot(a[:, : D // 2], w_own[:, cols]) + dot(a[:, D // 2 :], w_other[:, cols])
            if i == 0:
                out = out + bias_ref[layer : layer + 1, tile(p, cw)]
            if i == 2:
                out = out + bias_ref[layer : layer + 1, tile(p + n_p, cw)]
            qkv[:, cols] = out.astype(BF)
        vt[...] = jnp.transpose(qkv[:, 2 * cw : 3 * cw].astype(F32)).astype(BF)

        @pl.loop(0, tokens // Q_TILE)
        def _(t):
            here = tile(t, Q_TILE)
            allowed = allowed_pairs(col_ref[...], row_ref[:, here])
            for pair in range(cw // LANES):
                lanes = slice(pair * LANES, (pair + 1) * LANES)
                q2 = qkv[here, lanes]
                k2 = qkv[:, cw + pair * LANES : cw + (pair + 1) * LANES]
                total = None
                for head in range(2):
                    probs = probs_by_key(k2, q2, allowed, head).astype(BF)
                    part = dot(keep_head(vt[lanes, :], head, 0), probs)
                    total = part if total is None else total + part
                attended[here, lanes] = jnp.transpose(total).astype(BF)

        for j in range(n_p):
            o = attended[j * rows : (j + 1) * rows, :]
            low, high = o[:, : cw // 2], o[:, cw // 2 :]
            own, other = jnp.where(c == 0, low, high), jnp.where(c == 0, high, low)
            outs[j][...] = (dot(own, p_own[...]) + dot(other, p_other[...])).astype(BF)

    outs = [((rows, D), BF)] * n_p + [((tokens, 3 * cw), BF), ((tokens, cw), BF)]
    scratch = [pltpu.VMEM((cw, tokens), BF)]
    ins = [*blocks, bias, *weight, *proj]
    if first:
        ins += list(norm)
        outs = [((1, tokens), jnp.int32), ((tokens, 1), jnp.int32), ((tokens, D), BF)] + outs
    else:
        ins += list(codes)
        scratch.append(pltpu.VMEM((tokens, D), BF))
    got = run("attend", body, outs, ins, net.place, scratch, flops=2 * tokens * D * 4 * cw)
    normed = blocks
    if first:
        codes, normed, got = got[:2], [got[2]], got[3:]
    return got[:n_p], got[n_p], got[n_p + 1], codes, normed


def attend_back(net, blocks, proj, qkv, codes, weight, tokens_in):
    n_p = net.n_p
    rows = blocks[0].shape[0]
    tokens = n_p * rows
    cw = D // n_p
    n_t = len(tokens_in)

    def body(place, *refs):
        p_own, p_other, qkv_ref, row_ref, col_ref, w_own, w_other = refs[n_p : n_p + 7]
        token_refs = refs[n_p + 7 : n_p + 7 + n_t]
        refs_out = refs[n_p + 7 + n_t :]
        outs = refs_out[:n_p]
        dqkv, sums, norm_sums, do, kt, dk, dv = refs_out[n_p:]
        c = place[1]
        for j in range(n_p):
            here = slice(j * rows, (j + 1) * rows)
            own, other = dot_nt(refs[j][...], p_own[...]), dot_nt(refs[j][...], p_other[...])
            do[here, : cw // 2] = jnp.where(c == 0, own, other).astype(BF)
            do[here, cw // 2 :] = jnp.where(c == 0, other, own).astype(BF)
        kt[...] = jnp.transpose(qkv_ref[:, cw : 2 * cw].astype(F32)).astype(BF)
        dk[...] = jnp.zeros_like(dk)
        dv[...] = jnp.zeros_like(dv)

        @pl.loop(0, tokens // Q_TILE)
        def _(t):
            here = tile(t, Q_TILE)
            allowed = allowed_pairs(col_ref[...], row_ref[:, here])
            for pair in range(cw // LANES):
                lanes = slice(pair * LANES, (pair + 1) * LANES)
                q2 = qkv_ref[here, lanes]
                k2 = qkv_ref[:, cw + pair * LANES : cw + (pair + 1) * LANES]
                v2 = qkv_ref[:, 2 * cw + pair * LANES : 2 * cw + (pair + 1) * LANES]
                do2 = do[here, lanes]
                total = None
                for head in range(2):
                    probs = probs_by_key(k2, q2, allowed, head)
                    dp = dot_nt(keep_head(v2, head, 1), do2)
                    mean = jnp.sum(probs * dp, axis=0, keepdims=True)
                    ds = (probs * (dp - mean)).astype(BF)
                    dv[:, lanes] += dot(probs.astype(BF), keep_head(do2, head, 1))
                    dk[:, lanes] += dot(ds, keep_head(q2, head, 1))
                    part = dot(keep_head(kt[lanes, :], head, 0), ds)
                    total = part if total is None else total + part
                dqkv[here, lanes] = (jnp.transpose(total) * SCALE).astype(BF)

        dqkv[:, cw : 2 * cw] = (dk[...] * SCALE).astype(BF)
        dqkv[:, 2 * cw :] = dv[...].astype(BF)
        sums[...] = jnp.sum(dqkv[...].astype(F32), axis=0, keepdims=True)
        norm_sums[...] = jnp.zeros_like(norm_sums)
        for j in range(n_p):
            normed = None
            if n_t:
                normed = own_first(norm_rows(token_refs[j][0:rows, :].astype(F32))[0], n_p, c)
            for k, w in enumerate((w_own, w_other)):
                cols = slice(k * (D // 2), (k + 1) * (D // 2))
                da1 = dot_nt(dqkv[j * rows : (j + 1) * rows, :], w[...])
                outs[j][:, cols] = da1.astype(BF)
                if n_t:
                    norm_sums[0:1, cols] += jnp.sum(da1 * normed[k], axis=0, keepdims=True)
                    norm_sums[1:2, cols] += jnp.sum(da1, axis=0, keepdims=True)

    outs = [((rows, D), BF)] * n_p + [((tokens, 3 * cw), BF), ((1, 3 * cw), F32), ((2, D), F32)]
    scratch = [
        pltpu.VMEM((tokens, cw), BF),
        pltpu.VMEM((cw, tokens), BF),
        pltpu.VMEM((tokens, cw), F32),
        pltpu.VMEM((tokens, cw), F32),
    ]
    ins = [*blocks, *proj, qkv, *codes, *weight, *tokens_in]
    got = run("attend_back", body, outs, ins, net.place, scratch, flops=2 * tokens * D * 8 * cw)
    return got[:n_p], got[n_p], got[n_p + 1], got[n_p + 2]


F_TILE = 256


def feed_forward(net, layer, blocks, up, bias, down):
    n_p = net.n_p
    rows = blocks[0].shape[0]
    tokens = n_p * rows
    fw = FF // n_p

    def body(place, *refs):
        up_own, up_other, bias_ref, d_own, d_other = refs[n_p : n_p + 5]
        outs = refs[n_p + 5 : 2 * n_p + 5]
        z_ref, slope_ref, a_ref = refs[2 * n_p + 5 :]
        p, c = place[0], place[1]
        gather_rows(refs[:n_p], a_ref)

        @pl.loop(0, fw // F_TILE)
        def _(t):
            cols = tile(t, F_TILE)
            there = pl.ds(pl.multiple_of(p * fw + t * F_TILE, F_TILE), F_TILE)
            u = dot(a_ref[:, : D // 2], up_own[:, cols]) + dot(a_ref[:, D // 2 :], up_other[:, cols])
            u = u + bias_ref[layer : layer + 1, there]
            phi = 0.5 * (1.0 + lax.erf(u * 0.7071067811865476))
            z_ref[:, cols] = (u * phi).astype(BF)
            slope_ref[:, cols] = phi + u * (jnp.exp(-0.5 * u * u) * 0.3989422804014327)

        for j in range(n_p):
            here = slice(j * rows, (j + 1) * rows)
            own, other = z_ref[here, tile(c, fw // 2)], z_ref[here, tile(1 - c, fw // 2)]
            outs[j][...] = (dot(own, d_own[...]) + dot(other, d_other[...])).astype(BF)

    outs = [((rows, D), BF)] * n_p + [((tokens, fw), BF), ((tokens, fw), F32)]
    scratch = [pltpu.VMEM((tokens, D), BF)]
    ins = [*blocks, *up, bias, *down]
    got = run("feed_forward", body, outs, ins, net.place, scratch, flops=4 * tokens * D * fw)
    return got[:n_p], got[n_p], got[n_p + 1]


def feed_back(net, blocks, down, slope, up):
    n_p = net.n_p
    rows = blocks[0].shape[0]
    tokens = n_p * rows
    fw = FF // n_p

    def body(place, *refs):
        d_own, d_other, slope_ref, up_own, up_other = refs[n_p : n_p + 5]
        outs = refs[n_p + 5 : 2 * n_p + 5]
        du_ref, sums, dm = refs[2 * n_p + 5 :]
        c = place[1]
        gather_rows(refs[:n_p], dm)
        for w, core in ((d_own, c), (d_other, 1 - c)):

            @pl.loop(0, fw // (2 * F_TILE))
            def _(t):
                start = core * (fw // 2) + t * F_TILE
                cols = pl.ds(pl.multiple_of(start, F_TILE), F_TILE)
                dz = dot_nt(dm[...], w[tile(t, F_TILE), :])
                du = (dz * slope_ref[:, cols]).astype(BF)
                du_ref[:, cols] = du
                sums[:, cols] = jnp.sum(du.astype(F32), axis=0, keepdims=True)

        for j in range(n_p):
            du = du_ref[j * rows : (j + 1) * rows, :]
            outs[j][:, : D // 2] = dot_nt(du, up_own[...]).astype(BF)
            outs[j][:, D // 2 :] = dot_nt(du, up_other[...]).astype(BF)

    outs = [((rows, D), BF)] * n_p + [((tokens, fw), BF), ((1, fw), F32)]
    scratch = [pltpu.VMEM((tokens, D), BF)]
    ins = [*blocks, *down, slope, *up]
    got = run("feed_back", body, outs, ins, net.place, scratch, flops=4 * tokens * D * fw)
    return got[:n_p], got[n_p], got[n_p + 1]


def down_weight_grad(net, z, dm):
    n_r = len(dm)
    tokens, m = z.shape
    half = m // 2

    def body(place, z_ref, *refs):
        keep, send, b = refs[n_r:]
        c = place[1]
        gather_rows(refs[:n_r], b)
        keep[...] = dot_tn(z_ref[:, tile(c, half)], b[...]).astype(BF)
        send[...] = dot_tn(z_ref[:, tile(1 - c, half)], b[...]).astype(BF)

    outs = [((half, D), BF)] * 2
    scratch = [pltpu.VMEM((tokens, D), BF)]
    return run("down_weight_grad", body, outs, [z, *dm], net.place, scratch, flops=2 * tokens * m * D)


def up_weight_grad(net, a2, du):
    n_l = len(a2)
    tokens, n = du.shape

    def body(place, *refs):
        du_ref, out, a = refs[n_l:]
        c = place[1]
        gather_rows(refs[:n_l], a)
        out[c] = dot_tn(a[:, : D // 2], du_ref[...]).astype(BF)
        out[1 - c] = dot_tn(a[:, D // 2 :], du_ref[...]).astype(BF)

    scratch = [pltpu.VMEM((tokens, D), BF)]
    outs = [((2, D // 2, n), BF)]
    return run("up_weight_grad", body, outs, [*a2, du], net.place, scratch, flops=2 * tokens * D * n)[0]


def attend_weight_grad(net, a1, dqkv, attended, dy, small):
    n_p = net.n_p
    n_a = len(a1)
    tokens, width = dqkv.shape
    cw = D // n_p
    rows = D // net.n_f
    extra = 16 if small else 0
    flat = [v for of_layer in small[1] for v in of_layer] if small else []
    sizes = small[0] if small else []
    starts = [sum(sizes[:i]) for i in range(len(sizes))]

    def put_small(place, refs, low):
        p, c = place[0], place[1]
        low[...] = jnp.zeros_like(low)
        for k, (ref, (_, kind)) in enumerate(zip(refs, flat)):
            layer, which = divmod(k, len(sizes))
            at, size = starts[which], sizes[which]
            half = at // width
            row = slice(2 * layer + half, 2 * layer + half + 1)
            cols = slice(at - half * width, at - half * width + size)
            if kind == "chip":
                low[0, p, row, cols] = ref[:, :size]
                low[1, p, row, cols] = ref[:, size:]
            elif kind == "heads":
                low[p % 2, p // 2, row, cols] = ref[:, :size]
                low[p % 2, p // 2 + n_p // 2, row, cols] = ref[:, 2 * size :]
            elif kind == "own":
                for i in range(n_p):
                    low[c, i, row, cols] = ref[:, i * size : (i + 1) * size]
                    low[1 - c, i, row, cols] = ref[:, D // 2 + i * size : D // 2 + (i + 1) * size]
            else:
                for i in range(n_p):
                    for core in range(2):
                        to = (2 * i + core) * size
                        low[core, i, row, cols] = ref[:, to : to + size]

    def body(place, *refs):
        dqkv_ref, attended_ref = refs[n_a : n_a + 2]
        smalls = refs[n_a + 2 + n_p : n_a + 2 + n_p + len(flat)]
        out, a, b, low, lines = refs[n_a + 2 + n_p + len(flat) :]
        c = place[1]
        gather_rows(refs[:n_a], a)
        for k, core in ((0, c), (1, 1 - c)):
            both = dot_tn(a[:, k * (D // 2) : (k + 1) * (D // 2)], dqkv_ref[...]).astype(BF)
            for i in range(n_p):
                out[core, i * (rows + extra) : i * (rows + extra) + rows, :width] = both[i * rows : (i + 1) * rows]
        gather_rows(refs[n_a + 2 : n_a + 2 + n_p], b)
        low[...] = dot_tn(attended_ref[...], b[...]).astype(BF)
        for core in range(2):
            for i in range(n_p):
                here = slice(i * (rows + extra), i * (rows + extra) + rows)
                out[core, here, width:] = low[core * rows : (core + 1) * rows, i * cw : (i + 1) * cw]
        if extra:
            put_small(place, smalls, lines)
            for core in range(2):
                for i in range(n_p):
                    here = slice(i * (rows + extra) + rows, (i + 1) * (rows + extra))
                    out[core, here, :width] = lines[core, i].astype(BF)
                    out[core, here, width:] = jnp.zeros((extra, cw), BF)

    outs = [((2, n_p * (rows + extra), width + cw), BF)]
    scratch = [pltpu.VMEM((tokens, D), BF), pltpu.VMEM((tokens, D), BF), pltpu.VMEM((cw, D), BF)]
    scratch.append(pltpu.VMEM((2, n_p, 16, width), F32))
    flops = 2 * tokens * D * (width + cw)
    ins = [*a1, dqkv, attended, *dy, *[v for v, _ in flat]]
    return run("attend_weight_grad", body, outs, ins, net.place, scratch, flops=flops)[0]


def add_halves(a, b):
    rows, width = a.shape
    half = width // 2

    def body(a_ref, b_ref, *outs):
        for k in range(2):
            cols = slice(k * half, (k + 1) * half)
            outs[k][...] = (a_ref[:, cols].astype(F32) + b_ref[:, cols].astype(F32)).astype(BF)

    return run("add_halves", body, [((rows, half), BF)] * 2, [a, b])


def add_pair(both):
    _, rows, width = both.shape
    half = width // 2

    def body(ref, *outs):
        for k in range(2):
            cols = slice(k * half, (k + 1) * half)
            outs[k][...] = (ref[0, :, cols].astype(F32) + ref[1, :, cols].astype(F32)).astype(BF)

    return run("add_pair", body, [((rows, half), BF)] * 2, [both])


def cut_rows(net, first, second, extra):
    n_p = net.n_p
    rows = first.shape[0] // n_p
    width, more = first.shape[1], second.shape[1]
    split = extra is not None
    taken = more // 2 if split else more

    def body(place, a, b, *outs):
        p = place[0]
        for j in range(n_p):
            here = tile(p ^ j, rows)
            outs[j][:, :width] = a[here, :]
            outs[j][:, width:] = b[here, :taken]
        if split:
            for i in range(n_p):
                outs[n_p][:, i * taken : (i + 1) * taken] = b[i * rows : (i + 1) * rows - extra, taken:]

    outs = [((rows, width + taken), BF)] * n_p
    if split:
        outs.append(((rows - extra, n_p * taken), BF))
    return run("cut_rows", body, outs, [first, second], net.place)


def sum_small(layers, pieces, sizes, rows):
    width = pieces[0].shape[1]
    starts = [sum(sizes[:i]) for i in range(len(sizes))]

    def body(*refs):
        total = refs[0][rows:, :].astype(F32)
        for ref in refs[1 : len(pieces)]:
            total = total + ref[rows:, :].astype(F32)
        for out, at, size in zip(refs[len(pieces) :], starts, sizes):
            half = at // width
            for layer in range(layers):
                row = 2 * layer + half
                out[layer : layer + 1, :] = total[row : row + 1, at - half * width : at - half * width + size]

    return run("sum_small", body, [((layers, size), F32) for size in sizes], pieces)


def take_if(here, a, b, rows):
    def body(flag, a_ref, b_ref, out):
        @pl.when(flag[0] != 0)
        def _():
            count = min(rows, a.shape[0])
            out[0:count, :] = a_ref[0:count, :]

        @pl.when(flag[0] == 0)
        def _():
            count = min(rows, b.shape[0])
            out[0:count, :] = b_ref[0:count, :]

    return run("take_if", body, [((rows, a.shape[1]), BF)], [a, b], here.astype(jnp.int32).reshape(1))[0]


def turn(net, wanted):
    flat, flags, outs = [], [], []
    for one, two, outer in wanted:
        flat += one + (two or [])
        rows = max(one[0].shape[0], two[0].shape[0] if two else 0)
        outs.append(((rows, one[0].shape[1]), BF))
        flags.append(jnp.zeros((), jnp.int32) if outer is None else outer.astype(jnp.int32))

    def put(refs, out):
        rows = refs[0].shape[0]
        if len(refs) == 1:
            out[0:rows, :] = refs[0][...]
            return
        total = refs[0][...].astype(F32)
        for ref in refs[1:]:
            total = total + ref[0:rows, :].astype(F32)
        out[0:rows, :] = total.astype(BF)

    def body(flag, *refs):
        at = 0
        for k, (one, two, outer) in enumerate(wanted):
            out = refs[len(flat) + k]
            first = refs[at : at + len(one)]
            at += len(one)
            if outer is None:
                put(first, out)
                continue
            second = refs[at : at + len(two)]
            at += len(two)
            pl.when(flag[k] != 0)(lambda first=first, out=out: put(first, out))
            pl.when(flag[k] == 0)(lambda second=second, out=out: put(second, out))

    return run("turn", body, outs, flat, jnp.stack(flags))


class Chunk:
    def __init__(self, value):
        self.terms = [value]
        self.step = 0

    @property
    def value(self):
        return self.terms[0]


class Flow:
    def __init__(self, net):
        self.net = net
        self.queue = []
        self.moving = []

    def first(self, step):
        for chunk in self.queue:
            if chunk.step == step:
                return chunk
        return None

    def start(self):
        net = self.net
        n = net.n_s
        half = n // 2
        moves, wanted = [], []
        for k in range(half):
            inward = self.first(k)
            outward = None if k == half - 1 else self.first(n - 2 - k)
            into = [(k, k + 1), (n - 1 - k, n - 2 - k)]
            out = [(k + 1, k), (n - 2 - k, n - 1 - k)]
            outer = (net.s == k) | (net.s == n - 1 - k)
            both = inward is not None and outward is not None
            if both and inward.value.shape[1] == outward.value.shape[1]:
                moves.append((inward, outward, outer, into + out))
                wanted.append((inward.terms, outward.terms, outer))
                continue
            if inward is not None:
                moves.append((inward, None, outer, into))
                wanted.append((inward.terms, None, None))
            if outward is not None:
                moves.append((None, outward, outer, out))
                wanted.append((outward.terms, None, None))
        sent = [w[0][0] for w in wanted]
        work = [k for k, w in enumerate(wanted) if len(w[0]) > 1 or w[1] is not None]
        if work:
            for k, value in zip(work, turn(net, [wanted[k] for k in work])):
                sent[k] = value
        self.moving = [(*m[:3], v, lax.ppermute(v, "seq", m[3])) for m, v in zip(moves, sent)]

    def collect(self, values, *new):
        values, news, got = fence((values, [c.value for c in new], [(m[3], m[4]) for m in self.moving]))
        for c, value in zip(new, news):
            c.terms = [value]
        n = self.net.n_s
        for (inward, outward, outer, _, _), (sent, arrived) in zip(self.moving, got):
            if inward is not None:
                middle = inward.step == n // 2 - 1
                inward.terms = [sent, arrived] if middle else [*inward.terms, arrived]
                inward.step += 1
            if outward is not None:
                outward.terms = [take_if(outer, arrived, sent, outward.value.shape[0])]
                outward.step += 1
        self.queue = [c for c in self.queue if c.step < n - 1] + list(new)
        self.start()
        return values


def write_layer(net, layer, layers, before, down, proj, up, qkv):
    n_p = net.n_p
    rows = up[0].shape[0]
    cw, fw = D // n_p, FF // n_p
    n_in = 3 + 2 * n_p
    skip = 0 if before is None else 4
    steps = min(4, rows // 16)
    part = rows // steps
    down_rows = down[0].shape[0]
    down_part = down_rows // steps

    def body(place, *refs):
        p = place[0]
        downs, proj_ref = refs[:2], refs[2]
        ups, qkvs = refs[3 : 3 + n_p], refs[3 + n_p : n_in]
        qkv_out, proj_out, up_out, down_out = refs[n_in + skip :]
        proj_out[0] = proj_ref[...].astype(F32)
        for k in range(2):
            down_out[0, :, k * (D // 2) : (k + 1) * (D // 2)] = downs[k][...].astype(F32)
        for j in range(n_p):
            up_out[0, :, tile(p ^ j, fw)] = ups[j][...].astype(F32)
            for i in range(3):
                to = tile(i * n_p + (p ^ j), cw)
                qkv_out[0, :, to] = qkvs[j][:, i * cw : (i + 1) * cw].astype(F32)

    def of_rows(v, size):
        return pl.BlockSpec((size, v.shape[1]), lambda i: (i, 0))

    ins = [*down, proj, *up, *qkv]
    specs = [IN_SMEM] + [of_rows(v, down_part) for v in down] + [of_rows(v, part) for v in [proj, *up, *qkv]]
    aliases = {}
    if before is not None:
        aliases = {1 + n_in + k: k for k in range(4)}
        specs += [IN_ANY] * 4
        ins = ins + list(before)
    shapes = [(rows, 3 * D), (rows, D), (rows, FF), (down_rows, D)]
    sizes = [part, part, part, down_part]
    return pl.pallas_call(
        body,
        grid=(steps,),
        out_shape=[jax.ShapeDtypeStruct((layers, *shape), F32) for shape in shapes],
        in_specs=specs,
        out_specs=[
            pl.BlockSpec((1, size, shape[1]), lambda i: (layer, i, 0)) for size, shape in zip(sizes, shapes)
        ],
        input_output_aliases=aliases,
        compiler_params=pltpu.CompilerParams(vmem_limit_bytes=16 << 20),
        name="write_layer",
    )(net.place, *ins)


def on_device(
    tokens,
    scene_ids,
    token_kind,
    out_grad,
    first_gain,
    first_shift,
    qkv_weight,
    qv_bias,
    proj_weight,
    proj_bias,
    second_gain,
    second_shift,
    up_weight,
    up_bias,
    down_weight,
    down_bias,
):
    net = Net()
    n_p = net.n_p
    layers = qkv_weight.shape[0]
    rows = tokens.shape[1]
    pair_groups = [[2 * i, 2 * i + 1] for i in range(n_p)]

    def swap_cores(both):
        return lax.all_to_all(both, "fsdp", 0, 0, axis_index_groups=pair_groups)

    small_in = [first_gain, first_shift, qv_bias, proj_bias, second_gain, second_shift, up_bias, down_bias]
    sizes = [v.shape[1] for v in small_in]
    tok = net.to_planes(pack_tokens(tokens, scene_ids, token_kind))
    small = pack_small(small_in)
    small = [small, net.core(small)]
    qkv_got = net.exchange(cut_columns(net, qkv_weight, 0, 3, small))
    tok, qkv_got, later = fence((tok, qkv_got, (proj_weight, up_weight, down_weight, out_grad)))
    proj_weight, up_weight, down_weight, out_grad = later
    tokg = net.gather(tok)
    qkv_own, proj_own = stack_rows(net, qkv_got, proj_weight, 0)
    qkv_w, proj_w = (qkv_own, net.core(qkv_own)), (proj_own, net.core(proj_own))
    vectors = join_vectors(net, layers, qkv_got, sizes)
    gain1, shift1, qv_b, proj_b, gain2, shift2, up_b, down_b = vectors

    weights = []
    kept = []
    dm = None
    codes = None
    hidden = None
    for layer in range(layers):
        last = layer == layers - 1
        a1g = tokg if layer == 0 else net.gather(a1)
        a1g, qkv_w, proj_w, up_weight = fence((a1g, qkv_w, proj_w, up_weight))
        if layer == 0:
            tokg = a1g
            hidden = tokg[0]
        norm = (gain1, shift1) if layer == 0 else None
        y, qkv, og, codes, a1g = attend(net, layer, rows, a1g, norm, qkv_w, qv_b, codes, proj_w)
        up_got = net.exchange(cut_columns(net, up_weight, layer, 1, []))
        y, up_got, down_weight = fence((y, up_got, down_weight))
        parts = net.exchange(y)
        up_own, down_own = stack_rows(net, up_got, down_weight, layer)
        up_w, down_w = (up_own, net.core(up_own)), (down_own, net.core(down_own))
        parts, up_w, down_w = fence((parts, up_w, down_w))
        h2, a2 = add_and_norm(net, layer, hidden, parts, proj_b, (layer, gain2, shift2))
        a2g = net.gather(a2)
        a2g, qkv_weight, out_grad = fence((a2g, qkv_weight, out_grad))
        y, z, slope = feed_forward(net, layer, a2g, up_w, up_b, down_w)
        kept.append((hidden, a1g, qkv, og, h2, a2g, z, slope))
        weights.append((qkv_w, proj_w, up_w, down_w))
        if last:
            dmg = net.gather(dm)
            last_y, z, slope, dmg = fence((y, z, slope, dmg))
            break
        qkv_got = net.exchange(cut_columns(net, qkv_weight, layer + 1, 3, []))
        if layer == layers - 2:
            dm = net.to_planes(out_grad[0])
        y, qkv_got, proj_weight, dm = fence((y, qkv_got, proj_weight, dm))
        parts = net.exchange(y)
        qkv_own, proj_own = stack_rows(net, qkv_got, proj_weight, layer + 1)
        qkv_w, proj_w = (qkv_own, net.core(qkv_own)), (proj_own, net.core(proj_own))
        parts, qkv_w, proj_w = fence((parts, qkv_w, proj_w))
        hidden, a1 = add_and_norm(net, layer, h2, parts, down_b, (layer + 1, gain1, shift1))

    flow = Flow(net)
    small_grads = [None] * layers
    sums = [None] * layers
    out = None
    grad = dm
    down_b_grad = column_sums(dm)

    def chunks(halves):
        return [Chunk(v) for v in halves]

    for layer in reversed(range(layers)):
        last = layer == layers - 1
        qkv_w, proj_w, up_w, down_w = weights[layer]
        h1, a1g, qkv, og, h2, a2g, z, slope = kept[layer]
        keep, send = down_weight_grad(net, z, dmg)
        da2, du, up_b_grad = feed_back(net, dmg, down_w, slope, up_w)
        send = net.core(send)
        if layer == layers - 2:
            sent_out = net.from_planes(sent_out)
            da2, du, keep, send, sent_out = fence((da2, du, keep, send, sent_out))
        else:
            da2, du, keep, send = fence((da2, du, keep, send))
        down_g = chunks(add_halves(keep, send))
        da2 = flow.collect(da2, down_g[0])
        parts = net.exchange(da2)
        both = swap_cores(up_weight_grad(net, a2g, du))
        parts, both = flow.collect((parts, both), down_g[1])
        up_g = chunks(add_pair(both))
        dh2, dy, sums2 = norm_back(net, layer, grad, h2, parts, gain2)
        dyg = net.gather(dy)
        dyg = flow.collect(dyg, up_g[0])
        tokens_in = tokg if layer == 0 else []
        da1, dqkv, qkv_b_grad, norm_sums = attend_back(net, dyg, proj_w, qkv, codes, qkv_w, tokens_in)
        if last:
            last_parts = net.exchange(last_y)
            da1, dqkv, last_parts = flow.collect((da1, dqkv, last_parts), up_g[1])
            (sent_out,) = add_and_norm(net, layer, h2, last_parts, down_b, None)
        else:
            up_pieces = net.exchange(cut_rows(net, *[c.value for c in sums[layer + 1][1]], None))
            da1, dqkv, up_pieces = flow.collect((da1, dqkv, up_pieces), up_g[1])
        parts = net.exchange(da1)
        names = [None, None, "heads", None, None, None, "chip", None]
        of_layer = [None, None, qkv_b_grad, sums2[2:3], sums2[0:1], sums2[1:2], up_b_grad, down_b_grad]
        small = None
        if layer == 0:
            of_layer[0], of_layer[1] = norm_sums[0:1], norm_sums[1:2]
            names[0] = names[1] = "own"
            small_grads[layer] = list(zip(of_layer, names))
            small = (sizes, small_grads)
        both = swap_cores(attend_weight_grad(net, a1g, dqkv, og, dyg, small))
        parts, both = fence((parts, both))
        attend_g = chunks(add_pair(both))
        grad, dm, sums1 = norm_back(net, layer, dh2, h1, parts, gain1)
        sums[layer] = (down_g, up_g, attend_g)
        dm = flow.collect(dm, attend_g[0])
        if layer > 0:
            of_layer[0], of_layer[1] = sums1[0:1], sums1[1:2]
            small_grads[layer] = list(zip(of_layer, names))
            dmg = net.gather(dm)
            down_b_grad = sums1[2:3]
            dmg, grad = flow.collect((dmg, grad), attend_g[1])

    input_grad = net.from_planes(dm)
    input_grad = flow.collect(input_grad, attend_g[1])
    flow.collect(())
    up_last = None
    pieces = None
    while flow.queue:
        if up_last is None and not [c for c in flow.queue if c in sums[0][1]]:
            up_last = net.exchange(cut_rows(net, *[c.value for c in sums[0][1]], None))
            up_last = flow.collect(up_last)
        elif up_last is not None and pieces is None:
            *pieces, proj_g = cut_rows(net, *[c.value for c in sums[1][2]], 0)
            pieces = net.exchange(pieces)
            pieces, proj_g = flow.collect((pieces, proj_g))
        else:
            flow.collect(())
    if pieces is None:
        *pieces, proj_g = cut_rows(net, *[c.value for c in sums[1][2]], 0)
        pieces = net.exchange(pieces)
    out = write_layer(net, 1, layers, None, [c.value for c in sums[1][0]], proj_g, up_pieces, pieces)
    if up_last is None:
        up_last = net.exchange(cut_rows(net, *[c.value for c in sums[0][1]], None))
    *pieces, proj_g = cut_rows(net, *[c.value for c in sums[0][2]], 16)
    pieces = net.exchange(pieces)
    small_out = sum_small(layers, pieces, sizes, D // net.n_f)
    out = write_layer(net, 0, layers, out, [c.value for c in sums[0][0]], proj_g, up_last, pieces)
    return (
        sent_out.astype(F32)[None],
        input_grad.astype(F32)[None],
        small_out[0],
        small_out[1],
        out[0],
        small_out[2],
        out[1],
        small_out[3],
        small_out[4],
        small_out[5],
        out[2],
        small_out[6],
        out[3],
        small_out[7],
    )


def solution(mesh):
    tok = P("fsdp", "seq", None)
    lab = P("fsdp", "seq")
    vec = P(None, "fsdp")
    mat = P(None, "fsdp", None)
    return jax.shard_map(
        on_device,
        mesh=mesh,
        in_specs=(tok, lab, lab, tok, vec, vec, mat, vec, mat, vec, vec, vec, mat, vec, mat, vec),
        out_specs=(tok, tok, vec, vec, mat, vec, mat, vec, vec, vec, mat, vec, mat, vec),
        check_vma=False,
    )
```

time: 568 us -> 501 us (0.88)
  starting transfers between devices: 210 us -> 150 us
  blocking collectives: 0 us -> 22.1 us
  waiting for transfers between devices: 222 us -> 201 us
  local copies, waits for them, and re-layouts: 19.9 us -> 7.75 us
    ppermute x36 -> x30, starting transfers between devices: 93.7 us -> 60.8 us  [the longest x26 50.6 us: start(): lax.ppermute(v, 'seq', m[3])]
    ppermute x75 -> x72, starting transfers between devices: 112 us -> 87.9 us  [chip(): return lax.ppermute(v, 'fsdp', xor_pairs(self.n_f, 2 * j))]
    all_to_all x0 -> x4, blocking collectives: none -> 22.1 us  [swap_cores(): return lax.all_to_all(both, 'fsdp', 0, 0, axis_index_groups=pair_groups)]
    ppermute x36 -> x30, waiting for transfers between devices: 57.9 us -> 38.3 us  [the longest x2 19.6 us: from_planes(): return lax.ppermute(v, ('seq', 'fsdp'), [(b, a) for a, b in self.moves()])]
    unnamed x127 -> x166, local copies, waits for them, and re-layouts: 14.3 us -> 7.71 us
    ppermute x75 -> x72, waiting for transfers between devices: 157 us -> 160 us  [chip(): return lax.ppermute(v, 'fsdp', xor_pairs(self.n_f, 2 * j))]
    pallas_call x67 -> x68, Pallas kernels: 94.9 us -> 96.5 us  [run(): pl.pallas_call(body, out_shape=[jax.ShapeDtypeStruct(shape, dtype) for sh...]
  transfers between devices with their start and end apart: 139 -> 113, of which waited for: 58 -> 44; matrix products, arithmetic and copies ran while one was open for 2% -> 1% of each run, Pallas kernels for 15% -> 15%
where the time goes in v3:
time: 501 us; the launch traced here: 492 us
  waiting for transfers between devices  201 us (40%)
  starting transfers between devices  150 us (30%)
  Pallas kernels  104 us (21%)
  blocking collectives  22.1 us (4%)
  local copies, waits for them, and re-layouts  7.75 us (2%)
    ppermute x72, waiting for transfers between devices, chip(): return lax.ppermute(v, 'fsdp', xor_pairs(self.n_f, 2 * j))  160 us
    pallas_call x68, Pallas kernels, run(): pl.pallas_call(body, out_shape=[jax.ShapeDtypeStruct(shape, dtype) for sh...  96.5 us
    ppermute x72, starting transfers between devices, chip(): return lax.ppermute(v, 'fsdp', xor_pairs(self.n_f, 2 * j))  87.9 us
    ppermute x26, starting transfers between devices, start(): lax.ppermute(v, 'seq', m[3])  50.6 us
    all_to_all x4, blocking collectives, swap_cores(): return lax.all_to_all(both, 'fsdp', 0, 0, axis_index_groups=pair_groups)  22.1 us
    ppermute x2, waiting for transfers between devices, from_planes(): return lax.ppermute(v, ('seq', 'fsdp'), [(b, a) for a, b in self.moves()])  19.6 us
    ppermute x26, waiting for transfers between devices, start(): lax.ppermute(v, 'seq', m[3])  18.7 us
  transfers between devices with their start and end apart: 113, of which 44 were waited for; matrix products, arithmetic and copies ran while one was open for 1% of the time, Pallas kernels for 15%

profile of v3, /device:TPU:10, one launch (start us, length us, event | category | flops | bytes accessed | tf_op | source)
XLA Modules:
  0.0 492.0 jit_solution(5113116568587256921)
XLA Ops:
  2.5 3.4 collective-permute-start
  14.2 9.0 %collective-permute-done.2.refs_1_ = bf16[144,768]{1,0:T(8,128)(2,1)S(1)} collective-permute-done((bf16[144,768]{1,0:T(8,128)(2,1)S(1)}, bf16[144,768]{1,0:T(8,128)(2,1)S(1)}, u32[]{:S(2)}, u32[]{:S(2)}) %collective-permute-start.2) | collective-permute-done | bytes 221216 | tf_op jit(solution)/shard_map/ppermute | solution.py:53
  23.2 4.7 collective-permute-done.4.refs_3_
  30.7 3.9 collective-permute-start.6
  36.2 4.3 collective-permute-done.5.refs_1_.refs_12_
  40.5 7.8 %collective-permute-done.6.refs_2_.refs_13_ = bf16[144,1024]{1,0:T(8,128)(2,1)S(1)} collective-permute-done((bf16[144,1024]{1,0:T(8,128)(2,1)S(1)}, bf16[144,1024]{1,0:T(8,128)(2,1)S(1)}, u32[]{:S(2)}, u32[]{:S(2)}) %collective-permute-start.6) | collective-permute-done | bytes 294944 | tf_op jit(solution)/shard_map/ppermute | solution.py:53
  53.2 6.0 %attend.2 = (s32[1,512]{1,0:T(1,128)S(1)}, s32[512,1]{1,0:T(8,128)S(1)}, bf16[512,1024]{1,0:T(8,128)(2,1)S(1)}, bf16[128,1024]{1,0:T(8,128)(2,1)S(1)}, bf16[128,...) custom-call(s32[2]{0:T(128)S(1)} %pad_add_fusion.2.place, ...), custom_call_target="tpu_custom_call" | custom-call | flops 1073741824 | bytes 3309576 | tf_op jit(solution)/shard_map/attend/pallas_call | solution.py:85
  60.2 3.5 collective-permute-done.11.refs_2_
  68.6 5.7 %collective-permute-done.13.refs_2_ = bf16[128,1024]{1,0:T(8,128)(2,1)S(1)} collective-permute-done((bf16[128,1024]{1,0:T(8,128)(2,1)S(1)}, bf16[128,1024]{1,0:T(8,128)(2,1)S(1)}, u32[]{:S(2)}, u32[]{:S(2)}) %collective-permute-start.13) | collective-permute-done | bytes 262176 | tf_op jit(solution)/shard_map/ppermute | solution.py:53
  74.3 5.0 %collective-permute-done.14.refs_3_ = bf16[128,1024]{1,0:T(8,128)(2,1)S(1)} collective-permute-done((bf16[128,1024]{1,0:T(8,128)(2,1)S(1)}, bf16[128,1024]{1,0:T(8,128)(2,1)S(1)}, u32[]{:S(2)}, u32[]{:S(2)}) %collective-permute-start.14) | collective-permute-done | bytes 262176 | tf_op jit(solution)/shard_map/ppermute | solution.py:53
  83.8 5.8 %collective-permute-done.18.refs_1_ = bf16[128,1024]{1,0:T(8,128)(2,1)S(1)} collective-permute-done((bf16[128,1024]{1,0:T(8,128)(2,1)S(1)}, bf16[128,1024]{1,0:T(8,128)(2,1)S(1)}, u32[]{:S(2)}, u32[]{:S(2)}) %collective-permute-start.18) | collective-permute-done | bytes 262176 | tf_op jit(solution)/shard_map/ppermute | solution.py:53
  89.5 4.8 collective-permute-done.19.refs_2_
  94.3 2.9 collective-permute-start.24
  98.1 3.3 collective-permute-start.21
  103.0 4.2 feed_forward.2
  108.2 3.0 collective-permute-done.21.refs_1_
  111.2 4.1 collective-permute-done.23.refs_3_
  117.1 3.9 collective-permute-start.26
  121.1 5.2 %collective-permute-done.25.refs_2_ = bf16[128,1024]{1,0:T(8,128)(2,1)S(1)} collective-permute-done((bf16[128,1024]{1,0:T(8,128)(2,1)S(1)}, bf16[128,1024]{1,0:T(8,128)(2,1)S(1)}, u32[]{:S(2)}, u32[]{:S(2)}) %collective-permute-start.25) | collective-permute-done | bytes 262176 | tf_op jit(solution)/shard_map/ppermute | solution.py:53
  126.2 7.1 %collective-permute-done.26.refs_3_ = bf16[128,1024]{1,0:T(8,128)(2,1)S(1)} collective-permute-done((bf16[128,1024]{1,0:T(8,128)(2,1)S(1)}, bf16[128,1024]{1,0:T(8,128)(2,1)S(1)}, u32[]{:S(2)}, u32[]{:S(2)}) %collective-permute-start.26) | collective-permute-done | bytes 262176 | tf_op jit(solution)/shard_map/ppermute | solution.py:53
  137.8 5.7 %collective-permute-done.30.refs_1_ = bf16[128,1024]{1,0:T(8,128)(2,1)S(1)} collective-permute-done((bf16[128,1024]{1,0:T(8,128)(2,1)S(1)}, bf16[128,1024]{1,0:T(8,128)(2,1)S(1)}, u32[]{:S(2)}, u32[]{:S(2)}) %collective-permute-start.30) | collective-permute-done | bytes 262176 | tf_op jit(solution)/shard_map/ppermute | solution.py:53
  143.6 5.4 %collective-permute-done.31.refs_2_ = bf16[128,1024]{1,0:T(8,128)(2,1)S(1)} collective-permute-done((bf16[128,1024]{1,0:T(8,128)(2,1)S(1)}, bf16[128,1024]{1,0:T(8,128)(2,1)S(1)}, u32[]{:S(2)}, u32[]{:S(2)}) %collective-permute-start.31) | collective-permute-done | bytes 262176 | tf_op jit(solution)/shard_map/ppermute | solution.py:53
  153.3 5.4 %attend.3 = (bf16[128,1024]{1,0:T(8,128)(2,1)S(1)}, bf16[128,1024]{1,0:T(8,128)(2,1)S(1)}, bf16[128,1024]{1,0:T(8,128)(2,1)S(1)}, bf16[128,1024]{1,0:T(8,128)(2,...) custom-call(s32[2]{0:T(128)S(1)} %pad_add_fusion.2.place, ...), custom_call_target="tpu_custom_call" | custom-call | flops 1073741824 | bytes 3166216 | tf_op jit(solution)/shard_map/attend/pallas_call | solution.py:85
  158.9 3.3 collective-permute-done.34.refs_2_
  167.1 5.7 %collective-permute-done.36.refs_2_ = bf16[128,1024]{1,0:T(8,128)(2,1)S(1)} collective-permute-done((bf16[128,1024]{1,0:T(8,128)(2,1)S(1)}, bf16[128,1024]{1,0:T(8,128)(2,1)S(1)}, u32[]{:S(2)}, u32[]{:S(2)}) %collective-permute-start.36) | collective-permute-done | bytes 262176 | tf_op jit(solution)/shard_map/ppermute | solution.py:53
  172.7 6.0 %collective-permute-done.37.refs_3_ = bf16[128,1024]{1,0:T(8,128)(2,1)S(1)} collective-permute-done((bf16[128,1024]{1,0:T(8,128)(2,1)S(1)}, bf16[128,1024]{1,0:T(8,128)(2,1)S(1)}, u32[]{:S(2)}, u32[]{:S(2)}) %collective-permute-start.37) | collective-permute-done | bytes 262176 | tf_op jit(solution)/shard_map/ppermute | solution.py:53
  185.4 3.6 collective-permute-done.41.refs_1_
  190.6 4.6 collective-permute-done.42.refs_2_
  195.1 4.1 feed_forward.3
  200.7 3.3 collective-permute-done.45.refs_2_
  206.0 5.6 %feed_back.2 = (bf16[128,1024]{1,0:T(8,128)(2,1)S(1)}, bf16[128,1024]{1,0:T(8,128)(2,1)S(1)}, bf16[128,1024]{1,0:T(8,128)(2,1)S(1)}, bf16[128,1024]{1,0:T(8,128)...) custom-call(s32[2]{0:T(128)S(1)} %pad_add_fusion.2.place, ...), custom_call_target="tpu_custom_call" | custom-call | flops 2147483648 | bytes 7340040 | tf_op jit(solution)/shard_map/feed_back/pallas_call | solution.py:85
  219.2 5.4 %all_to_all.20.ref = bf16[2,512,1024]{2,1,0:T(8,128)(2,1)S(1)} all-to-all(bf16[2,512,1024]{2,1,0:T(8,128)(2,1)S(1)} %up_weight_grad.2), channel_id=1, replica_groups={{0,1},{2,3},{4,5},{6,7},{8,9},{10,11},{12,13},{14,15},{16,17},{18,19},{..., dimensions={0} | all-to-all | bytes 4194304 | tf_op jit(solution)/shard_map/all_to_all | solution.py:925
  224.6 4.9 collective-permute-done.49.refs_2_
  241.8 5.7 %collective-permute-done.52.refs_1_.refs_7_ = bf16[128,1024]{1,0:T(8,128)(2,1)} collective-permute-done((bf16[128,1024]{1,0:T(8,128)(2,1)}, bf16[128,1024]{1,0:T(8,128)(2,1)}, u32[]{:S(2)}, u32[]{:S(2)}) %collective-permute-start.52) | collective-permute-done | bytes 262176 | tf_op jit(solution)/shard_map/ppermute | solution.py:53
  247.5 4.5 collective-permute-done.53.refs_2_.refs_8_
  262.3 9.6 %attend_back.2 = (bf16[128,1024]{1,0:T(8,128)(2,1)S(1)}, bf16[128,1024]{1,0:T(8,128)(2,1)S(1)}, bf16[128,1024]{1,0:T(8,128)(2,1)S(1)}, bf16[128,1024]{1,0:T(8,12...) custom-call(s32[2]{0:T(128)S(1)} %pad_add_fusion.2.place, ...), custom_call_target="tpu_custom_call" | custom-call | flops 2147483648 | bytes 3936264 | tf_op jit(solution)/shard_map/attend_back/pallas_call | solution.py:85
  272.9 3.2 collective-permute-start.66
  282.4 5.6 %all_to_all.21.ref = bf16[2,512,1024]{2,1,0:T(8,128)(2,1)S(1)} all-to-all(bf16[2,512,1024]{2,1,0:T(8,128)(2,1)S(1)} %attend_weight_grad.2), channel_id=1, replica_groups={{0,1},{2,3},{4,5},{6,7},{8,9},{10,11},{12,13},{14,15},{16,17},{18,19},{..., dimensions={0} | all-to-all | bytes 4194304 | tf_op jit(solution)/shard_map/all_to_all | solution.py:925
  297.3 5.7 %collective-permute-done.67.refs_1_ = bf16[128,1024]{1,0:T(8,128)(2,1)S(1)} collective-permute-done((bf16[128,1024]{1,0:T(8,128)(2,1)S(1)}, bf16[128,1024]{1,0:T(8,128)(2,1)S(1)}, u32[]{:S(2)}, u32[]{:S(2)}) %collective-permute-start.67) | collective-permute-done | bytes 262176 | tf_op jit(solution)/shard_map/ppermute | solution.py:53
  303.0 5.3 %collective-permute-done.68.refs_2_ = bf16[128,1024]{1,0:T(8,128)(2,1)S(1)} collective-permute-done((bf16[128,1024]{1,0:T(8,128)(2,1)S(1)}, bf16[128,1024]{1,0:T(8,128)(2,1)S(1)}, u32[]{:S(2)}, u32[]{:S(2)}) %collective-permute-start.68) | collective-permute-done | bytes 262176 | tf_op jit(solution)/shard_map/ppermute | solution.py:53
  311.4 3.4 collective-permute-start.75
  317.5 5.4 %feed_back.3 = (bf16[128,1024]{1,0:T(8,128)(2,1)S(1)}, bf16[128,1024]{1,0:T(8,128)(2,1)S(1)}, bf16[128,1024]{1,0:T(8,128)(2,1)S(1)}, bf16[128,1024]{1,0:T(8,128)...) custom-call(s32[2]{0:T(128)S(1)} %pad_add_fusion.2.place, ...), custom_call_target="tpu_custom_call" | custom-call | flops 2147483648 | bytes 7340040 | tf_op jit(solution)/shard_map/feed_back/pallas_call | solution.py:85
  322.9 6.0 %collective-permute-done.73 = bf16[128,1024]{1,0:T(8,128)(2,1)S(1)} collective-permute-done((bf16[128,1024]{1,0:T(8,128)(2,1)S(1)}, bf16[128,1024]{1,0:T(8,128)(2,1)S(1)}, u32[]{:S(2)}, u32[]{:S(2)}) %collective-permute-start.73) | collective-permute-done | bytes 262176 | tf_op jit(solution)/shard_map/ppermute | solution.py:50
  329.2 3.8 collective-permute-done.75.refs_2_
  333.9 5.9 %collective-permute-start.80 = (bf16[512,512]{1,0:T(8,128)(2,1)S(1)}, bf16[512,512]{1,0:T(8,128)(2,1)S(1)}, u32[]{:S(2)}, u32[]{:S(2)}) collective-permute-start(bf16[512,512]{1,0:T(8,128)(2,1)S(1)} %get-tuple-element.715.refs_1_), channel_id=1, source_target_pairs={{8,16},{16,8},{9,17},{17,9},{10,18},{18,10},{11,19},{19,11},{12,20... | collective-permute-start | bytes 1572872 | tf_op jit(solution)/shard_map/ppermute | solution.py:829
  340.0 3.4 collective-permute-start.78
  345.2 5.4 %all_to_all.22.ref = bf16[2,512,1024]{2,1,0:T(8,128)(2,1)S(1)} all-to-all(bf16[2,512,1024]{2,1,0:T(8,128)(2,1)S(1)} %up_weight_grad.3), channel_id=1, replica_groups={{0,1},{2,3},{4,5},{6,7},{8,9},{10,11},{12,13},{14,15},{16,17},{18,19},{..., dimensions={0} | all-to-all | bytes 4194304 | tf_op jit(solution)/shard_map/all_to_all | solution.py:925
  360.9 5.2 %collective-permute-done.81.refs_1_.refs_4_ = bf16[128,1024]{1,0:T(8,128)(2,1)S(1)} collective-permute-done((bf16[128,1024]{1,0:T(8,128)(2,1)S(1)}, bf16[128,1024]{1,0:T(8,128)(2,1)S(1)}, u32[]{:S(2)}, u32[]{:S(2)}) %collective-permute-start.81) | collective-permute-done | bytes 262176 | tf_op jit(solution)/shard_map/ppermute | solution.py:53
  366.1 4.3 collective-permute-done.82.refs_2_.refs_5_
  371.7 3.3 collective-permute-start.90
  379.5 9.5 %attend_back.3 = (bf16[128,1024]{1,0:T(8,128)(2,1)S(1)}, bf16[128,1024]{1,0:T(8,128)(2,1)S(1)}, bf16[128,1024]{1,0:T(8,128)(2,1)S(1)}, bf16[128,1024]{1,0:T(8,12...) custom-call(s32[2]{0:T(128)S(1)} %pad_add_fusion.2.place, ...), custom_call_target="tpu_custom_call" | custom-call | flops 2147483648 | bytes 5115912 | tf_op jit(solution)/shard_map/attend_back/pallas_call | solution.py:85
  398.1 5.6 %all_to_all.23.ref = bf16[2,576,1024]{2,1,0:T(8,128)(2,1)S(1)} all-to-all(bf16[2,576,1024]{2,1,0:T(8,128)(2,1)S(1)} %attend_weight_grad.3), channel_id=1, replica_groups={{0,1},{2,3},{4,5},{6,7},{8,9},{10,11},{12,13},{14,15},{16,17},{18,19},{..., dimensions={0} | all-to-all | bytes 4718592 | tf_op jit(solution)/shard_map/all_to_all | solution.py:925
  406.9 3.2 collective-permute-start.98
  412.1 13.6 %collective-permute-done.96 = bf16[128,1024]{1,0:T(8,128)(2,1)S(1)} collective-permute-done((bf16[128,1024]{1,0:T(8,128)(2,1)S(1)}, bf16[128,1024]{1,0:T(8,128)(2,1)S(1)}, u32[]{:S(2)}, u32[]{:S(2)}) %collective-permute-start.96) | collective-permute-done | bytes 262176 | tf_op jit(solution)/shard_map/ppermute | solution.py:50
  429.0 5.6 %collective-permute-start.100 = (bf16[576,512]{1,0:T(8,128)(2,1)S(1)}, bf16[576,512]{1,0:T(8,128)(2,1)S(1)}, u32[]{:S(2)}, u32[]{:S(2)}) collective-permute-start(bf16[576,512]{1,0:T(8,128)(2,1)S(1)} %get-tuple-element.793.refs_0_), channel_id=1, source_target_pairs={{8,16},{16,8},{9,17},{17,9},{10,18},{18,10},{11,19},{19,11},{12,20... | collective-permute-start | bytes 1769480 | tf_op jit(solution)/shard_map/ppermute | solution.py:829
  434.6 7.4 %collective-permute-done.99.a_ref.refs_3_ = bf16[576,512]{1,0:T(8,128)(2,1)S(1)} collective-permute-done((bf16[576,512]{1,0:T(8,128)(2,1)S(1)}, bf16[576,512]{1,0:T(8,128)(2,1)S(1)}, u32[]{:S(2)}, u32[]{:S(2)}) %collective-permute-start.99) | collective-permute-done | bytes 589856 | tf_op jit(solution)/shard_map/ppermute | solution.py:829
  442.1 5.1 %collective-permute-done.100.refs_1_ = bf16[576,512]{1,0:T(8,128)(2,1)S(1)} collective-permute-done((bf16[576,512]{1,0:T(8,128)(2,1)S(1)}, bf16[576,512]{1,0:T(8,128)(2,1)S(1)}, u32[]{:S(2)}, u32[]{:S(2)}) %collective-permute-start.100) | collective-permute-done | bytes 589856 | tf_op jit(solution)/shard_map/ppermute | solution.py:829
  449.3 3.6 collective-permute-start.105
  454.1 3.1 collective-permute-start.103
  457.2 5.4 %collective-permute-done.101.refs_4_ = bf16[128,1024]{1,0:T(8,128)(2,1)S(1)} collective-permute-done((bf16[128,1024]{1,0:T(8,128)(2,1)S(1)}, bf16[128,1024]{1,0:T(8,128)(2,1)S(1)}, u32[]{:S(2)}, u32[]{:S(2)}) %collective-permute-start.101) | collective-permute-done | bytes 262176 | tf_op jit(solution)/shard_map/ppermute | solution.py:53
  462.6 2.9 collective-permute-done.102.refs_5_
  473.6 4.4 collective-permute-done.107.refs_9_
  483.1 3.5 write_layer.2
  488.0 3.5 write_layer.3
  (413 shorter events, 166.0 us)
Async XLA Ops:
  2.5 25.4 %collective-permute-start = (bf16[144,1024]{1,0:T(8,128)(2,1)S(1)}, bf16[144,1024]{1,0:T(8,128)(2,1)S(1)}, u32[]{:S(2)}, u32[]{:S(2)}) collective-permute-start(bf16[144,1024]{1,0:T(8,128)(2,1)S(1)} %pad_add_fusion), channel_id=1, source_target_pairs={{0,0},{1,1},{2,10},{3,11},{4,20},{5,21},{6,30},{7,31},{12,16},{13,... | collective-permute-start | bytes 884744 | tf_op jit(solution)/shard_map/ppermute | solution.py:47
  10.2 13.0 %collective-permute-start.2 = (bf16[144,768]{1,0:T(8,128)(2,1)S(1)}, bf16[144,768]{1,0:T(8,128)(2,1)S(1)}, u32[]{:S(2)}, u32[]{:S(2)}) collective-permute-start(bf16[144,768]{1,0:T(8,128)(2,1)S(1)} %get-tuple-element.432), channel_id=1, source_target_pairs={{0,2},{1,3},{2,0},{3,1},{4,6},{5,7},{6,4},{7,5},{8,10},{9,11},{10,... | collective-permute-start | bytes 663560 | tf_op jit(solution)/shard_map/ppermute | solution.py:53
  12.8 15.0 %collective-permute-start.4 = (bf16[144,768]{1,0:T(8,128)(2,1)S(1)}, bf16[144,768]{1,0:T(8,128)(2,1)S(1)}, u32[]{:S(2)}, u32[]{:S(2)}) collective-permute-start(bf16[144,768]{1,0:T(8,128)(2,1)S(1)} %get-tuple-element.434), channel_id=1, source_target_pairs={{0,6},{1,7},{2,4},{3,5},{4,2},{5,3},{6,0},{7,1},{8,14},{9,15},{10,... | collective-permute-start | bytes 663560 | tf_op jit(solution)/shard_map/ppermute | solution.py:53
  30.6 17.7 %collective-permute-start.8 = (bf16[512,768]{1,0:T(8,128)(2,1)S(1)}, bf16[512,768]{1,0:T(8,128)(2,1)S(1)}, u32[]{:S(2)}, u32[]{:S(2)}) collective-permute-start(bf16[512,768]{1,0:T(8,128)(2,1)S(1)} %get-tuple-element.449.refs_5_.refs_9_), channel_id=1, source_target_pairs={{0,1},{1,0},{2,3},{3,2},{4,5},{5,4},{6,7},{7,6},{8,9},{9,8},{10,11... | collective-permute-start | bytes 2359304 | tf_op jit(solution)/shard_map/ppermute | solution.py:56
  30.7 17.6 %collective-permute-start.6 = (bf16[144,1024]{1,0:T(8,128)(2,1)S(1)}, bf16[144,1024]{1,0:T(8,128)(2,1)S(1)}, u32[]{:S(2)}, u32[]{:S(2)}) collective-permute-start(bf16[144,1024]{1,0:T(8,128)(2,1)S(1)} %collective-permute-done.refs_0_.refs_11_.hidden_ref), channel_id=1, source_target_pairs={{0,4},{1,5},{2,6},{3,7},{4,0},{5,1},{6,2},{7,3},{8,12},{9,13},{10,... | collective-permute-start | bytes 884744 | tf_op jit(solution)/shard_map/ppermute | solution.py:53
  34.6 13.7 %collective-permute-start.7 = (bf16[144,1024]{1,0:T(8,128)(2,1)S(1)}, bf16[144,1024]{1,0:T(8,128)(2,1)S(1)}, u32[]{:S(2)}, u32[]{:S(2)}) collective-permute-start(bf16[144,1024]{1,0:T(8,128)(2,1)S(1)} %collective-permute-done.refs_0_.refs_11_.hidden_ref), channel_id=1, source_target_pairs={{0,6},{1,7},{2,4},{3,5},{4,2},{5,3},{6,0},{7,1},{8,14},{9,15},{10,... | collective-permute-start | bytes 884744 | tf_op jit(solution)/shard_map/ppermute | solution.py:53
  50.5 13.2 %collective-permute-start.11 = (bf16[128,1024]{1,0:T(8,128)(2,1)S(1)}, bf16[128,1024]{1,0:T(8,128)(2,1)S(1)}, u32[]{:S(2)}, u32[]{:S(2)}) collective-permute-start(bf16[128,1024]{1,0:T(8,128)(2,1)S(1)} %get-tuple-element.462), channel_id=1, source_target_pairs={{0,4},{1,5},{2,6},{3,7},{4,0},{5,1},{6,2},{7,3},{8,12},{9,13},{10,... | collective-permute-start | bytes 786440 | tf_op jit(solution)/shard_map/ppermute | solution.py:53
  51.1 12.6 %collective-permute-start.12 = (bf16[128,1024]{1,0:T(8,128)(2,1)S(1)}, bf16[128,1024]{1,0:T(8,128)(2,1)S(1)}, u32[]{:S(2)}, u32[]{:S(2)}) collective-permute-start(bf16[128,1024]{1,0:T(8,128)(2,1)S(1)} %get-tuple-element.463), channel_id=1, source_target_pairs={{0,6},{1,7},{2,4},{3,5},{4,2},{5,3},{6,0},{7,1},{8,14},{9,15},{10,... | collective-permute-start | bytes 786440 | tf_op jit(solution)/shard_map/ppermute | solution.py:53
  64.5 14.7 %collective-permute-start.16 = (bf16[512,1024]{1,0:T(8,128)(2,1)S(1)}, bf16[512,1024]{1,0:T(8,128)(2,1)S(1)}, u32[]{:S(2)}, u32[]{:S(2)}) collective-permute-start(bf16[512,1024]{1,0:T(8,128)(2,1)S(1)} %get-tuple-element.489.refs_4_.refs_7_), channel_id=1, source_target_pairs={{0,1},{1,0},{2,3},{3,2},{4,5},{5,4},{6,7},{7,6},{8,9},{9,8},{10,11... | collective-permute-start | bytes 3145736 | tf_op jit(solution)/shard_map/ppermute | solution.py:56
  64.6 14.6 %collective-permute-start.17 = (bf16[512,1024]{1,0:T(8,128)(2,1)S(1)}, bf16[512,1024]{1,0:T(8,128)(2,1)S(1)}, u32[]{:S(2)}, u32[]{:S(2)}) collective-permute-start(bf16[512,1024]{1,0:T(8,128)(2,1)S(1)} %get-tuple-element.492.refs_7_.refs_4_), channel_id=1, source_target_pairs={{0,1},{1,0},{2,3},{3,2},{4,5},{5,4},{6,7},{7,6},{8,9},{9,8},{10,11... | collective-permute-start | bytes 3145736 | tf_op jit(solution)/shard_map/ppermute | solution.py:56
  65.6 13.6 %collective-permute-start.14 = (bf16[128,1024]{1,0:T(8,128)(2,1)S(1)}, bf16[128,1024]{1,0:T(8,128)(2,1)S(1)}, u32[]{:S(2)}, u32[]{:S(2)}) collective-permute-start(bf16[128,1024]{1,0:T(8,128)(2,1)S(1)} %get-tuple-element.467), channel_id=1, source_target_pairs={{0,4},{1,5},{2,6},{3,7},{4,0},{5,1},{6,2},{7,3},{8,12},{9,13},{10,... | collective-permute-start | bytes 786440 | tf_op jit(solution)/shard_map/ppermute | solution.py:53
  94.3 21.0 %collective-permute-start.24 = (bf16[128,1024]{1,0:T(8,128)(2,1)S(1)}, bf16[128,1024]{1,0:T(8,128)(2,1)S(1)}, u32[]{:S(2)}, u32[]{:S(2)}) collective-permute-start(bf16[128,1024]{1,0:T(8,128)(2,1)S(1)} %bitcast.12), channel_id=1, source_target_pairs={{0,0},{1,1},{2,10},{3,11},{4,20},{5,21},{6,30},{7,31},{12,16},{13,... | collective-permute-start | bytes 786440 | tf_op jit(solution)/shard_map/ppermute | solution.py:47
  98.1 13.1 %collective-permute-start.21 = (bf16[128,768]{1,0:T(8,128)(2,1)S(1)}, bf16[128,768]{1,0:T(8,128)(2,1)S(1)}, u32[]{:S(2)}, u32[]{:S(2)}) collective-permute-start(bf16[128,768]{1,0:T(8,128)(2,1)S(1)} %get-tuple-element.500), channel_id=1, source_target_pairs={{0,2},{1,3},{2,0},{3,1},{4,6},{5,7},{6,4},{7,5},{8,10},{9,11},{10,... | collective-permute-start | bytes 589832 | tf_op jit(solution)/shard_map/ppermute | solution.py:53
  101.4 13.9 %collective-permute-start.23 = (bf16[128,768]{1,0:T(8,128)(2,1)S(1)}, bf16[128,768]{1,0:T(8,128)(2,1)S(1)}, u32[]{:S(2)}, u32[]{:S(2)}) collective-permute-start(bf16[128,768]{1,0:T(8,128)(2,1)S(1)} %get-tuple-element.502), channel_id=1, source_target_pairs={{0,6},{1,7},{2,4},{3,5},{4,2},{5,3},{6,0},{7,1},{8,14},{9,15},{10,... | collective-permute-start | bytes 589832 | tf_op jit(solution)/shard_map/ppermute | solution.py:53
  117.0 16.4 %collective-permute-start.28 = (bf16[512,768]{1,0:T(8,128)(2,1)S(1)}, bf16[512,768]{1,0:T(8,128)(2,1)S(1)}, u32[]{:S(2)}, u32[]{:S(2)}) collective-permute-start(bf16[512,768]{1,0:T(8,128)(2,1)S(1)} %get-tuple-element.532.refs_5_.refs_9_), channel_id=1, source_target_pairs={{0,1},{1,0},{2,3},{3,2},{4,5},{5,4},{6,7},{7,6},{8,9},{9,8},{10,11... | collective-permute-start | bytes 2359304 | tf_op jit(solution)/shard_map/ppermute | solution.py:56
  117.1 16.2 %collective-permute-start.26 = (bf16[128,1024]{1,0:T(8,128)(2,1)S(1)}, bf16[128,1024]{1,0:T(8,128)(2,1)S(1)}, u32[]{:S(2)}, u32[]{:S(2)}) collective-permute-start(bf16[128,1024]{1,0:T(8,128)(2,1)S(1)} %get-tuple-element.508), channel_id=1, source_target_pairs={{0,4},{1,5},{2,6},{3,7},{4,0},{5,1},{6,2},{7,3},{8,12},{9,13},{10,... | collective-permute-start | bytes 786440 | tf_op jit(solution)/shard_map/ppermute | solution.py:53
  135.8 13.2 %collective-permute-start.31 = (bf16[128,1024]{1,0:T(8,128)(2,1)S(1)}, bf16[128,1024]{1,0:T(8,128)(2,1)S(1)}, u32[]{:S(2)}, u32[]{:S(2)}) collective-permute-start(bf16[128,1024]{1,0:T(8,128)(2,1)S(1)} %get-tuple-element.528.refs_0_), channel_id=1, source_target_pairs={{0,4},{1,5},{2,6},{3,7},{4,0},{5,1},{6,2},{7,3},{8,12},{9,13},{10,... | collective-permute-start | bytes 786440 | tf_op jit(solution)/shard_map/ppermute | solution.py:53
  136.4 12.7 %collective-permute-start.32 = (bf16[128,1024]{1,0:T(8,128)(2,1)S(1)}, bf16[128,1024]{1,0:T(8,128)(2,1)S(1)}, u32[]{:S(2)}, u32[]{:S(2)}) collective-permute-start(bf16[128,1024]{1,0:T(8,128)(2,1)S(1)} %get-tuple-element.528.refs_0_), channel_id=1, source_target_pairs={{0,6},{1,7},{2,4},{3,5},{4,2},{5,3},{6,0},{7,1},{8,14},{9,15},{10,... | collective-permute-start | bytes 786440 | tf_op jit(solution)/shard_map/ppermute | solution.py:53
  163.0 15.7 %collective-permute-start.39 = (bf16[512,1024]{1,0:T(8,128)(2,1)S(1)}, bf16[512,1024]{1,0:T(8,128)(2,1)S(1)}, u32[]{:S(2)}, u32[]{:S(2)}) collective-permute-start(bf16[512,1024]{1,0:T(8,128)(2,1)S(1)} %get-tuple-element.568.refs_4_.refs_7_), channel_id=1, source_target_pairs={{0,1},{1,0},{2,3},{3,2},{4,5},{5,4},{6,7},{7,6},{8,9},{9,8},{10,11... | collective-permute-start | bytes 3145736 | tf_op jit(solution)/shard_map/ppermute | solution.py:56
  163.1 15.7 %collective-permute-start.40 = (bf16[512,1024]{1,0:T(8,128)(2,1)S(1)}, bf16[512,1024]{1,0:T(8,128)(2,1)S(1)}, u32[]{:S(2)}, u32[]{:S(2)}) collective-permute-start(bf16[512,1024]{1,0:T(8,128)(2,1)S(1)} %get-tuple-element.570.refs_7_.refs_4_), channel_id=1, source_target_pairs={{0,1},{1,0},{2,3},{3,2},{4,5},{5,4},{6,7},{7,6},{8,9},{9,8},{10,11... | collective-permute-start | bytes 3145736 | tf_op jit(solution)/shard_map/ppermute | solution.py:56
  165.1 13.6 %collective-permute-start.37 = (bf16[128,1024]{1,0:T(8,128)(2,1)S(1)}, bf16[128,1024]{1,0:T(8,128)(2,1)S(1)}, u32[]{:S(2)}, u32[]{:S(2)}) collective-permute-start(bf16[128,1024]{1,0:T(8,128)(2,1)S(1)} %get-tuple-element.549), channel_id=1, source_target_pairs={{0,4},{1,5},{2,6},{3,7},{4,0},{5,1},{6,2},{7,3},{8,12},{9,13},{10,... | collective-permute-start | bytes 786440 | tf_op jit(solution)/shard_map/ppermute | solution.py:53
  165.6 13.1 %collective-permute-start.38 = (bf16[128,1024]{1,0:T(8,128)(2,1)S(1)}, bf16[128,1024]{1,0:T(8,128)(2,1)S(1)}, u32[]{:S(2)}, u32[]{:S(2)}) collective-permute-start(bf16[128,1024]{1,0:T(8,128)(2,1)S(1)} %get-tuple-element.550), channel_id=1, source_target_pairs={{0,6},{1,7},{2,4},{3,5},{4,2},{5,3},{6,0},{7,1},{8,14},{9,15},{10,... | collective-permute-start | bytes 786440 | tf_op jit(solution)/shard_map/ppermute | solution.py:53
  180.3 14.9 %collective-permute-start.42 = (bf16[128,1024]{1,0:T(8,128)(2,1)S(1)}, bf16[128,1024]{1,0:T(8,128)(2,1)S(1)}, u32[]{:S(2)}, u32[]{:S(2)}) collective-permute-start(bf16[128,1024]{1,0:T(8,128)(2,1)S(1)} %get-tuple-element.564.refs_0_), channel_id=1, source_target_pairs={{0,4},{1,5},{2,6},{3,7},{4,0},{5,1},{6,2},{7,3},{8,12},{9,13},{10,... | collective-permute-start | bytes 786440 | tf_op jit(solution)/shard_map/ppermute | solution.py:53
  181.9 13.2 %collective-permute-start.43 = (bf16[128,1024]{1,0:T(8,128)(2,1)S(1)}, bf16[128,1024]{1,0:T(8,128)(2,1)S(1)}, u32[]{:S(2)}, u32[]{:S(2)}) collective-permute-start(bf16[128,1024]{1,0:T(8,128)(2,1)S(1)} %get-tuple-element.564.refs_0_), channel_id=1, source_target_pairs={{0,6},{1,7},{2,4},{3,5},{4,2},{5,3},{6,0},{7,1},{8,14},{9,15},{10,... | collective-permute-start | bytes 786440 | tf_op jit(solution)/shard_map/ppermute | solution.py:53
  183.3 17.5 %collective-permute-start.44 = (bf16[128,1024]{1,0:T(8,128)(2,1)S(1)}, bf16[128,1024]{1,0:T(8,128)(2,1)S(1)}, u32[]{:S(2)}, u32[]{:S(2)}) collective-permute-start(bf16[128,1024]{1,0:T(8,128)(2,1)S(1)} %collective-permute-done.24.refs_0_.grad_ref.ref), channel_id=1, source_target_pairs={{0,2},{1,3},{2,0},{3,1},{4,6},{5,7},{6,4},{7,5},{8,10},{9,11},{10,... | collective-permute-start | bytes 786440 | tf_op jit(solution)/shard_map/ppermute | solution.py:53
  183.7 20.3 %collective-permute-start.45 = (bf16[128,1024]{1,0:T(8,128)(2,1)S(1)}, bf16[128,1024]{1,0:T(8,128)(2,1)S(1)}, u32[]{:S(2)}, u32[]{:S(2)}) collective-permute-start(bf16[128,1024]{1,0:T(8,128)(2,1)S(1)} %collective-permute-done.24.refs_0_.grad_ref.ref), channel_id=1, source_target_pairs={{0,4},{1,5},{2,6},{3,7},{4,0},{5,1},{6,2},{7,3},{8,12},{9,13},{10,... | collective-permute-start | bytes 786440 | tf_op jit(solution)/shard_map/ppermute | solution.py:53
  189.0 15.0 %collective-permute-start.46 = (bf16[128,1024]{1,0:T(8,128)(2,1)S(1)}, bf16[128,1024]{1,0:T(8,128)(2,1)S(1)}, u32[]{:S(2)}, u32[]{:S(2)}) collective-permute-start(bf16[128,1024]{1,0:T(8,128)(2,1)S(1)} %collective-permute-done.24.refs_0_.grad_ref.ref), channel_id=1, source_target_pairs={{0,6},{1,7},{2,4},{3,5},{4,2},{5,3},{6,0},{7,1},{8,14},{9,15},{10,... | collective-permute-start | bytes 786440 | tf_op jit(solution)/shard_map/ppermute | solution.py:53
  212.5 17.8 %collective-permute-start.51 = (bf16[512,512]{1,0:T(8,128)(2,1)S(1)}, bf16[512,512]{1,0:T(8,128)(2,1)S(1)}, u32[]{:S(2)}, u32[]{:S(2)}) collective-permute-start(bf16[512,512]{1,0:T(8,128)(2,1)S(1)} %get-tuple-element.602.refs_0_), channel_id=1, source_target_pairs={{0,8},{24,16},{1,9},{25,17},{2,10},{26,18},{3,11},{27,19},{4,12},{... | collective-permute-start | bytes 1572872 | tf_op jit(solution)/shard_map/ppermute | solution.py:829
  215.5 14.0 %collective-permute-start.49 = (bf16[128,1024]{1,0:T(8,128)(2,1)S(1)}, bf16[128,1024]{1,0:T(8,128)(2,1)S(1)}, u32[]{:S(2)}, u32[]{:S(2)}) collective-permute-start(bf16[128,1024]{1,0:T(8,128)(2,1)S(1)} %get-tuple-element.598), channel_id=1, source_target_pairs={{0,4},{1,5},{2,6},{3,7},{4,0},{5,1},{6,2},{7,3},{8,12},{9,13},{10,... | collective-permute-start | bytes 786440 | tf_op jit(solution)/shard_map/ppermute | solution.py:53
  215.9 13.6 %collective-permute-start.50 = (bf16[128,1024]{1,0:T(8,128)(2,1)S(1)}, bf16[128,1024]{1,0:T(8,128)(2,1)S(1)}, u32[]{:S(2)}, u32[]{:S(2)}) collective-permute-start(bf16[128,1024]{1,0:T(8,128)(2,1)S(1)} %get-tuple-element.599), channel_id=1, source_target_pairs={{0,6},{1,7},{2,4},{3,5},{4,2},{5,3},{6,0},{7,1},{8,14},{9,15},{10,... | collective-permute-start | bytes 786440 | tf_op jit(solution)/shard_map/ppermute | solution.py:53
  230.3 21.8 %collective-permute-start.55 = (bf16[512,512]{1,0:T(8,128)(2,1)}, bf16[512,512]{1,0:T(8,128)(2,1)}, u32[]{:S(2)}, u32[]{:S(2)}) collective-permute-start(bf16[512,512]{1,0:T(8,128)(2,1)} %get-tuple-element.611.refs_3_), channel_id=1, source_target_pairs={{0,8},{24,16},{1,9},{25,17},{2,10},{26,18},{3,11},{27,19},{4,12},{... | collective-permute-start | bytes 1572872 | tf_op jit(solution)/shard_map/ppermute | solution.py:829
  232.5 19.6 %collective-permute-start.56 = (bf16[512,512]{1,0:T(8,128)(2,1)}, bf16[512,512]{1,0:T(8,128)(2,1)}, u32[]{:S(2)}, u32[]{:S(2)}) collective-permute-start(bf16[512,512]{1,0:T(8,128)(2,1)} %turn.13.refs_1_), channel_id=1, source_target_pairs={{8,16},{16,8},{9,17},{17,9},{10,18},{18,10},{11,19},{19,11},{12,20... | collective-permute-start | bytes 1572872 | tf_op jit(solution)/shard_map/ppermute | solution.py:829
  238.7 13.3 %collective-permute-start.53 = (bf16[128,1024]{1,0:T(8,128)(2,1)}, bf16[128,1024]{1,0:T(8,128)(2,1)}, u32[]{:S(2)}, u32[]{:S(2)}) collective-permute-start(bf16[128,1024]{1,0:T(8,128)(2,1)} %get-tuple-element.613.refs_0_.refs_6_), channel_id=1, source_target_pairs={{0,4},{1,5},{2,6},{3,7},{4,0},{5,1},{6,2},{7,3},{8,12},{9,13},{10,... | collective-permute-start | bytes 786440 | tf_op jit(solution)/shard_map/ppermute | solution.py:53
  253.8 18.2 %collective-permute-start.60 = (bf16[512,512]{1,0:T(8,128)(2,1)S(1)}, bf16[512,512]{1,0:T(8,128)(2,1)S(1)}, u32[]{:S(2)}, u32[]{:S(2)}) collective-permute-start(bf16[512,512]{1,0:T(8,128)(2,1)S(1)} %get-tuple-element.823.b_ref), channel_id=1, source_target_pairs={{0,8},{24,16},{8,0},{16,24},{1,9},{25,17},{9,1},{17,25},{2,10},{26... | collective-permute-start | bytes 1572872 | tf_op jit(solution)/shard_map/ppermute | solution.py:829
  256.1 15.9 %collective-permute-start.61 = (bf16[512,512]{1,0:T(8,128)(2,1)S(1)}, bf16[512,512]{1,0:T(8,128)(2,1)S(1)}, u32[]{:S(2)}, u32[]{:S(2)}) collective-permute-start(bf16[512,512]{1,0:T(8,128)(2,1)S(1)} %get-tuple-element.648.refs_1_), channel_id=1, source_target_pairs={{8,16},{16,8},{9,17},{17,9},{10,18},{18,10},{11,19},{19,11},{12,20... | collective-permute-start | bytes 1572872 | tf_op jit(solution)/shard_map/ppermute | solution.py:829
  258.7 13.3 %collective-permute-start.57 = (bf16[128,1024]{1,0:T(8,128)(2,1)S(1)}, bf16[128,1024]{1,0:T(8,128)(2,1)S(1)}, u32[]{:S(2)}, u32[]{:S(2)}) collective-permute-start(bf16[128,1024]{1,0:T(8,128)(2,1)S(1)} %copy-done.71), channel_id=1, source_target_pairs={{0,2},{1,3},{2,0},{3,1},{4,6},{5,7},{6,4},{7,5},{8,10},{9,11},{10,... | collective-permute-start | bytes 786440 | tf_op jit(solution)/shard_map/ppermute | solution.py:53
  272.9 17.3 %collective-permute-start.65 = (bf16[512,512]{1,0:T(8,128)(2,1)S(1)}, bf16[512,512]{1,0:T(8,128)(2,1)S(1)}, u32[]{:S(2)}, u32[]{:S(2)}) collective-permute-start(bf16[512,512]{1,0:T(8,128)(2,1)S(1)} %get-tuple-element.824.b_ref), channel_id=1, source_target_pairs={{0,8},{24,16},{8,0},{16,24},{1,9},{25,17},{9,1},{17,25},{2,10},{26... | collective-permute-start | bytes 1572872 | tf_op jit(solution)/shard_map/ppermute | solution.py:829
  272.9 17.3 %collective-permute-start.66 = (bf16[512,512]{1,0:T(8,128)(2,1)S(1)}, bf16[512,512]{1,0:T(8,128)(2,1)S(1)}, u32[]{:S(2)}, u32[]{:S(2)}) collective-permute-start(bf16[512,512]{1,0:T(8,128)(2,1)S(1)} %get-tuple-element.657.refs_1_), channel_id=1, source_target_pairs={{8,16},{16,8},{9,17},{17,9},{10,18},{18,10},{11,19},{19,11},{12,20... | collective-permute-start | bytes 1572872 | tf_op jit(solution)/shard_map/ppermute | solution.py:829
  291.0 17.2 %collective-permute-start.70 = (bf16[512,512]{1,0:T(8,128)(2,1)S(1)}, bf16[512,512]{1,0:T(8,128)(2,1)S(1)}, u32[]{:S(2)}, u32[]{:S(2)}) collective-permute-start(bf16[512,512]{1,0:T(8,128)(2,1)S(1)} %get-tuple-element.730.b_ref), channel_id=1, source_target_pairs={{0,8},{24,16},{8,0},{16,24},{1,9},{25,17},{9,1},{17,25},{2,10},{26... | collective-permute-start | bytes 1572872 | tf_op jit(solution)/shard_map/ppermute | solution.py:829
  291.1 17.2 %collective-permute-start.71 = (bf16[512,512]{1,0:T(8,128)(2,1)S(1)}, bf16[512,512]{1,0:T(8,128)(2,1)S(1)}, u32[]{:S(2)}, u32[]{:S(2)}) collective-permute-start(bf16[512,512]{1,0:T(8,128)(2,1)S(1)} %get-tuple-element.689.refs_1_), channel_id=1, source_target_pairs={{8,16},{16,8},{9,17},{17,9},{10,18},{18,10},{11,19},{19,11},{12,20... | collective-permute-start | bytes 1572872 | tf_op jit(solution)/shard_map/ppermute | solution.py:829
  295.0 13.2 %collective-permute-start.68 = (bf16[128,1024]{1,0:T(8,128)(2,1)S(1)}, bf16[128,1024]{1,0:T(8,128)(2,1)S(1)}, u32[]{:S(2)}, u32[]{:S(2)}) collective-permute-start(bf16[128,1024]{1,0:T(8,128)(2,1)S(1)} %get-tuple-element.662.refs_0_), channel_id=1, source_target_pairs={{0,4},{1,5},{2,6},{3,7},{4,0},{5,1},{6,2},{7,3},{8,12},{9,13},{10,... | collective-permute-start | bytes 786440 | tf_op jit(solution)/shard_map/ppermute | solution.py:53
  310.2 18.7 %collective-permute-start.72 = (bf16[512,1024]{1,0:T(8,128)(2,1)S(1)}, bf16[512,1024]{1,0:T(8,128)(2,1)S(1)}, u32[]{:S(2)}, u32[]{:S(2)}) collective-permute-start(bf16[512,1024]{1,0:T(8,128)(2,1)S(1)} %get-tuple-element.674), channel_id=1, source_target_pairs={{0,1},{1,0},{2,3},{3,2},{4,5},{5,4},{6,7},{7,6},{8,9},{9,8},{10,11... | collective-permute-start | bytes 3145736 | tf_op jit(solution)/shard_map/ppermute | solution.py:56
  311.1 18.1 %collective-permute-start.74 = (bf16[512,512]{1,0:T(8,128)(2,1)S(1)}, bf16[512,512]{1,0:T(8,128)(2,1)S(1)}, u32[]{:S(2)}, u32[]{:S(2)}) collective-permute-start(bf16[512,512]{1,0:T(8,128)(2,1)S(1)} %get-tuple-element.731.b_ref), channel_id=1, source_target_pairs={{0,8},{24,16},{8,0},{16,24},{1,9},{25,17},{9,1},{17,25},{2,10},{26... | collective-permute-start | bytes 1572872 | tf_op jit(solution)/shard_map/ppermute | solution.py:829
  311.4 21.6 %collective-permute-start.75 = (bf16[512,512]{1,0:T(8,128)(2,1)S(1)}, bf16[512,512]{1,0:T(8,128)(2,1)S(1)}, u32[]{:S(2)}, u32[]{:S(2)}) collective-permute-start(bf16[512,512]{1,0:T(8,128)(2,1)S(1)} %get-tuple-element.701.refs_1_), channel_id=1, source_target_pairs={{8,16},{16,8},{9,17},{17,9},{10,18},{18,10},{11,19},{19,11},{12,20... | collective-permute-start | bytes 1572872 | tf_op jit(solution)/shard_map/ppermute | solution.py:829
  315.5 13.4 %collective-permute-start.73 = (bf16[128,1024]{1,0:T(8,128)(2,1)S(1)}, bf16[128,1024]{1,0:T(8,128)(2,1)S(1)}, u32[]{:S(2)}, u32[]{:S(2)}) collective-permute-start(bf16[128,1024]{1,0:T(8,128)(2,1)S(1)} %add_and_norm.7), channel_id=1, source_target_pairs={{0,0},{1,1},{10,2},{11,3},{20,4},{21,5},{30,6},{31,7},{16,12},{17,... | collective-permute-start | bytes 786440 | tf_op jit(solution)/shard_map/ppermute | solution.py:50
  333.8 19.0 %collective-permute-start.79 = (bf16[512,512]{1,0:T(8,128)(2,1)S(1)}, bf16[512,512]{1,0:T(8,128)(2,1)S(1)}, u32[]{:S(2)}, u32[]{:S(2)}) collective-permute-start(bf16[512,512]{1,0:T(8,128)(2,1)S(1)} %get-tuple-element.799.b_ref), channel_id=1, source_target_pairs={{0,8},{24,16},{8,0},{16,24},{1,9},{25,17},{9,1},{17,25},{2,10},{26... | collective-permute-start | bytes 1572872 | tf_op jit(solution)/shard_map/ppermute | solution.py:829
  333.9 18.9 %collective-permute-start.80 = (bf16[512,512]{1,0:T(8,128)(2,1)S(1)}, bf16[512,512]{1,0:T(8,128)(2,1)S(1)}, u32[]{:S(2)}, u32[]{:S(2)}) collective-permute-start(bf16[512,512]{1,0:T(8,128)(2,1)S(1)} %get-tuple-element.715.refs_1_), channel_id=1, source_target_pairs={{8,16},{16,8},{9,17},{17,9},{10,18},{18,10},{11,19},{19,11},{12,20... | collective-permute-start | bytes 1572872 | tf_op jit(solution)/shard_map/ppermute | solution.py:829
  339.9 12.9 %collective-permute-start.77 = (bf16[128,1024]{1,0:T(8,128)(2,1)S(1)}, bf16[128,1024]{1,0:T(8,128)(2,1)S(1)}, u32[]{:S(2)}, u32[]{:S(2)}) collective-permute-start(bf16[128,1024]{1,0:T(8,128)(2,1)S(1)} %get-tuple-element.696), channel_id=1, source_target_pairs={{0,4},{1,5},{2,6},{3,7},{4,0},{5,1},{6,2},{7,3},{8,12},{9,13},{10,... | collective-permute-start | bytes 786440 | tf_op jit(solution)/shard_map/ppermute | solution.py:53
  340.0 12.8 %collective-permute-start.78 = (bf16[128,1024]{1,0:T(8,128)(2,1)S(1)}, bf16[128,1024]{1,0:T(8,128)(2,1)S(1)}, u32[]{:S(2)}, u32[]{:S(2)}) collective-permute-start(bf16[128,1024]{1,0:T(8,128)(2,1)S(1)} %get-tuple-element.697), channel_id=1, source_target_pairs={{0,6},{1,7},{2,4},{3,5},{4,2},{5,3},{6,0},{7,1},{8,14},{9,15},{10,... | collective-permute-start | bytes 786440 | tf_op jit(solution)/shard_map/ppermute | solution.py:53
  353.6 16.8 %collective-permute-start.84 = (bf16[512,512]{1,0:T(8,128)(2,1)S(1)}, bf16[512,512]{1,0:T(8,128)(2,1)S(1)}, u32[]{:S(2)}, u32[]{:S(2)}) collective-permute-start(bf16[512,512]{1,0:T(8,128)(2,1)S(1)} %get-tuple-element.800.b_ref), channel_id=1, source_target_pairs={{0,8},{24,16},{8,0},{16,24},{1,9},{25,17},{9,1},{17,25},{2,10},{26... | collective-permute-start | bytes 1572872 | tf_op jit(solution)/shard_map/ppermute | solution.py:829
  353.7 16.7 %collective-permute-start.85 = (bf16[512,512]{1,0:T(8,128)(2,1)S(1)}, bf16[512,512]{1,0:T(8,128)(2,1)S(1)}, u32[]{:S(2)}, u32[]{:S(2)}) collective-permute-start(bf16[512,512]{1,0:T(8,128)(2,1)S(1)} %get-tuple-element.738.refs_1_), channel_id=1, source_target_pairs={{8,16},{16,8},{9,17},{17,9},{10,18},{18,10},{11,19},{19,11},{12,20... | collective-permute-start | bytes 1572872 | tf_op jit(solution)/shard_map/ppermute | solution.py:829
  371.2 17.9 %collective-permute-start.89 = (bf16[512,512]{1,0:T(8,128)(2,1)S(1)}, bf16[512,512]{1,0:T(8,128)(2,1)S(1)}, u32[]{:S(2)}, u32[]{:S(2)}) collective-permute-start(bf16[512,512]{1,0:T(8,128)(2,1)S(1)} %get-tuple-element.816.b_ref), channel_id=1, source_target_pairs={{0,8},{24,16},{8,0},{16,24},{1,9},{25,17},{9,1},{17,25},{2,10},{26... | collective-permute-start | bytes 1572872 | tf_op jit(solution)/shard_map/ppermute | solution.py:829
  371.7 17.4 %collective-permute-start.90 = (bf16[512,512]{1,0:T(8,128)(2,1)S(1)}, bf16[512,512]{1,0:T(8,128)(2,1)S(1)}, u32[]{:S(2)}, u32[]{:S(2)}) collective-permute-start(bf16[512,512]{1,0:T(8,128)(2,1)S(1)} %get-tuple-element.766.refs_1_), channel_id=1, source_target_pairs={{8,16},{16,8},{9,17},{17,9},{10,18},{18,10},{11,19},{19,11},{12,20... | collective-permute-start | bytes 1572872 | tf_op jit(solution)/shard_map/ppermute | solution.py:829
  375.8 13.2 %collective-permute-start.86 = (bf16[128,1024]{1,0:T(8,128)(2,1)S(1)}, bf16[128,1024]{1,0:T(8,128)(2,1)S(1)}, u32[]{:S(2)}, u32[]{:S(2)}) collective-permute-start(bf16[128,1024]{1,0:T(8,128)(2,1)S(1)} %get-tuple-element.733), channel_id=1, source_target_pairs={{0,2},{1,3},{2,0},{3,1},{4,6},{5,7},{6,4},{7,5},{8,10},{9,11},{10,... | collective-permute-start | bytes 786440 | tf_op jit(solution)/shard_map/ppermute | solution.py:53
  376.2 12.8 %collective-permute-start.87 = (bf16[128,1024]{1,0:T(8,128)(2,1)S(1)}, bf16[128,1024]{1,0:T(8,128)(2,1)S(1)}, u32[]{:S(2)}, u32[]{:S(2)}) collective-permute-start(bf16[128,1024]{1,0:T(8,128)(2,1)S(1)} %get-tuple-element.734), channel_id=1, source_target_pairs={{0,4},{1,5},{2,6},{3,7},{4,0},{5,1},{6,2},{7,3},{8,12},{9,13},{10,... | collective-permute-start | bytes 786440 | tf_op jit(solution)/shard_map/ppermute | solution.py:53
  389.9 16.1 %collective-permute-start.94 = (bf16[512,512]{1,0:T(8,128)(2,1)S(1)}, bf16[512,512]{1,0:T(8,128)(2,1)S(1)}, u32[]{:S(2)}, u32[]{:S(2)}) collective-permute-start(bf16[512,512]{1,0:T(8,128)(2,1)S(1)} %get-tuple-element.817.b_ref), channel_id=1, source_target_pairs={{0,8},{24,16},{8,0},{16,24},{1,9},{25,17},{9,1},{17,25},{2,10},{26... | collective-permute-start | bytes 1572872 | tf_op jit(solution)/shard_map/ppermute | solution.py:829
  390.0 16.1 %collective-permute-start.95 = (bf16[512,512]{1,0:T(8,128)(2,1)S(1)}, bf16[512,512]{1,0:T(8,128)(2,1)S(1)}, u32[]{:S(2)}, u32[]{:S(2)}) collective-permute-start(bf16[512,512]{1,0:T(8,128)(2,1)S(1)} %get-tuple-element.774.refs_1_), channel_id=1, source_target_pairs={{8,16},{16,8},{9,17},{17,9},{10,18},{18,10},{11,19},{19,11},{12,20... | collective-permute-start | bytes 1572872 | tf_op jit(solution)/shard_map/ppermute | solution.py:829
  406.8 20.5 %collective-permute-start.97 = (bf16[576,512]{1,0:T(8,128)(2,1)S(1)}, bf16[576,512]{1,0:T(8,128)(2,1)S(1)}, u32[]{:S(2)}, u32[]{:S(2)}) collective-permute-start(bf16[576,512]{1,0:T(8,128)(2,1)S(1)} %get-tuple-element.781.b_ref), channel_id=1, source_target_pairs={{0,8},{24,16},{8,0},{16,24},{1,9},{25,17},{9,1},{17,25},{2,10},{26... | collective-permute-start | bytes 1769480 | tf_op jit(solution)/shard_map/ppermute | solution.py:829
  406.9 20.4 %collective-permute-start.98 = (bf16[512,512]{1,0:T(8,128)(2,1)S(1)}, bf16[512,512]{1,0:T(8,128)(2,1)S(1)}, u32[]{:S(2)}, u32[]{:S(2)}) collective-permute-start(bf16[512,512]{1,0:T(8,128)(2,1)S(1)} %get-tuple-element.783.refs_1_), channel_id=1, source_target_pairs={{8,16},{16,8},{9,17},{17,9},{10,18},{18,10},{11,19},{19,11},{12,20... | collective-permute-start | bytes 1572872 | tf_op jit(solution)/shard_map/ppermute | solution.py:829
  410.2 15.5 %collective-permute-start.96 = (bf16[128,1024]{1,0:T(8,128)(2,1)S(1)}, bf16[128,1024]{1,0:T(8,128)(2,1)S(1)}, u32[]{:S(2)}, u32[]{:S(2)}) collective-permute-start(bf16[128,1024]{1,0:T(8,128)(2,1)S(1)} %get-tuple-element.771), channel_id=1, source_target_pairs={{0,0},{1,1},{10,2},{11,3},{20,4},{21,5},{30,6},{31,7},{16,12},{17,... | collective-permute-start | bytes 786440 | tf_op jit(solution)/shard_map/ppermute | solution.py:50
  428.1 13.9 %collective-permute-start.99 = (bf16[576,512]{1,0:T(8,128)(2,1)S(1)}, bf16[576,512]{1,0:T(8,128)(2,1)S(1)}, u32[]{:S(2)}, u32[]{:S(2)}) collective-permute-start(bf16[576,512]{1,0:T(8,128)(2,1)S(1)} %get-tuple-element.788.b_ref), channel_id=1, source_target_pairs={{0,8},{24,16},{8,0},{16,24},{1,9},{25,17},{9,1},{17,25},{2,10},{26... | collective-permute-start | bytes 1769480 | tf_op jit(solution)/shard_map/ppermute | solution.py:829
  429.0 18.2 %collective-permute-start.100 = (bf16[576,512]{1,0:T(8,128)(2,1)S(1)}, bf16[576,512]{1,0:T(8,128)(2,1)S(1)}, u32[]{:S(2)}, u32[]{:S(2)}) collective-permute-start(bf16[576,512]{1,0:T(8,128)(2,1)S(1)} %get-tuple-element.793.refs_0_), channel_id=1, source_target_pairs={{8,16},{16,8},{9,17},{17,9},{10,18},{18,10},{11,19},{19,11},{12,20... | collective-permute-start | bytes 1769480 | tf_op jit(solution)/shard_map/ppermute | solution.py:829
  448.0 17.5 %collective-permute-start.104 = (bf16[576,512]{1,0:T(8,128)(2,1)S(1)}, bf16[576,512]{1,0:T(8,128)(2,1)S(1)}, u32[]{:S(2)}, u32[]{:S(2)}) collective-permute-start(bf16[576,512]{1,0:T(8,128)(2,1)S(1)} %get-tuple-element.798.b_ref), channel_id=1, source_target_pairs={{8,0},{16,24},{9,1},{17,25},{10,2},{18,26},{11,3},{19,27},{12,4},{... | collective-permute-start | bytes 1769480 | tf_op jit(solution)/shard_map/ppermute | solution.py:829
  449.3 16.2 %collective-permute-start.105 = (bf16[576,512]{1,0:T(8,128)(2,1)S(1)}, bf16[576,512]{1,0:T(8,128)(2,1)S(1)}, u32[]{:S(2)}, u32[]{:S(2)}) collective-permute-start(bf16[576,512]{1,0:T(8,128)(2,1)S(1)} %get-tuple-element.806.refs_0_), channel_id=1, source_target_pairs={{8,16},{16,8},{9,17},{17,9},{10,18},{18,10},{11,19},{19,11},{12,20... | collective-permute-start | bytes 1769480 | tf_op jit(solution)/shard_map/ppermute | solution.py:829
  (132 other events, 1961.2 us)

commit v4 on v3

--- a/solution.py
+++ b/solution.py
@@ -29,31 +29,45 @@
         self.f = lax.axis_index("fsdp")
         self.p = self.f // 2
         self.c = self.f % 2
-        self.place = jnp.stack([self.p, self.c]).astype(jnp.int32)
+        self.place = jnp.stack([self.p, self.c, self.s % 2]).astype(jnp.int32)
 
     def moves(self):
-        n, n_p = self.n_f, self.n_p
-        square = [[s ^ q for s in range(self.n_s)] for q in range(n_p)]
-        if n_p == 4:
+        square = [[s ^ q for s in range(self.n_s)] for q in range(self.n_p)]
+        if self.n_p == 4:
             square = [[0, 2, 1, 3], [1, 3, 2, 0], [2, 0, 3, 1], [3, 1, 0, 2]]
-        pairs = []
-        for s in range(self.n_s):
-            for q in range(n_p):
-                p = square[q][s]
-                pairs += [(s * n + 2 * p + c, p * n + 2 * q + c) for c in range(2)]
-        return pairs
-
-    def to_planes(self, v):
-        return lax.ppermute(v, ("seq", "fsdp"), self.moves())
-
-    def from_planes(self, v):
-        return lax.ppermute(v, ("seq", "fsdp"), [(b, a) for a, b in self.moves()])
+        return [(s, square[q][s], q) for s in range(self.n_s) for q in range(self.n_p)]
+
+    def send(self, v, moves):
+        n = self.n_f
+        pairs = [(s * n + 2 * p + c, t * n + 2 * q + c) for s, p, t, q in moves for c in range(2)]
+        return lax.ppermute(v, ("seq", "fsdp"), pairs)
+
+    def to_place(self, v):
+        return self.send(v, [(s, p, p, q) for s, p, q in self.moves()])
+
+    def from_place(self, v):
+        return self.send(v, [(p, q, s, p) for s, p, q in self.moves()])
+
+    def to_chip(self, v):
+        return self.send(v, [(s, p, s, q) for s, p, q in self.moves()])
+
+    def to_plane(self, v):
+        return self.send(v, [(s, q, p, q) for s, p, q in self.moves()])
+
+    def from_plane(self, v):
+        return self.send(v, [(p, q, s, q) for s, p, q in self.moves()])
+
+    def from_chip(self, v):
+        return self.send(v, [(s, q, s, p) for s, p, q in self.moves()])
 
     def chip(self, v, j):
         return lax.ppermute(v, "fsdp", xor_pairs(self.n_f, 2 * j))
 
     def core(self, v):
         return lax.ppermute(v, "fsdp", xor_pairs(self.n_f, 1))
+
+    def next_plane(self, v):
+        return lax.ppermute(v, "seq", xor_pairs(self.n_s, 1))
 
     def gather(self, v):
         return [v] + [self.chip(v, j) for j in range(1, self.n_p)]
@@ -139,22 +153,67 @@
     return jnp.concatenate(out, axis=1)
 
 
-def stack_rows(net, pieces, weight, layer):
+def cut_columns(net, weight, layer, groups):
     n_p = net.n_p
-    rows, width = D // net.n_f, pieces[0].shape[1]
-    more, depth = weight.shape[1:]
-
-    def body(place, *refs):
-        p = place[0]
-        own, rest, sems = refs[n_p + 1 :]
-        pairs = [(refs[j].at[0:rows], own.at[tile(p ^ j, rows)]) for j in range(n_p)]
-        for copy in copy_all([*pairs, (refs[n_p].at[layer], rest)], sems):
+    rows = weight.shape[1] // 2
+    width = weight.shape[2] // (groups * n_p)
+
+    def body(place, weight_ref, *refs):
+        p, half = place[0], place[2]
+        outs, sems = refs[: n_p - 1], refs[-1]
+        pairs = []
+        for j in range(1, n_p):
+            for i in range(groups):
+                cols = tile(i * n_p + (p ^ j), width)
+                to = outs[j - 1].at[:, i * width : (i + 1) * width]
+                pairs.append((weight_ref.at[layer, tile(half, rows), cols], to))
+        for copy in copy_all(pairs, sems):
             copy.wait()
 
-    outs = [((n_p * rows, width), BF), ((more, depth), BF)]
-    specs = [IN_ANY] * n_p + [IN_HBM]
-    scratch = [pltpu.SemaphoreType.DMA((n_p + 1,))]
-    return run("stack_rows", body, outs, [*pieces, weight], net.place, scratch, ins_at=specs)
+    outs = [((rows, groups * width), BF)] * (n_p - 1)
+    scratch = [pltpu.SemaphoreType.DMA((groups * (n_p - 1),))]
+    return run("cut_columns", body, outs, [weight], net.place, scratch, ins_at=[IN_HBM])
+
+
+def stack_halves(pieces):
+    rows, width = pieces[0].shape
+    count = len(pieces)
+
+    def body(*refs):
+        out, sems = refs[count:]
+        pairs = [(refs[j], out.at[j * rows : (j + 1) * rows]) for j in range(count)]
+        for copy in copy_all(pairs, sems):
+            copy.wait()
+
+    outs = [((count * rows, width), BF)]
+    scratch = [pltpu.SemaphoreType.DMA((count,))]
+    return run("stack_halves", body, outs, pieces, None, scratch, ins_at=[IN_ANY] * count)[0]
+
+
+def stack_rows(net, mine, theirs, weight, groups, more, layer):
+    n_p = net.n_p
+    half_rows = weight.shape[1] // 2
+    rows = 2 * half_rows
+    width = weight.shape[2] // (groups * n_p)
+
+    def body(place, mine_ref, their_ref, weight_ref, more_ref, own, rest, sems):
+        p, half = place[0], place[2]
+        pairs = [(more_ref.at[layer], rest)]
+        for i in range(groups):
+            to = own.at[tile(p, rows), i * width : (i + 1) * width]
+            pairs.append((weight_ref.at[layer, :, tile(i * n_p + p, width)], to))
+        for j in range(1, n_p):
+            here = slice((j - 1) * half_rows, j * half_rows)
+            at = (p ^ j) * 2
+            pairs.append((mine_ref.at[here], own.at[tile(at + half, half_rows)]))
+            pairs.append((their_ref.at[here], own.at[tile(at + 1 - half, half_rows)]))
+        for copy in copy_all(pairs, sems):
+            copy.wait()
+
+    outs = [((n_p * rows, groups * width), BF), (more.shape[1:], BF)]
+    scratch = [pltpu.SemaphoreType.DMA((1 + groups + 2 * (n_p - 1),))]
+    specs = [IN_ANY] * 2 + [IN_HBM] * 2
+    return run("stack_rows", body, outs, [mine, theirs, weight, more], net.place, scratch, ins_at=specs)
 
 
 def pack_tokens(tokens, scene_ids, token_kind):
@@ -173,59 +232,39 @@
     return total
 
 
-def cut_columns(net, weight, layer, groups, small):
+def put_small(tokens, own, other):
+    rows = tokens.shape[0] - 16
+    width = own.shape[1] // 2
+
+    def body(token_ref, own_ref, other_ref, out, lines):
+        out[0:rows, :] = token_ref[0:rows, :]
+        lines[...] = token_ref[rows:, :].astype(F32)
+        row = 1
+        for ref in (own_ref, other_ref):
+            low = ref[...].astype(F32)
+            for layer in range(own.shape[0]):
+                for half in range(2):
+                    lines[row : row + 1, 0:width] = low[layer : layer + 1, half * width : (half + 1) * width]
+                    row += 1
+        out[rows:, :] = lines[...].astype(BF)
+
+    scratch = [pltpu.VMEM((16, D), F32)]
+    return run("put_small", body, [(tokens.shape, BF)], [tokens, own, other], None, scratch)[0]
+
+
+def join_vectors(net, layers, blocks, sizes, rows):
     n_p = net.n_p
-    rows = weight.shape[1]
-    width = weight.shape[2] // (groups * n_p)
-    extra = 16 if small else 0
-
-    def body(place, weight_ref, *refs):
-        p = place[0]
-        outs, sems = refs[len(small) : len(small) + n_p], refs[-1]
-        pairs = []
-        for j in range(n_p):
-            for i in range(groups):
-                cols = tile(i * n_p + (p ^ j), width)
-                to = outs[j].at[0:rows, i * width : (i + 1) * width]
-                pairs.append((weight_ref.at[layer, :, cols], to))
-        copies = copy_all(pairs, sems)
-        if extra:
-            lines = refs[2 + n_p]
-            lines[...] = jnp.zeros_like(lines)
-            row = 0
-            for ref in refs[:2]:
-                low = ref[...].astype(F32)
-                for k in range(ref.shape[0]):
-                    for half in range(2):
-                        cols = slice(half * groups * width, (half + 1) * groups * width)
-                        lines[row : row + 1, :] = low[k : k + 1, cols]
-                        row += 1
-            for j in range(n_p):
-                outs[j][rows : rows + extra, :] = lines[...].astype(BF)
-        for copy in copies:
-            copy.wait()
-
-    outs = [((rows + extra, groups * width), BF)] * n_p
-    specs = [IN_HBM] + [IN_VMEM] * len(small)
-    scratch = [pltpu.VMEM((16, groups * width), F32)] if extra else []
-    scratch.append(pltpu.SemaphoreType.DMA((groups * n_p,)))
-    return list(run("cut_columns", body, outs, [weight, *small], net.place, scratch, ins_at=specs))
-
-
-def join_vectors(net, layers, pieces, sizes):
-    n_p = net.n_p
-    width = pieces[0].shape[1]
+    width = sum(sizes) // 2
     starts = [sum(sizes[:i]) for i in range(len(sizes))]
-    first_row = D // net.n_f
 
     def body(place, *refs):
         p, c = place[0], place[1]
         ins, outs = refs[:n_p], refs[n_p:]
         for j in range(n_p):
-            low = ins[j][first_row : first_row + 16, :].astype(F32)
+            low = ins[j][rows : rows + 16, 0:width].astype(F32)
             for layer in range(layers):
                 for half in range(2):
-                    row = layer * 2 + half
+                    row = 1 + layer * 2 + half
                     own = low[row : row + 1, :]
                     other = low[2 * layers + row : 2 * layers + row + 1, :]
                     first = jnp.where(c == 0, own, other)
@@ -238,7 +277,7 @@
                         outs[k][layer : layer + 1, tile(p ^ j, 2 * size)] = both
 
     outs = [((layers, 2 * n_p * size), F32) for size in sizes]
-    return run("join_vectors", body, outs, pieces, net.place)
+    return run("join_vectors", body, outs, blocks, net.place)
 
 
 def norm_rows(hidden):
@@ -326,8 +365,7 @@
 
 
 def probs_by_key(k2, q2, allowed, head):
-    scores = dot_nt(keep_head(k2, head, 1), q2) * SCALE
-    scores = jnp.where(allowed, scores, NEG)
+    scores = jnp.where(allowed, dot_nt(keep_head(k2, head, 1), q2), NEG)
     powers = jnp.exp(scores - jnp.max(scores, axis=0, keepdims=True))
     return powers * (1.0 / jnp.sum(powers, axis=0, keepdims=True))
 
@@ -389,7 +427,7 @@
                 k2 = qkv[:, cw + pair * LANES : cw + (pair + 1) * LANES]
                 total = None
                 for head in range(2):
-                    probs = probs_by_key(k2, q2, allowed, head).astype(BF)
+                    probs = probs_by_key(k2, q2 * BF(SCALE), allowed, head).astype(BF)
                     part = dot(keep_head(vt[lanes, :], head, 0), probs)
                     total = part if total is None else total + part
                 attended[here, lanes] = jnp.transpose(total).astype(BF)
@@ -451,7 +489,7 @@
                 do2 = do[here, lanes]
                 total = None
                 for head in range(2):
-                    probs = probs_by_key(k2, q2, allowed, head)
+                    probs = probs_by_key(k2, q2 * BF(SCALE), allowed, head)
                     dp = dot_nt(keep_head(v2, head, 1), do2)
                     mean = jnp.sum(probs * dp, axis=0, keepdims=True)
                     ds = (probs * (dp - mean)).astype(BF)
@@ -710,21 +748,47 @@
     return run("cut_rows", body, outs, [first, second], net.place)
 
 
-def sum_small(layers, pieces, sizes, rows):
-    width = pieces[0].shape[1]
+def cut_part(net, v, groups, extra=None):
+    n_p = net.n_p
+    rows = v.shape[0] // n_p
+    taken = groups * (D // n_p)
+    rest = v.shape[1] - taken
+
+    def body(place, ref, *outs):
+        p = place[0]
+        for j in range(n_p):
+            outs[j][...] = ref[tile(p ^ j, rows), :taken]
+        if extra is not None:
+            for i in range(n_p):
+                outs[n_p][:, i * rest : (i + 1) * rest] = ref[i * rows : (i + 1) * rows - extra, taken:]
+
+    outs = [((rows, taken), BF)] * n_p
+    if extra is not None:
+        outs.append(((rows - extra, n_p * rest), BF))
+    return run("cut_part", body, outs, [v], net.place)
+
+
+def sum_small(layers, first, second, sizes, rows):
+    count = len(first)
+    split = first[0].shape[1]
+    width = split + second[0].shape[1]
     starts = [sum(sizes[:i]) for i in range(len(sizes))]
 
     def body(*refs):
-        total = refs[0][rows:, :].astype(F32)
-        for ref in refs[1 : len(pieces)]:
-            total = total + ref[rows:, :].astype(F32)
-        for out, at, size in zip(refs[len(pieces) :], starts, sizes):
+        parts = []
+        for group in (refs[:count], refs[count : 2 * count]):
+            total = group[0][rows:, :].astype(F32)
+            for ref in group[1:]:
+                total = total + ref[rows:, :].astype(F32)
+            parts.append(total)
+        total = jnp.concatenate(parts, axis=1)
+        for out, at, size in zip(refs[2 * count :], starts, sizes):
             half = at // width
             for layer in range(layers):
                 row = 2 * layer + half
                 out[layer : layer + 1, :] = total[row : row + 1, at - half * width : at - half * width + size]
 
-    return run("sum_small", body, [((layers, size), F32) for size in sizes], pieces)
+    return run("sum_small", body, [((layers, size), F32) for size in sizes], [*first, *second])
 
 
 def take_if(here, a, b, rows):
@@ -850,7 +914,9 @@
     n_p = net.n_p
     rows = up[0].shape[0]
     cw, fw = D // n_p, FF // n_p
-    n_in = 3 + 2 * n_p
+    split = isinstance(qkv[0], tuple)
+    flat = [v for pair in qkv for v in pair] if split else list(qkv)
+    n_in = 3 + n_p + len(flat)
     skip = 0 if before is None else 4
     steps = min(4, rows // 16)
     part = rows // steps
@@ -869,13 +935,14 @@
             up_out[0, :, tile(p ^ j, fw)] = ups[j][...].astype(F32)
             for i in range(3):
                 to = tile(i * n_p + (p ^ j), cw)
-                qkv_out[0, :, to] = qkvs[j][:, i * cw : (i + 1) * cw].astype(F32)
+                ref, at = (qkvs[2 * j + i // 2], i % 2) if split else (qkvs[j], i)
+                qkv_out[0, :, to] = ref[:, at * cw : (at + 1) * cw].astype(F32)
 
     def of_rows(v, size):
         return pl.BlockSpec((size, v.shape[1]), lambda i: (i, 0))
 
-    ins = [*down, proj, *up, *qkv]
-    specs = [IN_SMEM] + [of_rows(v, down_part) for v in down] + [of_rows(v, part) for v in [proj, *up, *qkv]]
+    ins = [*down, proj, *up, *flat]
+    specs = [IN_SMEM] + [of_rows(v, down_part) for v in down] + [of_rows(v, part) for v in [proj, *up, *flat]]
     aliases = {}
     if before is not None:
         aliases = {1 + n_in + k: k for k in range(4)}
@@ -921,22 +988,29 @@
     rows = tokens.shape[1]
     pair_groups = [[2 * i, 2 * i + 1] for i in range(n_p)]
 
+    def fetch(weight, layer, groups):
+        pieces = cut_columns(net, weight, layer, groups)
+        return stack_halves([net.chip(v, j) for j, v in enumerate(pieces, 1)])
+
+    def complete(mine, theirs, weight, groups, more, layer):
+        own, rest = stack_rows(net, mine, theirs, weight, groups, more, layer)
+        return (own, net.core(own)), (rest, net.core(rest))
+
     def swap_cores(both):
         return lax.all_to_all(both, "fsdp", 0, 0, axis_index_groups=pair_groups)
 
     small_in = [first_gain, first_shift, qv_bias, proj_bias, second_gain, second_shift, up_bias, down_bias]
     sizes = [v.shape[1] for v in small_in]
-    tok = net.to_planes(pack_tokens(tokens, scene_ids, token_kind))
+    tok = net.to_place(pack_tokens(tokens, scene_ids, token_kind))
+    qkv_half = fetch(qkv_weight, 0, 3)
     small = pack_small(small_in)
-    small = [small, net.core(small)]
-    qkv_got = net.exchange(cut_columns(net, qkv_weight, 0, 3, small))
-    tok, qkv_got, later = fence((tok, qkv_got, (proj_weight, up_weight, down_weight, out_grad)))
-    proj_weight, up_weight, down_weight, out_grad = later
-    tokg = net.gather(tok)
-    qkv_own, proj_own = stack_rows(net, qkv_got, proj_weight, 0)
-    qkv_w, proj_w = (qkv_own, net.core(qkv_own)), (proj_own, net.core(proj_own))
-    vectors = join_vectors(net, layers, qkv_got, sizes)
-    gain1, shift1, qv_b, proj_b, gain2, shift2, up_b, down_b = vectors
+    small_other = net.core(small)
+    later = (qkv_weight, proj_weight, up_weight, down_weight, out_grad)
+    tok, qkv_half, small, small_other, later = fence((tok, qkv_half, small, small_other, later))
+    qkv_weight, proj_weight, up_weight, down_weight, out_grad = later
+    tokg = net.gather(put_small(tok, small, small_other))
+    qkv_next = net.next_plane(qkv_half)
+    tokg, qkv_half, qkv_next = fence((tokg, qkv_half, qkv_next))
 
     weights = []
     kept = []
@@ -946,21 +1020,24 @@
     for layer in range(layers):
         last = layer == layers - 1
         a1g = tokg if layer == 0 else net.gather(a1)
+        qkv_w, proj_w = complete(qkv_half, qkv_next, qkv_weight, 3, proj_weight, layer)
         a1g, qkv_w, proj_w, up_weight = fence((a1g, qkv_w, proj_w, up_weight))
         if layer == 0:
             tokg = a1g
             hidden = tokg[0]
+            vectors = join_vectors(net, layers, tokg, sizes, rows)
+            gain1, shift1, qv_b, proj_b, gain2, shift2, up_b, down_b = vectors
         norm = (gain1, shift1) if layer == 0 else None
         y, qkv, og, codes, a1g = attend(net, layer, rows, a1g, norm, qkv_w, qv_b, codes, proj_w)
-        up_got = net.exchange(cut_columns(net, up_weight, layer, 1, []))
-        y, up_got, down_weight = fence((y, up_got, down_weight))
+        up_half = fetch(up_weight, layer, 1)
+        y, up_half, down_weight = fence((y, up_half, down_weight))
         parts = net.exchange(y)
-        up_own, down_own = stack_rows(net, up_got, down_weight, layer)
-        up_w, down_w = (up_own, net.core(up_own)), (down_own, net.core(down_own))
-        parts, up_w, down_w = fence((parts, up_w, down_w))
+        up_next = net.next_plane(up_half)
+        parts, up_next = fence((parts, up_next))
         h2, a2 = add_and_norm(net, layer, hidden, parts, proj_b, (layer, gain2, shift2))
         a2g = net.gather(a2)
-        a2g, qkv_weight, out_grad = fence((a2g, qkv_weight, out_grad))
+        up_w, down_w = complete(up_half, up_next, up_weight, 1, down_weight, layer)
+        a2g, up_w, down_w, qkv_weight, out_grad = fence((a2g, up_w, down_w, qkv_weight, out_grad))
         y, z, slope = feed_forward(net, layer, a2g, up_w, up_b, down_w)
         kept.append((hidden, a1g, qkv, og, h2, a2g, z, slope))
         weights.append((qkv_w, proj_w, up_w, down_w))
@@ -968,14 +1045,15 @@
             dmg = net.gather(dm)
             last_y, z, slope, dmg = fence((y, z, slope, dmg))
             break
-        qkv_got = net.exchange(cut_columns(net, qkv_weight, layer + 1, 3, []))
+        qkv_half = fetch(qkv_weight, layer + 1, 3)
         if layer == layers - 2:
-            dm = net.to_planes(out_grad[0])
-        y, qkv_got, proj_weight, dm = fence((y, qkv_got, proj_weight, dm))
+            dm = net.to_chip(out_grad[0])
+        y, qkv_half, proj_weight, dm = fence((y, qkv_half, proj_weight, dm))
         parts = net.exchange(y)
-        qkv_own, proj_own = stack_rows(net, qkv_got, proj_weight, layer + 1)
-        qkv_w, proj_w = (qkv_own, net.core(qkv_own)), (proj_own, net.core(proj_own))
-        parts, qkv_w, proj_w = fence((parts, qkv_w, proj_w))
+        qkv_next = net.next_plane(qkv_half)
+        if layer == layers - 2:
+            dm = net.to_plane(dm)
+        parts, qkv_next, dm = fence((parts, qkv_next, dm))
         hidden, a1 = add_and_norm(net, layer, h2, parts, down_b, (layer + 1, gain1, shift1))
 
     flow = Flow(net)
@@ -995,11 +1073,7 @@
         keep, send = down_weight_grad(net, z, dmg)
         da2, du, up_b_grad = feed_back(net, dmg, down_w, slope, up_w)
         send = net.core(send)
-        if layer == layers - 2:
-            sent_out = net.from_planes(sent_out)
-            da2, du, keep, send, sent_out = fence((da2, du, keep, send, sent_out))
-        else:
-            da2, du, keep, send = fence((da2, du, keep, send))
+        da2, du, keep, send = fence((da2, du, keep, send))
         down_g = chunks(add_halves(keep, send))
         da2 = flow.collect(da2, down_g[0])
         parts = net.exchange(da2)
@@ -1016,8 +1090,7 @@
             da1, dqkv, last_parts = flow.collect((da1, dqkv, last_parts), up_g[1])
             (sent_out,) = add_and_norm(net, layer, h2, last_parts, down_b, None)
         else:
-            up_pieces = net.exchange(cut_rows(net, *[c.value for c in sums[layer + 1][1]], None))
-            da1, dqkv, up_pieces = flow.collect((da1, dqkv, up_pieces), up_g[1])
+            da1, dqkv = flow.collect((da1, dqkv), up_g[1])
         parts = net.exchange(da1)
         names = [None, None, "heads", None, None, None, "chip", None]
         of_layer = [None, None, qkv_b_grad, sums2[2:3], sums2[0:1], sums2[1:2], up_b_grad, down_b_grad]
@@ -1040,31 +1113,35 @@
             down_b_grad = sums1[2:3]
             dmg, grad = flow.collect((dmg, grad), attend_g[1])
 
-    input_grad = net.from_planes(dm)
-    input_grad = flow.collect(input_grad, attend_g[1])
-    flow.collect(())
+    def to_owners(chunks, extra):
+        *pieces, rest = [*cut_rows(net, *[c.value for c in chunks], extra), None][: n_p + 1]
+        return net.exchange(pieces), rest
+
+    up_pieces, _ = to_owners(sums[1][1], None)
+    dm, up_pieces = flow.collect((dm, up_pieces), attend_g[1])
+    qkv_pieces, proj_g = to_owners(sums[1][2], 0)
+    dm, sent_out, qkv_pieces, proj_g = flow.collect((dm, sent_out, qkv_pieces, proj_g))
+    both_out = jnp.concatenate([dm, sent_out], axis=0)
     up_last = None
-    pieces = None
+    first_part = None
     while flow.queue:
         if up_last is None and not [c for c in flow.queue if c in sums[0][1]]:
-            up_last = net.exchange(cut_rows(net, *[c.value for c in sums[0][1]], None))
-            up_last = flow.collect(up_last)
-        elif up_last is not None and pieces is None:
-            *pieces, proj_g = cut_rows(net, *[c.value for c in sums[1][2]], 0)
-            pieces = net.exchange(pieces)
-            pieces, proj_g = flow.collect((pieces, proj_g))
+            up_last, _ = to_owners(sums[0][1], None)
+            both_out, up_last = flow.collect((both_out, up_last))
+        elif up_last is not None and first_part is None and attend_g[0] not in flow.queue:
+            first_part = net.exchange(cut_part(net, attend_g[0].value, 2))
+            both_out = net.from_plane(both_out)
+            both_out, first_part = flow.collect((both_out, first_part))
         else:
-            flow.collect(())
-    if pieces is None:
-        *pieces, proj_g = cut_rows(net, *[c.value for c in sums[1][2]], 0)
-        pieces = net.exchange(pieces)
-    out = write_layer(net, 1, layers, None, [c.value for c in sums[1][0]], proj_g, up_pieces, pieces)
-    if up_last is None:
-        up_last = net.exchange(cut_rows(net, *[c.value for c in sums[0][1]], None))
-    *pieces, proj_g = cut_rows(net, *[c.value for c in sums[0][2]], 16)
-    pieces = net.exchange(pieces)
-    small_out = sum_small(layers, pieces, sizes, D // net.n_f)
-    out = write_layer(net, 0, layers, out, [c.value for c in sums[0][0]], proj_g, up_last, pieces)
+            both_out = flow.collect(both_out)
+    both_out = net.from_chip(both_out).astype(F32)
+    input_grad, sent_out = both_out[:rows], both_out[rows:]
+    *pieces, proj_last = cut_part(net, attend_g[1].value, 1, 16)
+    second_part = net.exchange(pieces)
+    out = write_layer(net, 1, layers, None, [c.value for c in sums[1][0]], proj_g, up_pieces, qkv_pieces)
+    small_out = sum_small(layers, first_part, second_part, sizes, D // net.n_f)
+    qkv_pieces = list(zip(first_part, second_part))
+    out = write_layer(net, 0, layers, out, [c.value for c in sums[0][0]], proj_last, up_last, qkv_pieces)
     return (
         sent_out.astype(F32)[None],
         input_grad.astype(F32)[None],

time: 501 us -> 488 us (0.974)
  waiting for transfers between devices: 201 us -> 180 us
  starting transfers between devices: 150 us -> 161 us
    ppermute x4 -> x9, starting transfers between devices: 10.2 us -> 25.2 us  [the longest x5 16.4 us: send(): return lax.ppermute(v, ('seq', 'fsdp'), pairs)]
    ppermute x4 -> x9, waiting for transfers between devices: 19.6 us -> 9.38 us  [the longest x5 9.37 us: send(): return lax.ppermute(v, ('seq', 'fsdp'), pairs)]
    ppermute x26, waiting for transfers between devices: 18.7 us -> 9.5 us  [start(): lax.ppermute(v, 'seq', m[3])]
    ppermute x26, starting transfers between devices: 50.6 us -> 44 us  [start(): lax.ppermute(v, 'seq', m[3])]
    pallas_call x68 -> x74, Pallas kernels: 96.5 us -> 100 us  [run(): pl.pallas_call(body, out_shape=[jax.ShapeDtypeStruct(shape, dtype) for sh...]
    ppermute x72 -> x75, starting transfers between devices: 87.9 us -> 89.4 us  [chip(): return lax.ppermute(v, 'fsdp', xor_pairs(self.n_f, 2 * j))]
    ppermute x72 -> x75, waiting for transfers between devices: 160 us -> 159 us  [chip(): return lax.ppermute(v, 'fsdp', xor_pairs(self.n_f, 2 * j))]
  transfers between devices with their start and end apart: 113 -> 121, of which waited for: 44 -> 43; matrix products, arithmetic and copies ran while one was open for 1% -> 0% of each run, Pallas kernels for 15% -> 18%
where the time goes in v4:
time: 488 us; the launch traced here: 480 us
  waiting for transfers between devices  180 us (37%)
  starting transfers between devices  161 us (33%)
  Pallas kernels  107 us (22%)
  blocking collectives  21.9 us (4%)
  local copies, waits for them, and re-layouts  5.16 us (1%)
    ppermute x75, waiting for transfers between devices, chip(): return lax.ppermute(v, 'fsdp', xor_pairs(self.n_f, 2 * j))  159 us
    pallas_call x74, Pallas kernels, run(): pl.pallas_call(body, out_shape=[jax.ShapeDtypeStruct(shape, dtype) for sh...  100 us
    ppermute x75, starting transfers between devices, chip(): return lax.ppermute(v, 'fsdp', xor_pairs(self.n_f, 2 * j))  89.4 us
    ppermute x26, starting transfers between devices, start(): lax.ppermute(v, 'seq', m[3])  44 us
    all_to_all x4, blocking collectives, swap_cores(): return lax.all_to_all(both, 'fsdp', 0, 0, axis_index_groups=pair_groups)  21.9 us
    ppermute x5, starting transfers between devices, send(): return lax.ppermute(v, ('seq', 'fsdp'), pairs)  16.4 us
  transfers between devices with their start and end apart: 121, of which 43 were waited for; matrix products, arithmetic and copies ran while one was open for 0% of the time, Pallas kernels for 18%

profile of v4, /device:TPU:10, one launch (start us, length us, event | category | flops | bytes accessed | tf_op | source)
XLA Modules:
  0.0 480.0 jit_solution(2597423781007313510)
XLA Ops:
  2.5 3.4 collective-permute-start
  12.4 8.2 %collective-permute-done.1.refs_0_ = bf16[64,768]{1,0:T(8,128)(2,1)S(1)} collective-permute-done((bf16[64,768]{1,0:T(8,128)(2,1)S(1)}, bf16[64,768]{1,0:T(8,128)(2,1)S(1)}, u32[]{:S(2)}, u32[]{:S(2)}) %collective-permute-start.1) | collective-permute-done | bytes 98336 | tf_op jit(solution)/shard_map/ppermute | solution.py:64
  27.0 3.3 collective-permute-start.8
  30.3 2.8 collective-permute-done.5.refs_1_.refs_12_
  33.2 7.1 %collective-permute-done.6.refs_2_.refs_13_ = bf16[144,1024]{1,0:T(8,128)(2,1)S(1)} collective-permute-done((bf16[144,1024]{1,0:T(8,128)(2,1)S(1)}, bf16[144,1024]{1,0:T(8,128)(2,1)S(1)}, u32[]{:S(2)}, u32[]{:S(2)}) %collective-permute-start.6) | collective-permute-done | bytes 294944 | tf_op jit(solution)/shard_map/ppermute | solution.py:64
  49.4 6.0 %attend.2 = (s32[1,512]{1,0:T(1,128)S(1)}, s32[512,1]{1,0:T(8,128)S(1)}, bf16[512,1024]{1,0:T(8,128)(2,1)S(1)}, bf16[128,1024]{1,0:T(8,128)(2,1)S(1)}, bf16[128,...) custom-call(s32[3]{0:T(128)S(1)} %pad_add_fusion.2.place, ...), custom_call_target="tpu_custom_call" | custom-call | flops 1073741824 | bytes 3309580 | tf_op jit(solution)/shard_map/attend/pallas_call | solution.py:99
  56.1 3.3 collective-permute-start.17
  62.9 5.8 %collective-permute-done.14.refs_2_ = bf16[128,1024]{1,0:T(8,128)(2,1)S(1)} collective-permute-done((bf16[128,1024]{1,0:T(8,128)(2,1)S(1)}, bf16[128,1024]{1,0:T(8,128)(2,1)S(1)}, u32[]{:S(2)}, u32[]{:S(2)}) %collective-permute-start.14) | collective-permute-done | bytes 262176 | tf_op jit(solution)/shard_map/ppermute | solution.py:64
  68.7 3.9 collective-permute-done.15.refs_3_
  79.4 5.7 %collective-permute-done.18.refs_1_ = bf16[128,1024]{1,0:T(8,128)(2,1)S(1)} collective-permute-done((bf16[128,1024]{1,0:T(8,128)(2,1)S(1)}, bf16[128,1024]{1,0:T(8,128)(2,1)S(1)}, u32[]{:S(2)}, u32[]{:S(2)}) %collective-permute-start.18) | collective-permute-done | bytes 262176 | tf_op jit(solution)/shard_map/ppermute | solution.py:64
  85.1 4.1 collective-permute-done.19.refs_2_
  91.1 2.6 collective-permute-start.26
  97.9 4.1 feed_forward.2
  108.7 5.2 %collective-permute-start.31 = (bf16[128,1024]{1,0:T(8,128)(2,1)S(1)}, bf16[128,1024]{1,0:T(8,128)(2,1)S(1)}, u32[]{:S(2)}, u32[]{:S(2)}) collective-permute-start(bf16[128,1024]{1,0:T(8,128)(2,1)S(1)} %collective-permute-done.26), channel_id=1, source_target_pairs={{0,0},{1,1},{2,10},{3,11},{4,20},{5,21},{6,30},{7,31},{8,16},{9,17... | collective-permute-start | bytes 786440 | tf_op jit(solution)/shard_map/ppermute | solution.py:43
  114.4 3.0 collective-permute-done.28.refs_3_
  124.0 5.6 %collective-permute-done.32.refs_1_ = bf16[128,1024]{1,0:T(8,128)(2,1)S(1)} collective-permute-done((bf16[128,1024]{1,0:T(8,128)(2,1)S(1)}, bf16[128,1024]{1,0:T(8,128)(2,1)S(1)}, u32[]{:S(2)}, u32[]{:S(2)}) %collective-permute-start.32) | collective-permute-done | bytes 262176 | tf_op jit(solution)/shard_map/ppermute | solution.py:64
  129.6 6.1 %collective-permute-done.33.refs_2_ = bf16[128,1024]{1,0:T(8,128)(2,1)S(1)} collective-permute-done((bf16[128,1024]{1,0:T(8,128)(2,1)S(1)}, bf16[128,1024]{1,0:T(8,128)(2,1)S(1)}, u32[]{:S(2)}, u32[]{:S(2)}) %collective-permute-start.33) | collective-permute-done | bytes 262176 | tf_op jit(solution)/shard_map/ppermute | solution.py:64
  140.0 5.4 %attend.3 = (bf16[128,1024]{1,0:T(8,128)(2,1)S(1)}, bf16[128,1024]{1,0:T(8,128)(2,1)S(1)}, bf16[128,1024]{1,0:T(8,128)(2,1)S(1)}, bf16[128,1024]{1,0:T(8,128)(2,...) custom-call(s32[3]{0:T(128)S(1)} %pad_add_fusion.2.place, ...), custom_call_target="tpu_custom_call" | custom-call | flops 1073741824 | bytes 3166220 | tf_op jit(solution)/shard_map/attend/pallas_call | solution.py:99
  151.7 5.8 %collective-permute-done.40.refs_2_ = bf16[128,1024]{1,0:T(8,128)(2,1)S(1)} collective-permute-done((bf16[128,1024]{1,0:T(8,128)(2,1)S(1)}, bf16[128,1024]{1,0:T(8,128)(2,1)S(1)}, u32[]{:S(2)}, u32[]{:S(2)}) %collective-permute-start.40) | collective-permute-done | bytes 262176 | tf_op jit(solution)/shard_map/ppermute | solution.py:64
  157.4 4.3 collective-permute-done.41.refs_3_
  168.5 5.7 %collective-permute-done.44.refs_1_ = bf16[128,1024]{1,0:T(8,128)(2,1)S(1)} collective-permute-done((bf16[128,1024]{1,0:T(8,128)(2,1)S(1)}, bf16[128,1024]{1,0:T(8,128)(2,1)S(1)}, u32[]{:S(2)}, u32[]{:S(2)}) %collective-permute-start.44) | collective-permute-done | bytes 262176 | tf_op jit(solution)/shard_map/ppermute | solution.py:64
  174.7 4.6 collective-permute-done.45.refs_2_
  182.1 4.1 feed_forward.3
  187.0 4.4 collective-permute-done.50.refs_2_
  193.3 5.4 %feed_back.2 = (bf16[128,1024]{1,0:T(8,128)(2,1)S(1)}, bf16[128,1024]{1,0:T(8,128)(2,1)S(1)}, bf16[128,1024]{1,0:T(8,128)(2,1)S(1)}, bf16[128,1024]{1,0:T(8,128)...) custom-call(s32[3]{0:T(128)S(1)} %pad_add_fusion.2.place, ...), custom_call_target="tpu_custom_call" | custom-call | flops 2147483648 | bytes 7340044 | tf_op jit(solution)/shard_map/feed_back/pallas_call | solution.py:99
  206.6 5.4 %all_to_all.20.ref = bf16[2,512,1024]{2,1,0:T(8,128)(2,1)S(1)} all-to-all(bf16[2,512,1024]{2,1,0:T(8,128)(2,1)S(1)} %up_weight_grad.2), channel_id=1, replica_groups={{0,1},{2,3},{4,5},{6,7},{8,9},{10,11},{12,13},{14,15},{16,17},{18,19},{..., dimensions={0} | all-to-all | bytes 4194304 | tf_op jit(solution)/shard_map/all_to_all | solution.py:1000
  212.0 4.6 collective-permute-done.54.refs_2_
  218.8 3.0 collective-permute-start.61
  228.4 5.7 %collective-permute-done.57.refs_1_.refs_7_ = bf16[128,1024]{1,0:T(8,128)(2,1)} collective-permute-done((bf16[128,1024]{1,0:T(8,128)(2,1)}, bf16[128,1024]{1,0:T(8,128)(2,1)}, u32[]{:S(2)}, u32[]{:S(2)}) %collective-permute-start.57) | collective-permute-done | bytes 262176 | tf_op jit(solution)/shard_map/ppermute | solution.py:64
  234.1 5.2 %collective-permute-done.58.refs_2_.refs_8_ = bf16[128,1024]{1,0:T(8,128)(2,1)} collective-permute-done((bf16[128,1024]{1,0:T(8,128)(2,1)}, bf16[128,1024]{1,0:T(8,128)(2,1)}, u32[]{:S(2)}, u32[]{:S(2)}) %collective-permute-start.58) | collective-permute-done | bytes 262176 | tf_op jit(solution)/shard_map/ppermute | solution.py:64
  242.1 3.8 collective-permute-start.66
  249.5 9.6 %attend_back.2 = (bf16[128,1024]{1,0:T(8,128)(2,1)S(1)}, bf16[128,1024]{1,0:T(8,128)(2,1)S(1)}, bf16[128,1024]{1,0:T(8,128)(2,1)S(1)}, bf16[128,1024]{1,0:T(8,12...) custom-call(s32[3]{0:T(128)S(1)} %pad_add_fusion.2.place, ...), custom_call_target="tpu_custom_call" | custom-call | flops 2147483648 | bytes 3936268 | tf_op jit(solution)/shard_map/attend_back/pallas_call | solution.py:99
  265.8 2.6 attend_weight_grad.2
  268.4 5.4 %all_to_all.21.ref = bf16[2,512,1024]{2,1,0:T(8,128)(2,1)S(1)} all-to-all(bf16[2,512,1024]{2,1,0:T(8,128)(2,1)S(1)} %attend_weight_grad.2), channel_id=1, replica_groups={{0,1},{2,3},{4,5},{6,7},{8,9},{10,11},{12,13},{14,15},{16,17},{18,19},{..., dimensions={0} | all-to-all | bytes 4194304 | tf_op jit(solution)/shard_map/all_to_all | solution.py:1000
  277.5 3.5 collective-permute-start.76
  284.5 5.7 %collective-permute-done.72.refs_1_ = bf16[128,1024]{1,0:T(8,128)(2,1)S(1)} collective-permute-done((bf16[128,1024]{1,0:T(8,128)(2,1)S(1)}, bf16[128,1024]{1,0:T(8,128)(2,1)S(1)}, u32[]{:S(2)}, u32[]{:S(2)}) %collective-permute-start.72) | collective-permute-done | bytes 262176 | tf_op jit(solution)/shard_map/ppermute | solution.py:64
  290.6 4.5 collective-permute-done.74.refs_3_
  298.0 2.6 collective-permute-start.79
  300.6 5.4 %feed_back.3 = (bf16[128,1024]{1,0:T(8,128)(2,1)S(1)}, bf16[128,1024]{1,0:T(8,128)(2,1)S(1)}, bf16[128,1024]{1,0:T(8,128)(2,1)S(1)}, bf16[128,1024]{1,0:T(8,128)...) custom-call(s32[3]{0:T(128)S(1)} %pad_add_fusion.2.place, ...), custom_call_target="tpu_custom_call" | custom-call | flops 2147483648 | bytes 7340044 | tf_op jit(solution)/shard_map/feed_back/pallas_call | solution.py:99
  306.3 5.9 %collective-permute-done.78.refs_4_.a_ref = bf16[512,512]{1,0:T(8,128)(2,1)S(1)} collective-permute-done((bf16[512,512]{1,0:T(8,128)(2,1)S(1)}, bf16[512,512]{1,0:T(8,128)(2,1)S(1)}, u32[]{:S(2)}, u32[]{:S(2)}) %collective-permute-start.78) | collective-permute-done | bytes 524320 | tf_op jit(solution)/shard_map/ppermute | solution.py:893
  322.9 5.4 %all_to_all.22.ref = bf16[2,512,1024]{2,1,0:T(8,128)(2,1)S(1)} all-to-all(bf16[2,512,1024]{2,1,0:T(8,128)(2,1)S(1)} %up_weight_grad.3), channel_id=1, replica_groups={{0,1},{2,3},{4,5},{6,7},{8,9},{10,11},{12,13},{14,15},{16,17},{18,19},{..., dimensions={0} | all-to-all | bytes 4194304 | tf_op jit(solution)/shard_map/all_to_all | solution.py:1000
  328.4 3.3 collective-permute-done.81.refs_2_
  333.0 3.2 collective-permute-start.89
  341.3 5.3 %collective-permute-done.85.refs_1_.refs_4_ = bf16[128,1024]{1,0:T(8,128)(2,1)S(1)} collective-permute-done((bf16[128,1024]{1,0:T(8,128)(2,1)S(1)}, bf16[128,1024]{1,0:T(8,128)(2,1)S(1)}, u32[]{:S(2)}, u32[]{:S(2)}) %collective-permute-start.85) | collective-permute-done | bytes 262176 | tf_op jit(solution)/shard_map/ppermute | solution.py:64
  346.6 3.4 collective-permute-done.86.refs_2_.refs_5_
  350.9 2.8 collective-permute-start.91
  353.9 9.2 %attend_back.3 = (bf16[128,1024]{1,0:T(8,128)(2,1)S(1)}, bf16[128,1024]{1,0:T(8,128)(2,1)S(1)}, bf16[128,1024]{1,0:T(8,128)(2,1)S(1)}, bf16[128,1024]{1,0:T(8,12...) custom-call(s32[3]{0:T(128)S(1)} %pad_add_fusion.2.place, ...), custom_call_target="tpu_custom_call" | custom-call | flops 2147483648 | bytes 5115916 | tf_op jit(solution)/shard_map/attend_back/pallas_call | solution.py:99
  364.1 3.3 collective-permute-start.96
  373.0 5.6 %all_to_all.23.ref = bf16[2,576,1024]{2,1,0:T(8,128)(2,1)S(1)} all-to-all(bf16[2,576,1024]{2,1,0:T(8,128)(2,1)S(1)} %attend_weight_grad.3), channel_id=1, replica_groups={{0,1},{2,3},{4,5},{6,7},{8,9},{10,11},{12,13},{14,15},{16,17},{18,19},{..., dimensions={0} | all-to-all | bytes 4718592 | tf_op jit(solution)/shard_map/all_to_all | solution.py:1000
  381.7 2.6 collective-permute-start.101
  388.6 5.7 %collective-permute-done.97.refs_4_ = bf16[128,1024]{1,0:T(8,128)(2,1)S(1)} collective-permute-done((bf16[128,1024]{1,0:T(8,128)(2,1)S(1)}, bf16[128,1024]{1,0:T(8,128)(2,1)S(1)}, u32[]{:S(2)}, u32[]{:S(2)}) %collective-permute-start.97) | collective-permute-done | bytes 262176 | tf_op jit(solution)/shard_map/ppermute | solution.py:64
  394.3 5.4 %collective-permute-done.98.refs_5_ = bf16[128,1024]{1,0:T(8,128)(2,1)S(1)} collective-permute-done((bf16[128,1024]{1,0:T(8,128)(2,1)S(1)}, bf16[128,1024]{1,0:T(8,128)(2,1)S(1)}, u32[]{:S(2)}, u32[]{:S(2)}) %collective-permute-start.98) | collective-permute-done | bytes 262176 | tf_op jit(solution)/shard_map/ppermute | solution.py:64
  400.6 3.4 collective-permute-start.106
  409.0 3.2 collective-permute-done.102.refs_8_
  412.2 2.8 collective-permute-done.103.refs_9_
  418.8 3.3 collective-permute-start.111
  426.4 5.0 %collective-permute-done.107.refs_4_ = bf16[128,1024]{1,0:T(8,128)(2,1)S(1)} collective-permute-done((bf16[128,1024]{1,0:T(8,128)(2,1)S(1)}, bf16[128,1024]{1,0:T(8,128)(2,1)S(1)}, u32[]{:S(2)}, u32[]{:S(2)}) %collective-permute-start.107) | collective-permute-done | bytes 262176 | tf_op jit(solution)/shard_map/ppermute | solution.py:64
  431.4 3.6 collective-permute-done.108.refs_5_
  444.3 3.2 collective-permute-done.114.refs_2_.refs_11_
  447.5 8.8 %collective-permute-done.112 = bf16[256,1024]{1,0:T(8,128)(2,1)S(1)} collective-permute-done((bf16[256,1024]{1,0:T(8,128)(2,1)S(1)}, bf16[256,1024]{1,0:T(8,128)(2,1)S(1)}, u32[]{:S(2)}, u32[]{:S(2)}) %collective-permute-start.112) | collective-permute-done | bytes 524320 | tf_op jit(solution)/shard_map/ppermute | solution.py:43
  456.3 3.3 collective-permute-start.117
  464.0 3.5 write_layer.2
  467.6 6.6 %collective-permute-done.119.refs_6_.refs_12_ = bf16[144,256]{1,0:T(8,128)(2,1)S(1)} collective-permute-done((bf16[144,256]{1,0:T(8,128)(2,1)S(1)}, bf16[144,256]{1,0:T(8,128)(2,1)S(1)}, u32[]{:S(2)}, u32[]{:S(2)}) %collective-permute-start.119) | collective-permute-done | bytes 73760 | tf_op jit(solution)/shard_map/ppermute | solution.py:64
  474.8 3.5 write_layer.3
  (450 shorter events, 178.4 us)
Async XLA Ops:
  2.5 20.5 %collective-permute-start = (bf16[144,1024]{1,0:T(8,128)(2,1)S(1)}, bf16[144,1024]{1,0:T(8,128)(2,1)S(1)}, u32[]{:S(2)}, u32[]{:S(2)}) collective-permute-start(bf16[144,1024]{1,0:T(8,128)(2,1)S(1)} %pad_add_fusion), channel_id=1, source_target_pairs={{0,0},{1,1},{2,10},{3,11},{4,20},{5,21},{6,30},{7,31},{12,16},{13,... | collective-permute-start | bytes 884744 | tf_op jit(solution)/shard_map/ppermute | solution.py:43
  8.1 12.4 %collective-permute-start.1 = (bf16[64,768]{1,0:T(8,128)(2,1)S(1)}, bf16[64,768]{1,0:T(8,128)(2,1)S(1)}, u32[]{:S(2)}, u32[]{:S(2)}) collective-permute-start(bf16[64,768]{1,0:T(8,128)(2,1)S(1)} %get-tuple-element.435), channel_id=1, source_target_pairs={{0,2},{1,3},{2,0},{3,1},{4,6},{5,7},{6,4},{7,5},{8,10},{9,11},{10,... | collective-permute-start | bytes 294920 | tf_op jit(solution)/shard_map/ppermute | solution.py:64
  25.3 15.0 %collective-permute-start.6 = (bf16[144,1024]{1,0:T(8,128)(2,1)S(1)}, bf16[144,1024]{1,0:T(8,128)(2,1)S(1)}, u32[]{:S(2)}, u32[]{:S(2)}) collective-permute-start(bf16[144,1024]{1,0:T(8,128)(2,1)S(1)} %put_small.1.refs_0_.refs_11_.hidden_ref), channel_id=1, source_target_pairs={{0,4},{1,5},{2,6},{3,7},{4,0},{5,1},{6,2},{7,3},{8,12},{9,13},{10,... | collective-permute-start | bytes 884744 | tf_op jit(solution)/shard_map/ppermute | solution.py:64
  27.0 13.2 %collective-permute-start.7 = (bf16[144,1024]{1,0:T(8,128)(2,1)S(1)}, bf16[144,1024]{1,0:T(8,128)(2,1)S(1)}, u32[]{:S(2)}, u32[]{:S(2)}) collective-permute-start(bf16[144,1024]{1,0:T(8,128)(2,1)S(1)} %put_small.1.refs_0_.refs_11_.hidden_ref), channel_id=1, source_target_pairs={{0,6},{1,7},{2,4},{3,5},{4,2},{5,3},{6,0},{7,1},{8,14},{9,15},{10,... | collective-permute-start | bytes 884744 | tf_op jit(solution)/shard_map/ppermute | solution.py:64
  27.0 13.2 %collective-permute-start.8 = (bf16[192,768]{1,0:T(8,128)(2,1)S(1)}, bf16[192,768]{1,0:T(8,128)(2,1)S(1)}, u32[]{:S(2)}, u32[]{:S(2)}) collective-permute-start(bf16[192,768]{1,0:T(8,128)(2,1)S(1)} %stack_halves.4.mine_ref), channel_id=1, source_target_pairs={{0,8},{8,0},{16,24},{24,16},{1,9},{9,1},{17,25},{25,17},{2,10},{10... | collective-permute-start | bytes 884744 | tf_op jit(solution)/shard_map/ppermute | solution.py:70
  56.1 16.5 %collective-permute-start.17 = (bf16[192,1024]{1,0:T(8,128)(2,1)S(1)}, bf16[192,1024]{1,0:T(8,128)(2,1)S(1)}, u32[]{:S(2)}, u32[]{:S(2)}) collective-permute-start(bf16[192,1024]{1,0:T(8,128)(2,1)S(1)} %stack_halves.5.mine_ref), channel_id=1, source_target_pairs={{0,8},{8,0},{16,24},{24,16},{1,9},{9,1},{17,25},{25,17},{2,10},{10... | collective-permute-start | bytes 1179656 | tf_op jit(solution)/shard_map/ppermute | solution.py:70
  60.0 12.6 %collective-permute-start.15 = (bf16[128,1024]{1,0:T(8,128)(2,1)S(1)}, bf16[128,1024]{1,0:T(8,128)(2,1)S(1)}, u32[]{:S(2)}, u32[]{:S(2)}) collective-permute-start(bf16[128,1024]{1,0:T(8,128)(2,1)S(1)} %get-tuple-element.475), channel_id=1, source_target_pairs={{0,4},{1,5},{2,6},{3,7},{4,0},{5,1},{6,2},{7,3},{8,12},{9,13},{10,... | collective-permute-start | bytes 786440 | tf_op jit(solution)/shard_map/ppermute | solution.py:64
  74.4 16.7 %collective-permute-start.21 = (bf16[512,1024]{1,0:T(8,128)(2,1)S(1)}, bf16[512,1024]{1,0:T(8,128)(2,1)S(1)}, u32[]{:S(2)}, u32[]{:S(2)}) collective-permute-start(bf16[512,1024]{1,0:T(8,128)(2,1)S(1)} %get-tuple-element.495.refs_4_.refs_7_), channel_id=1, source_target_pairs={{0,1},{1,0},{2,3},{3,2},{4,5},{5,4},{6,7},{7,6},{8,9},{9,8},{10,11... | collective-permute-start | bytes 3145736 | tf_op jit(solution)/shard_map/ppermute | solution.py:67
  74.4 16.6 %collective-permute-start.22 = (bf16[512,1024]{1,0:T(8,128)(2,1)S(1)}, bf16[512,1024]{1,0:T(8,128)(2,1)S(1)}, u32[]{:S(2)}, u32[]{:S(2)}) collective-permute-start(bf16[512,1024]{1,0:T(8,128)(2,1)S(1)} %get-tuple-element.498.refs_7_.refs_4_), channel_id=1, source_target_pairs={{0,1},{1,0},{2,3},{3,2},{4,5},{5,4},{6,7},{7,6},{8,9},{9,8},{10,11... | collective-permute-start | bytes 3145736 | tf_op jit(solution)/shard_map/ppermute | solution.py:67
  78.0 13.0 %collective-permute-start.20 = (bf16[128,1024]{1,0:T(8,128)(2,1)S(1)}, bf16[128,1024]{1,0:T(8,128)(2,1)S(1)}, u32[]{:S(2)}, u32[]{:S(2)}) collective-permute-start(bf16[128,1024]{1,0:T(8,128)(2,1)S(1)} %get-tuple-element.491.refs_0_), channel_id=1, source_target_pairs={{0,6},{1,7},{2,4},{3,5},{4,2},{5,3},{6,0},{7,1},{8,14},{9,15},{10,... | collective-permute-start | bytes 786440 | tf_op jit(solution)/shard_map/ppermute | solution.py:64
  91.1 14.0 %collective-permute-start.26 = (bf16[128,1024]{1,0:T(8,128)(2,1)S(1)}, bf16[128,1024]{1,0:T(8,128)(2,1)S(1)}, u32[]{:S(2)}, u32[]{:S(2)}) collective-permute-start(bf16[128,1024]{1,0:T(8,128)(2,1)S(1)} %bitcast.11), channel_id=1, source_target_pairs={{0,0},{1,1},{2,2},{3,3},{4,4},{5,5},{6,6},{7,7},{12,8},{13,9},{14,... | collective-permute-start | bytes 786440 | tf_op jit(solution)/shard_map/ppermute | solution.py:43
  105.0 12.9 %collective-permute-start.30 = (bf16[192,768]{1,0:T(8,128)(2,1)S(1)}, bf16[192,768]{1,0:T(8,128)(2,1)S(1)}, u32[]{:S(2)}, u32[]{:S(2)}) collective-permute-start(bf16[192,768]{1,0:T(8,128)(2,1)S(1)} %stack_halves.6.mine_ref), channel_id=1, source_target_pairs={{0,8},{8,0},{16,24},{24,16},{1,9},{9,1},{17,25},{25,17},{2,10},{10... | collective-permute-start | bytes 884744 | tf_op jit(solution)/shard_map/ppermute | solution.py:70
  119.5 16.3 %collective-permute-start.35 = (bf16[512,768]{1,0:T(8,128)(2,1)S(1)}, bf16[512,768]{1,0:T(8,128)(2,1)S(1)}, u32[]{:S(2)}, u32[]{:S(2)}) collective-permute-start(bf16[512,768]{1,0:T(8,128)(2,1)S(1)} %get-tuple-element.532.refs_5_.refs_9_), channel_id=1, source_target_pairs={{0,1},{1,0},{2,3},{3,2},{4,5},{5,4},{6,7},{7,6},{8,9},{9,8},{10,11... | collective-permute-start | bytes 2359304 | tf_op jit(solution)/shard_map/ppermute | solution.py:67
  121.7 14.0 %collective-permute-start.33 = (bf16[128,1024]{1,0:T(8,128)(2,1)S(1)}, bf16[128,1024]{1,0:T(8,128)(2,1)S(1)}, u32[]{:S(2)}, u32[]{:S(2)}) collective-permute-start(bf16[128,1024]{1,0:T(8,128)(2,1)S(1)} %get-tuple-element.528.refs_0_), channel_id=1, source_target_pairs={{0,4},{1,5},{2,6},{3,7},{4,0},{5,1},{6,2},{7,3},{8,12},{9,13},{10,... | collective-permute-start | bytes 786440 | tf_op jit(solution)/shard_map/ppermute | solution.py:64
  123.3 12.4 %collective-permute-start.34 = (bf16[128,1024]{1,0:T(8,128)(2,1)S(1)}, bf16[128,1024]{1,0:T(8,128)(2,1)S(1)}, u32[]{:S(2)}, u32[]{:S(2)}) collective-permute-start(bf16[128,1024]{1,0:T(8,128)(2,1)S(1)} %get-tuple-element.528.refs_0_), channel_id=1, source_target_pairs={{0,6},{1,7},{2,4},{3,5},{4,2},{5,3},{6,0},{7,1},{8,14},{9,15},{10,... | collective-permute-start | bytes 786440 | tf_op jit(solution)/shard_map/ppermute | solution.py:64
  146.1 15.6 %collective-permute-start.43 = (bf16[192,1024]{1,0:T(8,128)(2,1)S(1)}, bf16[192,1024]{1,0:T(8,128)(2,1)S(1)}, u32[]{:S(2)}, u32[]{:S(2)}) collective-permute-start(bf16[192,1024]{1,0:T(8,128)(2,1)S(1)} %stack_halves.7.mine_ref), channel_id=1, source_target_pairs={{0,8},{8,0},{16,24},{24,16},{1,9},{9,1},{17,25},{25,17},{2,10},{10... | collective-permute-start | bytes 1179656 | tf_op jit(solution)/shard_map/ppermute | solution.py:70
  149.7 12.0 %collective-permute-start.41 = (bf16[128,1024]{1,0:T(8,128)(2,1)S(1)}, bf16[128,1024]{1,0:T(8,128)(2,1)S(1)}, u32[]{:S(2)}, u32[]{:S(2)}) collective-permute-start(bf16[128,1024]{1,0:T(8,128)(2,1)S(1)} %get-tuple-element.548), channel_id=1, source_target_pairs={{0,4},{1,5},{2,6},{3,7},{4,0},{5,1},{6,2},{7,3},{8,12},{9,13},{10,... | collective-permute-start | bytes 786440 | tf_op jit(solution)/shard_map/ppermute | solution.py:64
  163.5 18.6 %collective-permute-start.47 = (bf16[512,1024]{1,0:T(8,128)(2,1)S(1)}, bf16[512,1024]{1,0:T(8,128)(2,1)S(1)}, u32[]{:S(2)}, u32[]{:S(2)}) collective-permute-start(bf16[512,1024]{1,0:T(8,128)(2,1)S(1)} %get-tuple-element.565.refs_4_.refs_7_), channel_id=1, source_target_pairs={{0,1},{1,0},{2,3},{3,2},{4,5},{5,4},{6,7},{7,6},{8,9},{9,8},{10,11... | collective-permute-start | bytes 3145736 | tf_op jit(solution)/shard_map/ppermute | solution.py:67
  163.5 18.6 %collective-permute-start.48 = (bf16[512,1024]{1,0:T(8,128)(2,1)S(1)}, bf16[512,1024]{1,0:T(8,128)(2,1)S(1)}, u32[]{:S(2)}, u32[]{:S(2)}) collective-permute-start(bf16[512,1024]{1,0:T(8,128)(2,1)S(1)} %get-tuple-element.567.refs_7_.refs_4_), channel_id=1, source_target_pairs={{0,1},{1,0},{2,3},{3,2},{4,5},{5,4},{6,7},{7,6},{8,9},{9,8},{10,11... | collective-permute-start | bytes 3145736 | tf_op jit(solution)/shard_map/ppermute | solution.py:67
  165.6 13.8 %collective-permute-start.45 = (bf16[128,1024]{1,0:T(8,128)(2,1)S(1)}, bf16[128,1024]{1,0:T(8,128)(2,1)S(1)}, u32[]{:S(2)}, u32[]{:S(2)}) collective-permute-start(bf16[128,1024]{1,0:T(8,128)(2,1)S(1)} %get-tuple-element.561.refs_0_), channel_id=1, source_target_pairs={{0,4},{1,5},{2,6},{3,7},{4,0},{5,1},{6,2},{7,3},{8,12},{9,13},{10,... | collective-permute-start | bytes 786440 | tf_op jit(solution)/shard_map/ppermute | solution.py:64
  166.9 12.9 %collective-permute-start.46 = (bf16[128,1024]{1,0:T(8,128)(2,1)S(1)}, bf16[128,1024]{1,0:T(8,128)(2,1)S(1)}, u32[]{:S(2)}, u32[]{:S(2)}) collective-permute-start(bf16[128,1024]{1,0:T(8,128)(2,1)S(1)} %get-tuple-element.561.refs_0_), channel_id=1, source_target_pairs={{0,6},{1,7},{2,4},{3,5},{4,2},{5,3},{6,0},{7,1},{8,14},{9,15},{10,... | collective-permute-start | bytes 786440 | tf_op jit(solution)/shard_map/ppermute | solution.py:64
  174.2 12.8 %collective-permute-start.49 = (bf16[128,1024]{1,0:T(8,128)(2,1)S(1)}, bf16[128,1024]{1,0:T(8,128)(2,1)S(1)}, u32[]{:S(2)}, u32[]{:S(2)}) collective-permute-start(bf16[128,1024]{1,0:T(8,128)(2,1)S(1)} %collective-permute-done.31.refs_0_.grad_ref.ref), channel_id=1, source_target_pairs={{0,2},{1,3},{2,0},{3,1},{4,6},{5,7},{6,4},{7,5},{8,10},{9,11},{10,... | collective-permute-start | bytes 786440 | tf_op jit(solution)/shard_map/ppermute | solution.py:64
  179.4 12.0 %collective-permute-start.50 = (bf16[128,1024]{1,0:T(8,128)(2,1)S(1)}, bf16[128,1024]{1,0:T(8,128)(2,1)S(1)}, u32[]{:S(2)}, u32[]{:S(2)}) collective-permute-start(bf16[128,1024]{1,0:T(8,128)(2,1)S(1)} %collective-permute-done.31.refs_0_.grad_ref.ref), channel_id=1, source_target_pairs={{0,4},{1,5},{2,6},{3,7},{4,0},{5,1},{6,2},{7,3},{8,12},{9,13},{10,... | collective-permute-start | bytes 786440 | tf_op jit(solution)/shard_map/ppermute | solution.py:64
  199.7 16.9 %collective-permute-start.56 = (bf16[512,512]{1,0:T(8,128)(2,1)S(1)}, bf16[512,512]{1,0:T(8,128)(2,1)S(1)}, u32[]{:S(2)}, u32[]{:S(2)}) collective-permute-start(bf16[512,512]{1,0:T(8,128)(2,1)S(1)} %get-tuple-element.599.refs_0_), channel_id=1, source_target_pairs={{0,8},{24,16},{1,9},{25,17},{2,10},{26,18},{3,11},{27,19},{4,12},{... | collective-permute-start | bytes 1572872 | tf_op jit(solution)/shard_map/ppermute | solution.py:893
  202.5 14.1 %collective-permute-start.54 = (bf16[128,1024]{1,0:T(8,128)(2,1)S(1)}, bf16[128,1024]{1,0:T(8,128)(2,1)S(1)}, u32[]{:S(2)}, u32[]{:S(2)}) collective-permute-start(bf16[128,1024]{1,0:T(8,128)(2,1)S(1)} %get-tuple-element.595), channel_id=1, source_target_pairs={{0,4},{1,5},{2,6},{3,7},{4,0},{5,1},{6,2},{7,3},{8,12},{9,13},{10,... | collective-permute-start | bytes 786440 | tf_op jit(solution)/shard_map/ppermute | solution.py:64
  202.5 14.1 %collective-permute-start.55 = (bf16[128,1024]{1,0:T(8,128)(2,1)S(1)}, bf16[128,1024]{1,0:T(8,128)(2,1)S(1)}, u32[]{:S(2)}, u32[]{:S(2)}) collective-permute-start(bf16[128,1024]{1,0:T(8,128)(2,1)S(1)} %get-tuple-element.596), channel_id=1, source_target_pairs={{0,6},{1,7},{2,4},{3,5},{4,2},{5,3},{6,0},{7,1},{8,14},{9,15},{10,... | collective-permute-start | bytes 786440 | tf_op jit(solution)/shard_map/ppermute | solution.py:64
  216.6 22.7 %collective-permute-start.60 = (bf16[512,512]{1,0:T(8,128)(2,1)}, bf16[512,512]{1,0:T(8,128)(2,1)}, u32[]{:S(2)}, u32[]{:S(2)}) collective-permute-start(bf16[512,512]{1,0:T(8,128)(2,1)} %get-tuple-element.608.refs_3_), channel_id=1, source_target_pairs={{0,8},{24,16},{1,9},{25,17},{2,10},{26,18},{3,11},{27,19},{4,12},{... | collective-permute-start | bytes 1572872 | tf_op jit(solution)/shard_map/ppermute | solution.py:893
  218.8 20.5 %collective-permute-start.61 = (bf16[512,512]{1,0:T(8,128)(2,1)}, bf16[512,512]{1,0:T(8,128)(2,1)}, u32[]{:S(2)}, u32[]{:S(2)}) collective-permute-start(bf16[512,512]{1,0:T(8,128)(2,1)} %turn.13.refs_1_), channel_id=1, source_target_pairs={{8,16},{16,8},{9,17},{17,9},{10,18},{18,10},{11,19},{19,11},{12,20... | collective-permute-start | bytes 1572872 | tf_op jit(solution)/shard_map/ppermute | solution.py:893
  226.0 13.3 %collective-permute-start.58 = (bf16[128,1024]{1,0:T(8,128)(2,1)}, bf16[128,1024]{1,0:T(8,128)(2,1)}, u32[]{:S(2)}, u32[]{:S(2)}) collective-permute-start(bf16[128,1024]{1,0:T(8,128)(2,1)} %get-tuple-element.610.refs_0_.refs_6_), channel_id=1, source_target_pairs={{0,4},{1,5},{2,6},{3,7},{4,0},{5,1},{6,2},{7,3},{8,12},{9,13},{10,... | collective-permute-start | bytes 786440 | tf_op jit(solution)/shard_map/ppermute | solution.py:64
  226.9 12.4 %collective-permute-start.59 = (bf16[128,1024]{1,0:T(8,128)(2,1)}, bf16[128,1024]{1,0:T(8,128)(2,1)}, u32[]{:S(2)}, u32[]{:S(2)}) collective-permute-start(bf16[128,1024]{1,0:T(8,128)(2,1)} %get-tuple-element.610.refs_0_.refs_6_), channel_id=1, source_target_pairs={{0,6},{1,7},{2,4},{3,5},{4,2},{5,3},{6,0},{7,1},{8,14},{9,15},{10,... | collective-permute-start | bytes 786440 | tf_op jit(solution)/shard_map/ppermute | solution.py:64
  241.1 18.2 %collective-permute-start.65 = (bf16[512,512]{1,0:T(8,128)(2,1)S(1)}, bf16[512,512]{1,0:T(8,128)(2,1)S(1)}, u32[]{:S(2)}, u32[]{:S(2)}) collective-permute-start(bf16[512,512]{1,0:T(8,128)(2,1)S(1)} %get-tuple-element.831.b_ref), channel_id=1, source_target_pairs={{0,8},{24,16},{8,0},{16,24},{1,9},{25,17},{9,1},{17,25},{2,10},{26... | collective-permute-start | bytes 1572872 | tf_op jit(solution)/shard_map/ppermute | solution.py:893
  242.1 17.2 %collective-permute-start.66 = (bf16[512,512]{1,0:T(8,128)(2,1)S(1)}, bf16[512,512]{1,0:T(8,128)(2,1)S(1)}, u32[]{:S(2)}, u32[]{:S(2)}) collective-permute-start(bf16[512,512]{1,0:T(8,128)(2,1)S(1)} %get-tuple-element.645.refs_1_), channel_id=1, source_target_pairs={{8,16},{16,8},{9,17},{17,9},{10,18},{18,10},{11,19},{19,11},{12,20... | collective-permute-start | bytes 1572872 | tf_op jit(solution)/shard_map/ppermute | solution.py:893
  245.9 13.3 %collective-permute-start.62 = (bf16[128,1024]{1,0:T(8,128)(2,1)S(1)}, bf16[128,1024]{1,0:T(8,128)(2,1)S(1)}, u32[]{:S(2)}, u32[]{:S(2)}) collective-permute-start(bf16[128,1024]{1,0:T(8,128)(2,1)S(1)} %copy-done.70), channel_id=1, source_target_pairs={{0,2},{1,3},{2,0},{3,1},{4,6},{5,7},{6,4},{7,5},{8,10},{9,11},{10,... | collective-permute-start | bytes 786440 | tf_op jit(solution)/shard_map/ppermute | solution.py:64
  246.6 12.6 %collective-permute-start.63 = (bf16[128,1024]{1,0:T(8,128)(2,1)S(1)}, bf16[128,1024]{1,0:T(8,128)(2,1)S(1)}, u32[]{:S(2)}, u32[]{:S(2)}) collective-permute-start(bf16[128,1024]{1,0:T(8,128)(2,1)S(1)} %copy-done.68), channel_id=1, source_target_pairs={{0,4},{1,5},{2,6},{3,7},{4,0},{5,1},{6,2},{7,3},{8,12},{9,13},{10,... | collective-permute-start | bytes 786440 | tf_op jit(solution)/shard_map/ppermute | solution.py:64
  260.1 15.9 %collective-permute-start.70 = (bf16[512,512]{1,0:T(8,128)(2,1)S(1)}, bf16[512,512]{1,0:T(8,128)(2,1)S(1)}, u32[]{:S(2)}, u32[]{:S(2)}) collective-permute-start(bf16[512,512]{1,0:T(8,128)(2,1)S(1)} %get-tuple-element.832.b_ref), channel_id=1, source_target_pairs={{0,8},{24,16},{8,0},{16,24},{1,9},{25,17},{9,1},{17,25},{2,10},{26... | collective-permute-start | bytes 1572872 | tf_op jit(solution)/shard_map/ppermute | solution.py:893
  260.2 15.8 %collective-permute-start.71 = (bf16[512,512]{1,0:T(8,128)(2,1)S(1)}, bf16[512,512]{1,0:T(8,128)(2,1)S(1)}, u32[]{:S(2)}, u32[]{:S(2)}) collective-permute-start(bf16[512,512]{1,0:T(8,128)(2,1)S(1)} %get-tuple-element.654.refs_1_), channel_id=1, source_target_pairs={{8,16},{16,8},{9,17},{17,9},{10,18},{18,10},{11,19},{19,11},{12,20... | collective-permute-start | bytes 1572872 | tf_op jit(solution)/shard_map/ppermute | solution.py:893
  276.8 18.2 %collective-permute-start.75 = (bf16[512,512]{1,0:T(8,128)(2,1)S(1)}, bf16[512,512]{1,0:T(8,128)(2,1)S(1)}, u32[]{:S(2)}, u32[]{:S(2)}) collective-permute-start(bf16[512,512]{1,0:T(8,128)(2,1)S(1)} %get-tuple-element.758.b_ref), channel_id=1, source_target_pairs={{0,8},{24,16},{8,0},{16,24},{1,9},{25,17},{9,1},{17,25},{2,10},{26... | collective-permute-start | bytes 1572872 | tf_op jit(solution)/shard_map/ppermute | solution.py:893
  277.5 17.6 %collective-permute-start.76 = (bf16[512,512]{1,0:T(8,128)(2,1)S(1)}, bf16[512,512]{1,0:T(8,128)(2,1)S(1)}, u32[]{:S(2)}, u32[]{:S(2)}) collective-permute-start(bf16[512,512]{1,0:T(8,128)(2,1)S(1)} %get-tuple-element.681.refs_1_), channel_id=1, source_target_pairs={{8,16},{16,8},{9,17},{17,9},{10,18},{18,10},{11,19},{19,11},{12,20... | collective-permute-start | bytes 1572872 | tf_op jit(solution)/shard_map/ppermute | solution.py:893
  283.0 12.0 %collective-permute-start.74 = (bf16[128,1024]{1,0:T(8,128)(2,1)S(1)}, bf16[128,1024]{1,0:T(8,128)(2,1)S(1)}, u32[]{:S(2)}, u32[]{:S(2)}) collective-permute-start(bf16[128,1024]{1,0:T(8,128)(2,1)S(1)} %get-tuple-element.660.refs_0_), channel_id=1, source_target_pairs={{0,6},{1,7},{2,4},{3,5},{4,2},{5,3},{6,0},{7,1},{8,14},{9,15},{10,... | collective-permute-start | bytes 786440 | tf_op jit(solution)/shard_map/ppermute | solution.py:64
  297.9 14.4 %collective-permute-start.78 = (bf16[512,512]{1,0:T(8,128)(2,1)S(1)}, bf16[512,512]{1,0:T(8,128)(2,1)S(1)}, u32[]{:S(2)}, u32[]{:S(2)}) collective-permute-start(bf16[512,512]{1,0:T(8,128)(2,1)S(1)} %get-tuple-element.759.b_ref), channel_id=1, source_target_pairs={{0,8},{24,16},{8,0},{16,24},{1,9},{25,17},{9,1},{17,25},{2,10},{26... | collective-permute-start | bytes 1572872 | tf_op jit(solution)/shard_map/ppermute | solution.py:893
  298.0 16.2 %collective-permute-start.79 = (bf16[512,512]{1,0:T(8,128)(2,1)S(1)}, bf16[512,512]{1,0:T(8,128)(2,1)S(1)}, u32[]{:S(2)}, u32[]{:S(2)}) collective-permute-start(bf16[512,512]{1,0:T(8,128)(2,1)S(1)} %get-tuple-element.693.refs_1_), channel_id=1, source_target_pairs={{8,16},{16,8},{9,17},{17,9},{10,18},{18,10},{11,19},{19,11},{12,20... | collective-permute-start | bytes 1572872 | tf_op jit(solution)/shard_map/ppermute | solution.py:893
  315.0 16.7 %collective-permute-start.83 = (bf16[512,512]{1,0:T(8,128)(2,1)S(1)}, bf16[512,512]{1,0:T(8,128)(2,1)S(1)}, u32[]{:S(2)}, u32[]{:S(2)}) collective-permute-start(bf16[512,512]{1,0:T(8,128)(2,1)S(1)} %get-tuple-element.776.b_ref), channel_id=1, source_target_pairs={{0,8},{24,16},{8,0},{16,24},{1,9},{25,17},{9,1},{17,25},{2,10},{26... | collective-permute-start | bytes 1572872 | tf_op jit(solution)/shard_map/ppermute | solution.py:893
  315.1 16.7 %collective-permute-start.84 = (bf16[512,512]{1,0:T(8,128)(2,1)S(1)}, bf16[512,512]{1,0:T(8,128)(2,1)S(1)}, u32[]{:S(2)}, u32[]{:S(2)}) collective-permute-start(bf16[512,512]{1,0:T(8,128)(2,1)S(1)} %get-tuple-element.707.refs_1_), channel_id=1, source_target_pairs={{8,16},{16,8},{9,17},{17,9},{10,18},{18,10},{11,19},{19,11},{12,20... | collective-permute-start | bytes 1572872 | tf_op jit(solution)/shard_map/ppermute | solution.py:893
  318.8 12.9 %collective-permute-start.81 = (bf16[128,1024]{1,0:T(8,128)(2,1)S(1)}, bf16[128,1024]{1,0:T(8,128)(2,1)S(1)}, u32[]{:S(2)}, u32[]{:S(2)}) collective-permute-start(bf16[128,1024]{1,0:T(8,128)(2,1)S(1)} %get-tuple-element.688), channel_id=1, source_target_pairs={{0,4},{1,5},{2,6},{3,7},{4,0},{5,1},{6,2},{7,3},{8,12},{9,13},{10,... | collective-permute-start | bytes 786440 | tf_op jit(solution)/shard_map/ppermute | solution.py:64
  319.7 12.0 %collective-permute-start.82 = (bf16[128,1024]{1,0:T(8,128)(2,1)S(1)}, bf16[128,1024]{1,0:T(8,128)(2,1)S(1)}, u32[]{:S(2)}, u32[]{:S(2)}) collective-permute-start(bf16[128,1024]{1,0:T(8,128)(2,1)S(1)} %get-tuple-element.689), channel_id=1, source_target_pairs={{0,6},{1,7},{2,4},{3,5},{4,2},{5,3},{6,0},{7,1},{8,14},{9,15},{10,... | collective-permute-start | bytes 786440 | tf_op jit(solution)/shard_map/ppermute | solution.py:64
  332.5 17.5 %collective-permute-start.88 = (bf16[512,512]{1,0:T(8,128)(2,1)S(1)}, bf16[512,512]{1,0:T(8,128)(2,1)S(1)}, u32[]{:S(2)}, u32[]{:S(2)}) collective-permute-start(bf16[512,512]{1,0:T(8,128)(2,1)S(1)} %get-tuple-element.777.b_ref), channel_id=1, source_target_pairs={{0,8},{24,16},{8,0},{16,24},{1,9},{25,17},{9,1},{17,25},{2,10},{26... | collective-permute-start | bytes 1572872 | tf_op jit(solution)/shard_map/ppermute | solution.py:893
  333.0 17.0 %collective-permute-start.89 = (bf16[512,512]{1,0:T(8,128)(2,1)S(1)}, bf16[512,512]{1,0:T(8,128)(2,1)S(1)}, u32[]{:S(2)}, u32[]{:S(2)}) collective-permute-start(bf16[512,512]{1,0:T(8,128)(2,1)S(1)} %get-tuple-element.724.refs_1_), channel_id=1, source_target_pairs={{8,16},{16,8},{9,17},{17,9},{10,18},{18,10},{11,19},{19,11},{12,20... | collective-permute-start | bytes 1572872 | tf_op jit(solution)/shard_map/ppermute | solution.py:893
  350.8 12.4 %collective-permute-start.90 = (bf16[512,512]{1,0:T(8,128)(2,1)S(1)}, bf16[512,512]{1,0:T(8,128)(2,1)S(1)}, u32[]{:S(2)}, u32[]{:S(2)}) collective-permute-start(bf16[512,512]{1,0:T(8,128)(2,1)S(1)} %get-tuple-element.824.b_ref), channel_id=1, source_target_pairs={{0,8},{24,16},{8,0},{16,24},{1,9},{25,17},{9,1},{17,25},{2,10},{26... | collective-permute-start | bytes 1572872 | tf_op jit(solution)/shard_map/ppermute | solution.py:893
  350.9 12.3 %collective-permute-start.91 = (bf16[512,512]{1,0:T(8,128)(2,1)S(1)}, bf16[512,512]{1,0:T(8,128)(2,1)S(1)}, u32[]{:S(2)}, u32[]{:S(2)}) collective-permute-start(bf16[512,512]{1,0:T(8,128)(2,1)S(1)} %get-tuple-element.752.refs_1_), channel_id=1, source_target_pairs={{8,16},{16,8},{9,17},{17,9},{10,18},{18,10},{11,19},{19,11},{12,20... | collective-permute-start | bytes 1572872 | tf_op jit(solution)/shard_map/ppermute | solution.py:893
  364.0 16.8 %collective-permute-start.95 = (bf16[512,512]{1,0:T(8,128)(2,1)S(1)}, bf16[512,512]{1,0:T(8,128)(2,1)S(1)}, u32[]{:S(2)}, u32[]{:S(2)}) collective-permute-start(bf16[512,512]{1,0:T(8,128)(2,1)S(1)} %get-tuple-element.825.b_ref), channel_id=1, source_target_pairs={{0,8},{24,16},{8,0},{16,24},{1,9},{25,17},{9,1},{17,25},{2,10},{26... | collective-permute-start | bytes 1572872 | tf_op jit(solution)/shard_map/ppermute | solution.py:893
  364.1 16.7 %collective-permute-start.96 = (bf16[512,512]{1,0:T(8,128)(2,1)S(1)}, bf16[512,512]{1,0:T(8,128)(2,1)S(1)}, u32[]{:S(2)}, u32[]{:S(2)}) collective-permute-start(bf16[512,512]{1,0:T(8,128)(2,1)S(1)} %get-tuple-element.766.refs_1_), channel_id=1, source_target_pairs={{8,16},{16,8},{9,17},{17,9},{10,18},{18,10},{11,19},{19,11},{12,20... | collective-permute-start | bytes 1572872 | tf_op jit(solution)/shard_map/ppermute | solution.py:893
  381.6 18.0 %collective-permute-start.100 = (bf16[576,512]{1,0:T(8,128)(2,1)S(1)}, bf16[576,512]{1,0:T(8,128)(2,1)S(1)}, u32[]{:S(2)}, u32[]{:S(2)}) collective-permute-start(bf16[576,512]{1,0:T(8,128)(2,1)S(1)} %get-tuple-element.791.b_ref), channel_id=1, source_target_pairs={{0,8},{24,16},{8,0},{16,24},{1,9},{25,17},{9,1},{17,25},{2,10},{26... | collective-permute-start | bytes 1769480 | tf_op jit(solution)/shard_map/ppermute | solution.py:893
  381.7 18.0 %collective-permute-start.101 = (bf16[512,512]{1,0:T(8,128)(2,1)S(1)}, bf16[512,512]{1,0:T(8,128)(2,1)S(1)}, u32[]{:S(2)}, u32[]{:S(2)}) collective-permute-start(bf16[512,512]{1,0:T(8,128)(2,1)S(1)} %get-tuple-element.784.refs_1_), channel_id=1, source_target_pairs={{8,16},{16,8},{9,17},{17,9},{10,18},{18,10},{11,19},{19,11},{12,20... | collective-permute-start | bytes 1572872 | tf_op jit(solution)/shard_map/ppermute | solution.py:893
  386.3 13.4 %collective-permute-start.98 = (bf16[128,1024]{1,0:T(8,128)(2,1)S(1)}, bf16[128,1024]{1,0:T(8,128)(2,1)S(1)}, u32[]{:S(2)}, u32[]{:S(2)}) collective-permute-start(bf16[128,1024]{1,0:T(8,128)(2,1)S(1)} %get-tuple-element.762), channel_id=1, source_target_pairs={{0,4},{1,5},{2,6},{3,7},{4,0},{5,1},{6,2},{7,3},{8,12},{9,13},{10,... | collective-permute-start | bytes 786440 | tf_op jit(solution)/shard_map/ppermute | solution.py:64
  387.6 12.1 %collective-permute-start.99 = (bf16[128,1024]{1,0:T(8,128)(2,1)S(1)}, bf16[128,1024]{1,0:T(8,128)(2,1)S(1)}, u32[]{:S(2)}, u32[]{:S(2)}) collective-permute-start(bf16[128,1024]{1,0:T(8,128)(2,1)S(1)} %get-tuple-element.763), channel_id=1, source_target_pairs={{0,6},{1,7},{2,4},{3,5},{4,2},{5,3},{6,0},{7,1},{8,14},{9,15},{10,... | collective-permute-start | bytes 786440 | tf_op jit(solution)/shard_map/ppermute | solution.py:64
  400.5 14.5 %collective-permute-start.105 = (bf16[576,512]{1,0:T(8,128)(2,1)S(1)}, bf16[576,512]{1,0:T(8,128)(2,1)S(1)}, u32[]{:S(2)}, u32[]{:S(2)}) collective-permute-start(bf16[576,512]{1,0:T(8,128)(2,1)S(1)} %get-tuple-element.793.b_ref), channel_id=1, source_target_pairs={{0,8},{24,16},{8,0},{16,24},{1,9},{25,17},{9,1},{17,25},{2,10},{26... | collective-permute-start | bytes 1769480 | tf_op jit(solution)/shard_map/ppermute | solution.py:893
  400.6 16.0 %collective-permute-start.106 = (bf16[576,512]{1,0:T(8,128)(2,1)S(1)}, bf16[576,512]{1,0:T(8,128)(2,1)S(1)}, u32[]{:S(2)}, u32[]{:S(2)}) collective-permute-start(bf16[576,512]{1,0:T(8,128)(2,1)S(1)} %get-tuple-element.798.refs_0_), channel_id=1, source_target_pairs={{8,16},{16,8},{9,17},{17,9},{10,18},{18,10},{11,19},{19,11},{12,20... | collective-permute-start | bytes 1769480 | tf_op jit(solution)/shard_map/ppermute | solution.py:893
  417.4 17.6 %collective-permute-start.110 = (bf16[576,512]{1,0:T(8,128)(2,1)S(1)}, bf16[576,512]{1,0:T(8,128)(2,1)S(1)}, u32[]{:S(2)}, u32[]{:S(2)}) collective-permute-start(bf16[576,512]{1,0:T(8,128)(2,1)S(1)} %get-tuple-element.804.b_ref), channel_id=1, source_target_pairs={{8,0},{16,24},{9,1},{17,25},{10,2},{18,26},{11,3},{19,27},{12,4},{... | collective-permute-start | bytes 1769480 | tf_op jit(solution)/shard_map/ppermute | solution.py:893
  418.8 16.3 %collective-permute-start.111 = (bf16[576,512]{1,0:T(8,128)(2,1)S(1)}, bf16[576,512]{1,0:T(8,128)(2,1)S(1)}, u32[]{:S(2)}, u32[]{:S(2)}) collective-permute-start(bf16[576,512]{1,0:T(8,128)(2,1)S(1)} %get-tuple-element.809.refs_0_), channel_id=1, source_target_pairs={{8,16},{16,8},{9,17},{17,9},{10,18},{18,10},{11,19},{19,11},{12,20... | collective-permute-start | bytes 1769480 | tf_op jit(solution)/shard_map/ppermute | solution.py:893
  435.2 21.1 %collective-permute-start.116 = (bf16[576,512]{1,0:T(8,128)(2,1)S(1)}, bf16[576,512]{1,0:T(8,128)(2,1)S(1)}, u32[]{:S(2)}, u32[]{:S(2)}) collective-permute-start(bf16[576,512]{1,0:T(8,128)(2,1)S(1)} %turn.25.b_ref), channel_id=1, source_target_pairs={{8,0},{16,24},{9,1},{17,25},{10,2},{18,26},{11,3},{19,27},{12,4},{... | collective-permute-start | bytes 1769480 | tf_op jit(solution)/shard_map/ppermute | solution.py:893
  436.5 19.8 %collective-permute-start.112 = (bf16[256,1024]{1,0:T(8,128)(2,1)S(1)}, bf16[256,1024]{1,0:T(8,128)(2,1)S(1)}, u32[]{:S(2)}, u32[]{:S(2)}) collective-permute-start(bf16[256,1024]{1,0:T(8,128)(2,1)S(1)} %pad_maximum_fusion), channel_id=1, source_target_pairs={{0,0},{1,1},{10,2},{11,3},{20,4},{21,5},{30,6},{31,7},{16,8},{17,9... | collective-permute-start | bytes 1572872 | tf_op jit(solution)/shard_map/ppermute | solution.py:43
  456.3 22.1 %collective-permute-start.117 = (bf16[256,1024]{1,0:T(8,128)(2,1)S(1)}, bf16[256,1024]{1,0:T(8,128)(2,1)S(1)}, u32[]{:S(2)}, u32[]{:S(2)}) collective-permute-start(bf16[256,1024]{1,0:T(8,128)(2,1)S(1)} %collective-permute-done.112), channel_id=1, source_target_pairs={{0,0},{1,1},{2,2},{3,3},{4,4},{5,5},{6,6},{7,7},{8,12},{9,13},{10,... | collective-permute-start | bytes 1572872 | tf_op jit(solution)/shard_map/ppermute | solution.py:43
  461.5 12.7 %collective-permute-start.119 = (bf16[144,256]{1,0:T(8,128)(2,1)S(1)}, bf16[144,256]{1,0:T(8,128)(2,1)S(1)}, u32[]{:S(2)}, u32[]{:S(2)}) collective-permute-start(bf16[144,256]{1,0:T(8,128)(2,1)S(1)} %get-tuple-element.820), channel_id=1, source_target_pairs={{0,4},{1,5},{2,6},{3,7},{4,0},{5,1},{6,2},{7,3},{8,12},{9,13},{10,... | collective-permute-start | bytes 221192 | tf_op jit(solution)/shard_map/ppermute | solution.py:64
  461.5 12.7 %collective-permute-start.120 = (bf16[144,256]{1,0:T(8,128)(2,1)S(1)}, bf16[144,256]{1,0:T(8,128)(2,1)S(1)}, u32[]{:S(2)}, u32[]{:S(2)}) collective-permute-start(bf16[144,256]{1,0:T(8,128)(2,1)S(1)} %get-tuple-element.821), channel_id=1, source_target_pairs={{0,6},{1,7},{2,4},{3,5},{4,2},{5,3},{6,0},{7,1},{8,14},{9,15},{10,... | collective-permute-start | bytes 221192 | tf_op jit(solution)/shard_map/ppermute | solution.py:64
  (147 other events, 2049.6 us)

commit v5 on v4

--- a/solution.py
+++ b/solution.py
@@ -153,26 +153,35 @@
     return jnp.concatenate(out, axis=1)
 
 
-def cut_columns(net, weight, layer, groups):
+def columns_of(net, weight, groups):
+    return weight.shape[2] // (groups * net.n_p) if groups else weight.shape[2]
+
+
+def cut_columns(net, layer, weights):
     n_p = net.n_p
-    rows = weight.shape[1] // 2
-    width = weight.shape[2] // (groups * n_p)
-
-    def body(place, weight_ref, *refs):
+    rows = weights[0][0].shape[1] // 2
+    widths = [columns_of(net, w, groups) for w, groups in weights]
+    count = sum(groups or 1 for _, groups in weights)
+    total = sum(width * (groups or 1) for width, (_, groups) in zip(widths, weights))
+
+    def body(place, *refs):
         p, half = place[0], place[2]
-        outs, sems = refs[: n_p - 1], refs[-1]
+        outs, sems = refs[len(weights) : -1], refs[-1]
         pairs = []
         for j in range(1, n_p):
-            for i in range(groups):
-                cols = tile(i * n_p + (p ^ j), width)
-                to = outs[j - 1].at[:, i * width : (i + 1) * width]
-                pairs.append((weight_ref.at[layer, tile(half, rows), cols], to))
+            at = 0
+            for ref, width, (_, groups) in zip(refs, widths, weights):
+                for i in range(groups or 1):
+                    cols = tile(i * n_p + (p ^ j), width) if groups else slice(0, width)
+                    pairs.append((ref.at[layer, tile(half, rows), cols], outs[j - 1].at[:, at : at + width]))
+                    at += width
         for copy in copy_all(pairs, sems):
             copy.wait()
 
-    outs = [((rows, groups * width), BF)] * (n_p - 1)
-    scratch = [pltpu.SemaphoreType.DMA((groups * (n_p - 1),))]
-    return run("cut_columns", body, outs, [weight], net.place, scratch, ins_at=[IN_HBM])
+    outs = [((rows, total), BF)] * (n_p - 1)
+    scratch = [pltpu.SemaphoreType.DMA((count * (n_p - 1),))]
+    ins = [w for w, _ in weights]
+    return run("cut_columns", body, outs, ins, net.place, scratch, ins_at=[IN_HBM] * len(ins))
 
 
 def stack_halves(pieces):
@@ -190,30 +199,37 @@
     return run("stack_halves", body, outs, pieces, None, scratch, ins_at=[IN_ANY] * count)[0]
 
 
-def stack_rows(net, mine, theirs, weight, groups, more, layer):
+def stack_rows(net, mine, theirs, parts, more, layer):
     n_p = net.n_p
-    half_rows = weight.shape[1] // 2
+    half_rows = parts[0][0].shape[1] // 2
     rows = 2 * half_rows
-    width = weight.shape[2] // (groups * n_p)
-
-    def body(place, mine_ref, their_ref, weight_ref, more_ref, own, rest, sems):
+    widths = [columns_of(net, w, groups) for w, groups, _ in parts]
+    count = len(more) + sum((groups or 1) + 2 * (n_p - 1) for _, groups, _ in parts)
+
+    def body(place, mine_ref, their_ref, *refs):
         p, half = place[0], place[2]
-        pairs = [(more_ref.at[layer], rest)]
-        for i in range(groups):
-            to = own.at[tile(p, rows), i * width : (i + 1) * width]
-            pairs.append((weight_ref.at[layer, :, tile(i * n_p + p, width)], to))
-        for j in range(1, n_p):
-            here = slice((j - 1) * half_rows, j * half_rows)
-            at = (p ^ j) * 2
-            pairs.append((mine_ref.at[here], own.at[tile(at + half, half_rows)]))
-            pairs.append((their_ref.at[here], own.at[tile(at + 1 - half, half_rows)]))
+        ins, outs, sems = refs[: len(parts) + len(more)], refs[len(parts) + len(more) : -1], refs[-1]
+        pairs = [(ref.at[layer], out) for ref, out in zip(ins[len(parts) :], outs[len(parts) :])]
+        for ref, own, width, (_, groups, first) in zip(ins, outs, widths, parts):
+            for i in range(groups or 1):
+                to = own.at[tile(p, rows), i * width : (i + 1) * width]
+                cols = tile(i * n_p + p, width) if groups else slice(0, width)
+                pairs.append((ref.at[layer, :, cols], to))
+            cols = slice(first, first + (groups or 1) * width)
+            for j in range(1, n_p):
+                here = slice((j - 1) * half_rows, j * half_rows)
+                at = (p ^ j) * 2
+                pairs.append((mine_ref.at[here, cols], own.at[tile(at + half, half_rows)]))
+                pairs.append((their_ref.at[here, cols], own.at[tile(at + 1 - half, half_rows)]))
         for copy in copy_all(pairs, sems):
             copy.wait()
 
-    outs = [((n_p * rows, groups * width), BF), (more.shape[1:], BF)]
-    scratch = [pltpu.SemaphoreType.DMA((1 + groups + 2 * (n_p - 1),))]
-    specs = [IN_ANY] * 2 + [IN_HBM] * 2
-    return run("stack_rows", body, outs, [mine, theirs, weight, more], net.place, scratch, ins_at=specs)
+    outs = [((n_p * rows, (g or 1) * width), BF) for (_, g, _), width in zip(parts, widths)]
+    outs += [(w.shape[1:], BF) for w in more]
+    ins = [mine, theirs, *[w for w, _, _ in parts], *more]
+    specs = [IN_ANY] * 2 + [IN_HBM] * (len(parts) + len(more))
+    scratch = [pltpu.SemaphoreType.DMA((count,))]
+    return run("stack_rows", body, outs, ins, net.place, scratch, ins_at=specs)
 
 
 def pack_tokens(tokens, scene_ids, token_kind):
@@ -287,28 +303,63 @@
     return centred * inverse, inverse
 
 
-def add_and_norm(net, layer, hidden, parts, bias, norm):
+def close_layer(net, layer, hidden, parts, bias):
     rows = parts[0].shape[0]
     count = len(parts)
 
+    def body(hidden_ref, bias_ref, *refs):
+        total = hidden_ref[...] + bias_ref[layer : layer + 1, :]
+        for part in refs[:count]:
+            total = total + part[...].astype(F32)
+        refs[count][...] = total
+        refs[count + 1][...] = total.astype(BF)
+
+    outs = [((rows, D), F32), ((rows, D), BF)]
+    return run("close_layer", body, outs, [hidden, bias, *parts])
+
+
+def close_attention(net, layer, hidden, blocks, pieces, proj, bias, gain, shift):
+    n_p = net.n_p
+    tokens, cw = pieces[0].shape
+    rows = tokens // n_p
+    half = cw // 2
+
     def body(place, *refs):
-        total = refs[0][0:rows, :].astype(F32) + refs[1 + count][layer : layer + 1, :]
-        for part in refs[1 : 1 + count]:
-            total = total + part[...].astype(F32)
-        if norm is None:
-            refs[2 + count][...] = total.astype(BF)
-            return
-        gain, shift, out, low = refs[2 + count : 6 + count]
-        normed, _ = norm_rows(total)
-        row = slice(norm[0], norm[0] + 1)
-        out[...] = total
-        own, other = own_first(normed * gain[row, :] + shift[row, :], net.n_p, place[1])
-        low[:, : D // 2] = own.astype(BF)
-        low[:, D // 2 :] = other.astype(BF)
-
-    ins = [hidden, *parts, bias] + ([] if norm is None else list(norm[1:]))
-    outs = [((rows, D), BF)] if norm is None else [((rows, D), F32), ((rows, D), BF)]
-    return run("add_and_norm", body, outs, ins, net.place)
+        hiddens, os = refs[:n_p], refs[n_p : 2 * n_p]
+        p_own, p_other, bias_ref, gain_ref, shift_ref, out, low, acc, o = refs[2 * n_p :]
+        p, c = place[0], place[1]
+        aligned = half % LANES == 0
+        for j in range(n_p):
+            for i in range(n_p):
+                there, here = slice(i * rows, (i + 1) * rows), slice((i ^ j) * rows, ((i ^ j) + 1) * rows)
+                first, second = os[j][there, :half], os[j][there, half:]
+                own, other = jnp.where(c == 0, first, second), jnp.where(c == 0, second, first)
+                if aligned:
+                    o[here, tile(p ^ j, half)] = own
+                    o[here, tile(n_p + (p ^ j), half)] = other
+                    continue
+                part = dot(own, p_own[tile(p ^ j, half), :]) + dot(other, p_other[tile(p ^ j, half), :])
+                if j == 0:
+                    acc[here, :] = part
+                else:
+                    acc[here, :] += part
+        if aligned:
+            acc[...] = dot(o[:, : D // 2], p_own[...]) + dot(o[:, D // 2 :], p_other[...])
+        line = slice(layer, layer + 1)
+        for j in range(n_p):
+            here = slice(j * rows, (j + 1) * rows)
+            total = acc[here, :] + hiddens[j][0:rows, :].astype(F32) + bias_ref[line, :]
+            if j == 0:
+                out[...] = total
+            normed, _ = norm_rows(total)
+            own, other = own_first(normed * gain_ref[line, :] + shift_ref[line, :], n_p, c)
+            low[here, : D // 2] = own.astype(BF)
+            low[here, D // 2 :] = other.astype(BF)
+
+    outs = [((rows, D), F32), ((tokens, D), BF)]
+    scratch = [pltpu.VMEM((tokens, D), F32), pltpu.VMEM((tokens, D), BF)]
+    ins = [hidden, *blocks[1:], *pieces, *proj, bias, gain, shift]
+    return run("close_attention", body, outs, ins, net.place, scratch, flops=2 * tokens * D * D)
 
 
 def norm_back(net, layer, grad, hidden, parts, gain):
@@ -373,47 +424,38 @@
 Q_TILE = 256
 
 
-def attend(net, layer, rows, blocks, norm, weight, bias, codes, proj):
+def attend(net, layer, rows, blocks, gain, shift, weight, bias, codes):
     n_p = net.n_p
     tokens = n_p * rows
     cw = D // n_p
-    first = norm is not None
+    n_c = 0 if codes is None else 2
 
     def body(place, *refs):
-        bias_ref, w_own, w_other, p_own, p_other = refs[n_p : n_p + 5]
-        if first:
-            gain_ref, shift_ref = refs[n_p + 5 : n_p + 7]
-            row_ref, col_ref, a = refs[n_p + 7 : n_p + 10]
-            outs = refs[n_p + 10 : 2 * n_p + 10]
-            qkv, attended, vt = refs[2 * n_p + 10 :]
-        else:
-            row_ref, col_ref = refs[n_p + 5 : n_p + 7]
-            outs = refs[n_p + 7 : 2 * n_p + 7]
-            qkv, attended, vt, a = refs[2 * n_p + 7 :]
+        bias_ref, w_own, w_other, gain_ref, shift_ref, row_ref, col_ref = refs[n_p : n_p + 7]
+        a, qkv, attended, vt = refs[n_p + 7 :]
         p, c = place[0], place[1]
-        if first:
-            eye = lax.broadcasted_iota(jnp.int32, (rows, rows), 0) == lax.broadcasted_iota(
-                jnp.int32, (rows, rows), 1
-            )
-            for j in range(n_p):
-                here = slice(j * rows, (j + 1) * rows)
-                line = refs[j][rows : rows + 1, 0:rows].astype(F32)
-                row_ref[:, here] = line.astype(jnp.int32)
-                column = jnp.sum(jnp.where(eye, line, 0.0), axis=1, keepdims=True)
+        eye = lax.broadcasted_iota(jnp.int32, (rows, rows), 0) == lax.broadcasted_iota(
+            jnp.int32, (rows, rows), 1
+        )
+        line = slice(layer, layer + 1)
+        for j in range(n_p):
+            here = slice(j * rows, (j + 1) * rows)
+            if codes is None:
+                code = refs[j][rows : rows + 1, 0:rows].astype(F32)
+                row_ref[:, here] = code.astype(jnp.int32)
+                column = jnp.sum(jnp.where(eye, code, 0.0), axis=1, keepdims=True)
                 col_ref[here, :] = column.astype(jnp.int32)
-                normed, _ = norm_rows(refs[j][0:rows, :].astype(F32))
-                own, other = own_first(normed * gain_ref[0:1, :] + shift_ref[0:1, :], n_p, c)
-                a[here, : D // 2] = own.astype(BF)
-                a[here, D // 2 :] = other.astype(BF)
-        else:
-            gather_rows(refs[:n_p], a)
+            normed, _ = norm_rows(refs[j][0:rows, :].astype(F32))
+            own, other = own_first(normed * gain_ref[line, :] + shift_ref[line, :], n_p, c)
+            a[here, : D // 2] = own.astype(BF)
+            a[here, D // 2 :] = other.astype(BF)
         for i in range(3):
             cols = slice(i * cw, (i + 1) * cw)
             out = dot(a[:, : D // 2], w_own[:, cols]) + dot(a[:, D // 2 :], w_other[:, cols])
             if i == 0:
-                out = out + bias_ref[layer : layer + 1, tile(p, cw)]
+                out = out + bias_ref[line, tile(p, cw)]
             if i == 2:
-                out = out + bias_ref[layer : layer + 1, tile(p + n_p, cw)]
+                out = out + bias_ref[line, tile(p + n_p, cw)]
             qkv[:, cols] = out.astype(BF)
         vt[...] = jnp.transpose(qkv[:, 2 * cw : 3 * cw].astype(F32)).astype(BF)
 
@@ -432,26 +474,15 @@
                     total = part if total is None else total + part
                 attended[here, lanes] = jnp.transpose(total).astype(BF)
 
-        for j in range(n_p):
-            o = attended[j * rows : (j + 1) * rows, :]
-            low, high = o[:, : cw // 2], o[:, cw // 2 :]
-            own, other = jnp.where(c == 0, low, high), jnp.where(c == 0, high, low)
-            outs[j][...] = (dot(own, p_own[...]) + dot(other, p_other[...])).astype(BF)
-
-    outs = [((rows, D), BF)] * n_p + [((tokens, 3 * cw), BF), ((tokens, cw), BF)]
+    outs = [((tokens, D), BF), ((tokens, 3 * cw), BF), ((tokens, cw), BF)]
+    if codes is None:
+        outs = [((1, tokens), jnp.int32), ((tokens, 1), jnp.int32)] + outs
+    ins = [*blocks, bias, *weight, gain, shift] + list(codes or [])
     scratch = [pltpu.VMEM((cw, tokens), BF)]
-    ins = [*blocks, bias, *weight, *proj]
-    if first:
-        ins += list(norm)
-        outs = [((1, tokens), jnp.int32), ((tokens, 1), jnp.int32), ((tokens, D), BF)] + outs
-    else:
-        ins += list(codes)
-        scratch.append(pltpu.VMEM((tokens, D), BF))
-    got = run("attend", body, outs, ins, net.place, scratch, flops=2 * tokens * D * 4 * cw)
-    normed = blocks
-    if first:
-        codes, normed, got = got[:2], [got[2]], got[3:]
-    return got[:n_p], got[n_p], got[n_p + 1], codes, normed
+    got = run("attend", body, outs, ins, net.place, scratch, flops=2 * tokens * D * 3 * cw)
+    if codes is None:
+        codes, got = got[:2], got[2:]
+    return (*got, codes)
 
 
 def attend_back(net, blocks, proj, qkv, codes, weight, tokens_in):
@@ -468,9 +499,10 @@
         outs = refs_out[:n_p]
         dqkv, sums, norm_sums, do, kt, dk, dv = refs_out[n_p:]
         c = place[1]
+        mine = tile(place[0], cw // 2)
         for j in range(n_p):
             here = slice(j * rows, (j + 1) * rows)
-            own, other = dot_nt(refs[j][...], p_own[...]), dot_nt(refs[j][...], p_other[...])
+            own, other = dot_nt(refs[j][...], p_own[mine, :]), dot_nt(refs[j][...], p_other[mine, :])
             do[here, : cw // 2] = jnp.where(c == 0, own, other).astype(BF)
             do[here, cw // 2 :] = jnp.where(c == 0, other, own).astype(BF)
         kt[...] = jnp.transpose(qkv_ref[:, cw : 2 * cw].astype(F32)).astype(BF)
@@ -530,18 +562,15 @@
 F_TILE = 256
 
 
-def feed_forward(net, layer, blocks, up, bias, down):
+def feed_forward(net, layer, a2, up, bias, down):
     n_p = net.n_p
-    rows = blocks[0].shape[0]
-    tokens = n_p * rows
+    tokens = a2.shape[0]
+    rows = tokens // n_p
     fw = FF // n_p
 
-    def body(place, *refs):
-        up_own, up_other, bias_ref, d_own, d_other = refs[n_p : n_p + 5]
-        outs = refs[n_p + 5 : 2 * n_p + 5]
-        z_ref, slope_ref, a_ref = refs[2 * n_p + 5 :]
+    def body(place, a_ref, up_own, up_other, bias_ref, d_own, d_other, *refs):
+        outs, z_ref, slope_ref = refs[:n_p], refs[n_p], refs[n_p + 1]
         p, c = place[0], place[1]
-        gather_rows(refs[:n_p], a_ref)
 
         @pl.loop(0, fw // F_TILE)
         def _(t):
@@ -559,9 +588,8 @@
             outs[j][...] = (dot(own, d_own[...]) + dot(other, d_other[...])).astype(BF)
 
     outs = [((rows, D), BF)] * n_p + [((tokens, fw), BF), ((tokens, fw), F32)]
-    scratch = [pltpu.VMEM((tokens, D), BF)]
-    ins = [*blocks, *up, bias, *down]
-    got = run("feed_forward", body, outs, ins, net.place, scratch, flops=4 * tokens * D * fw)
+    ins = [a2, *up, bias, *down]
+    got = run("feed_forward", body, outs, ins, net.place, flops=4 * tokens * D * fw)
     return got[:n_p], got[n_p], got[n_p + 1]
 
 
@@ -988,13 +1016,13 @@
     rows = tokens.shape[1]
     pair_groups = [[2 * i, 2 * i + 1] for i in range(n_p)]
 
-    def fetch(weight, layer, groups):
-        pieces = cut_columns(net, weight, layer, groups)
+    def fetch(layer, *weights):
+        pieces = cut_columns(net, layer, weights)
         return stack_halves([net.chip(v, j) for j, v in enumerate(pieces, 1)])
 
-    def complete(mine, theirs, weight, groups, more, layer):
-        own, rest = stack_rows(net, mine, theirs, weight, groups, more, layer)
-        return (own, net.core(own)), (rest, net.core(rest))
+    def complete(mine, theirs, parts, more, layer):
+        own = stack_rows(net, mine, theirs, parts, more, layer)
+        return [(v, net.core(v)) for v in own]
 
     def swap_cores(both):
         return lax.all_to_all(both, "fsdp", 0, 0, axis_index_groups=pair_groups)
@@ -1002,59 +1030,58 @@
     small_in = [first_gain, first_shift, qv_bias, proj_bias, second_gain, second_shift, up_bias, down_bias]
     sizes = [v.shape[1] for v in small_in]
     tok = net.to_place(pack_tokens(tokens, scene_ids, token_kind))
-    qkv_half = fetch(qkv_weight, 0, 3)
+    mine = fetch(0, (qkv_weight, 3), (proj_weight, None))
     small = pack_small(small_in)
     small_other = net.core(small)
     later = (qkv_weight, proj_weight, up_weight, down_weight, out_grad)
-    tok, qkv_half, small, small_other, later = fence((tok, qkv_half, small, small_other, later))
+    tok, mine, small, small_other, later = fence((tok, mine, small, small_other, later))
     qkv_weight, proj_weight, up_weight, down_weight, out_grad = later
     tokg = net.gather(put_small(tok, small, small_other))
-    qkv_next = net.next_plane(qkv_half)
-    tokg, qkv_half, qkv_next = fence((tokg, qkv_half, qkv_next))
+    theirs = net.next_plane(mine)
+    tokg, mine, theirs = fence((tokg, mine, theirs))
 
     weights = []
     kept = []
     dm = None
     codes = None
-    hidden = None
+    qkv_cols = 3 * D // n_p
     for layer in range(layers):
         last = layer == layers - 1
-        a1g = tokg if layer == 0 else net.gather(a1)
-        qkv_w, proj_w = complete(qkv_half, qkv_next, qkv_weight, 3, proj_weight, layer)
-        a1g, qkv_w, proj_w, up_weight = fence((a1g, qkv_w, proj_w, up_weight))
+        blocks = tokg if layer == 0 else net.gather(low)
+        parts = [(qkv_weight, 3, 0), (proj_weight, None, qkv_cols)]
+        qkv_w, proj_w = complete(mine, theirs, parts, [], layer)
+        blocks, qkv_w, proj_w, up_weight, out_grad = fence((blocks, qkv_w, proj_w, up_weight, out_grad))
         if layer == 0:
-            tokg = a1g
+            tokg = blocks
             hidden = tokg[0]
             vectors = join_vectors(net, layers, tokg, sizes, rows)
             gain1, shift1, qv_b, proj_b, gain2, shift2, up_b, down_b = vectors
-        norm = (gain1, shift1) if layer == 0 else None
-        y, qkv, og, codes, a1g = attend(net, layer, rows, a1g, norm, qkv_w, qv_b, codes, proj_w)
-        up_half = fetch(up_weight, layer, 1)
-        y, up_half, down_weight = fence((y, up_half, down_weight))
-        parts = net.exchange(y)
-        up_next = net.next_plane(up_half)
-        parts, up_next = fence((parts, up_next))
-        h2, a2 = add_and_norm(net, layer, hidden, parts, proj_b, (layer, gain2, shift2))
-        a2g = net.gather(a2)
-        up_w, down_w = complete(up_half, up_next, up_weight, 1, down_weight, layer)
-        a2g, up_w, down_w, qkv_weight, out_grad = fence((a2g, up_w, down_w, qkv_weight, out_grad))
+        a1g, qkv, og, codes = attend(net, layer, rows, blocks, gain1, shift1, qkv_w, qv_b, codes)
+        mine = fetch(layer, (up_weight, 1))
+        if last:
+            dm = net.to_chip(out_grad[0])
+        a1g, qkv, og, mine, dm, down_weight = fence((a1g, qkv, og, mine, dm, down_weight))
+        pieces = net.gather(og)
+        theirs = net.next_plane(mine)
+        if last:
+            dm = net.to_plane(dm)
+        pieces, theirs, dm = fence((pieces, theirs, dm))
+        up_w, down_w = complete(mine, theirs, [(up_weight, 1, 0)], [down_weight], layer)
+        h2, a2g = close_attention(net, layer, hidden, blocks, pieces, proj_w, proj_b, gain2, shift2)
+        a2g, up_w, down_w, qkv_weight, proj_weight = fence((a2g, up_w, down_w, qkv_weight, proj_weight))
         y, z, slope = feed_forward(net, layer, a2g, up_w, up_b, down_w)
-        kept.append((hidden, a1g, qkv, og, h2, a2g, z, slope))
+        kept.append((hidden, [a1g], qkv, og, h2, [a2g], z, slope))
         weights.append((qkv_w, proj_w, up_w, down_w))
         if last:
             dmg = net.gather(dm)
             last_y, z, slope, dmg = fence((y, z, slope, dmg))
             break
-        qkv_half = fetch(qkv_weight, layer + 1, 3)
-        if layer == layers - 2:
-            dm = net.to_chip(out_grad[0])
-        y, qkv_half, proj_weight, dm = fence((y, qkv_half, proj_weight, dm))
+        mine = fetch(layer + 1, (qkv_weight, 3), (proj_weight, None))
+        y, mine = fence((y, mine))
         parts = net.exchange(y)
-        qkv_next = net.next_plane(qkv_half)
-        if layer == layers - 2:
-            dm = net.to_plane(dm)
-        parts, qkv_next, dm = fence((parts, qkv_next, dm))
-        hidden, a1 = add_and_norm(net, layer, h2, parts, down_b, (layer + 1, gain1, shift1))
+        theirs = net.next_plane(mine)
+        parts, theirs = fence((parts, theirs))
+        hidden, low = close_layer(net, layer, h2, parts, down_b)
 
     flow = Flow(net)
     small_grads = [None] * layers
@@ -1088,7 +1115,7 @@
         if last:
             last_parts = net.exchange(last_y)
             da1, dqkv, last_parts = flow.collect((da1, dqkv, last_parts), up_g[1])
-            (sent_out,) = add_and_norm(net, layer, h2, last_parts, down_b, None)
+            _, sent_out = close_layer(net, layer, h2, last_parts, down_b)
         else:
             da1, dqkv = flow.collect((da1, dqkv), up_g[1])
         parts = net.exchange(da1)
@@ -1143,8 +1170,8 @@
     qkv_pieces = list(zip(first_part, second_part))
     out = write_layer(net, 0, layers, out, [c.value for c in sums[0][0]], proj_last, up_last, qkv_pieces)
     return (
-        sent_out.astype(F32)[None],
-        input_grad.astype(F32)[None],
+        sent_out[None],
+        input_grad[None],
         small_out[0],
         small_out[1],
         out[0],

time: 488 us -> 480 us (0.984)
  the two profiles are of different devices: /device:TPU:10 before, /device:TPU:26 now
where the time goes in v5:
time: 480 us; the launch traced here: 472 us
  waiting for transfers between devices  171 us (36%)
  starting transfers between devices  157 us (33%)
  Pallas kernels  109 us (23%)
  blocking collectives  21.9 us (5%)
  local copies, waits for them, and re-layouts  7.86 us (2%)
    ppermute x69, waiting for transfers between devices, chip(): return lax.ppermute(v, 'fsdp', xor_pairs(self.n_f, 2 * j))  145 us
    pallas_call x74, Pallas kernels, run(): pl.pallas_call(body, out_shape=[jax.ShapeDtypeStruct(shape, dtype) for sh...  102 us
    ppermute x69, starting transfers between devices, chip(): return lax.ppermute(v, 'fsdp', xor_pairs(self.n_f, 2 * j))  83.1 us
    ppermute x26, starting transfers between devices, start(): lax.ppermute(v, 'seq', m[3])  42.6 us
    all_to_all x4, blocking collectives, swap_cores(): return lax.all_to_all(both, 'fsdp', 0, 0, axis_index_groups=pair_groups)  21.9 us
    ppermute x5, starting transfers between devices, send(): return lax.ppermute(v, ('seq', 'fsdp'), pairs)  20.8 us
    ppermute x26, waiting for transfers between devices, start(): lax.ppermute(v, 'seq', m[3])  17.9 us
  transfers between devices with their start and end apart: 115, of which 52 were waited for; matrix products, arithmetic and copies ran while one was open for 0% of the time, Pallas kernels for 18%

profile of v5, /device:TPU:26, one launch (start us, length us, event | category | flops | bytes accessed | tf_op | source)
XLA Modules:
  0.0 471.6 jit_solution(4719376917730360448)
XLA Ops:
  2.4 3.2 collective-permute-start
  12.7 4.9 %collective-permute-done.1.refs_0_ = bf16[64,1792]{1,0:T(8,128)(2,1)S(1)} collective-permute-done((bf16[64,1792]{1,0:T(8,128)(2,1)S(1)}, bf16[64,1792]{1,0:T(8,128)(2,1)S(1)}, u32[]{:S(2)}, u32[]{:S(2)}) %collective-permute-start.1) | collective-permute-done | bytes 229408 | tf_op jit(solution)/shard_map/ppermute | solution.py:64
  17.6 8.9 %collective-permute-done.2.refs_1_ = bf16[64,1792]{1,0:T(8,128)(2,1)S(1)} collective-permute-done((bf16[64,1792]{1,0:T(8,128)(2,1)S(1)}, bf16[64,1792]{1,0:T(8,128)(2,1)S(1)}, u32[]{:S(2)}, u32[]{:S(2)}) %collective-permute-start.2) | collective-permute-done | bytes 229408 | tf_op jit(solution)/shard_map/ppermute | solution.py:64
  27.4 4.2 collective-permute-start.8
  31.8 3.4 collective-permute-start.7
  35.2 6.5 %collective-permute-done.5.refs_1_.refs_12_ = bf16[144,1024]{1,0:T(8,128)(2,1)S(1)} collective-permute-done((bf16[144,1024]{1,0:T(8,128)(2,1)S(1)}, bf16[144,1024]{1,0:T(8,128)(2,1)S(1)}, u32[]{:S(2)}, u32[]{:S(2)}) %collective-permute-start.5) | collective-permute-done | bytes 294944 | tf_op jit(solution)/shard_map/ppermute | solution.py:64
  41.7 4.1 collective-permute-done.6.refs_2_.refs_13_
  47.9 3.3 collective-permute-done.9.refs_6_.refs_10_
  56.0 5.3 %attend.2 = (s32[1,512]{1,0:T(1,128)S(1)}, s32[512,1]{1,0:T(8,128)S(1)}, bf16[512,1024]{1,0:T(8,128)(2,1)S(1)}, bf16[512,768]{1,0:T(8,128)(2,1)S(1)}, bf16[512,256]{1,0:T(8,128)(2,1)S(1)}) custom-call(s32[3]{0:T(128)S(1)} %pad_add_fusion.2.place, bf16[144,1024]{1,0:T(8,128)(2,1)S(1)} %put_small.1.refs_0_.refs_11_.hidden_ref, ...), custom_call_target="tpu_custom_call" | custom-call | flops 805306368 | bytes 2785292 | tf_op jit(solution)/shard_map/attend/pallas_call | solution.py:99
  67.2 5.8 %collective-permute-done.14.refs_5_ = bf16[512,256]{1,0:T(8,128)(2,1)S(1)} collective-permute-done((bf16[512,256]{1,0:T(8,128)(2,1)S(1)}, bf16[512,256]{1,0:T(8,128)(2,1)S(1)}, u32[]{:S(2)}, u32[]{:S(2)}) %collective-permute-start.14) | collective-permute-done | bytes 262176 | tf_op jit(solution)/shard_map/ppermute | solution.py:64
  73.0 3.7 collective-permute-done.15.refs_6_
  79.1 2.7 close_attention.2
  87.1 4.1 feed_forward.2
  92.6 4.9 %collective-permute-done.21.refs_1_ = bf16[64,1792]{1,0:T(8,128)(2,1)S(1)} collective-permute-done((bf16[64,1792]{1,0:T(8,128)(2,1)S(1)}, bf16[64,1792]{1,0:T(8,128)(2,1)S(1)}, u32[]{:S(2)}, u32[]{:S(2)}) %collective-permute-start.21) | collective-permute-done | bytes 229408 | tf_op jit(solution)/shard_map/ppermute | solution.py:64
  102.4 5.8 %collective-permute-done.23.refs_1_ = bf16[128,1024]{1,0:T(8,128)(2,1)S(1)} collective-permute-done((bf16[128,1024]{1,0:T(8,128)(2,1)S(1)}, bf16[128,1024]{1,0:T(8,128)(2,1)S(1)}, u32[]{:S(2)}, u32[]{:S(2)}) %collective-permute-start.23) | collective-permute-done | bytes 262176 | tf_op jit(solution)/shard_map/ppermute | solution.py:64
  108.1 2.7 collective-permute-done.24.refs_2_
  120.0 5.7 %collective-permute-done.27.refs_1_ = bf16[128,1024]{1,0:T(8,128)(2,1)S(1)} collective-permute-done((bf16[128,1024]{1,0:T(8,128)(2,1)S(1)}, bf16[128,1024]{1,0:T(8,128)(2,1)S(1)}, u32[]{:S(2)}, u32[]{:S(2)}) %collective-permute-start.27) | collective-permute-done | bytes 262176 | tf_op jit(solution)/shard_map/ppermute | solution.py:64
  125.7 5.0 %collective-permute-done.28.refs_2_ = bf16[128,1024]{1,0:T(8,128)(2,1)S(1)} collective-permute-done((bf16[128,1024]{1,0:T(8,128)(2,1)S(1)}, bf16[128,1024]{1,0:T(8,128)(2,1)S(1)}, u32[]{:S(2)}, u32[]{:S(2)}) %collective-permute-start.28) | collective-permute-done | bytes 262176 | tf_op jit(solution)/shard_map/ppermute | solution.py:64
  130.8 4.0 collective-permute-start.35
  138.9 5.3 %attend.3 = (bf16[512,1024]{1,0:T(8,128)(2,1)S(1)}, bf16[512,768]{1,0:T(8,128)(2,1)S(1)}, bf16[512,256]{1,0:T(8,128)(2,1)S(1)}) custom-call(s32[3]{0:T(128)S(1)} %pad_add_fusion.2.place, bf16[128,1024]{1,0:T(8,128)(2,1)S(1)} %get-tuple-element.505.refs_0_, bf16[128,1024]{1,0:T(8,128)(2,1)S(1)} %collective-permute-done.27.refs_1_, ...), custom_call_target="tpu_custom_call" | custom-call | flops 805306368 | bytes 2658316 | tf_op jit(solution)/shard_map/attend/pallas_call | solution.py:99
  149.7 2.5 collective-permute-start.38
  152.2 4.8 %collective-permute-start.40 = (bf16[128,1024]{1,0:T(8,128)(2,1)S(1)}, bf16[128,1024]{1,0:T(8,128)(2,1)S(1)}, u32[]{:S(2)}, u32[]{:S(2)}) collective-permute-start(bf16[128,1024]{1,0:T(8,128)(2,1)S(1)} %collective-permute-done.35), channel_id=1, source_target_pairs={{0,0},{1,1},{2,10},{3,11},{4,20},{5,21},{6,30},{7,31},{8,16},{9,17... | collective-permute-start | bytes 786440 | tf_op jit(solution)/shard_map/ppermute | solution.py:43
  157.9 2.8 collective-permute-done.37.refs_6_
  164.8 2.6 collective-permute-start.44
  168.9 2.7 close_attention.3
  171.6 4.1 feed_forward.3
  175.8 3.0 collective-permute-done.44.refs_2_
  182.7 5.4 %feed_back.2 = (bf16[128,1024]{1,0:T(8,128)(2,1)S(1)}, bf16[128,1024]{1,0:T(8,128)(2,1)S(1)}, bf16[128,1024]{1,0:T(8,128)(2,1)S(1)}, bf16[128,1024]{1,0:T(8,128)...) custom-call(s32[3]{0:T(128)S(1)} %pad_add_fusion.2.place, ...), custom_call_target="tpu_custom_call" | custom-call | flops 2147483648 | bytes 7340044 | tf_op jit(solution)/shard_map/feed_back/pallas_call | solution.py:99
  189.1 2.8 collective-permute-start.50
  197.3 5.4 %all_to_all.20.ref = bf16[2,512,1024]{2,1,0:T(8,128)(2,1)S(1)} all-to-all(bf16[2,512,1024]{2,1,0:T(8,128)(2,1)S(1)} %up_weight_grad.2), channel_id=1, replica_groups={{0,1},{2,3},{4,5},{6,7},{8,9},{10,11},{12,13},{14,15},{16,17},{18,19},{..., dimensions={0} | all-to-all | bytes 4194304 | tf_op jit(solution)/shard_map/all_to_all | solution.py:1028
  202.8 2.7 collective-permute-done.48.refs_2_
  218.5 5.7 %collective-permute-done.51.refs_1_.refs_4_ = bf16[128,1024]{1,0:T(8,128)(2,1)} collective-permute-done((bf16[128,1024]{1,0:T(8,128)(2,1)}, bf16[128,1024]{1,0:T(8,128)(2,1)}, u32[]{:S(2)}, u32[]{:S(2)}) %collective-permute-start.51) | collective-permute-done | bytes 262176 | tf_op jit(solution)/shard_map/ppermute | solution.py:64
  224.5 4.0 collective-permute-done.53.refs_3_.refs_6_
  235.7 9.6 %attend_back.2 = (bf16[128,1024]{1,0:T(8,128)(2,1)S(1)}, bf16[128,1024]{1,0:T(8,128)(2,1)S(1)}, bf16[128,1024]{1,0:T(8,128)(2,1)S(1)}, bf16[128,1024]{1,0:T(8,12...) custom-call(s32[3]{0:T(128)S(1)} %pad_add_fusion.2.place, ...), custom_call_target="tpu_custom_call" | custom-call | flops 2147483648 | bytes 5509132 | tf_op jit(solution)/shard_map/attend_back/pallas_call | solution.py:99
  246.2 3.6 collective-permute-start.64
  254.0 2.6 attend_weight_grad.2
  256.6 5.4 %all_to_all.21.ref = bf16[2,512,1024]{2,1,0:T(8,128)(2,1)S(1)} all-to-all(bf16[2,512,1024]{2,1,0:T(8,128)(2,1)S(1)} %attend_weight_grad.2), channel_id=1, replica_groups={{0,1},{2,3},{4,5},{6,7},{8,9},{10,11},{12,13},{14,15},{16,17},{18,19},{..., dimensions={0} | all-to-all | bytes 4194304 | tf_op jit(solution)/shard_map/all_to_all | solution.py:1028
  265.0 3.2 collective-permute-start.69
  272.6 5.7 %collective-permute-done.66.refs_1_ = bf16[128,1024]{1,0:T(8,128)(2,1)S(1)} collective-permute-done((bf16[128,1024]{1,0:T(8,128)(2,1)S(1)}, bf16[128,1024]{1,0:T(8,128)(2,1)S(1)}, u32[]{:S(2)}, u32[]{:S(2)}) %collective-permute-start.66) | collective-permute-done | bytes 262176 | tf_op jit(solution)/shard_map/ppermute | solution.py:64
  278.3 5.6 %collective-permute-done.67.refs_2_ = bf16[128,1024]{1,0:T(8,128)(2,1)S(1)} collective-permute-done((bf16[128,1024]{1,0:T(8,128)(2,1)S(1)}, bf16[128,1024]{1,0:T(8,128)(2,1)S(1)}, u32[]{:S(2)}, u32[]{:S(2)}) %collective-permute-start.67) | collective-permute-done | bytes 262176 | tf_op jit(solution)/shard_map/ppermute | solution.py:64
  289.2 5.4 %feed_back.3 = (bf16[128,1024]{1,0:T(8,128)(2,1)S(1)}, bf16[128,1024]{1,0:T(8,128)(2,1)S(1)}, bf16[128,1024]{1,0:T(8,128)(2,1)S(1)}, bf16[128,1024]{1,0:T(8,128)...) custom-call(s32[3]{0:T(128)S(1)} %pad_add_fusion.2.place, ...), custom_call_target="tpu_custom_call" | custom-call | flops 2147483648 | bytes 7340044 | tf_op jit(solution)/shard_map/feed_back/pallas_call | solution.py:99
  294.9 6.2 %collective-permute-done.72.refs_4_.a_ref = bf16[512,512]{1,0:T(8,128)(2,1)S(1)} collective-permute-done((bf16[512,512]{1,0:T(8,128)(2,1)S(1)}, bf16[512,512]{1,0:T(8,128)(2,1)S(1)}, u32[]{:S(2)}, u32[]{:S(2)}) %collective-permute-start.72) | collective-permute-done | bytes 524320 | tf_op jit(solution)/shard_map/ppermute | solution.py:921
  301.8 3.8 collective-permute-start.77
  311.6 5.4 %all_to_all.22.ref = bf16[2,512,1024]{2,1,0:T(8,128)(2,1)S(1)} all-to-all(bf16[2,512,1024]{2,1,0:T(8,128)(2,1)S(1)} %up_weight_grad.3), channel_id=1, replica_groups={{0,1},{2,3},{4,5},{6,7},{8,9},{10,11},{12,13},{14,15},{16,17},{18,19},{..., dimensions={0} | all-to-all | bytes 4194304 | tf_op jit(solution)/shard_map/all_to_all | solution.py:1028
  317.1 2.5 collective-permute-done.76.refs_3_
  320.3 3.3 collective-permute-start.82
  329.4 5.5 %collective-permute-done.79.refs_1_.refs_4_ = bf16[128,1024]{1,0:T(8,128)(2,1)S(1)} collective-permute-done((bf16[128,1024]{1,0:T(8,128)(2,1)S(1)}, bf16[128,1024]{1,0:T(8,128)(2,1)S(1)}, u32[]{:S(2)}, u32[]{:S(2)}) %collective-permute-start.79) | collective-permute-done | bytes 262176 | tf_op jit(solution)/shard_map/ppermute | solution.py:64
  334.9 3.7 collective-permute-done.80.refs_2_.refs_5_
  342.3 9.3 %attend_back.3 = (bf16[128,1024]{1,0:T(8,128)(2,1)S(1)}, bf16[128,1024]{1,0:T(8,128)(2,1)S(1)}, bf16[128,1024]{1,0:T(8,128)(2,1)S(1)}, bf16[128,1024]{1,0:T(8,12...) custom-call(s32[3]{0:T(128)S(1)} %pad_add_fusion.2.place, ...), custom_call_target="tpu_custom_call" | custom-call | flops 2147483648 | bytes 6688780 | tf_op jit(solution)/shard_map/attend_back/pallas_call | solution.py:99
  352.4 3.0 collective-permute-start.89
  361.7 5.6 %all_to_all.23.ref = bf16[2,576,1024]{2,1,0:T(8,128)(2,1)S(1)} all-to-all(bf16[2,576,1024]{2,1,0:T(8,128)(2,1)S(1)} %attend_weight_grad.3), channel_id=1, replica_groups={{0,1},{2,3},{4,5},{6,7},{8,9},{10,11},{12,13},{14,15},{16,17},{18,19},{..., dimensions={0} | all-to-all | bytes 4718592 | tf_op jit(solution)/shard_map/all_to_all | solution.py:1028
  377.3 5.7 %collective-permute-done.91.refs_4_ = bf16[128,1024]{1,0:T(8,128)(2,1)S(1)} collective-permute-done((bf16[128,1024]{1,0:T(8,128)(2,1)S(1)}, bf16[128,1024]{1,0:T(8,128)(2,1)S(1)}, u32[]{:S(2)}, u32[]{:S(2)}) %collective-permute-start.91) | collective-permute-done | bytes 262176 | tf_op jit(solution)/shard_map/ppermute | solution.py:64
  383.4 4.8 %collective-permute-done.93.refs_6_ = bf16[128,1024]{1,0:T(8,128)(2,1)S(1)} collective-permute-done((bf16[128,1024]{1,0:T(8,128)(2,1)S(1)}, bf16[128,1024]{1,0:T(8,128)(2,1)S(1)}, u32[]{:S(2)}, u32[]{:S(2)}) %collective-permute-start.93) | collective-permute-done | bytes 262176 | tf_op jit(solution)/shard_map/ppermute | solution.py:64
  388.9 2.6 collective-permute-start.99
  397.6 3.0 collective-permute-done.96.refs_8_
  400.7 2.9 collective-permute-done.97.refs_9_
  411.1 5.7 %collective-permute-done.101.refs_4_ = bf16[128,1024]{1,0:T(8,128)(2,1)S(1)} collective-permute-done((bf16[128,1024]{1,0:T(8,128)(2,1)S(1)}, bf16[128,1024]{1,0:T(8,128)(2,1)S(1)}, u32[]{:S(2)}, u32[]{:S(2)}) %collective-permute-start.101) | collective-permute-done | bytes 262176 | tf_op jit(solution)/shard_map/ppermute | solution.py:64
  416.8 3.5 collective-permute-done.102.refs_5_
  422.7 7.0 %collective-permute-start.106 = (bf16[256,1024]{1,0:T(8,128)(2,1)S(1)}, bf16[256,1024]{1,0:T(8,128)(2,1)S(1)}, u32[]{:S(2)}, u32[]{:S(2)}) collective-permute-start(bf16[256,1024]{1,0:T(8,128)(2,1)S(1)} %pad_maximum_fusion), channel_id=1, source_target_pairs={{0,0},{1,1},{10,2},{11,3},{20,4},{21,5},{30,6},{31,7},{16,8},{17,9... | collective-permute-start | bytes 1572872 | tf_op jit(solution)/shard_map/ppermute | solution.py:43
  437.7 10.4 %collective-permute-done.110.a_ref = bf16[576,512]{1,0:T(8,128)(2,1)S(1)} collective-permute-done((bf16[576,512]{1,0:T(8,128)(2,1)S(1)}, bf16[576,512]{1,0:T(8,128)(2,1)S(1)}, u32[]{:S(2)}, u32[]{:S(2)}) %collective-permute-start.110) | collective-permute-done | bytes 589856 | tf_op jit(solution)/shard_map/ppermute | solution.py:921
  450.6 2.7 collective-permute-start.112
  455.1 3.5 write_layer.2
  458.7 4.0 collective-permute-done.112.refs_5_.refs_10_
  466.4 3.5 write_layer.3
  (416 shorter events, 177.8 us)
Async XLA Ops:
  2.4 24.9 %collective-permute-start = (bf16[144,1024]{1,0:T(8,128)(2,1)S(1)}, bf16[144,1024]{1,0:T(8,128)(2,1)S(1)}, u32[]{:S(2)}, u32[]{:S(2)}) collective-permute-start(bf16[144,1024]{1,0:T(8,128)(2,1)S(1)} %pad_add_fusion), channel_id=1, source_target_pairs={{0,0},{1,1},{2,10},{3,11},{4,20},{5,21},{6,30},{7,31},{12,16},{13,... | collective-permute-start | bytes 884744 | tf_op jit(solution)/shard_map/ppermute | solution.py:43
  9.5 17.0 %collective-permute-start.2 = (bf16[64,1792]{1,0:T(8,128)(2,1)S(1)}, bf16[64,1792]{1,0:T(8,128)(2,1)S(1)}, u32[]{:S(2)}, u32[]{:S(2)}) collective-permute-start(bf16[64,1792]{1,0:T(8,128)(2,1)S(1)} %get-tuple-element.423), channel_id=1, source_target_pairs={{0,4},{1,5},{2,6},{3,7},{4,0},{5,1},{6,2},{7,3},{8,12},{9,13},{10,... | collective-permute-start | bytes 688136 | tf_op jit(solution)/shard_map/ppermute | solution.py:64
  11.2 15.2 %collective-permute-start.3 = (bf16[64,1792]{1,0:T(8,128)(2,1)S(1)}, bf16[64,1792]{1,0:T(8,128)(2,1)S(1)}, u32[]{:S(2)}, u32[]{:S(2)}) collective-permute-start(bf16[64,1792]{1,0:T(8,128)(2,1)S(1)} %get-tuple-element.424), channel_id=1, source_target_pairs={{0,6},{1,7},{2,4},{3,5},{4,2},{5,3},{6,0},{7,1},{8,14},{9,15},{10,... | collective-permute-start | bytes 688136 | tf_op jit(solution)/shard_map/ppermute | solution.py:64
  12.6 14.7 %collective-permute-start.4 = (bf16[2,1536]{1,0:T(2,128)(2,1)S(1)}, bf16[2,1536]{1,0:T(2,128)(2,1)S(1)}, u32[]{:S(2)}, u32[]{:S(2)}) collective-permute-start(bf16[2,1536]{1,0:T(2,128)(2,1)S(1)} %pad_add_fusion.1.own_ref), channel_id=1, source_target_pairs={{0,1},{1,0},{2,3},{3,2},{4,5},{5,4},{6,7},{7,6},{8,9},{9,8},{10,11... | collective-permute-start | bytes 18440 | tf_op jit(solution)/shard_map/ppermute | solution.py:67
  27.4 18.9 %collective-permute-start.8 = (bf16[192,1792]{1,0:T(8,128)(2,1)S(1)}, bf16[192,1792]{1,0:T(8,128)(2,1)S(1)}, u32[]{:S(2)}, u32[]{:S(2)}) collective-permute-start(bf16[192,1792]{1,0:T(8,128)(2,1)S(1)} %stack_halves.4.mine_ref), channel_id=1, source_target_pairs={{0,8},{8,0},{16,24},{24,16},{1,9},{9,1},{17,25},{25,17},{2,10},{10... | collective-permute-start | bytes 2064392 | tf_op jit(solution)/shard_map/ppermute | solution.py:70
  31.8 14.0 %collective-permute-start.6 = (bf16[144,1024]{1,0:T(8,128)(2,1)S(1)}, bf16[144,1024]{1,0:T(8,128)(2,1)S(1)}, u32[]{:S(2)}, u32[]{:S(2)}) collective-permute-start(bf16[144,1024]{1,0:T(8,128)(2,1)S(1)} %put_small.1.refs_0_.refs_11_.hidden_ref), channel_id=1, source_target_pairs={{0,4},{1,5},{2,6},{3,7},{4,0},{5,1},{6,2},{7,3},{8,12},{9,13},{10,... | collective-permute-start | bytes 884744 | tf_op jit(solution)/shard_map/ppermute | solution.py:64
  31.8 14.0 %collective-permute-start.7 = (bf16[144,1024]{1,0:T(8,128)(2,1)S(1)}, bf16[144,1024]{1,0:T(8,128)(2,1)S(1)}, u32[]{:S(2)}, u32[]{:S(2)}) collective-permute-start(bf16[144,1024]{1,0:T(8,128)(2,1)S(1)} %put_small.1.refs_0_.refs_11_.hidden_ref), channel_id=1, source_target_pairs={{0,6},{1,7},{2,4},{3,5},{4,2},{5,3},{6,0},{7,1},{8,14},{9,15},{10,... | collective-permute-start | bytes 884744 | tf_op jit(solution)/shard_map/ppermute | solution.py:64
  62.3 14.4 %collective-permute-start.17 = (bf16[192,1024]{1,0:T(8,128)(2,1)S(1)}, bf16[192,1024]{1,0:T(8,128)(2,1)S(1)}, u32[]{:S(2)}, u32[]{:S(2)}) collective-permute-start(bf16[192,1024]{1,0:T(8,128)(2,1)S(1)} %stack_halves.5.mine_ref), channel_id=1, source_target_pairs={{0,8},{8,0},{16,24},{24,16},{1,9},{9,1},{17,25},{25,17},{2,10},{10... | collective-permute-start | bytes 1179656 | tf_op jit(solution)/shard_map/ppermute | solution.py:70
  64.3 12.4 %collective-permute-start.15 = (bf16[512,256]{1,0:T(8,128)(2,1)S(1)}, bf16[512,256]{1,0:T(8,128)(2,1)S(1)}, u32[]{:S(2)}, u32[]{:S(2)}) collective-permute-start(bf16[512,256]{1,0:T(8,128)(2,1)S(1)} %get-tuple-element.460.refs_4_.refs_2_), channel_id=1, source_target_pairs={{0,4},{1,5},{2,6},{3,7},{4,0},{5,1},{6,2},{7,3},{8,12},{9,13},{10,... | collective-permute-start | bytes 786440 | tf_op jit(solution)/shard_map/ppermute | solution.py:64
  65.0 11.7 %collective-permute-start.16 = (bf16[512,256]{1,0:T(8,128)(2,1)S(1)}, bf16[512,256]{1,0:T(8,128)(2,1)S(1)}, u32[]{:S(2)}, u32[]{:S(2)}) collective-permute-start(bf16[512,256]{1,0:T(8,128)(2,1)S(1)} %get-tuple-element.460.refs_4_.refs_2_), channel_id=1, source_target_pairs={{0,6},{1,7},{2,4},{3,5},{4,2},{5,3},{6,0},{7,1},{8,14},{9,15},{10,... | collective-permute-start | bytes 786440 | tf_op jit(solution)/shard_map/ppermute | solution.py:64
  85.2 12.3 %collective-permute-start.21 = (bf16[64,1792]{1,0:T(8,128)(2,1)S(1)}, bf16[64,1792]{1,0:T(8,128)(2,1)S(1)}, u32[]{:S(2)}, u32[]{:S(2)}) collective-permute-start(bf16[64,1792]{1,0:T(8,128)(2,1)S(1)} %get-tuple-element.489), channel_id=1, source_target_pairs={{0,4},{1,5},{2,6},{3,7},{4,0},{5,1},{6,2},{7,3},{8,12},{9,13},{10,... | collective-permute-start | bytes 688136 | tf_op jit(solution)/shard_map/ppermute | solution.py:64
  85.5 12.0 %collective-permute-start.22 = (bf16[64,1792]{1,0:T(8,128)(2,1)S(1)}, bf16[64,1792]{1,0:T(8,128)(2,1)S(1)}, u32[]{:S(2)}, u32[]{:S(2)}) collective-permute-start(bf16[64,1792]{1,0:T(8,128)(2,1)S(1)} %get-tuple-element.490), channel_id=1, source_target_pairs={{0,6},{1,7},{2,4},{3,5},{4,2},{5,3},{6,0},{7,1},{8,14},{9,15},{10,... | collective-permute-start | bytes 688136 | tf_op jit(solution)/shard_map/ppermute | solution.py:64
  98.4 16.2 %collective-permute-start.26 = (bf16[192,1792]{1,0:T(8,128)(2,1)S(1)}, bf16[192,1792]{1,0:T(8,128)(2,1)S(1)}, u32[]{:S(2)}, u32[]{:S(2)}) collective-permute-start(bf16[192,1792]{1,0:T(8,128)(2,1)S(1)} %stack_halves.6.mine_ref), channel_id=1, source_target_pairs={{0,8},{8,0},{16,24},{24,16},{1,9},{9,1},{17,25},{25,17},{2,10},{10... | collective-permute-start | bytes 2064392 | tf_op jit(solution)/shard_map/ppermute | solution.py:70
  100.9 11.8 %collective-permute-start.25 = (bf16[128,1024]{1,0:T(8,128)(2,1)S(1)}, bf16[128,1024]{1,0:T(8,128)(2,1)S(1)}, u32[]{:S(2)}, u32[]{:S(2)}) collective-permute-start(bf16[128,1024]{1,0:T(8,128)(2,1)S(1)} %get-tuple-element.494), channel_id=1, source_target_pairs={{0,6},{1,7},{2,4},{3,5},{4,2},{5,3},{6,0},{7,1},{8,14},{9,15},{10,... | collective-permute-start | bytes 786440 | tf_op jit(solution)/shard_map/ppermute | solution.py:64
  115.6 15.1 %collective-permute-start.31 = (bf16[512,1024]{1,0:T(8,128)(2,1)S(1)}, bf16[512,1024]{1,0:T(8,128)(2,1)S(1)}, u32[]{:S(2)}, u32[]{:S(2)}) collective-permute-start(bf16[512,1024]{1,0:T(8,128)(2,1)S(1)} %get-tuple-element.530.refs_8_.refs_4_), channel_id=1, source_target_pairs={{0,1},{1,0},{2,3},{3,2},{4,5},{5,4},{6,7},{7,6},{8,9},{9,8},{10,11... | collective-permute-start | bytes 3145736 | tf_op jit(solution)/shard_map/ppermute | solution.py:67
  115.7 15.0 %collective-permute-start.30 = (bf16[512,768]{1,0:T(8,128)(2,1)S(1)}, bf16[512,768]{1,0:T(8,128)(2,1)S(1)}, u32[]{:S(2)}, u32[]{:S(2)}) collective-permute-start(bf16[512,768]{1,0:T(8,128)(2,1)S(1)} %get-tuple-element.509.refs_5_.refs_9_), channel_id=1, source_target_pairs={{0,1},{1,0},{2,3},{3,2},{4,5},{5,4},{6,7},{7,6},{8,9},{9,8},{10,11... | collective-permute-start | bytes 2359304 | tf_op jit(solution)/shard_map/ppermute | solution.py:67
  117.1 13.6 %collective-permute-start.28 = (bf16[128,1024]{1,0:T(8,128)(2,1)S(1)}, bf16[128,1024]{1,0:T(8,128)(2,1)S(1)}, u32[]{:S(2)}, u32[]{:S(2)}) collective-permute-start(bf16[128,1024]{1,0:T(8,128)(2,1)S(1)} %get-tuple-element.505.refs_0_), channel_id=1, source_target_pairs={{0,4},{1,5},{2,6},{3,7},{4,0},{5,1},{6,2},{7,3},{8,12},{9,13},{10,... | collective-permute-start | bytes 786440 | tf_op jit(solution)/shard_map/ppermute | solution.py:64
  118.8 11.9 %collective-permute-start.29 = (bf16[128,1024]{1,0:T(8,128)(2,1)S(1)}, bf16[128,1024]{1,0:T(8,128)(2,1)S(1)}, u32[]{:S(2)}, u32[]{:S(2)}) collective-permute-start(bf16[128,1024]{1,0:T(8,128)(2,1)S(1)} %get-tuple-element.505.refs_0_), channel_id=1, source_target_pairs={{0,6},{1,7},{2,4},{3,5},{4,2},{5,3},{6,0},{7,1},{8,14},{9,15},{10,... | collective-permute-start | bytes 786440 | tf_op jit(solution)/shard_map/ppermute | solution.py:64
  130.8 16.1 %collective-permute-start.35 = (bf16[128,1024]{1,0:T(8,128)(2,1)S(1)}, bf16[128,1024]{1,0:T(8,128)(2,1)S(1)}, u32[]{:S(2)}, u32[]{:S(2)}) collective-permute-start(bf16[128,1024]{1,0:T(8,128)(2,1)S(1)} %bitcast.11), channel_id=1, source_target_pairs={{0,0},{1,1},{2,2},{3,3},{4,4},{5,5},{6,6},{7,7},{12,8},{13,9},{14,... | collective-permute-start | bytes 786440 | tf_op jit(solution)/shard_map/ppermute | solution.py:43
  146.9 15.2 %collective-permute-start.39 = (bf16[192,1024]{1,0:T(8,128)(2,1)S(1)}, bf16[192,1024]{1,0:T(8,128)(2,1)S(1)}, u32[]{:S(2)}, u32[]{:S(2)}) collective-permute-start(bf16[192,1024]{1,0:T(8,128)(2,1)S(1)} %stack_halves.7.mine_ref), channel_id=1, source_target_pairs={{0,8},{8,0},{16,24},{24,16},{1,9},{9,1},{17,25},{25,17},{2,10},{10... | collective-permute-start | bytes 1179656 | tf_op jit(solution)/shard_map/ppermute | solution.py:70
  149.0 11.7 %collective-permute-start.37 = (bf16[512,256]{1,0:T(8,128)(2,1)S(1)}, bf16[512,256]{1,0:T(8,128)(2,1)S(1)}, u32[]{:S(2)}, u32[]{:S(2)}) collective-permute-start(bf16[512,256]{1,0:T(8,128)(2,1)S(1)} %get-tuple-element.526.refs_4_.refs_2_), channel_id=1, source_target_pairs={{0,4},{1,5},{2,6},{3,7},{4,0},{5,1},{6,2},{7,3},{8,12},{9,13},{10,... | collective-permute-start | bytes 786440 | tf_op jit(solution)/shard_map/ppermute | solution.py:64
  164.8 14.0 %collective-permute-start.44 = (bf16[128,1024]{1,0:T(8,128)(2,1)S(1)}, bf16[128,1024]{1,0:T(8,128)(2,1)S(1)}, u32[]{:S(2)}, u32[]{:S(2)}) collective-permute-start(bf16[128,1024]{1,0:T(8,128)(2,1)S(1)} %collective-permute-done.40.refs_0_.grad_ref.ref), channel_id=1, source_target_pairs={{0,4},{1,5},{2,6},{3,7},{4,0},{5,1},{6,2},{7,3},{8,12},{9,13},{10,... | collective-permute-start | bytes 786440 | tf_op jit(solution)/shard_map/ppermute | solution.py:64
  167.4 13.3 %collective-permute-start.45 = (bf16[128,1024]{1,0:T(8,128)(2,1)S(1)}, bf16[128,1024]{1,0:T(8,128)(2,1)S(1)}, u32[]{:S(2)}, u32[]{:S(2)}) collective-permute-start(bf16[128,1024]{1,0:T(8,128)(2,1)S(1)} %collective-permute-done.40.refs_0_.grad_ref.ref), channel_id=1, source_target_pairs={{0,6},{1,7},{2,4},{3,5},{4,2},{5,3},{6,0},{7,1},{8,14},{9,15},{10,... | collective-permute-start | bytes 786440 | tf_op jit(solution)/shard_map/ppermute | solution.py:64
  189.1 18.1 %collective-permute-start.50 = (bf16[512,512]{1,0:T(8,128)(2,1)S(1)}, bf16[512,512]{1,0:T(8,128)(2,1)S(1)}, u32[]{:S(2)}, u32[]{:S(2)}) collective-permute-start(bf16[512,512]{1,0:T(8,128)(2,1)S(1)} %get-tuple-element.573.refs_0_), channel_id=1, source_target_pairs={{0,8},{24,16},{1,9},{25,17},{2,10},{26,18},{3,11},{27,19},{4,12},{... | collective-permute-start | bytes 1572872 | tf_op jit(solution)/shard_map/ppermute | solution.py:921
  193.5 12.0 %collective-permute-start.48 = (bf16[128,1024]{1,0:T(8,128)(2,1)S(1)}, bf16[128,1024]{1,0:T(8,128)(2,1)S(1)}, u32[]{:S(2)}, u32[]{:S(2)}) collective-permute-start(bf16[128,1024]{1,0:T(8,128)(2,1)S(1)} %get-tuple-element.569), channel_id=1, source_target_pairs={{0,4},{1,5},{2,6},{3,7},{4,0},{5,1},{6,2},{7,3},{8,12},{9,13},{10,... | collective-permute-start | bytes 786440 | tf_op jit(solution)/shard_map/ppermute | solution.py:64
  194.0 13.2 %collective-permute-start.49 = (bf16[128,1024]{1,0:T(8,128)(2,1)S(1)}, bf16[128,1024]{1,0:T(8,128)(2,1)S(1)}, u32[]{:S(2)}, u32[]{:S(2)}) collective-permute-start(bf16[128,1024]{1,0:T(8,128)(2,1)S(1)} %get-tuple-element.570), channel_id=1, source_target_pairs={{0,6},{1,7},{2,4},{3,5},{4,2},{5,3},{6,0},{7,1},{8,14},{9,15},{10,... | collective-permute-start | bytes 786440 | tf_op jit(solution)/shard_map/ppermute | solution.py:64
  207.2 21.3 %collective-permute-start.54 = (bf16[512,512]{1,0:T(8,128)(2,1)}, bf16[512,512]{1,0:T(8,128)(2,1)}, u32[]{:S(2)}, u32[]{:S(2)}) collective-permute-start(bf16[512,512]{1,0:T(8,128)(2,1)} %get-tuple-element.582.refs_3_), channel_id=1, source_target_pairs={{0,8},{24,16},{1,9},{25,17},{2,10},{26,18},{3,11},{27,19},{4,12},{... | collective-permute-start | bytes 1572872 | tf_op jit(solution)/shard_map/ppermute | solution.py:921
  210.5 18.1 %collective-permute-start.55 = (bf16[512,512]{1,0:T(8,128)(2,1)}, bf16[512,512]{1,0:T(8,128)(2,1)}, u32[]{:S(2)}, u32[]{:S(2)}) collective-permute-start(bf16[512,512]{1,0:T(8,128)(2,1)} %turn.13.refs_1_), channel_id=1, source_target_pairs={{8,16},{16,8},{9,17},{17,9},{10,18},{18,10},{11,19},{19,11},{12,20... | collective-permute-start | bytes 1572872 | tf_op jit(solution)/shard_map/ppermute | solution.py:921
  216.9 11.6 %collective-permute-start.53 = (bf16[128,1024]{1,0:T(8,128)(2,1)}, bf16[128,1024]{1,0:T(8,128)(2,1)}, u32[]{:S(2)}, u32[]{:S(2)}) collective-permute-start(bf16[128,1024]{1,0:T(8,128)(2,1)} %get-tuple-element.584.refs_0_.refs_3_), channel_id=1, source_target_pairs={{0,6},{1,7},{2,4},{3,5},{4,2},{5,3},{6,0},{7,1},{8,14},{9,15},{10,... | collective-permute-start | bytes 786440 | tf_op jit(solution)/shard_map/ppermute | solution.py:64
  230.2 15.2 %collective-permute-start.59 = (bf16[512,512]{1,0:T(8,128)(2,1)S(1)}, bf16[512,512]{1,0:T(8,128)(2,1)S(1)}, u32[]{:S(2)}, u32[]{:S(2)}) collective-permute-start(bf16[512,512]{1,0:T(8,128)(2,1)S(1)} %get-tuple-element.805.b_ref), channel_id=1, source_target_pairs={{0,8},{24,16},{8,0},{16,24},{1,9},{25,17},{9,1},{17,25},{2,10},{26... | collective-permute-start | bytes 1572872 | tf_op jit(solution)/shard_map/ppermute | solution.py:921
  230.3 15.1 %collective-permute-start.60 = (bf16[512,512]{1,0:T(8,128)(2,1)S(1)}, bf16[512,512]{1,0:T(8,128)(2,1)S(1)}, u32[]{:S(2)}, u32[]{:S(2)}) collective-permute-start(bf16[512,512]{1,0:T(8,128)(2,1)S(1)} %get-tuple-element.619.refs_1_), channel_id=1, source_target_pairs={{8,16},{16,8},{9,17},{17,9},{10,18},{18,10},{11,19},{19,11},{12,20... | collective-permute-start | bytes 1572872 | tf_op jit(solution)/shard_map/ppermute | solution.py:921
  231.0 14.4 %collective-permute-start.56 = (bf16[128,1024]{1,0:T(8,128)(2,1)S(1)}, bf16[128,1024]{1,0:T(8,128)(2,1)S(1)}, u32[]{:S(2)}, u32[]{:S(2)}) collective-permute-start(bf16[128,1024]{1,0:T(8,128)(2,1)S(1)} %copy-done.59), channel_id=1, source_target_pairs={{0,2},{1,3},{2,0},{3,1},{4,6},{5,7},{6,4},{7,5},{8,10},{9,11},{10,... | collective-permute-start | bytes 786440 | tf_op jit(solution)/shard_map/ppermute | solution.py:64
  232.5 12.9 %collective-permute-start.57 = (bf16[128,1024]{1,0:T(8,128)(2,1)S(1)}, bf16[128,1024]{1,0:T(8,128)(2,1)S(1)}, u32[]{:S(2)}, u32[]{:S(2)}) collective-permute-start(bf16[128,1024]{1,0:T(8,128)(2,1)S(1)} %copy-done.57), channel_id=1, source_target_pairs={{0,4},{1,5},{2,6},{3,7},{4,0},{5,1},{6,2},{7,3},{8,12},{9,13},{10,... | collective-permute-start | bytes 786440 | tf_op jit(solution)/shard_map/ppermute | solution.py:64
  233.4 12.0 %collective-permute-start.58 = (bf16[128,1024]{1,0:T(8,128)(2,1)S(1)}, bf16[128,1024]{1,0:T(8,128)(2,1)S(1)}, u32[]{:S(2)}, u32[]{:S(2)}) collective-permute-start(bf16[128,1024]{1,0:T(8,128)(2,1)S(1)} %copy-done.55), channel_id=1, source_target_pairs={{0,6},{1,7},{2,4},{3,5},{4,2},{5,3},{6,0},{7,1},{8,14},{9,15},{10,... | collective-permute-start | bytes 786440 | tf_op jit(solution)/shard_map/ppermute | solution.py:64
  246.2 18.1 %collective-permute-start.64 = (bf16[512,512]{1,0:T(8,128)(2,1)S(1)}, bf16[512,512]{1,0:T(8,128)(2,1)S(1)}, u32[]{:S(2)}, u32[]{:S(2)}) collective-permute-start(bf16[512,512]{1,0:T(8,128)(2,1)S(1)} %get-tuple-element.806.b_ref), channel_id=1, source_target_pairs={{0,8},{24,16},{8,0},{16,24},{1,9},{25,17},{9,1},{17,25},{2,10},{26... | collective-permute-start | bytes 1572872 | tf_op jit(solution)/shard_map/ppermute | solution.py:921
  249.8 14.5 %collective-permute-start.65 = (bf16[512,512]{1,0:T(8,128)(2,1)S(1)}, bf16[512,512]{1,0:T(8,128)(2,1)S(1)}, u32[]{:S(2)}, u32[]{:S(2)}) collective-permute-start(bf16[512,512]{1,0:T(8,128)(2,1)S(1)} %get-tuple-element.628.refs_1_), channel_id=1, source_target_pairs={{8,16},{16,8},{9,17},{17,9},{10,18},{18,10},{11,19},{19,11},{12,20... | collective-permute-start | bytes 1572872 | tf_op jit(solution)/shard_map/ppermute | solution.py:921
  265.0 19.0 %collective-permute-start.69 = (bf16[512,512]{1,0:T(8,128)(2,1)S(1)}, bf16[512,512]{1,0:T(8,128)(2,1)S(1)}, u32[]{:S(2)}, u32[]{:S(2)}) collective-permute-start(bf16[512,512]{1,0:T(8,128)(2,1)S(1)} %get-tuple-element.731.b_ref), channel_id=1, source_target_pairs={{0,8},{24,16},{8,0},{16,24},{1,9},{25,17},{9,1},{17,25},{2,10},{26... | collective-permute-start | bytes 1572872 | tf_op jit(solution)/shard_map/ppermute | solution.py:921
  268.2 15.8 %collective-permute-start.70 = (bf16[512,512]{1,0:T(8,128)(2,1)S(1)}, bf16[512,512]{1,0:T(8,128)(2,1)S(1)}, u32[]{:S(2)}, u32[]{:S(2)}) collective-permute-start(bf16[512,512]{1,0:T(8,128)(2,1)S(1)} %get-tuple-element.655.refs_1_), channel_id=1, source_target_pairs={{8,16},{16,8},{9,17},{17,9},{10,18},{18,10},{11,19},{19,11},{12,20... | collective-permute-start | bytes 1572872 | tf_op jit(solution)/shard_map/ppermute | solution.py:921
  270.5 13.4 %collective-permute-start.67 = (bf16[128,1024]{1,0:T(8,128)(2,1)S(1)}, bf16[128,1024]{1,0:T(8,128)(2,1)S(1)}, u32[]{:S(2)}, u32[]{:S(2)}) collective-permute-start(bf16[128,1024]{1,0:T(8,128)(2,1)S(1)} %get-tuple-element.634.refs_0_), channel_id=1, source_target_pairs={{0,4},{1,5},{2,6},{3,7},{4,0},{5,1},{6,2},{7,3},{8,12},{9,13},{10,... | collective-permute-start | bytes 786440 | tf_op jit(solution)/shard_map/ppermute | solution.py:64
  271.4 12.5 %collective-permute-start.68 = (bf16[128,1024]{1,0:T(8,128)(2,1)S(1)}, bf16[128,1024]{1,0:T(8,128)(2,1)S(1)}, u32[]{:S(2)}, u32[]{:S(2)}) collective-permute-start(bf16[128,1024]{1,0:T(8,128)(2,1)S(1)} %get-tuple-element.634.refs_0_), channel_id=1, source_target_pairs={{0,6},{1,7},{2,4},{3,5},{4,2},{5,3},{6,0},{7,1},{8,14},{9,15},{10,... | collective-permute-start | bytes 786440 | tf_op jit(solution)/shard_map/ppermute | solution.py:64
  286.7 14.4 %collective-permute-start.72 = (bf16[512,512]{1,0:T(8,128)(2,1)S(1)}, bf16[512,512]{1,0:T(8,128)(2,1)S(1)}, u32[]{:S(2)}, u32[]{:S(2)}) collective-permute-start(bf16[512,512]{1,0:T(8,128)(2,1)S(1)} %get-tuple-element.732.b_ref), channel_id=1, source_target_pairs={{0,8},{24,16},{8,0},{16,24},{1,9},{25,17},{9,1},{17,25},{2,10},{26... | collective-permute-start | bytes 1572872 | tf_op jit(solution)/shard_map/ppermute | solution.py:921
  288.4 12.6 %collective-permute-start.73 = (bf16[512,512]{1,0:T(8,128)(2,1)S(1)}, bf16[512,512]{1,0:T(8,128)(2,1)S(1)}, u32[]{:S(2)}, u32[]{:S(2)}) collective-permute-start(bf16[512,512]{1,0:T(8,128)(2,1)S(1)} %get-tuple-element.667.refs_1_), channel_id=1, source_target_pairs={{8,16},{16,8},{9,17},{17,9},{10,18},{18,10},{11,19},{19,11},{12,20... | collective-permute-start | bytes 1572872 | tf_op jit(solution)/shard_map/ppermute | solution.py:921
  301.8 17.8 %collective-permute-start.77 = (bf16[512,512]{1,0:T(8,128)(2,1)S(1)}, bf16[512,512]{1,0:T(8,128)(2,1)S(1)}, u32[]{:S(2)}, u32[]{:S(2)}) collective-permute-start(bf16[512,512]{1,0:T(8,128)(2,1)S(1)} %get-tuple-element.750.b_ref), channel_id=1, source_target_pairs={{0,8},{24,16},{8,0},{16,24},{1,9},{25,17},{9,1},{17,25},{2,10},{26... | collective-permute-start | bytes 1572872 | tf_op jit(solution)/shard_map/ppermute | solution.py:921
  305.5 14.1 %collective-permute-start.78 = (bf16[512,512]{1,0:T(8,128)(2,1)S(1)}, bf16[512,512]{1,0:T(8,128)(2,1)S(1)}, u32[]{:S(2)}, u32[]{:S(2)}) collective-permute-start(bf16[512,512]{1,0:T(8,128)(2,1)S(1)} %get-tuple-element.681.refs_1_), channel_id=1, source_target_pairs={{8,16},{16,8},{9,17},{17,9},{10,18},{18,10},{11,19},{19,11},{12,20... | collective-permute-start | bytes 1572872 | tf_op jit(solution)/shard_map/ppermute | solution.py:921
  320.3 18.4 %collective-permute-start.82 = (bf16[512,512]{1,0:T(8,128)(2,1)S(1)}, bf16[512,512]{1,0:T(8,128)(2,1)S(1)}, u32[]{:S(2)}, u32[]{:S(2)}) collective-permute-start(bf16[512,512]{1,0:T(8,128)(2,1)S(1)} %get-tuple-element.751.b_ref), channel_id=1, source_target_pairs={{0,8},{24,16},{8,0},{16,24},{1,9},{25,17},{9,1},{17,25},{2,10},{26... | collective-permute-start | bytes 1572872 | tf_op jit(solution)/shard_map/ppermute | solution.py:921
  323.7 15.0 %collective-permute-start.83 = (bf16[512,512]{1,0:T(8,128)(2,1)S(1)}, bf16[512,512]{1,0:T(8,128)(2,1)S(1)}, u32[]{:S(2)}, u32[]{:S(2)}) collective-permute-start(bf16[512,512]{1,0:T(8,128)(2,1)S(1)} %get-tuple-element.698.refs_1_), channel_id=1, source_target_pairs={{8,16},{16,8},{9,17},{17,9},{10,18},{18,10},{11,19},{19,11},{12,20... | collective-permute-start | bytes 1572872 | tf_op jit(solution)/shard_map/ppermute | solution.py:921
  327.1 11.6 %collective-permute-start.80 = (bf16[128,1024]{1,0:T(8,128)(2,1)S(1)}, bf16[128,1024]{1,0:T(8,128)(2,1)S(1)}, u32[]{:S(2)}, u32[]{:S(2)}) collective-permute-start(bf16[128,1024]{1,0:T(8,128)(2,1)S(1)} %get-tuple-element.686.refs_0_.refs_3_), channel_id=1, source_target_pairs={{0,4},{1,5},{2,6},{3,7},{4,0},{5,1},{6,2},{7,3},{8,12},{9,13},{10,... | collective-permute-start | bytes 786440 | tf_op jit(solution)/shard_map/ppermute | solution.py:64
  339.4 12.2 %collective-permute-start.84 = (bf16[512,512]{1,0:T(8,128)(2,1)S(1)}, bf16[512,512]{1,0:T(8,128)(2,1)S(1)}, u32[]{:S(2)}, u32[]{:S(2)}) collective-permute-start(bf16[512,512]{1,0:T(8,128)(2,1)S(1)} %get-tuple-element.798.b_ref), channel_id=1, source_target_pairs={{0,8},{24,16},{8,0},{16,24},{1,9},{25,17},{9,1},{17,25},{2,10},{26... | collective-permute-start | bytes 1572872 | tf_op jit(solution)/shard_map/ppermute | solution.py:921
  352.4 17.2 %collective-permute-start.89 = (bf16[512,512]{1,0:T(8,128)(2,1)S(1)}, bf16[512,512]{1,0:T(8,128)(2,1)S(1)}, u32[]{:S(2)}, u32[]{:S(2)}) collective-permute-start(bf16[512,512]{1,0:T(8,128)(2,1)S(1)} %get-tuple-element.799.b_ref), channel_id=1, source_target_pairs={{0,8},{24,16},{8,0},{16,24},{1,9},{25,17},{9,1},{17,25},{2,10},{26... | collective-permute-start | bytes 1572872 | tf_op jit(solution)/shard_map/ppermute | solution.py:921
  355.4 14.2 %collective-permute-start.90 = (bf16[512,512]{1,0:T(8,128)(2,1)S(1)}, bf16[512,512]{1,0:T(8,128)(2,1)S(1)}, u32[]{:S(2)}, u32[]{:S(2)}) collective-permute-start(bf16[512,512]{1,0:T(8,128)(2,1)S(1)} %get-tuple-element.739.refs_1_), channel_id=1, source_target_pairs={{8,16},{16,8},{9,17},{17,9},{10,18},{18,10},{11,19},{19,11},{12,20... | collective-permute-start | bytes 1572872 | tf_op jit(solution)/shard_map/ppermute | solution.py:921
  370.3 17.9 %collective-permute-start.94 = (bf16[576,512]{1,0:T(8,128)(2,1)S(1)}, bf16[576,512]{1,0:T(8,128)(2,1)S(1)}, u32[]{:S(2)}, u32[]{:S(2)}) collective-permute-start(bf16[576,512]{1,0:T(8,128)(2,1)S(1)} %get-tuple-element.765.b_ref), channel_id=1, source_target_pairs={{0,8},{24,16},{8,0},{16,24},{1,9},{25,17},{9,1},{17,25},{2,10},{26... | collective-permute-start | bytes 1769480 | tf_op jit(solution)/shard_map/ppermute | solution.py:921
  372.3 15.8 %collective-permute-start.95 = (bf16[512,512]{1,0:T(8,128)(2,1)S(1)}, bf16[512,512]{1,0:T(8,128)(2,1)S(1)}, u32[]{:S(2)}, u32[]{:S(2)}) collective-permute-start(bf16[512,512]{1,0:T(8,128)(2,1)S(1)} %get-tuple-element.758.refs_1_), channel_id=1, source_target_pairs={{8,16},{16,8},{9,17},{17,9},{10,18},{18,10},{11,19},{19,11},{12,20... | collective-permute-start | bytes 1572872 | tf_op jit(solution)/shard_map/ppermute | solution.py:921
  375.8 12.4 %collective-permute-start.93 = (bf16[128,1024]{1,0:T(8,128)(2,1)S(1)}, bf16[128,1024]{1,0:T(8,128)(2,1)S(1)}, u32[]{:S(2)}, u32[]{:S(2)}) collective-permute-start(bf16[128,1024]{1,0:T(8,128)(2,1)S(1)} %get-tuple-element.736), channel_id=1, source_target_pairs={{0,6},{1,7},{2,4},{3,5},{4,2},{5,3},{6,0},{7,1},{8,14},{9,15},{10,... | collective-permute-start | bytes 786440 | tf_op jit(solution)/shard_map/ppermute | solution.py:64
  388.9 15.0 %collective-permute-start.99 = (bf16[576,512]{1,0:T(8,128)(2,1)S(1)}, bf16[576,512]{1,0:T(8,128)(2,1)S(1)}, u32[]{:S(2)}, u32[]{:S(2)}) collective-permute-start(bf16[576,512]{1,0:T(8,128)(2,1)S(1)} %get-tuple-element.767.b_ref), channel_id=1, source_target_pairs={{0,8},{24,16},{8,0},{16,24},{1,9},{25,17},{9,1},{17,25},{2,10},{26... | collective-permute-start | bytes 1769480 | tf_op jit(solution)/shard_map/ppermute | solution.py:921
  391.5 12.4 %collective-permute-start.100 = (bf16[576,512]{1,0:T(8,128)(2,1)S(1)}, bf16[576,512]{1,0:T(8,128)(2,1)S(1)}, u32[]{:S(2)}, u32[]{:S(2)}) collective-permute-start(bf16[576,512]{1,0:T(8,128)(2,1)S(1)} %get-tuple-element.772.refs_0_), channel_id=1, source_target_pairs={{8,16},{16,8},{9,17},{17,9},{10,18},{18,10},{11,19},{19,11},{12,20... | collective-permute-start | bytes 1769480 | tf_op jit(solution)/shard_map/ppermute | solution.py:921
  404.7 16.5 %collective-permute-start.104 = (bf16[576,512]{1,0:T(8,128)(2,1)S(1)}, bf16[576,512]{1,0:T(8,128)(2,1)S(1)}, u32[]{:S(2)}, u32[]{:S(2)}) collective-permute-start(bf16[576,512]{1,0:T(8,128)(2,1)S(1)} %get-tuple-element.778.b_ref), channel_id=1, source_target_pairs={{8,0},{16,24},{9,1},{17,25},{10,2},{18,26},{11,3},{19,27},{12,4},{... | collective-permute-start | bytes 1769480 | tf_op jit(solution)/shard_map/ppermute | solution.py:921
  406.0 15.2 %collective-permute-start.105 = (bf16[576,512]{1,0:T(8,128)(2,1)S(1)}, bf16[576,512]{1,0:T(8,128)(2,1)S(1)}, u32[]{:S(2)}, u32[]{:S(2)}) collective-permute-start(bf16[576,512]{1,0:T(8,128)(2,1)S(1)} %get-tuple-element.783.refs_0_), channel_id=1, source_target_pairs={{8,16},{16,8},{9,17},{17,9},{10,18},{18,10},{11,19},{19,11},{12,20... | collective-permute-start | bytes 1769480 | tf_op jit(solution)/shard_map/ppermute | solution.py:921
  408.5 11.8 %collective-permute-start.102 = (bf16[128,1024]{1,0:T(8,128)(2,1)S(1)}, bf16[128,1024]{1,0:T(8,128)(2,1)S(1)}, u32[]{:S(2)}, u32[]{:S(2)}) collective-permute-start(bf16[128,1024]{1,0:T(8,128)(2,1)S(1)} %get-tuple-element.770), channel_id=1, source_target_pairs={{0,4},{1,5},{2,6},{3,7},{4,0},{5,1},{6,2},{7,3},{8,12},{9,13},{10,... | collective-permute-start | bytes 786440 | tf_op jit(solution)/shard_map/ppermute | solution.py:64
  421.4 26.7 %collective-permute-start.110 = (bf16[576,512]{1,0:T(8,128)(2,1)S(1)}, bf16[576,512]{1,0:T(8,128)(2,1)S(1)}, u32[]{:S(2)}, u32[]{:S(2)}) collective-permute-start(bf16[576,512]{1,0:T(8,128)(2,1)S(1)} %turn.25.b_ref), channel_id=1, source_target_pairs={{8,0},{16,24},{9,1},{17,25},{10,2},{18,26},{11,3},{19,27},{12,4},{... | collective-permute-start | bytes 1769480 | tf_op jit(solution)/shard_map/ppermute | solution.py:921
  422.7 15.0 %collective-permute-start.106 = (bf16[256,1024]{1,0:T(8,128)(2,1)S(1)}, bf16[256,1024]{1,0:T(8,128)(2,1)S(1)}, u32[]{:S(2)}, u32[]{:S(2)}) collective-permute-start(bf16[256,1024]{1,0:T(8,128)(2,1)S(1)} %pad_maximum_fusion), channel_id=1, source_target_pairs={{0,0},{1,1},{10,2},{11,3},{20,4},{21,5},{30,6},{31,7},{16,8},{17,9... | collective-permute-start | bytes 1572872 | tf_op jit(solution)/shard_map/ppermute | solution.py:43
  448.1 21.9 %collective-permute-start.111 = (bf16[256,1024]{1,0:T(8,128)(2,1)S(1)}, bf16[256,1024]{1,0:T(8,128)(2,1)S(1)}, u32[]{:S(2)}, u32[]{:S(2)}) collective-permute-start(bf16[256,1024]{1,0:T(8,128)(2,1)S(1)} %collective-permute-done.106), channel_id=1, source_target_pairs={{0,0},{1,1},{2,2},{3,3},{4,4},{5,5},{6,6},{7,7},{8,12},{9,13},{10,... | collective-permute-start | bytes 1572872 | tf_op jit(solution)/shard_map/ppermute | solution.py:43
  450.6 12.1 %collective-permute-start.112 = (bf16[144,256]{1,0:T(8,128)(2,1)S(1)}, bf16[144,256]{1,0:T(8,128)(2,1)S(1)}, u32[]{:S(2)}, u32[]{:S(2)}) collective-permute-start(bf16[144,256]{1,0:T(8,128)(2,1)S(1)} %get-tuple-element.793), channel_id=1, source_target_pairs={{0,2},{1,3},{2,0},{3,1},{4,6},{5,7},{6,4},{7,5},{8,10},{9,11},{10,... | collective-permute-start | bytes 221192 | tf_op jit(solution)/shard_map/ppermute | solution.py:64
  453.4 11.6 %collective-permute-start.113 = (bf16[144,256]{1,0:T(8,128)(2,1)S(1)}, bf16[144,256]{1,0:T(8,128)(2,1)S(1)}, u32[]{:S(2)}, u32[]{:S(2)}) collective-permute-start(bf16[144,256]{1,0:T(8,128)(2,1)S(1)} %get-tuple-element.794), channel_id=1, source_target_pairs={{0,4},{1,5},{2,6},{3,7},{4,0},{5,1},{6,2},{7,3},{8,12},{9,13},{10,... | collective-permute-start | bytes 221192 | tf_op jit(solution)/shard_map/ppermute | solution.py:64
  454.2 11.6 %collective-permute-start.114 = (bf16[144,256]{1,0:T(8,128)(2,1)S(1)}, bf16[144,256]{1,0:T(8,128)(2,1)S(1)}, u32[]{:S(2)}, u32[]{:S(2)}) collective-permute-start(bf16[144,256]{1,0:T(8,128)(2,1)S(1)} %get-tuple-element.795), channel_id=1, source_target_pairs={{0,6},{1,7},{2,4},{3,5},{4,2},{5,3},{6,0},{7,1},{8,14},{9,15},{10,... | collective-permute-start | bytes 221192 | tf_op jit(solution)/shard_map/ppermute | solution.py:64
  (130 other events, 1742.3 us)

commit v6 on v5

--- a/solution.py
+++ b/solution.py
@@ -53,12 +53,6 @@
 
     def to_plane(self, v):
         return self.send(v, [(s, q, p, q) for s, p, q in self.moves()])
-
-    def from_plane(self, v):
-        return self.send(v, [(p, q, s, q) for s, p, q in self.moves()])
-
-    def from_chip(self, v):
-        return self.send(v, [(s, q, s, p) for s, p, q in self.moves()])
 
     def chip(self, v, j):
         return lax.ppermute(v, "fsdp", xor_pairs(self.n_f, 2 * j))
@@ -233,9 +227,10 @@
 
 
 def pack_tokens(tokens, scene_ids, token_kind):
-    rows = tokens.shape[1]
+    half = tokens.shape[1] // 2
     code = (scene_ids * 2 + token_kind).astype(BF)
-    return jnp.pad(tokens[0], ((0, 16), (0, 0))) + jnp.pad(code, ((rows, 15), (0, D - rows)))
+    code = jnp.pad(code, ((half, 15), (0, D - 2 * half)))
+    return tokens[0, :half], jnp.pad(tokens[0, half:], ((0, 16), (0, 0))) + code
 
 
 def pack_small(vectors):
@@ -248,13 +243,15 @@
     return total
 
 
-def put_small(tokens, own, other):
-    rows = tokens.shape[0] - 16
+def put_small(first, second, own, other):
+    mid = first.shape[0]
+    rows = 2 * mid
     width = own.shape[1] // 2
 
-    def body(token_ref, own_ref, other_ref, out, lines):
-        out[0:rows, :] = token_ref[0:rows, :]
-        lines[...] = token_ref[rows:, :].astype(F32)
+    def body(first_ref, second_ref, own_ref, other_ref, out, lines):
+        out[0:mid, :] = first_ref[...]
+        out[mid:rows, :] = second_ref[0:mid, :]
+        lines[...] = second_ref[mid:, :].astype(F32)
         row = 1
         for ref in (own_ref, other_ref):
             low = ref[...].astype(F32)
@@ -265,7 +262,8 @@
         out[rows:, :] = lines[...].astype(BF)
 
     scratch = [pltpu.VMEM((16, D), F32)]
-    return run("put_small", body, [(tokens.shape, BF)], [tokens, own, other], None, scratch)[0]
+    outs = [((rows + 16, D), BF)]
+    return run("put_small", body, outs, [first, second, own, other], None, scratch)[0]
 
 
 def join_vectors(net, layers, blocks, sizes, rows):
@@ -667,7 +665,8 @@
     tokens, width = dqkv.shape
     cw = D // n_p
     rows = D // net.n_f
-    extra = 16 if small else 0
+    lines_each = 2 * len(small[1]) if small else 0
+    extra = n_p * lines_each
     flat = [v for of_layer in small[1] for v in of_layer] if small else []
     sizes = small[0] if small else []
     starts = [sum(sizes[:i]) for i in range(len(sizes))]
@@ -700,30 +699,31 @@
     def body(place, *refs):
         dqkv_ref, attended_ref = refs[n_a : n_a + 2]
         smalls = refs[n_a + 2 + n_p : n_a + 2 + n_p + len(flat)]
-        out, a, b, low, lines = refs[n_a + 2 + n_p + len(flat) :]
+        out, a, b, low, lines, under = refs[n_a + 2 + n_p + len(flat) :]
         c = place[1]
         gather_rows(refs[:n_a], a)
         for k, core in ((0, c), (1, 1 - c)):
             both = dot_tn(a[:, k * (D // 2) : (k + 1) * (D // 2)], dqkv_ref[...]).astype(BF)
             for i in range(n_p):
-                out[core, i * (rows + extra) : i * (rows + extra) + rows, :width] = both[i * rows : (i + 1) * rows]
+                out[core, i * rows : (i + 1) * rows, :width] = both[i * rows : (i + 1) * rows]
         gather_rows(refs[n_a + 2 : n_a + 2 + n_p], b)
         low[...] = dot_tn(attended_ref[...], b[...]).astype(BF)
         for core in range(2):
             for i in range(n_p):
-                here = slice(i * (rows + extra), i * (rows + extra) + rows)
+                here = slice(i * rows, (i + 1) * rows)
                 out[core, here, width:] = low[core * rows : (core + 1) * rows, i * cw : (i + 1) * cw]
         if extra:
             put_small(place, smalls, lines)
             for core in range(2):
                 for i in range(n_p):
-                    here = slice(i * (rows + extra) + rows, (i + 1) * (rows + extra))
-                    out[core, here, :width] = lines[core, i].astype(BF)
-                    out[core, here, width:] = jnp.zeros((extra, cw), BF)
-
-    outs = [((2, n_p * (rows + extra), width + cw), BF)]
+                    for r in range(lines_each):
+                        under[i * lines_each + r : i * lines_each + r + 1, :] = lines[core, i, r : r + 1, :]
+                out[core, n_p * rows :, :width] = under[...].astype(BF)
+                out[core, n_p * rows :, width:] = jnp.zeros((extra, cw), BF)
+
+    outs = [((2, n_p * rows + extra, width + cw), BF)]
     scratch = [pltpu.VMEM((tokens, D), BF), pltpu.VMEM((tokens, D), BF), pltpu.VMEM((cw, D), BF)]
-    scratch.append(pltpu.VMEM((2, n_p, 16, width), F32))
+    scratch += [pltpu.VMEM((2, n_p, 8, width), F32), pltpu.VMEM((max(extra, 8), width), F32)]
     flops = 2 * tokens * D * (width + cw)
     ins = [*a1, dqkv, attended, *dy, *[v for v, _ in flat]]
     return run("attend_weight_grad", body, outs, ins, net.place, scratch, flops=flops)[0]
@@ -755,68 +755,54 @@
 
 def cut_rows(net, first, second, extra):
     n_p = net.n_p
-    rows = first.shape[0] // n_p
+    split = extra is not None
+    under = extra or 0
+    rows = (first.shape[0] - under) // n_p
     width, more = first.shape[1], second.shape[1]
-    split = extra is not None
     taken = more // 2 if split else more
 
     def body(place, a, b, *outs):
         p = place[0]
         for j in range(n_p):
             here = tile(p ^ j, rows)
-            outs[j][:, :width] = a[here, :]
-            outs[j][:, width:] = b[here, :taken]
+            outs[j][0:rows, :width] = a[here, :]
+            outs[j][0:rows, width:] = b[here, :taken]
+            if under:
+                outs[j][rows:, :width] = a[n_p * rows :, :]
+                outs[j][rows:, width:] = b[n_p * rows :, :taken]
         if split:
             for i in range(n_p):
-                outs[n_p][:, i * taken : (i + 1) * taken] = b[i * rows : (i + 1) * rows - extra, taken:]
-
-    outs = [((rows, width + taken), BF)] * n_p
+                outs[n_p][:, i * taken : (i + 1) * taken] = b[i * rows : (i + 1) * rows, taken:]
+
+    outs = [((rows + under, width + taken), BF)] * n_p
     if split:
-        outs.append(((rows - extra, n_p * taken), BF))
+        outs.append(((rows, n_p * taken), BF))
     return run("cut_rows", body, outs, [first, second], net.place)
 
 
-def cut_part(net, v, groups, extra=None):
-    n_p = net.n_p
-    rows = v.shape[0] // n_p
-    taken = groups * (D // n_p)
-    rest = v.shape[1] - taken
-
-    def body(place, ref, *outs):
-        p = place[0]
-        for j in range(n_p):
-            outs[j][...] = ref[tile(p ^ j, rows), :taken]
-        if extra is not None:
-            for i in range(n_p):
-                outs[n_p][:, i * rest : (i + 1) * rest] = ref[i * rows : (i + 1) * rows - extra, taken:]
-
-    outs = [((rows, taken), BF)] * n_p
-    if extra is not None:
-        outs.append(((rows - extra, n_p * rest), BF))
-    return run("cut_part", body, outs, [v], net.place)
-
-
-def sum_small(layers, first, second, sizes, rows):
-    count = len(first)
-    split = first[0].shape[1]
-    width = split + second[0].shape[1]
+def sum_small(net, layers, pieces, sizes, rows, more):
+    width = pieces[0].shape[1]
+    count = len(pieces)
     starts = [sum(sizes[:i]) for i in range(len(sizes))]
 
-    def body(*refs):
-        parts = []
-        for group in (refs[:count], refs[count : 2 * count]):
-            total = group[0][rows:, :].astype(F32)
-            for ref in group[1:]:
-                total = total + ref[rows:, :].astype(F32)
-            parts.append(total)
-        total = jnp.concatenate(parts, axis=1)
-        for out, at, size in zip(refs[2 * count :], starts, sizes):
+    def body(place, *refs):
+        every = refs[0][rows:, :].astype(F32)
+        for ref in refs[1:count]:
+            every = every + ref[rows:, :].astype(F32)
+        total = jnp.zeros((2 * layers, width), F32)
+        for i in range(net.n_p):
+            total = jnp.where(place[0] == i, every[i * 2 * layers : (i + 1) * 2 * layers], total)
+        outs = refs[count + len(more) :]
+        for out, at, size in zip(outs, starts, sizes):
             half = at // width
             for layer in range(layers):
                 row = 2 * layer + half
                 out[layer : layer + 1, :] = total[row : row + 1, at - half * width : at - half * width + size]
-
-    return run("sum_small", body, [((layers, size), F32) for size in sizes], [*first, *second])
+        for ref, out in zip(refs[count : count + len(more)], outs[len(sizes) :]):
+            out[...] = ref[...].astype(F32)
+
+    outs = [((layers, size), F32) for size in sizes] + [(v.shape, F32) for v in more]
+    return run("sum_small", body, outs, [*pieces, *more], net.place)
 
 
 def take_if(here, a, b, rows):
@@ -978,6 +964,7 @@
         ins = ins + list(before)
     shapes = [(rows, 3 * D), (rows, D), (rows, FF), (down_rows, D)]
     sizes = [part, part, part, down_part]
+    moved = 6 * sum(a * b for a, b in shapes)
     return pl.pallas_call(
         body,
         grid=(steps,),
@@ -988,6 +975,7 @@
         ],
         input_output_aliases=aliases,
         compiler_params=pltpu.CompilerParams(vmem_limit_bytes=16 << 20),
+        cost_estimate=pl.CostEstimate(flops=0, bytes_accessed=moved, transcendentals=0),
         name="write_layer",
     )(net.place, *ins)
 
@@ -1029,14 +1017,15 @@
 
     small_in = [first_gain, first_shift, qv_bias, proj_bias, second_gain, second_shift, up_bias, down_bias]
     sizes = [v.shape[1] for v in small_in]
-    tok = net.to_place(pack_tokens(tokens, scene_ids, token_kind))
+    tok, tok_rest = pack_tokens(tokens, scene_ids, token_kind)
+    tok, tok_rest = net.to_plane(net.to_chip(tok)), net.to_place(tok_rest)
     mine = fetch(0, (qkv_weight, 3), (proj_weight, None))
     small = pack_small(small_in)
     small_other = net.core(small)
     later = (qkv_weight, proj_weight, up_weight, down_weight, out_grad)
-    tok, mine, small, small_other, later = fence((tok, mine, small, small_other, later))
+    tok, tok_rest, mine, small, small_other, later = fence((tok, tok_rest, mine, small, small_other, later))
     qkv_weight, proj_weight, up_weight, down_weight, out_grad = later
-    tokg = net.gather(put_small(tok, small, small_other))
+    tokg = net.gather(put_small(tok, tok_rest, small, small_other))
     theirs = net.next_plane(mine)
     tokg, mine, theirs = fence((tokg, mine, theirs))
 
@@ -1112,12 +1101,7 @@
         dyg = flow.collect(dyg, up_g[0])
         tokens_in = tokg if layer == 0 else []
         da1, dqkv, qkv_b_grad, norm_sums = attend_back(net, dyg, proj_w, qkv, codes, qkv_w, tokens_in)
-        if last:
-            last_parts = net.exchange(last_y)
-            da1, dqkv, last_parts = flow.collect((da1, dqkv, last_parts), up_g[1])
-            _, sent_out = close_layer(net, layer, h2, last_parts, down_b)
-        else:
-            da1, dqkv = flow.collect((da1, dqkv), up_g[1])
+        da1, dqkv = flow.collect((da1, dqkv), up_g[1])
         parts = net.exchange(da1)
         names = [None, None, "heads", None, None, None, "chip", None]
         of_layer = [None, None, qkv_b_grad, sums2[2:3], sums2[0:1], sums2[1:2], up_b_grad, down_b_grad]
@@ -1144,31 +1128,24 @@
         *pieces, rest = [*cut_rows(net, *[c.value for c in chunks], extra), None][: n_p + 1]
         return net.exchange(pieces), rest
 
+    last_parts = net.exchange(last_y)
+    dm, last_parts = flow.collect((dm, last_parts), attend_g[1])
+    _, sent_out = close_layer(net, layers - 1, kept[-1][4], last_parts, down_b)
     up_pieces, _ = to_owners(sums[1][1], None)
-    dm, up_pieces = flow.collect((dm, up_pieces), attend_g[1])
+    dm, up_pieces = flow.collect((dm, up_pieces))
     qkv_pieces, proj_g = to_owners(sums[1][2], 0)
     dm, sent_out, qkv_pieces, proj_g = flow.collect((dm, sent_out, qkv_pieces, proj_g))
-    both_out = jnp.concatenate([dm, sent_out], axis=0)
-    up_last = None
-    first_part = None
+    while [c for c in flow.queue if c in sums[0][1]]:
+        dm = flow.collect(dm)
+    up_last, _ = to_owners(sums[0][1], None)
+    dm, sent_out, up_last = flow.collect((dm, sent_out, up_last))
     while flow.queue:
-        if up_last is None and not [c for c in flow.queue if c in sums[0][1]]:
-            up_last, _ = to_owners(sums[0][1], None)
-            both_out, up_last = flow.collect((both_out, up_last))
-        elif up_last is not None and first_part is None and attend_g[0] not in flow.queue:
-            first_part = net.exchange(cut_part(net, attend_g[0].value, 2))
-            both_out = net.from_plane(both_out)
-            both_out, first_part = flow.collect((both_out, first_part))
-        else:
-            both_out = flow.collect(both_out)
-    both_out = net.from_chip(both_out).astype(F32)
-    input_grad, sent_out = both_out[:rows], both_out[rows:]
-    *pieces, proj_last = cut_part(net, attend_g[1].value, 1, 16)
-    second_part = net.exchange(pieces)
+        dm = flow.collect(dm)
+    pieces, proj_last = to_owners(sums[0][2], 2 * layers * n_p)
+    dm, sent_out = net.from_place(dm), net.from_place(sent_out)
     out = write_layer(net, 1, layers, None, [c.value for c in sums[1][0]], proj_g, up_pieces, qkv_pieces)
-    small_out = sum_small(layers, first_part, second_part, sizes, D // net.n_f)
-    qkv_pieces = list(zip(first_part, second_part))
-    out = write_layer(net, 0, layers, out, [c.value for c in sums[0][0]], proj_last, up_last, qkv_pieces)
+    *small_out, input_grad, sent_out = sum_small(net, layers, pieces, sizes, D // net.n_f, [dm, sent_out])
+    out = write_layer(net, 0, layers, out, [c.value for c in sums[0][0]], proj_last, up_last, pieces)
     return (
         sent_out[None],
         input_grad[None],

time: 480 us -> 466 us (0.971)
  the two profiles are of different devices: /device:TPU:26 before, /device:TPU:16 now
where the time goes in v6:
time: 466 us; the launch traced here: 457 us
  waiting for transfers between devices  163 us (35%)
  starting transfers between devices  153 us (33%)
  Pallas kernels  110 us (24%)
  blocking collectives  21.7 us (5%)
  local copies, waits for them, and re-layouts  6.08 us (1%)
    ppermute x66, waiting for transfers between devices, chip(): return lax.ppermute(v, 'fsdp', xor_pairs(self.n_f, 2 * j))  148 us
    pallas_call x73, Pallas kernels, run(): pl.pallas_call(body, out_shape=[jax.ShapeDtypeStruct(shape, dtype) for sh...  103 us
    ppermute x66, starting transfers between devices, chip(): return lax.ppermute(v, 'fsdp', xor_pairs(self.n_f, 2 * j))  79.1 us
    ppermute x26, starting transfers between devices, start(): lax.ppermute(v, 'seq', m[3])  44.2 us
    all_to_all x4, blocking collectives, swap_cores(): return lax.all_to_all(both, 'fsdp', 0, 0, axis_index_groups=pair_groups)  21.7 us
    ppermute x7, starting transfers between devices, send(): return lax.ppermute(v, ('seq', 'fsdp'), pairs)  20.8 us
  transfers between devices with their start and end apart: 114, of which 45 were waited for; matrix products, arithmetic and copies ran while one was open for 0% of the time, Pallas kernels for 19%

profile of v6, /device:TPU:16, one launch (start us, length us, event | category | flops | bytes accessed | tf_op | source)
XLA Modules:
  0.0 456.9 jit_solution(4590814673883052775)
XLA Ops:
  1.8 4.4 collective-permute-start
  11.6 3.5 collective-permute-start.4
  15.6 3.0 collective-permute-start.1
  18.8 9.2 %collective-permute-done.4.refs_1_ = bf16[64,1792]{1,0:T(8,128)(2,1)S(1)} collective-permute-done((bf16[64,1792]{1,0:T(8,128)(2,1)S(1)}, bf16[64,1792]{1,0:T(8,128)(2,1)S(1)}, u32[]{:S(2)}, u32[]{:S(2)}) %collective-permute-start.4) | collective-permute-done | bytes 229408 | tf_op jit(solution)/shard_map/ppermute | solution.py:58
  31.6 3.3 collective-permute-start.9
  34.8 5.9 %collective-permute-done.7.refs_1_.refs_12_ = bf16[144,1024]{1,0:T(8,128)(2,1)S(1)} collective-permute-done((bf16[144,1024]{1,0:T(8,128)(2,1)S(1)}, bf16[144,1024]{1,0:T(8,128)(2,1)S(1)}, u32[]{:S(2)}, u32[]{:S(2)}) %collective-permute-start.7) | collective-permute-done | bytes 294944 | tf_op jit(solution)/shard_map/ppermute | solution.py:58
  40.7 4.6 %collective-permute-done.8.refs_2_.refs_13_ = bf16[144,1024]{1,0:T(8,128)(2,1)S(1)} collective-permute-done((bf16[144,1024]{1,0:T(8,128)(2,1)S(1)}, bf16[144,1024]{1,0:T(8,128)(2,1)S(1)}, u32[]{:S(2)}, u32[]{:S(2)}) %collective-permute-start.8) | collective-permute-done | bytes 294944 | tf_op jit(solution)/shard_map/ppermute | solution.py:58
  47.0 3.3 collective-permute-done.11.refs_6_.refs_10_
  55.1 5.3 %attend.2 = (s32[1,512]{1,0:T(1,128)S(1)}, s32[512,1]{1,0:T(8,128)S(1)}, bf16[512,1024]{1,0:T(8,128)(2,1)S(1)}, bf16[512,768]{1,0:T(8,128)(2,1)S(1)}, bf16[512,256]{1,0:T(8,128)(2,1)S(1)}) custom-call(s32[3]{0:T(128)S(1)} %pad_add_fusion.2.place, bf16[144,1024]{1,0:T(8,128)(2,1)S(1)} %put_small.1.refs_0_.refs_11_.hidden_ref, ...), custom_call_target="tpu_custom_call" | custom-call | flops 805306368 | bytes 2785292 | tf_op jit(solution)/shard_map/attend/pallas_call | solution.py:93
  65.7 5.8 %collective-permute-done.16.refs_5_ = bf16[512,256]{1,0:T(8,128)(2,1)S(1)} collective-permute-done((bf16[512,256]{1,0:T(8,128)(2,1)S(1)}, bf16[512,256]{1,0:T(8,128)(2,1)S(1)}, u32[]{:S(2)}, u32[]{:S(2)}) %collective-permute-start.16) | collective-permute-done | bytes 262176 | tf_op jit(solution)/shard_map/ppermute | solution.py:58
  71.4 4.8 %collective-permute-done.17.refs_6_ = bf16[512,256]{1,0:T(8,128)(2,1)S(1)} collective-permute-done((bf16[512,256]{1,0:T(8,128)(2,1)S(1)}, bf16[512,256]{1,0:T(8,128)(2,1)S(1)}, u32[]{:S(2)}, u32[]{:S(2)}) %collective-permute-start.17) | collective-permute-done | bytes 262176 | tf_op jit(solution)/shard_map/ppermute | solution.py:58
  78.6 2.7 close_attention.2
  86.6 4.1 feed_forward.2
  92.1 3.7 collective-permute-done.23.refs_1_
  101.4 5.8 %collective-permute-done.25.refs_1_ = bf16[128,1024]{1,0:T(8,128)(2,1)S(1)} collective-permute-done((bf16[128,1024]{1,0:T(8,128)(2,1)S(1)}, bf16[128,1024]{1,0:T(8,128)(2,1)S(1)}, u32[]{:S(2)}, u32[]{:S(2)}) %collective-permute-start.25) | collective-permute-done | bytes 262176 | tf_op jit(solution)/shard_map/ppermute | solution.py:58
  107.2 2.6 collective-permute-done.26.refs_2_
  118.5 5.7 %collective-permute-done.29.refs_1_ = bf16[128,1024]{1,0:T(8,128)(2,1)S(1)} collective-permute-done((bf16[128,1024]{1,0:T(8,128)(2,1)S(1)}, bf16[128,1024]{1,0:T(8,128)(2,1)S(1)}, u32[]{:S(2)}, u32[]{:S(2)}) %collective-permute-start.29) | collective-permute-done | bytes 262176 | tf_op jit(solution)/shard_map/ppermute | solution.py:58
  124.1 4.1 collective-permute-done.30.refs_2_
  130.1 4.1 collective-permute-start.37
  138.4 5.3 %attend.3 = (bf16[512,1024]{1,0:T(8,128)(2,1)S(1)}, bf16[512,768]{1,0:T(8,128)(2,1)S(1)}, bf16[512,256]{1,0:T(8,128)(2,1)S(1)}) custom-call(s32[3]{0:T(128)S(1)} %pad_add_fusion.2.place, bf16[128,1024]{1,0:T(8,128)(2,1)S(1)} %get-tuple-element.502.refs_0_, bf16[128,1024]{1,0:T(8,128)(2,1)S(1)} %collective-permute-done.29.refs_1_, ...), custom_call_target="tpu_custom_call" | custom-call | flops 805306368 | bytes 2658316 | tf_op jit(solution)/shard_map/attend/pallas_call | solution.py:93
  152.8 3.6 collective-permute-done.38.refs_5_
  156.4 2.8 collective-permute-done.39.refs_6_
  165.5 2.7 close_attention.3
  168.3 4.1 feed_forward.3
  172.4 4.9 %collective-permute-done.46.refs_2_ = bf16[128,1024]{1,0:T(8,128)(2,1)S(1)} collective-permute-done((bf16[128,1024]{1,0:T(8,128)(2,1)S(1)}, bf16[128,1024]{1,0:T(8,128)(2,1)S(1)}, u32[]{:S(2)}, u32[]{:S(2)}) %collective-permute-start.46) | collective-permute-done | bytes 262176 | tf_op jit(solution)/shard_map/ppermute | solution.py:58
  179.3 5.4 %feed_back.2 = (bf16[128,1024]{1,0:T(8,128)(2,1)S(1)}, bf16[128,1024]{1,0:T(8,128)(2,1)S(1)}, bf16[128,1024]{1,0:T(8,128)(2,1)S(1)}, bf16[128,1024]{1,0:T(8,128)...) custom-call(s32[3]{0:T(128)S(1)} %pad_add_fusion.2.place, ...), custom_call_target="tpu_custom_call" | custom-call | flops 2147483648 | bytes 7340044 | tf_op jit(solution)/shard_map/feed_back/pallas_call | solution.py:93
  192.5 5.4 %all_to_all.20.ref = bf16[2,512,1024]{2,1,0:T(8,128)(2,1)S(1)} all-to-all(bf16[2,512,1024]{2,1,0:T(8,128)(2,1)S(1)} %up_weight_grad.2), channel_id=1, replica_groups={{0,1},{2,3},{4,5},{6,7},{8,9},{10,11},{12,13},{14,15},{16,17},{18,19},{..., dimensions={0} | all-to-all | bytes 4194304 | tf_op jit(solution)/shard_map/all_to_all | solution.py:1016
  198.0 3.0 collective-permute-done.50.refs_2_
  214.0 5.7 %collective-permute-done.53.refs_1_.refs_4_ = bf16[128,1024]{1,0:T(8,128)(2,1)} collective-permute-done((bf16[128,1024]{1,0:T(8,128)(2,1)}, bf16[128,1024]{1,0:T(8,128)(2,1)}, u32[]{:S(2)}, u32[]{:S(2)}) %collective-permute-start.53) | collective-permute-done | bytes 262176 | tf_op jit(solution)/shard_map/ppermute | solution.py:58
  219.7 5.1 %collective-permute-done.54.refs_2_.refs_5_ = bf16[128,1024]{1,0:T(8,128)(2,1)} collective-permute-done((bf16[128,1024]{1,0:T(8,128)(2,1)}, bf16[128,1024]{1,0:T(8,128)(2,1)}, u32[]{:S(2)}, u32[]{:S(2)}) %collective-permute-start.54) | collective-permute-done | bytes 262176 | tf_op jit(solution)/shard_map/ppermute | solution.py:58
  228.2 3.3 collective-permute-start.59
  231.5 9.6 %attend_back.2 = (bf16[128,1024]{1,0:T(8,128)(2,1)S(1)}, bf16[128,1024]{1,0:T(8,128)(2,1)S(1)}, bf16[128,1024]{1,0:T(8,128)(2,1)S(1)}, bf16[128,1024]{1,0:T(8,12...) custom-call(s32[3]{0:T(128)S(1)} %pad_add_fusion.2.place, ...), custom_call_target="tpu_custom_call" | custom-call | flops 2147483648 | bytes 5509132 | tf_op jit(solution)/shard_map/attend_back/pallas_call | solution.py:93
  251.5 5.4 %all_to_all.21.ref = bf16[2,512,1024]{2,1,0:T(8,128)(2,1)S(1)} all-to-all(bf16[2,512,1024]{2,1,0:T(8,128)(2,1)S(1)} %attend_weight_grad.2), channel_id=1, replica_groups={{0,1},{2,3},{4,5},{6,7},{8,9},{10,11},{12,13},{14,15},{16,17},{18,19},{..., dimensions={0} | all-to-all | bytes 4194304 | tf_op jit(solution)/shard_map/all_to_all | solution.py:1016
  260.3 3.5 collective-permute-start.69
  267.3 5.7 %collective-permute-done.65.refs_1_ = bf16[128,1024]{1,0:T(8,128)(2,1)S(1)} collective-permute-done((bf16[128,1024]{1,0:T(8,128)(2,1)S(1)}, bf16[128,1024]{1,0:T(8,128)(2,1)S(1)}, u32[]{:S(2)}, u32[]{:S(2)}) %collective-permute-start.65) | collective-permute-done | bytes 262176 | tf_op jit(solution)/shard_map/ppermute | solution.py:58
  273.0 5.0 %collective-permute-done.67.refs_3_ = bf16[128,1024]{1,0:T(8,128)(2,1)S(1)} collective-permute-done((bf16[128,1024]{1,0:T(8,128)(2,1)S(1)}, bf16[128,1024]{1,0:T(8,128)(2,1)S(1)}, u32[]{:S(2)}, u32[]{:S(2)}) %collective-permute-start.67) | collective-permute-done | bytes 262176 | tf_op jit(solution)/shard_map/ppermute | solution.py:58
  280.9 3.1 collective-permute-start.72
  284.1 5.4 %feed_back.3 = (bf16[128,1024]{1,0:T(8,128)(2,1)S(1)}, bf16[128,1024]{1,0:T(8,128)(2,1)S(1)}, bf16[128,1024]{1,0:T(8,128)(2,1)S(1)}, bf16[128,1024]{1,0:T(8,128)...) custom-call(s32[3]{0:T(128)S(1)} %pad_add_fusion.2.place, ...), custom_call_target="tpu_custom_call" | custom-call | flops 2147483648 | bytes 7340044 | tf_op jit(solution)/shard_map/feed_back/pallas_call | solution.py:93
  289.8 5.4 %collective-permute-done.71.refs_4_.a_ref = bf16[512,512]{1,0:T(8,128)(2,1)S(1)} collective-permute-done((bf16[512,512]{1,0:T(8,128)(2,1)S(1)}, bf16[512,512]{1,0:T(8,128)(2,1)S(1)}, u32[]{:S(2)}, u32[]{:S(2)}) %collective-permute-start.71) | collective-permute-done | bytes 524320 | tf_op jit(solution)/shard_map/ppermute | solution.py:907
  298.0 3.1 collective-permute-start.77
  306.6 5.4 %all_to_all.22.ref = bf16[2,512,1024]{2,1,0:T(8,128)(2,1)S(1)} all-to-all(bf16[2,512,1024]{2,1,0:T(8,128)(2,1)S(1)} %up_weight_grad.3), channel_id=1, replica_groups={{0,1},{2,3},{4,5},{6,7},{8,9},{10,11},{12,13},{14,15},{16,17},{18,19},{..., dimensions={0} | all-to-all | bytes 4194304 | tf_op jit(solution)/shard_map/all_to_all | solution.py:1016
  312.0 3.0 collective-permute-done.75.refs_3_
  315.9 3.1 collective-permute-start.82
  324.1 5.0 %collective-permute-done.78.refs_1_.refs_4_ = bf16[128,1024]{1,0:T(8,128)(2,1)S(1)} collective-permute-done((bf16[128,1024]{1,0:T(8,128)(2,1)S(1)}, bf16[128,1024]{1,0:T(8,128)(2,1)S(1)}, u32[]{:S(2)}, u32[]{:S(2)}) %collective-permute-start.78) | collective-permute-done | bytes 262176 | tf_op jit(solution)/shard_map/ppermute | solution.py:58
  329.1 3.9 collective-permute-done.79.refs_2_.refs_5_
  333.9 3.2 collective-permute-start.84
  337.3 9.2 %attend_back.3 = (bf16[128,1024]{1,0:T(8,128)(2,1)S(1)}, bf16[128,1024]{1,0:T(8,128)(2,1)S(1)}, bf16[128,1024]{1,0:T(8,128)(2,1)S(1)}, bf16[128,1024]{1,0:T(8,12...) custom-call(s32[3]{0:T(128)S(1)} %pad_add_fusion.2.place, ...), custom_call_target="tpu_custom_call" | custom-call | flops 2147483648 | bytes 6688780 | tf_op jit(solution)/shard_map/attend_back/pallas_call | solution.py:93
  347.4 2.9 collective-permute-start.89
  355.9 5.5 %all_to_all.23.ref = bf16[2,528,1024]{2,1,0:T(8,128)(2,1)S(1)} all-to-all(bf16[2,528,1024]{2,1,0:T(8,128)(2,1)S(1)} %attend_weight_grad.3), channel_id=1, replica_groups={{0,1},{2,3},{4,5},{6,7},{8,9},{10,11},{12,13},{14,15},{16,17},{18,19},{..., dimensions={0} | all-to-all | bytes 4325376 | tf_op jit(solution)/shard_map/all_to_all | solution.py:1016
  364.5 2.9 collective-permute-start.94
  371.0 5.7 %collective-permute-done.90.refs_1_ = bf16[128,1024]{1,0:T(8,128)(2,1)S(1)} collective-permute-done((bf16[128,1024]{1,0:T(8,128)(2,1)S(1)}, bf16[128,1024]{1,0:T(8,128)(2,1)S(1)}, u32[]{:S(2)}, u32[]{:S(2)}) %collective-permute-start.90) | collective-permute-done | bytes 262176 | tf_op jit(solution)/shard_map/ppermute | solution.py:58
  376.7 5.2 %collective-permute-done.91.refs_2_ = bf16[128,1024]{1,0:T(8,128)(2,1)S(1)} collective-permute-done((bf16[128,1024]{1,0:T(8,128)(2,1)S(1)}, bf16[128,1024]{1,0:T(8,128)(2,1)S(1)}, u32[]{:S(2)}, u32[]{:S(2)}) %collective-permute-start.91) | collective-permute-done | bytes 262176 | tf_op jit(solution)/shard_map/ppermute | solution.py:58
  382.8 2.9 collective-permute-start.99
  390.0 5.8 %collective-permute-done.95.refs_4_ = bf16[128,1024]{1,0:T(8,128)(2,1)S(1)} collective-permute-done((bf16[128,1024]{1,0:T(8,128)(2,1)S(1)}, bf16[128,1024]{1,0:T(8,128)(2,1)S(1)}, u32[]{:S(2)}, u32[]{:S(2)}) %collective-permute-start.95) | collective-permute-done | bytes 262176 | tf_op jit(solution)/shard_map/ppermute | solution.py:58
  395.8 3.9 collective-permute-done.96.refs_5_
  402.3 3.0 collective-permute-start.104
  411.8 3.2 collective-permute-done.101.refs_9_
  420.9 3.3 collective-permute-done.105.refs_4_
  424.2 3.0 collective-permute-done.106.refs_5_
  428.4 3.5 collective-permute-start.112
  438.7 3.5 write_layer.2
  442.2 4.7 %collective-permute-done.109.refs_1_.refs_8_ = bf16[144,768]{1,0:T(8,128)(2,1)S(1)} collective-permute-done((bf16[144,768]{1,0:T(8,128)(2,1)S(1)}, bf16[144,768]{1,0:T(8,128)(2,1)S(1)}, u32[]{:S(2)}, u32[]{:S(2)}) %collective-permute-start.109) | collective-permute-done | bytes 221216 | tf_op jit(solution)/shard_map/ppermute | solution.py:58
  447.1 4.3 collective-permute-done.111.refs_3_.refs_10_
  451.4 3.5 write_layer.3
  (415 shorter events, 170.7 us)
Async XLA Ops:
  1.8 13.8 %collective-permute-start = (bf16[64,1024]{1,0:T(8,128)(2,1)S(1)}, bf16[64,1024]{1,0:T(8,128)(2,1)S(1)}, u32[]{:S(2)}, u32[]{:S(2)}) collective-permute-start(bf16[64,1024]{1,0:T(8,128)(2,1)S(1)} %get-tuple-element.823), channel_id=1, source_target_pairs={{0,0},{1,1},{2,2},{3,3},{4,4},{5,5},{6,6},{7,7},{12,8},{13,9},{14,... | collective-permute-start | bytes 393224 | tf_op jit(solution)/shard_map/ppermute | solution.py:43
  9.7 19.2 %collective-permute-start.2 = (bf16[80,1024]{1,0:T(8,128)(2,1)S(1)}, bf16[80,1024]{1,0:T(8,128)(2,1)S(1)}, u32[]{:S(2)}, u32[]{:S(2)}) collective-permute-start(bf16[80,1024]{1,0:T(8,128)(2,1)S(1)} %pad_add_fusion), channel_id=1, source_target_pairs={{0,0},{1,1},{2,10},{3,11},{4,20},{5,21},{6,30},{7,31},{12,16},{13,... | collective-permute-start | bytes 491528 | tf_op jit(solution)/shard_map/ppermute | solution.py:43
  11.6 16.4 %collective-permute-start.4 = (bf16[64,1792]{1,0:T(8,128)(2,1)S(1)}, bf16[64,1792]{1,0:T(8,128)(2,1)S(1)}, u32[]{:S(2)}, u32[]{:S(2)}) collective-permute-start(bf16[64,1792]{1,0:T(8,128)(2,1)S(1)} %get-tuple-element.419), channel_id=1, source_target_pairs={{0,4},{1,5},{2,6},{3,7},{4,0},{5,1},{6,2},{7,3},{8,12},{9,13},{10,... | collective-permute-start | bytes 688136 | tf_op jit(solution)/shard_map/ppermute | solution.py:58
  15.1 12.9 %collective-permute-start.5 = (bf16[64,1792]{1,0:T(8,128)(2,1)S(1)}, bf16[64,1792]{1,0:T(8,128)(2,1)S(1)}, u32[]{:S(2)}, u32[]{:S(2)}) collective-permute-start(bf16[64,1792]{1,0:T(8,128)(2,1)S(1)} %get-tuple-element.420), channel_id=1, source_target_pairs={{0,6},{1,7},{2,4},{3,5},{4,2},{5,3},{6,0},{7,1},{8,14},{9,15},{10,... | collective-permute-start | bytes 688136 | tf_op jit(solution)/shard_map/ppermute | solution.py:58
  15.6 13.4 %collective-permute-start.1 = (bf16[64,1024]{1,0:T(8,128)(2,1)S(1)}, bf16[64,1024]{1,0:T(8,128)(2,1)S(1)}, u32[]{:S(2)}, u32[]{:S(2)}) collective-permute-start(bf16[64,1024]{1,0:T(8,128)(2,1)S(1)} %collective-permute-done), channel_id=1, source_target_pairs={{0,0},{1,1},{2,10},{3,11},{4,20},{5,21},{6,30},{7,31},{8,16},{9,17... | collective-permute-start | bytes 393224 | tf_op jit(solution)/shard_map/ppermute | solution.py:43
  28.9 16.4 %collective-permute-start.10 = (bf16[192,1792]{1,0:T(8,128)(2,1)S(1)}, bf16[192,1792]{1,0:T(8,128)(2,1)S(1)}, u32[]{:S(2)}, u32[]{:S(2)}) collective-permute-start(bf16[192,1792]{1,0:T(8,128)(2,1)S(1)} %stack_halves.4.mine_ref), channel_id=1, source_target_pairs={{0,8},{8,0},{16,24},{24,16},{1,9},{9,1},{17,25},{25,17},{2,10},{10... | collective-permute-start | bytes 2064392 | tf_op jit(solution)/shard_map/ppermute | solution.py:64
  31.5 13.8 %collective-permute-start.8 = (bf16[144,1024]{1,0:T(8,128)(2,1)S(1)}, bf16[144,1024]{1,0:T(8,128)(2,1)S(1)}, u32[]{:S(2)}, u32[]{:S(2)}) collective-permute-start(bf16[144,1024]{1,0:T(8,128)(2,1)S(1)} %put_small.1.refs_0_.refs_11_.hidden_ref), channel_id=1, source_target_pairs={{0,4},{1,5},{2,6},{3,7},{4,0},{5,1},{6,2},{7,3},{8,12},{9,13},{10,... | collective-permute-start | bytes 884744 | tf_op jit(solution)/shard_map/ppermute | solution.py:58
  31.6 13.8 %collective-permute-start.9 = (bf16[144,1024]{1,0:T(8,128)(2,1)S(1)}, bf16[144,1024]{1,0:T(8,128)(2,1)S(1)}, u32[]{:S(2)}, u32[]{:S(2)}) collective-permute-start(bf16[144,1024]{1,0:T(8,128)(2,1)S(1)} %put_small.1.refs_0_.refs_11_.hidden_ref), channel_id=1, source_target_pairs={{0,6},{1,7},{2,4},{3,5},{4,2},{5,3},{6,0},{7,1},{8,14},{9,15},{10,... | collective-permute-start | bytes 884744 | tf_op jit(solution)/shard_map/ppermute | solution.py:58
  61.0 15.2 %collective-permute-start.19 = (bf16[192,1024]{1,0:T(8,128)(2,1)S(1)}, bf16[192,1024]{1,0:T(8,128)(2,1)S(1)}, u32[]{:S(2)}, u32[]{:S(2)}) collective-permute-start(bf16[192,1024]{1,0:T(8,128)(2,1)S(1)} %stack_halves.5.mine_ref), channel_id=1, source_target_pairs={{0,8},{8,0},{16,24},{24,16},{1,9},{9,1},{17,25},{25,17},{2,10},{10... | collective-permute-start | bytes 1179656 | tf_op jit(solution)/shard_map/ppermute | solution.py:64
  63.7 12.6 %collective-permute-start.17 = (bf16[512,256]{1,0:T(8,128)(2,1)S(1)}, bf16[512,256]{1,0:T(8,128)(2,1)S(1)}, u32[]{:S(2)}, u32[]{:S(2)}) collective-permute-start(bf16[512,256]{1,0:T(8,128)(2,1)S(1)} %get-tuple-element.457.refs_4_.refs_2_), channel_id=1, source_target_pairs={{0,4},{1,5},{2,6},{3,7},{4,0},{5,1},{6,2},{7,3},{8,12},{9,13},{10,... | collective-permute-start | bytes 786440 | tf_op jit(solution)/shard_map/ppermute | solution.py:58
  63.9 12.3 %collective-permute-start.18 = (bf16[512,256]{1,0:T(8,128)(2,1)S(1)}, bf16[512,256]{1,0:T(8,128)(2,1)S(1)}, u32[]{:S(2)}, u32[]{:S(2)}) collective-permute-start(bf16[512,256]{1,0:T(8,128)(2,1)S(1)} %get-tuple-element.457.refs_4_.refs_2_), channel_id=1, source_target_pairs={{0,6},{1,7},{2,4},{3,5},{4,2},{5,3},{6,0},{7,1},{8,14},{9,15},{10,... | collective-permute-start | bytes 786440 | tf_op jit(solution)/shard_map/ppermute | solution.py:58
  83.5 12.3 %collective-permute-start.23 = (bf16[64,1792]{1,0:T(8,128)(2,1)S(1)}, bf16[64,1792]{1,0:T(8,128)(2,1)S(1)}, u32[]{:S(2)}, u32[]{:S(2)}) collective-permute-start(bf16[64,1792]{1,0:T(8,128)(2,1)S(1)} %get-tuple-element.486), channel_id=1, source_target_pairs={{0,4},{1,5},{2,6},{3,7},{4,0},{5,1},{6,2},{7,3},{8,12},{9,13},{10,... | collective-permute-start | bytes 688136 | tf_op jit(solution)/shard_map/ppermute | solution.py:58
  96.7 16.4 %collective-permute-start.28 = (bf16[192,1792]{1,0:T(8,128)(2,1)S(1)}, bf16[192,1792]{1,0:T(8,128)(2,1)S(1)}, u32[]{:S(2)}, u32[]{:S(2)}) collective-permute-start(bf16[192,1792]{1,0:T(8,128)(2,1)S(1)} %stack_halves.6.mine_ref), channel_id=1, source_target_pairs={{0,8},{8,0},{16,24},{24,16},{1,9},{9,1},{17,25},{25,17},{2,10},{10... | collective-permute-start | bytes 2064392 | tf_op jit(solution)/shard_map/ppermute | solution.py:64
  99.6 11.7 %collective-permute-start.27 = (bf16[128,1024]{1,0:T(8,128)(2,1)S(1)}, bf16[128,1024]{1,0:T(8,128)(2,1)S(1)}, u32[]{:S(2)}, u32[]{:S(2)}) collective-permute-start(bf16[128,1024]{1,0:T(8,128)(2,1)S(1)} %get-tuple-element.491), channel_id=1, source_target_pairs={{0,6},{1,7},{2,4},{3,5},{4,2},{5,3},{6,0},{7,1},{8,14},{9,15},{10,... | collective-permute-start | bytes 786440 | tf_op jit(solution)/shard_map/ppermute | solution.py:58
  114.1 16.0 %collective-permute-start.33 = (bf16[512,1024]{1,0:T(8,128)(2,1)S(1)}, bf16[512,1024]{1,0:T(8,128)(2,1)S(1)}, u32[]{:S(2)}, u32[]{:S(2)}) collective-permute-start(bf16[512,1024]{1,0:T(8,128)(2,1)S(1)} %get-tuple-element.527.refs_8_.refs_4_), channel_id=1, source_target_pairs={{0,1},{1,0},{2,3},{3,2},{4,5},{5,4},{6,7},{7,6},{8,9},{9,8},{10,11... | collective-permute-start | bytes 3145736 | tf_op jit(solution)/shard_map/ppermute | solution.py:61
  114.2 15.9 %collective-permute-start.32 = (bf16[512,768]{1,0:T(8,128)(2,1)S(1)}, bf16[512,768]{1,0:T(8,128)(2,1)S(1)}, u32[]{:S(2)}, u32[]{:S(2)}) collective-permute-start(bf16[512,768]{1,0:T(8,128)(2,1)S(1)} %get-tuple-element.506.refs_5_.refs_9_), channel_id=1, source_target_pairs={{0,1},{1,0},{2,3},{3,2},{4,5},{5,4},{6,7},{7,6},{8,9},{9,8},{10,11... | collective-permute-start | bytes 2359304 | tf_op jit(solution)/shard_map/ppermute | solution.py:61
  116.4 11.8 %collective-permute-start.30 = (bf16[128,1024]{1,0:T(8,128)(2,1)S(1)}, bf16[128,1024]{1,0:T(8,128)(2,1)S(1)}, u32[]{:S(2)}, u32[]{:S(2)}) collective-permute-start(bf16[128,1024]{1,0:T(8,128)(2,1)S(1)} %get-tuple-element.502.refs_0_), channel_id=1, source_target_pairs={{0,4},{1,5},{2,6},{3,7},{4,0},{5,1},{6,2},{7,3},{8,12},{9,13},{10,... | collective-permute-start | bytes 786440 | tf_op jit(solution)/shard_map/ppermute | solution.py:58
  117.1 13.0 %collective-permute-start.31 = (bf16[128,1024]{1,0:T(8,128)(2,1)S(1)}, bf16[128,1024]{1,0:T(8,128)(2,1)S(1)}, u32[]{:S(2)}, u32[]{:S(2)}) collective-permute-start(bf16[128,1024]{1,0:T(8,128)(2,1)S(1)} %get-tuple-element.502.refs_0_), channel_id=1, source_target_pairs={{0,6},{1,7},{2,4},{3,5},{4,2},{5,3},{6,0},{7,1},{8,14},{9,15},{10,... | collective-permute-start | bytes 786440 | tf_op jit(solution)/shard_map/ppermute | solution.py:58
  130.1 15.3 %collective-permute-start.37 = (bf16[128,1024]{1,0:T(8,128)(2,1)S(1)}, bf16[128,1024]{1,0:T(8,128)(2,1)S(1)}, u32[]{:S(2)}, u32[]{:S(2)}) collective-permute-start(bf16[128,1024]{1,0:T(8,128)(2,1)S(1)} %bitcast.13), channel_id=1, source_target_pairs={{0,0},{1,1},{2,2},{3,3},{4,4},{5,5},{6,6},{7,7},{12,8},{13,9},{14,... | collective-permute-start | bytes 786440 | tf_op jit(solution)/shard_map/ppermute | solution.py:43
  145.4 13.9 %collective-permute-start.41 = (bf16[192,1024]{1,0:T(8,128)(2,1)S(1)}, bf16[192,1024]{1,0:T(8,128)(2,1)S(1)}, u32[]{:S(2)}, u32[]{:S(2)}) collective-permute-start(bf16[192,1024]{1,0:T(8,128)(2,1)S(1)} %stack_halves.7.mine_ref), channel_id=1, source_target_pairs={{0,8},{8,0},{16,24},{24,16},{1,9},{9,1},{17,25},{25,17},{2,10},{10... | collective-permute-start | bytes 1179656 | tf_op jit(solution)/shard_map/ppermute | solution.py:64
  147.8 11.5 %collective-permute-start.39 = (bf16[512,256]{1,0:T(8,128)(2,1)S(1)}, bf16[512,256]{1,0:T(8,128)(2,1)S(1)}, u32[]{:S(2)}, u32[]{:S(2)}) collective-permute-start(bf16[512,256]{1,0:T(8,128)(2,1)S(1)} %get-tuple-element.523.refs_4_.refs_2_), channel_id=1, source_target_pairs={{0,4},{1,5},{2,6},{3,7},{4,0},{5,1},{6,2},{7,3},{8,12},{9,13},{10,... | collective-permute-start | bytes 786440 | tf_op jit(solution)/shard_map/ppermute | solution.py:58
  163.3 14.0 %collective-permute-start.46 = (bf16[128,1024]{1,0:T(8,128)(2,1)S(1)}, bf16[128,1024]{1,0:T(8,128)(2,1)S(1)}, u32[]{:S(2)}, u32[]{:S(2)}) collective-permute-start(bf16[128,1024]{1,0:T(8,128)(2,1)S(1)} %collective-permute-done.42.refs_0_.grad_ref.ref), channel_id=1, source_target_pairs={{0,4},{1,5},{2,6},{3,7},{4,0},{5,1},{6,2},{7,3},{8,12},{9,13},{10,... | collective-permute-start | bytes 786440 | tf_op jit(solution)/shard_map/ppermute | solution.py:58
  165.5 11.9 %collective-permute-start.47 = (bf16[128,1024]{1,0:T(8,128)(2,1)S(1)}, bf16[128,1024]{1,0:T(8,128)(2,1)S(1)}, u32[]{:S(2)}, u32[]{:S(2)}) collective-permute-start(bf16[128,1024]{1,0:T(8,128)(2,1)S(1)} %collective-permute-done.42.refs_0_.grad_ref.ref), channel_id=1, source_target_pairs={{0,6},{1,7},{2,4},{3,5},{4,2},{5,3},{6,0},{7,1},{8,14},{9,15},{10,... | collective-permute-start | bytes 786440 | tf_op jit(solution)/shard_map/ppermute | solution.py:58
  185.7 17.0 %collective-permute-start.52 = (bf16[512,512]{1,0:T(8,128)(2,1)S(1)}, bf16[512,512]{1,0:T(8,128)(2,1)S(1)}, u32[]{:S(2)}, u32[]{:S(2)}) collective-permute-start(bf16[512,512]{1,0:T(8,128)(2,1)S(1)} %get-tuple-element.570.refs_0_), channel_id=1, source_target_pairs={{0,8},{24,16},{1,9},{25,17},{2,10},{26,18},{3,11},{27,19},{4,12},{... | collective-permute-start | bytes 1572872 | tf_op jit(solution)/shard_map/ppermute | solution.py:907
  188.7 12.2 %collective-permute-start.50 = (bf16[128,1024]{1,0:T(8,128)(2,1)S(1)}, bf16[128,1024]{1,0:T(8,128)(2,1)S(1)}, u32[]{:S(2)}, u32[]{:S(2)}) collective-permute-start(bf16[128,1024]{1,0:T(8,128)(2,1)S(1)} %get-tuple-element.566), channel_id=1, source_target_pairs={{0,4},{1,5},{2,6},{3,7},{4,0},{5,1},{6,2},{7,3},{8,12},{9,13},{10,... | collective-permute-start | bytes 786440 | tf_op jit(solution)/shard_map/ppermute | solution.py:58
  189.2 13.5 %collective-permute-start.51 = (bf16[128,1024]{1,0:T(8,128)(2,1)S(1)}, bf16[128,1024]{1,0:T(8,128)(2,1)S(1)}, u32[]{:S(2)}, u32[]{:S(2)}) collective-permute-start(bf16[128,1024]{1,0:T(8,128)(2,1)S(1)} %get-tuple-element.567), channel_id=1, source_target_pairs={{0,6},{1,7},{2,4},{3,5},{4,2},{5,3},{6,0},{7,1},{8,14},{9,15},{10,... | collective-permute-start | bytes 786440 | tf_op jit(solution)/shard_map/ppermute | solution.py:58
  202.7 22.1 %collective-permute-start.56 = (bf16[512,512]{1,0:T(8,128)(2,1)}, bf16[512,512]{1,0:T(8,128)(2,1)}, u32[]{:S(2)}, u32[]{:S(2)}) collective-permute-start(bf16[512,512]{1,0:T(8,128)(2,1)} %get-tuple-element.579.refs_3_), channel_id=1, source_target_pairs={{0,8},{24,16},{1,9},{25,17},{2,10},{26,18},{3,11},{27,19},{4,12},{... | collective-permute-start | bytes 1572872 | tf_op jit(solution)/shard_map/ppermute | solution.py:907
  204.9 19.9 %collective-permute-start.57 = (bf16[512,512]{1,0:T(8,128)(2,1)}, bf16[512,512]{1,0:T(8,128)(2,1)}, u32[]{:S(2)}, u32[]{:S(2)}) collective-permute-start(bf16[512,512]{1,0:T(8,128)(2,1)} %turn.13.refs_1_), channel_id=1, source_target_pairs={{8,16},{16,8},{9,17},{17,9},{10,18},{18,10},{11,19},{19,11},{12,20... | collective-permute-start | bytes 1572872 | tf_op jit(solution)/shard_map/ppermute | solution.py:907
  211.6 13.3 %collective-permute-start.54 = (bf16[128,1024]{1,0:T(8,128)(2,1)}, bf16[128,1024]{1,0:T(8,128)(2,1)}, u32[]{:S(2)}, u32[]{:S(2)}) collective-permute-start(bf16[128,1024]{1,0:T(8,128)(2,1)} %get-tuple-element.581.refs_0_.refs_3_), channel_id=1, source_target_pairs={{0,4},{1,5},{2,6},{3,7},{4,0},{5,1},{6,2},{7,3},{8,12},{9,13},{10,... | collective-permute-start | bytes 786440 | tf_op jit(solution)/shard_map/ppermute | solution.py:58
  212.5 12.4 %collective-permute-start.55 = (bf16[128,1024]{1,0:T(8,128)(2,1)}, bf16[128,1024]{1,0:T(8,128)(2,1)}, u32[]{:S(2)}, u32[]{:S(2)}) collective-permute-start(bf16[128,1024]{1,0:T(8,128)(2,1)} %get-tuple-element.581.refs_0_.refs_3_), channel_id=1, source_target_pairs={{0,6},{1,7},{2,4},{3,5},{4,2},{5,3},{6,0},{7,1},{8,14},{9,15},{10,... | collective-permute-start | bytes 786440 | tf_op jit(solution)/shard_map/ppermute | solution.py:58
  226.6 14.6 %collective-permute-start.58 = (bf16[512,512]{1,0:T(8,128)(2,1)S(1)}, bf16[512,512]{1,0:T(8,128)(2,1)S(1)}, u32[]{:S(2)}, u32[]{:S(2)}) collective-permute-start(bf16[512,512]{1,0:T(8,128)(2,1)S(1)} %get-tuple-element.797.b_ref), channel_id=1, source_target_pairs={{0,8},{24,16},{8,0},{16,24},{1,9},{25,17},{9,1},{17,25},{2,10},{26... | collective-permute-start | bytes 1572872 | tf_op jit(solution)/shard_map/ppermute | solution.py:907
  228.2 13.9 %collective-permute-start.59 = (bf16[512,512]{1,0:T(8,128)(2,1)S(1)}, bf16[512,512]{1,0:T(8,128)(2,1)S(1)}, u32[]{:S(2)}, u32[]{:S(2)}) collective-permute-start(bf16[512,512]{1,0:T(8,128)(2,1)S(1)} %get-tuple-element.612.refs_1_), channel_id=1, source_target_pairs={{8,16},{16,8},{9,17},{17,9},{10,18},{18,10},{11,19},{19,11},{12,20... | collective-permute-start | bytes 1572872 | tf_op jit(solution)/shard_map/ppermute | solution.py:907
  242.9 16.2 %collective-permute-start.63 = (bf16[512,512]{1,0:T(8,128)(2,1)S(1)}, bf16[512,512]{1,0:T(8,128)(2,1)S(1)}, u32[]{:S(2)}, u32[]{:S(2)}) collective-permute-start(bf16[512,512]{1,0:T(8,128)(2,1)S(1)} %get-tuple-element.798.b_ref), channel_id=1, source_target_pairs={{0,8},{24,16},{8,0},{16,24},{1,9},{25,17},{9,1},{17,25},{2,10},{26... | collective-permute-start | bytes 1572872 | tf_op jit(solution)/shard_map/ppermute | solution.py:907
  243.0 16.1 %collective-permute-start.64 = (bf16[512,512]{1,0:T(8,128)(2,1)S(1)}, bf16[512,512]{1,0:T(8,128)(2,1)S(1)}, u32[]{:S(2)}, u32[]{:S(2)}) collective-permute-start(bf16[512,512]{1,0:T(8,128)(2,1)S(1)} %get-tuple-element.621.refs_1_), channel_id=1, source_target_pairs={{8,16},{16,8},{9,17},{17,9},{10,18},{18,10},{11,19},{19,11},{12,20... | collective-permute-start | bytes 1572872 | tf_op jit(solution)/shard_map/ppermute | solution.py:907
  245.4 11.5 %collective-permute-start.60 = (bf16[128,1024]{1,0:T(8,128)(2,1)S(1)}, bf16[128,1024]{1,0:T(8,128)(2,1)S(1)}, u32[]{:S(2)}, u32[]{:S(2)}) collective-permute-start(bf16[128,1024]{1,0:T(8,128)(2,1)S(1)} %get-tuple-element.599), channel_id=1, source_target_pairs={{0,2},{1,3},{2,0},{3,1},{4,6},{5,7},{6,4},{7,5},{8,10},{9,11},{10,... | collective-permute-start | bytes 786440 | tf_op jit(solution)/shard_map/ppermute | solution.py:58
  260.0 18.1 %collective-permute-start.68 = (bf16[512,512]{1,0:T(8,128)(2,1)S(1)}, bf16[512,512]{1,0:T(8,128)(2,1)S(1)}, u32[]{:S(2)}, u32[]{:S(2)}) collective-permute-start(bf16[512,512]{1,0:T(8,128)(2,1)S(1)} %get-tuple-element.736.b_ref), channel_id=1, source_target_pairs={{0,8},{24,16},{8,0},{16,24},{1,9},{25,17},{9,1},{17,25},{2,10},{26... | collective-permute-start | bytes 1572872 | tf_op jit(solution)/shard_map/ppermute | solution.py:907
  260.3 17.8 %collective-permute-start.69 = (bf16[512,512]{1,0:T(8,128)(2,1)S(1)}, bf16[512,512]{1,0:T(8,128)(2,1)S(1)}, u32[]{:S(2)}, u32[]{:S(2)}) collective-permute-start(bf16[512,512]{1,0:T(8,128)(2,1)S(1)} %get-tuple-element.648.refs_1_), channel_id=1, source_target_pairs={{8,16},{16,8},{9,17},{17,9},{10,18},{18,10},{11,19},{19,11},{12,20... | collective-permute-start | bytes 1572872 | tf_op jit(solution)/shard_map/ppermute | solution.py:907
  265.6 12.4 %collective-permute-start.67 = (bf16[128,1024]{1,0:T(8,128)(2,1)S(1)}, bf16[128,1024]{1,0:T(8,128)(2,1)S(1)}, u32[]{:S(2)}, u32[]{:S(2)}) collective-permute-start(bf16[128,1024]{1,0:T(8,128)(2,1)S(1)} %get-tuple-element.627.refs_0_), channel_id=1, source_target_pairs={{0,6},{1,7},{2,4},{3,5},{4,2},{5,3},{6,0},{7,1},{8,14},{9,15},{10,... | collective-permute-start | bytes 786440 | tf_op jit(solution)/shard_map/ppermute | solution.py:58
  280.9 14.4 %collective-permute-start.71 = (bf16[512,512]{1,0:T(8,128)(2,1)S(1)}, bf16[512,512]{1,0:T(8,128)(2,1)S(1)}, u32[]{:S(2)}, u32[]{:S(2)}) collective-permute-start(bf16[512,512]{1,0:T(8,128)(2,1)S(1)} %get-tuple-element.737.b_ref), channel_id=1, source_target_pairs={{0,8},{24,16},{8,0},{16,24},{1,9},{25,17},{9,1},{17,25},{2,10},{26... | collective-permute-start | bytes 1572872 | tf_op jit(solution)/shard_map/ppermute | solution.py:907
  280.9 16.2 %collective-permute-start.72 = (bf16[512,512]{1,0:T(8,128)(2,1)S(1)}, bf16[512,512]{1,0:T(8,128)(2,1)S(1)}, u32[]{:S(2)}, u32[]{:S(2)}) collective-permute-start(bf16[512,512]{1,0:T(8,128)(2,1)S(1)} %get-tuple-element.660.refs_1_), channel_id=1, source_target_pairs={{8,16},{16,8},{9,17},{17,9},{10,18},{18,10},{11,19},{19,11},{12,20... | collective-permute-start | bytes 1572872 | tf_op jit(solution)/shard_map/ppermute | solution.py:907
  298.0 17.1 %collective-permute-start.76 = (bf16[512,512]{1,0:T(8,128)(2,1)S(1)}, bf16[512,512]{1,0:T(8,128)(2,1)S(1)}, u32[]{:S(2)}, u32[]{:S(2)}) collective-permute-start(bf16[512,512]{1,0:T(8,128)(2,1)S(1)} %get-tuple-element.754.b_ref), channel_id=1, source_target_pairs={{0,8},{24,16},{8,0},{16,24},{1,9},{25,17},{9,1},{17,25},{2,10},{26... | collective-permute-start | bytes 1572872 | tf_op jit(solution)/shard_map/ppermute | solution.py:907
  298.0 17.0 %collective-permute-start.77 = (bf16[512,512]{1,0:T(8,128)(2,1)S(1)}, bf16[512,512]{1,0:T(8,128)(2,1)S(1)}, u32[]{:S(2)}, u32[]{:S(2)}) collective-permute-start(bf16[512,512]{1,0:T(8,128)(2,1)S(1)} %get-tuple-element.674.refs_1_), channel_id=1, source_target_pairs={{8,16},{16,8},{9,17},{17,9},{10,18},{18,10},{11,19},{19,11},{12,20... | collective-permute-start | bytes 1572872 | tf_op jit(solution)/shard_map/ppermute | solution.py:907
  303.0 12.0 %collective-permute-start.75 = (bf16[128,1024]{1,0:T(8,128)(2,1)S(1)}, bf16[128,1024]{1,0:T(8,128)(2,1)S(1)}, u32[]{:S(2)}, u32[]{:S(2)}) collective-permute-start(bf16[128,1024]{1,0:T(8,128)(2,1)S(1)} %get-tuple-element.656), channel_id=1, source_target_pairs={{0,6},{1,7},{2,4},{3,5},{4,2},{5,3},{6,0},{7,1},{8,14},{9,15},{10,... | collective-permute-start | bytes 786440 | tf_op jit(solution)/shard_map/ppermute | solution.py:58
  315.9 17.1 %collective-permute-start.81 = (bf16[512,512]{1,0:T(8,128)(2,1)S(1)}, bf16[512,512]{1,0:T(8,128)(2,1)S(1)}, u32[]{:S(2)}, u32[]{:S(2)}) collective-permute-start(bf16[512,512]{1,0:T(8,128)(2,1)S(1)} %get-tuple-element.755.b_ref), channel_id=1, source_target_pairs={{0,8},{24,16},{8,0},{16,24},{1,9},{25,17},{9,1},{17,25},{2,10},{26... | collective-permute-start | bytes 1572872 | tf_op jit(solution)/shard_map/ppermute | solution.py:907
  315.9 17.1 %collective-permute-start.82 = (bf16[512,512]{1,0:T(8,128)(2,1)S(1)}, bf16[512,512]{1,0:T(8,128)(2,1)S(1)}, u32[]{:S(2)}, u32[]{:S(2)}) collective-permute-start(bf16[512,512]{1,0:T(8,128)(2,1)S(1)} %get-tuple-element.691.refs_1_), channel_id=1, source_target_pairs={{8,16},{16,8},{9,17},{17,9},{10,18},{18,10},{11,19},{19,11},{12,20... | collective-permute-start | bytes 1572872 | tf_op jit(solution)/shard_map/ppermute | solution.py:907
  321.2 11.8 %collective-permute-start.79 = (bf16[128,1024]{1,0:T(8,128)(2,1)S(1)}, bf16[128,1024]{1,0:T(8,128)(2,1)S(1)}, u32[]{:S(2)}, u32[]{:S(2)}) collective-permute-start(bf16[128,1024]{1,0:T(8,128)(2,1)S(1)} %get-tuple-element.679.refs_0_.refs_3_), channel_id=1, source_target_pairs={{0,4},{1,5},{2,6},{3,7},{4,0},{5,1},{6,2},{7,3},{8,12},{9,13},{10,... | collective-permute-start | bytes 786440 | tf_op jit(solution)/shard_map/ppermute | solution.py:58
  333.8 12.6 %collective-permute-start.83 = (bf16[512,512]{1,0:T(8,128)(2,1)S(1)}, bf16[512,512]{1,0:T(8,128)(2,1)S(1)}, u32[]{:S(2)}, u32[]{:S(2)}) collective-permute-start(bf16[512,512]{1,0:T(8,128)(2,1)S(1)} %get-tuple-element.790.b_ref), channel_id=1, source_target_pairs={{0,8},{24,16},{8,0},{16,24},{1,9},{25,17},{9,1},{17,25},{2,10},{26... | collective-permute-start | bytes 1572872 | tf_op jit(solution)/shard_map/ppermute | solution.py:907
  333.9 12.6 %collective-permute-start.84 = (bf16[512,512]{1,0:T(8,128)(2,1)S(1)}, bf16[512,512]{1,0:T(8,128)(2,1)S(1)}, u32[]{:S(2)}, u32[]{:S(2)}) collective-permute-start(bf16[512,512]{1,0:T(8,128)(2,1)S(1)} %get-tuple-element.718.refs_1_), channel_id=1, source_target_pairs={{8,16},{16,8},{9,17},{17,9},{10,18},{18,10},{11,19},{19,11},{12,20... | collective-permute-start | bytes 1572872 | tf_op jit(solution)/shard_map/ppermute | solution.py:907
  347.3 16.3 %collective-permute-start.88 = (bf16[512,512]{1,0:T(8,128)(2,1)S(1)}, bf16[512,512]{1,0:T(8,128)(2,1)S(1)}, u32[]{:S(2)}, u32[]{:S(2)}) collective-permute-start(bf16[512,512]{1,0:T(8,128)(2,1)S(1)} %get-tuple-element.791.b_ref), channel_id=1, source_target_pairs={{0,8},{24,16},{8,0},{16,24},{1,9},{25,17},{9,1},{17,25},{2,10},{26... | collective-permute-start | bytes 1572872 | tf_op jit(solution)/shard_map/ppermute | solution.py:907
  347.4 16.2 %collective-permute-start.89 = (bf16[512,512]{1,0:T(8,128)(2,1)S(1)}, bf16[512,512]{1,0:T(8,128)(2,1)S(1)}, u32[]{:S(2)}, u32[]{:S(2)}) collective-permute-start(bf16[512,512]{1,0:T(8,128)(2,1)S(1)} %get-tuple-element.730.refs_1_), channel_id=1, source_target_pairs={{8,16},{16,8},{9,17},{17,9},{10,18},{18,10},{11,19},{19,11},{12,20... | collective-permute-start | bytes 1572872 | tf_op jit(solution)/shard_map/ppermute | solution.py:907
  364.4 17.5 %collective-permute-start.93 = (bf16[528,512]{1,0:T(8,128)(2,1)S(1)}, bf16[528,512]{1,0:T(8,128)(2,1)S(1)}, u32[]{:S(2)}, u32[]{:S(2)}) collective-permute-start(bf16[528,512]{1,0:T(8,128)(2,1)S(1)} %get-tuple-element.770.b_ref), channel_id=1, source_target_pairs={{0,8},{24,16},{8,0},{16,24},{1,9},{25,17},{9,1},{17,25},{2,10},{26... | collective-permute-start | bytes 1622024 | tf_op jit(solution)/shard_map/ppermute | solution.py:907
  364.5 17.4 %collective-permute-start.94 = (bf16[512,512]{1,0:T(8,128)(2,1)S(1)}, bf16[512,512]{1,0:T(8,128)(2,1)S(1)}, u32[]{:S(2)}, u32[]{:S(2)}) collective-permute-start(bf16[512,512]{1,0:T(8,128)(2,1)S(1)} %get-tuple-element.743.refs_1_), channel_id=1, source_target_pairs={{8,16},{16,8},{9,17},{17,9},{10,18},{18,10},{11,19},{19,11},{12,20... | collective-permute-start | bytes 1572872 | tf_op jit(solution)/shard_map/ppermute | solution.py:907
  368.5 13.4 %collective-permute-start.91 = (bf16[128,1024]{1,0:T(8,128)(2,1)S(1)}, bf16[128,1024]{1,0:T(8,128)(2,1)S(1)}, u32[]{:S(2)}, u32[]{:S(2)}) collective-permute-start(bf16[128,1024]{1,0:T(8,128)(2,1)S(1)} %copy-done.57), channel_id=1, source_target_pairs={{0,4},{1,5},{2,6},{3,7},{4,0},{5,1},{6,2},{7,3},{8,12},{9,13},{10,... | collective-permute-start | bytes 786440 | tf_op jit(solution)/shard_map/ppermute | solution.py:58
  369.7 12.2 %collective-permute-start.92 = (bf16[128,1024]{1,0:T(8,128)(2,1)S(1)}, bf16[128,1024]{1,0:T(8,128)(2,1)S(1)}, u32[]{:S(2)}, u32[]{:S(2)}) collective-permute-start(bf16[128,1024]{1,0:T(8,128)(2,1)S(1)} %copy-done.55), channel_id=1, source_target_pairs={{0,6},{1,7},{2,4},{3,5},{4,2},{5,3},{6,0},{7,1},{8,14},{9,15},{10,... | collective-permute-start | bytes 786440 | tf_op jit(solution)/shard_map/ppermute | solution.py:58
  382.8 16.9 %collective-permute-start.98 = (bf16[528,512]{1,0:T(8,128)(2,1)S(1)}, bf16[528,512]{1,0:T(8,128)(2,1)S(1)}, u32[]{:S(2)}, u32[]{:S(2)}) collective-permute-start(bf16[528,512]{1,0:T(8,128)(2,1)S(1)} %get-tuple-element.771.b_ref), channel_id=1, source_target_pairs={{0,8},{24,16},{8,0},{16,24},{1,9},{25,17},{9,1},{17,25},{2,10},{26... | collective-permute-start | bytes 1622024 | tf_op jit(solution)/shard_map/ppermute | solution.py:907
  382.8 16.8 %collective-permute-start.99 = (bf16[528,512]{1,0:T(8,128)(2,1)S(1)}, bf16[528,512]{1,0:T(8,128)(2,1)S(1)}, u32[]{:S(2)}, u32[]{:S(2)}) collective-permute-start(bf16[528,512]{1,0:T(8,128)(2,1)S(1)} %get-tuple-element.761.refs_0_), channel_id=1, source_target_pairs={{8,16},{16,8},{9,17},{17,9},{10,18},{18,10},{11,19},{19,11},{12,20... | collective-permute-start | bytes 1622024 | tf_op jit(solution)/shard_map/ppermute | solution.py:907
  387.6 12.1 %collective-permute-start.96 = (bf16[128,1024]{1,0:T(8,128)(2,1)S(1)}, bf16[128,1024]{1,0:T(8,128)(2,1)S(1)}, u32[]{:S(2)}, u32[]{:S(2)}) collective-permute-start(bf16[128,1024]{1,0:T(8,128)(2,1)S(1)} %get-tuple-element.740), channel_id=1, source_target_pairs={{0,4},{1,5},{2,6},{3,7},{4,0},{5,1},{6,2},{7,3},{8,12},{9,13},{10,... | collective-permute-start | bytes 786440 | tf_op jit(solution)/shard_map/ppermute | solution.py:58
  400.5 14.5 %collective-permute-start.103 = (bf16[528,512]{1,0:T(8,128)(2,1)S(1)}, bf16[528,512]{1,0:T(8,128)(2,1)S(1)}, u32[]{:S(2)}, u32[]{:S(2)}) collective-permute-start(bf16[528,512]{1,0:T(8,128)(2,1)S(1)} %get-tuple-element.767.b_ref), channel_id=1, source_target_pairs={{8,0},{16,24},{9,1},{17,25},{10,2},{18,26},{11,3},{19,27},{12,4},{... | collective-permute-start | bytes 1622024 | tf_op jit(solution)/shard_map/ppermute | solution.py:907
  402.3 12.8 %collective-permute-start.104 = (bf16[528,512]{1,0:T(8,128)(2,1)S(1)}, bf16[528,512]{1,0:T(8,128)(2,1)S(1)}, u32[]{:S(2)}, u32[]{:S(2)}) collective-permute-start(bf16[528,512]{1,0:T(8,128)(2,1)S(1)} %get-tuple-element.776.refs_0_), channel_id=1, source_target_pairs={{8,16},{16,8},{9,17},{17,9},{10,18},{18,10},{11,19},{19,11},{12,20... | collective-permute-start | bytes 1622024 | tf_op jit(solution)/shard_map/ppermute | solution.py:907
  415.3 13.1 %collective-permute-start.108 = (bf16[528,512]{1,0:T(8,128)(2,1)S(1)}, bf16[528,512]{1,0:T(8,128)(2,1)S(1)}, u32[]{:S(2)}, u32[]{:S(2)}) collective-permute-start(bf16[528,512]{1,0:T(8,128)(2,1)S(1)} %turn.25.b_ref), channel_id=1, source_target_pairs={{8,0},{16,24},{9,1},{17,25},{10,2},{18,26},{11,3},{19,27},{12,4},{... | collective-permute-start | bytes 1622024 | tf_op jit(solution)/shard_map/ppermute | solution.py:907
  428.4 26.5 %collective-permute-start.112 = (bf16[128,1024]{1,0:T(8,128)(2,1)S(1)}, bf16[128,1024]{1,0:T(8,128)(2,1)S(1)}, u32[]{:S(2)}, u32[]{:S(2)}) collective-permute-start(bf16[128,1024]{1,0:T(8,128)(2,1)S(1)} %get-tuple-element.784), channel_id=1, source_target_pairs={{0,0},{1,1},{10,2},{11,3},{20,4},{21,5},{30,6},{31,7},{16,12},{17,... | collective-permute-start | bytes 786440 | tf_op jit(solution)/shard_map/ppermute | solution.py:43
  431.9 23.0 %collective-permute-start.113 = (bf16[128,1024]{1,0:T(8,128)(2,1)S(1)}, bf16[128,1024]{1,0:T(8,128)(2,1)S(1)}, u32[]{:S(2)}, u32[]{:S(2)}) collective-permute-start(bf16[128,1024]{1,0:T(8,128)(2,1)S(1)} %get-tuple-element.785), channel_id=1, source_target_pairs={{0,0},{1,1},{10,2},{11,3},{20,4},{21,5},{30,6},{31,7},{16,12},{17,... | collective-permute-start | bytes 786440 | tf_op jit(solution)/shard_map/ppermute | solution.py:43
  434.6 12.4 %collective-permute-start.109 = (bf16[144,768]{1,0:T(8,128)(2,1)S(1)}, bf16[144,768]{1,0:T(8,128)(2,1)S(1)}, u32[]{:S(2)}, u32[]{:S(2)}) collective-permute-start(bf16[144,768]{1,0:T(8,128)(2,1)S(1)} %get-tuple-element.781), channel_id=1, source_target_pairs={{0,2},{1,3},{2,0},{3,1},{4,6},{5,7},{6,4},{7,5},{8,10},{9,11},{10,... | collective-permute-start | bytes 663560 | tf_op jit(solution)/shard_map/ppermute | solution.py:58
  438.1 13.2 %collective-permute-start.111 = (bf16[144,768]{1,0:T(8,128)(2,1)S(1)}, bf16[144,768]{1,0:T(8,128)(2,1)S(1)}, u32[]{:S(2)}, u32[]{:S(2)}) collective-permute-start(bf16[144,768]{1,0:T(8,128)(2,1)S(1)} %get-tuple-element.783), channel_id=1, source_target_pairs={{0,6},{1,7},{2,4},{3,5},{4,2},{5,3},{6,0},{7,1},{8,14},{9,15},{10,... | collective-permute-start | bytes 663560 | tf_op jit(solution)/shard_map/ppermute | solution.py:58
  (131 other events, 1791.7 us)

commit v7 on v6

--- a/solution.py
+++ b/solution.py
@@ -767,14 +767,15 @@
             here = tile(p ^ j, rows)
             outs[j][0:rows, :width] = a[here, :]
             outs[j][0:rows, width:] = b[here, :taken]
-            if under:
-                outs[j][rows:, :width] = a[n_p * rows :, :]
-                outs[j][rows:, width:] = b[n_p * rows :, :taken]
+            for k in range(3 if under else 0):
+                at = slice(rows + k * under, rows + (k + 1) * under)
+                outs[j][at, :width] = a[n_p * rows :, :]
+                outs[j][at, width:] = b[n_p * rows :, :taken]
         if split:
             for i in range(n_p):
                 outs[n_p][:, i * taken : (i + 1) * taken] = b[i * rows : (i + 1) * rows, taken:]
 
-    outs = [((rows + under, width + taken), BF)] * n_p
+    outs = [((rows + 3 * under, width + taken), BF)] * n_p
     if split:
         outs.append(((rows, n_p * taken), BF))
     return run("cut_rows", body, outs, [first, second], net.place)
@@ -786,9 +787,10 @@
     starts = [sum(sizes[:i]) for i in range(len(sizes))]
 
     def body(place, *refs):
-        every = refs[0][rows:, :].astype(F32)
+        lines = slice(rows, rows + 2 * layers * net.n_p)
+        every = refs[0][lines, :].astype(F32)
         for ref in refs[1:count]:
-            every = every + ref[rows:, :].astype(F32)
+            every = every + ref[lines, :].astype(F32)
         total = jnp.zeros((2 * layers, width), F32)
         for i in range(net.n_p):
             total = jnp.where(place[0] == i, every[i * 2 * layers : (i + 1) * 2 * layers], total)

time: 466 us -> 466 us (level)
  the two profiles are of different devices: /device:TPU:16 before, /device:TPU:10 now
where the time goes in v7:
time: 466 us; the launch traced here: 457 us
  waiting for transfers between devices  162 us (35%)
  starting transfers between devices  154 us (33%)
  Pallas kernels  110 us (24%)
  blocking collectives  21.7 us (5%)
  local copies, waits for them, and re-layouts  6.02 us (1%)
    ppermute x66, waiting for transfers between devices, chip(): return lax.ppermute(v, 'fsdp', xor_pairs(self.n_f, 2 * j))  136 us
    pallas_call x73, Pallas kernels, run(): pl.pallas_call(body, out_shape=[jax.ShapeDtypeStruct(shape, dtype) for sh...  103 us
    ppermute x66, starting transfers between devices, chip(): return lax.ppermute(v, 'fsdp', xor_pairs(self.n_f, 2 * j))  79.8 us
    ppermute x26, starting transfers between devices, start(): lax.ppermute(v, 'seq', m[3])  44.1 us
    ppermute x7, starting transfers between devices, send(): return lax.ppermute(v, ('seq', 'fsdp'), pairs)  22.2 us
    all_to_all x4, blocking collectives, swap_cores(): return lax.all_to_all(both, 'fsdp', 0, 0, axis_index_groups=pair_groups)  21.7 us
    ppermute x7, waiting for transfers between devices, send(): return lax.ppermute(v, ('seq', 'fsdp'), pairs)  11.8 us
  transfers between devices with their start and end apart: 114, of which 48 were waited for; matrix products, arithmetic and copies ran while one was open for 0% of the time, Pallas kernels for 18%

profile of v7, /device:TPU:10, one launch (start us, length us, event | category | flops | bytes accessed | tf_op | source)
XLA Modules:
  0.0 456.8 jit_solution(18166430066551354264)
XLA Ops:
  1.8 3.4 collective-permute-start
  11.7 3.6 collective-permute-start.4
  15.3 3.4 collective-permute-start.1
  21.0 3.9 collective-permute-done.4.refs_1_
  33.0 5.4 %collective-permute-done.7.refs_1_.refs_12_ = bf16[144,1024]{1,0:T(8,128)(2,1)S(1)} collective-permute-done((bf16[144,1024]{1,0:T(8,128)(2,1)S(1)}, bf16[144,1024]{1,0:T(8,128)(2,1)S(1)}, u32[]{:S(2)}, u32[]{:S(2)}) %collective-permute-start.7) | collective-permute-done | bytes 294944 | tf_op jit(solution)/shard_map/ppermute | solution.py:58
  38.4 4.3 collective-permute-done.8.refs_2_.refs_13_
  45.7 3.3 collective-permute-done.11.refs_6_.refs_10_
  53.8 5.3 %attend.2 = (s32[1,512]{1,0:T(1,128)S(1)}, s32[512,1]{1,0:T(8,128)S(1)}, bf16[512,1024]{1,0:T(8,128)(2,1)S(1)}, bf16[512,768]{1,0:T(8,128)(2,1)S(1)}, bf16[512,256]{1,0:T(8,128)(2,1)S(1)}) custom-call(s32[3]{0:T(128)S(1)} %pad_add_fusion.2.place, bf16[144,1024]{1,0:T(8,128)(2,1)S(1)} %put_small.1.refs_0_.refs_11_.hidden_ref, ...), custom_call_target="tpu_custom_call" | custom-call | flops 805306368 | bytes 2785292 | tf_op jit(solution)/shard_map/attend/pallas_call | solution.py:93
  64.4 5.8 %collective-permute-done.16.refs_5_ = bf16[512,256]{1,0:T(8,128)(2,1)S(1)} collective-permute-done((bf16[512,256]{1,0:T(8,128)(2,1)S(1)}, bf16[512,256]{1,0:T(8,128)(2,1)S(1)}, u32[]{:S(2)}, u32[]{:S(2)}) %collective-permute-start.16) | collective-permute-done | bytes 262176 | tf_op jit(solution)/shard_map/ppermute | solution.py:58
  70.2 3.5 collective-permute-done.17.refs_6_
  77.4 2.7 close_attention.2
  85.4 4.1 feed_forward.2
  90.9 3.2 collective-permute-done.23.refs_1_
  101.2 5.8 %collective-permute-done.25.refs_1_ = bf16[128,1024]{1,0:T(8,128)(2,1)S(1)} collective-permute-done((bf16[128,1024]{1,0:T(8,128)(2,1)S(1)}, bf16[128,1024]{1,0:T(8,128)(2,1)S(1)}, u32[]{:S(2)}, u32[]{:S(2)}) %collective-permute-start.25) | collective-permute-done | bytes 262176 | tf_op jit(solution)/shard_map/ppermute | solution.py:58
  106.9 3.7 collective-permute-done.26.refs_2_
  118.0 5.7 %collective-permute-done.29.refs_1_ = bf16[128,1024]{1,0:T(8,128)(2,1)S(1)} collective-permute-done((bf16[128,1024]{1,0:T(8,128)(2,1)S(1)}, bf16[128,1024]{1,0:T(8,128)(2,1)S(1)}, u32[]{:S(2)}, u32[]{:S(2)}) %collective-permute-start.29) | collective-permute-done | bytes 262176 | tf_op jit(solution)/shard_map/ppermute | solution.py:58
  123.7 5.6 %collective-permute-done.30.refs_2_ = bf16[128,1024]{1,0:T(8,128)(2,1)S(1)} collective-permute-done((bf16[128,1024]{1,0:T(8,128)(2,1)S(1)}, bf16[128,1024]{1,0:T(8,128)(2,1)S(1)}, u32[]{:S(2)}, u32[]{:S(2)}) %collective-permute-start.30) | collective-permute-done | bytes 262176 | tf_op jit(solution)/shard_map/ppermute | solution.py:58
  129.4 3.0 collective-permute-start.37
  136.6 5.3 %attend.3 = (bf16[512,1024]{1,0:T(8,128)(2,1)S(1)}, bf16[512,768]{1,0:T(8,128)(2,1)S(1)}, bf16[512,256]{1,0:T(8,128)(2,1)S(1)}) custom-call(s32[3]{0:T(128)S(1)} %pad_add_fusion.2.place, bf16[128,1024]{1,0:T(8,128)(2,1)S(1)} %get-tuple-element.502.refs_0_, bf16[128,1024]{1,0:T(8,128)(2,1)S(1)} %collective-permute-done.29.refs_1_, ...), custom_call_target="tpu_custom_call" | custom-call | flops 805306368 | bytes 2658316 | tf_op jit(solution)/shard_map/attend/pallas_call | solution.py:93
  148.0 5.9 %collective-permute-start.42 = (bf16[128,1024]{1,0:T(8,128)(2,1)S(1)}, bf16[128,1024]{1,0:T(8,128)(2,1)S(1)}, u32[]{:S(2)}, u32[]{:S(2)}) collective-permute-start(bf16[128,1024]{1,0:T(8,128)(2,1)S(1)} %collective-permute-done.37), channel_id=1, source_target_pairs={{0,0},{1,1},{2,10},{3,11},{4,20},{5,21},{6,30},{7,31},{8,16},{9,17... | collective-permute-start | bytes 786440 | tf_op jit(solution)/shard_map/ppermute | solution.py:43
  153.9 3.4 collective-permute-done.39.refs_6_
  161.6 4.0 collective-permute-start.46
  165.6 2.7 close_attention.3
  168.4 4.1 feed_forward.3
  172.5 4.9 %collective-permute-done.46.refs_2_ = bf16[128,1024]{1,0:T(8,128)(2,1)S(1)} collective-permute-done((bf16[128,1024]{1,0:T(8,128)(2,1)S(1)}, bf16[128,1024]{1,0:T(8,128)(2,1)S(1)}, u32[]{:S(2)}, u32[]{:S(2)}) %collective-permute-start.46) | collective-permute-done | bytes 262176 | tf_op jit(solution)/shard_map/ppermute | solution.py:58
  179.4 5.4 %feed_back.2 = (bf16[128,1024]{1,0:T(8,128)(2,1)S(1)}, bf16[128,1024]{1,0:T(8,128)(2,1)S(1)}, bf16[128,1024]{1,0:T(8,128)(2,1)S(1)}, bf16[128,1024]{1,0:T(8,128)...) custom-call(s32[3]{0:T(128)S(1)} %pad_add_fusion.2.place, ...), custom_call_target="tpu_custom_call" | custom-call | flops 2147483648 | bytes 7340044 | tf_op jit(solution)/shard_map/feed_back/pallas_call | solution.py:93
  192.7 5.4 %all_to_all.20.ref = bf16[2,512,1024]{2,1,0:T(8,128)(2,1)S(1)} all-to-all(bf16[2,512,1024]{2,1,0:T(8,128)(2,1)S(1)} %up_weight_grad.2), channel_id=1, replica_groups={{0,1},{2,3},{4,5},{6,7},{8,9},{10,11},{12,13},{14,15},{16,17},{18,19},{..., dimensions={0} | all-to-all | bytes 4194304 | tf_op jit(solution)/shard_map/all_to_all | solution.py:1018
  198.1 2.9 collective-permute-done.50.refs_2_
  214.1 5.7 %collective-permute-done.53.refs_1_.refs_4_ = bf16[128,1024]{1,0:T(8,128)(2,1)} collective-permute-done((bf16[128,1024]{1,0:T(8,128)(2,1)}, bf16[128,1024]{1,0:T(8,128)(2,1)}, u32[]{:S(2)}, u32[]{:S(2)}) %collective-permute-start.53) | collective-permute-done | bytes 262176 | tf_op jit(solution)/shard_map/ppermute | solution.py:58
  219.8 5.1 %collective-permute-done.54.refs_2_.refs_5_ = bf16[128,1024]{1,0:T(8,128)(2,1)} collective-permute-done((bf16[128,1024]{1,0:T(8,128)(2,1)}, bf16[128,1024]{1,0:T(8,128)(2,1)}, u32[]{:S(2)}, u32[]{:S(2)}) %collective-permute-start.54) | collective-permute-done | bytes 262176 | tf_op jit(solution)/shard_map/ppermute | solution.py:58
  228.3 3.3 collective-permute-start.59
  231.6 9.6 %attend_back.2 = (bf16[128,1024]{1,0:T(8,128)(2,1)S(1)}, bf16[128,1024]{1,0:T(8,128)(2,1)S(1)}, bf16[128,1024]{1,0:T(8,128)(2,1)S(1)}, bf16[128,1024]{1,0:T(8,12...) custom-call(s32[3]{0:T(128)S(1)} %pad_add_fusion.2.place, ...), custom_call_target="tpu_custom_call" | custom-call | flops 2147483648 | bytes 5509132 | tf_op jit(solution)/shard_map/attend_back/pallas_call | solution.py:93
  248.9 2.6 attend_weight_grad.2
  251.5 5.4 %all_to_all.21.ref = bf16[2,512,1024]{2,1,0:T(8,128)(2,1)S(1)} all-to-all(bf16[2,512,1024]{2,1,0:T(8,128)(2,1)S(1)} %attend_weight_grad.2), channel_id=1, replica_groups={{0,1},{2,3},{4,5},{6,7},{8,9},{10,11},{12,13},{14,15},{16,17},{18,19},{..., dimensions={0} | all-to-all | bytes 4194304 | tf_op jit(solution)/shard_map/all_to_all | solution.py:1018
  260.4 3.5 collective-permute-start.69
  267.4 5.7 %collective-permute-done.65.refs_1_ = bf16[128,1024]{1,0:T(8,128)(2,1)S(1)} collective-permute-done((bf16[128,1024]{1,0:T(8,128)(2,1)S(1)}, bf16[128,1024]{1,0:T(8,128)(2,1)S(1)}, u32[]{:S(2)}, u32[]{:S(2)}) %collective-permute-start.65) | collective-permute-done | bytes 262176 | tf_op jit(solution)/shard_map/ppermute | solution.py:58
  273.1 5.0 %collective-permute-done.67.refs_3_ = bf16[128,1024]{1,0:T(8,128)(2,1)S(1)} collective-permute-done((bf16[128,1024]{1,0:T(8,128)(2,1)S(1)}, bf16[128,1024]{1,0:T(8,128)(2,1)S(1)}, u32[]{:S(2)}, u32[]{:S(2)}) %collective-permute-start.67) | collective-permute-done | bytes 262176 | tf_op jit(solution)/shard_map/ppermute | solution.py:58
  281.0 3.1 collective-permute-start.72
  284.2 5.4 %feed_back.3 = (bf16[128,1024]{1,0:T(8,128)(2,1)S(1)}, bf16[128,1024]{1,0:T(8,128)(2,1)S(1)}, bf16[128,1024]{1,0:T(8,128)(2,1)S(1)}, bf16[128,1024]{1,0:T(8,128)...) custom-call(s32[3]{0:T(128)S(1)} %pad_add_fusion.2.place, ...), custom_call_target="tpu_custom_call" | custom-call | flops 2147483648 | bytes 7340044 | tf_op jit(solution)/shard_map/feed_back/pallas_call | solution.py:93
  289.8 5.5 %collective-permute-done.71.refs_4_.a_ref = bf16[512,512]{1,0:T(8,128)(2,1)S(1)} collective-permute-done((bf16[512,512]{1,0:T(8,128)(2,1)S(1)}, bf16[512,512]{1,0:T(8,128)(2,1)S(1)}, u32[]{:S(2)}, u32[]{:S(2)}) %collective-permute-start.71) | collective-permute-done | bytes 524320 | tf_op jit(solution)/shard_map/ppermute | solution.py:909
  298.1 3.1 collective-permute-start.77
  306.7 5.4 %all_to_all.22.ref = bf16[2,512,1024]{2,1,0:T(8,128)(2,1)S(1)} all-to-all(bf16[2,512,1024]{2,1,0:T(8,128)(2,1)S(1)} %up_weight_grad.3), channel_id=1, replica_groups={{0,1},{2,3},{4,5},{6,7},{8,9},{10,11},{12,13},{14,15},{16,17},{18,19},{..., dimensions={0} | all-to-all | bytes 4194304 | tf_op jit(solution)/shard_map/all_to_all | solution.py:1018
  312.1 3.0 collective-permute-done.75.refs_3_
  316.0 3.1 collective-permute-start.82
  324.2 5.0 %collective-permute-done.78.refs_1_.refs_4_ = bf16[128,1024]{1,0:T(8,128)(2,1)S(1)} collective-permute-done((bf16[128,1024]{1,0:T(8,128)(2,1)S(1)}, bf16[128,1024]{1,0:T(8,128)(2,1)S(1)}, u32[]{:S(2)}, u32[]{:S(2)}) %collective-permute-start.78) | collective-permute-done | bytes 262176 | tf_op jit(solution)/shard_map/ppermute | solution.py:58
  329.3 3.8 collective-permute-done.79.refs_2_.refs_5_
  334.0 3.1 collective-permute-start.84
  337.3 9.2 %attend_back.3 = (bf16[128,1024]{1,0:T(8,128)(2,1)S(1)}, bf16[128,1024]{1,0:T(8,128)(2,1)S(1)}, bf16[128,1024]{1,0:T(8,128)(2,1)S(1)}, bf16[128,1024]{1,0:T(8,12...) custom-call(s32[3]{0:T(128)S(1)} %pad_add_fusion.2.place, ...), custom_call_target="tpu_custom_call" | custom-call | flops 2147483648 | bytes 6688780 | tf_op jit(solution)/shard_map/attend_back/pallas_call | solution.py:93
  347.4 3.0 collective-permute-start.89
  356.0 5.5 %all_to_all.23.ref = bf16[2,528,1024]{2,1,0:T(8,128)(2,1)S(1)} all-to-all(bf16[2,528,1024]{2,1,0:T(8,128)(2,1)S(1)} %attend_weight_grad.3), channel_id=1, replica_groups={{0,1},{2,3},{4,5},{6,7},{8,9},{10,11},{12,13},{14,15},{16,17},{18,19},{..., dimensions={0} | all-to-all | bytes 4325376 | tf_op jit(solution)/shard_map/all_to_all | solution.py:1018
  364.6 2.9 collective-permute-start.94
  371.1 5.7 %collective-permute-done.90.refs_1_ = bf16[128,1024]{1,0:T(8,128)(2,1)S(1)} collective-permute-done((bf16[128,1024]{1,0:T(8,128)(2,1)S(1)}, bf16[128,1024]{1,0:T(8,128)(2,1)S(1)}, u32[]{:S(2)}, u32[]{:S(2)}) %collective-permute-start.90) | collective-permute-done | bytes 262176 | tf_op jit(solution)/shard_map/ppermute | solution.py:58
  376.8 5.3 %collective-permute-done.91.refs_2_ = bf16[128,1024]{1,0:T(8,128)(2,1)S(1)} collective-permute-done((bf16[128,1024]{1,0:T(8,128)(2,1)S(1)}, bf16[128,1024]{1,0:T(8,128)(2,1)S(1)}, u32[]{:S(2)}, u32[]{:S(2)}) %collective-permute-start.91) | collective-permute-done | bytes 262176 | tf_op jit(solution)/shard_map/ppermute | solution.py:58
  382.9 2.9 collective-permute-start.99
  390.1 5.8 %collective-permute-done.95.refs_4_ = bf16[128,1024]{1,0:T(8,128)(2,1)S(1)} collective-permute-done((bf16[128,1024]{1,0:T(8,128)(2,1)S(1)}, bf16[128,1024]{1,0:T(8,128)(2,1)S(1)}, u32[]{:S(2)}, u32[]{:S(2)}) %collective-permute-start.95) | collective-permute-done | bytes 262176 | tf_op jit(solution)/shard_map/ppermute | solution.py:58
  395.9 3.9 collective-permute-done.96.refs_5_
  402.4 3.0 collective-permute-start.104
  411.9 3.2 collective-permute-done.101.refs_9_
  421.0 3.2 collective-permute-done.105.refs_4_
  424.2 4.2 collective-permute-done.106.refs_5_
  437.5 3.5 write_layer.2
  441.1 7.3 %collective-permute-done.112.refs_4_ = bf16[128,1024]{1,0:T(8,128)(2,1)S(1)} collective-permute-done((bf16[128,1024]{1,0:T(8,128)(2,1)S(1)}, bf16[128,1024]{1,0:T(8,128)(2,1)S(1)}, u32[]{:S(2)}, u32[]{:S(2)}) %collective-permute-start.112) | collective-permute-done | bytes 262176 | tf_op jit(solution)/shard_map/ppermute | solution.py:43
  448.4 2.8 collective-permute-done.113.refs_5_
  452.8 3.5 write_layer.3
  (415 shorter events, 172.7 us)
Async XLA Ops:
  1.8 13.5 %collective-permute-start = (bf16[64,1024]{1,0:T(8,128)(2,1)S(1)}, bf16[64,1024]{1,0:T(8,128)(2,1)S(1)}, u32[]{:S(2)}, u32[]{:S(2)}) collective-permute-start(bf16[64,1024]{1,0:T(8,128)(2,1)S(1)} %get-tuple-element.823), channel_id=1, source_target_pairs={{0,0},{1,1},{2,2},{3,3},{4,4},{5,5},{6,6},{7,7},{12,8},{13,9},{14,... | collective-permute-start | bytes 393224 | tf_op jit(solution)/shard_map/ppermute | solution.py:43
  8.6 12.4 %collective-permute-start.3 = (bf16[64,1792]{1,0:T(8,128)(2,1)S(1)}, bf16[64,1792]{1,0:T(8,128)(2,1)S(1)}, u32[]{:S(2)}, u32[]{:S(2)}) collective-permute-start(bf16[64,1792]{1,0:T(8,128)(2,1)S(1)} %get-tuple-element.418), channel_id=1, source_target_pairs={{0,2},{1,3},{2,0},{3,1},{4,6},{5,7},{6,4},{7,5},{8,10},{9,11},{10,... | collective-permute-start | bytes 688136 | tf_op jit(solution)/shard_map/ppermute | solution.py:58
  9.2 17.5 %collective-permute-start.2 = (bf16[80,1024]{1,0:T(8,128)(2,1)S(1)}, bf16[80,1024]{1,0:T(8,128)(2,1)S(1)}, u32[]{:S(2)}, u32[]{:S(2)}) collective-permute-start(bf16[80,1024]{1,0:T(8,128)(2,1)S(1)} %pad_add_fusion), channel_id=1, source_target_pairs={{0,0},{1,1},{2,10},{3,11},{4,20},{5,21},{6,30},{7,31},{12,16},{13,... | collective-permute-start | bytes 491528 | tf_op jit(solution)/shard_map/ppermute | solution.py:43
  11.7 13.3 %collective-permute-start.4 = (bf16[64,1792]{1,0:T(8,128)(2,1)S(1)}, bf16[64,1792]{1,0:T(8,128)(2,1)S(1)}, u32[]{:S(2)}, u32[]{:S(2)}) collective-permute-start(bf16[64,1792]{1,0:T(8,128)(2,1)S(1)} %get-tuple-element.419), channel_id=1, source_target_pairs={{0,4},{1,5},{2,6},{3,7},{4,0},{5,1},{6,2},{7,3},{8,12},{9,13},{10,... | collective-permute-start | bytes 688136 | tf_op jit(solution)/shard_map/ppermute | solution.py:58
  15.3 11.4 %collective-permute-start.1 = (bf16[64,1024]{1,0:T(8,128)(2,1)S(1)}, bf16[64,1024]{1,0:T(8,128)(2,1)S(1)}, u32[]{:S(2)}, u32[]{:S(2)}) collective-permute-start(bf16[64,1024]{1,0:T(8,128)(2,1)S(1)} %collective-permute-done), channel_id=1, source_target_pairs={{0,0},{1,1},{2,10},{3,11},{4,20},{5,21},{6,30},{7,31},{8,16},{9,17... | collective-permute-start | bytes 393224 | tf_op jit(solution)/shard_map/ppermute | solution.py:43
  26.7 17.3 %collective-permute-start.10 = (bf16[192,1792]{1,0:T(8,128)(2,1)S(1)}, bf16[192,1792]{1,0:T(8,128)(2,1)S(1)}, u32[]{:S(2)}, u32[]{:S(2)}) collective-permute-start(bf16[192,1792]{1,0:T(8,128)(2,1)S(1)} %stack_halves.4.mine_ref), channel_id=1, source_target_pairs={{0,8},{8,0},{16,24},{24,16},{1,9},{9,1},{17,25},{25,17},{2,10},{10... | collective-permute-start | bytes 2064392 | tf_op jit(solution)/shard_map/ppermute | solution.py:64
  29.1 13.6 %collective-permute-start.8 = (bf16[144,1024]{1,0:T(8,128)(2,1)S(1)}, bf16[144,1024]{1,0:T(8,128)(2,1)S(1)}, u32[]{:S(2)}, u32[]{:S(2)}) collective-permute-start(bf16[144,1024]{1,0:T(8,128)(2,1)S(1)} %put_small.1.refs_0_.refs_11_.hidden_ref), channel_id=1, source_target_pairs={{0,4},{1,5},{2,6},{3,7},{4,0},{5,1},{6,2},{7,3},{8,12},{9,13},{10,... | collective-permute-start | bytes 884744 | tf_op jit(solution)/shard_map/ppermute | solution.py:58
  31.6 12.4 %collective-permute-start.9 = (bf16[144,1024]{1,0:T(8,128)(2,1)S(1)}, bf16[144,1024]{1,0:T(8,128)(2,1)S(1)}, u32[]{:S(2)}, u32[]{:S(2)}) collective-permute-start(bf16[144,1024]{1,0:T(8,128)(2,1)S(1)} %put_small.1.refs_0_.refs_11_.hidden_ref), channel_id=1, source_target_pairs={{0,6},{1,7},{2,4},{3,5},{4,2},{5,3},{6,0},{7,1},{8,14},{9,15},{10,... | collective-permute-start | bytes 884744 | tf_op jit(solution)/shard_map/ppermute | solution.py:58
  59.9 15.0 %collective-permute-start.19 = (bf16[192,1024]{1,0:T(8,128)(2,1)S(1)}, bf16[192,1024]{1,0:T(8,128)(2,1)S(1)}, u32[]{:S(2)}, u32[]{:S(2)}) collective-permute-start(bf16[192,1024]{1,0:T(8,128)(2,1)S(1)} %stack_halves.5.mine_ref), channel_id=1, source_target_pairs={{0,8},{8,0},{16,24},{24,16},{1,9},{9,1},{17,25},{25,17},{2,10},{10... | collective-permute-start | bytes 1179656 | tf_op jit(solution)/shard_map/ppermute | solution.py:64
  63.5 11.5 %collective-permute-start.18 = (bf16[512,256]{1,0:T(8,128)(2,1)S(1)}, bf16[512,256]{1,0:T(8,128)(2,1)S(1)}, u32[]{:S(2)}, u32[]{:S(2)}) collective-permute-start(bf16[512,256]{1,0:T(8,128)(2,1)S(1)} %get-tuple-element.457.refs_4_.refs_2_), channel_id=1, source_target_pairs={{0,6},{1,7},{2,4},{3,5},{4,2},{5,3},{6,0},{7,1},{8,14},{9,15},{10,... | collective-permute-start | bytes 786440 | tf_op jit(solution)/shard_map/ppermute | solution.py:58
  82.8 11.3 %collective-permute-start.23 = (bf16[64,1792]{1,0:T(8,128)(2,1)S(1)}, bf16[64,1792]{1,0:T(8,128)(2,1)S(1)}, u32[]{:S(2)}, u32[]{:S(2)}) collective-permute-start(bf16[64,1792]{1,0:T(8,128)(2,1)S(1)} %get-tuple-element.486), channel_id=1, source_target_pairs={{0,4},{1,5},{2,6},{3,7},{4,0},{5,1},{6,2},{7,3},{8,12},{9,13},{10,... | collective-permute-start | bytes 688136 | tf_op jit(solution)/shard_map/ppermute | solution.py:58
  95.9 16.7 %collective-permute-start.28 = (bf16[192,1792]{1,0:T(8,128)(2,1)S(1)}, bf16[192,1792]{1,0:T(8,128)(2,1)S(1)}, u32[]{:S(2)}, u32[]{:S(2)}) collective-permute-start(bf16[192,1792]{1,0:T(8,128)(2,1)S(1)} %stack_halves.6.mine_ref), channel_id=1, source_target_pairs={{0,8},{8,0},{16,24},{24,16},{1,9},{9,1},{17,25},{25,17},{2,10},{10... | collective-permute-start | bytes 2064392 | tf_op jit(solution)/shard_map/ppermute | solution.py:64
  98.3 12.4 %collective-permute-start.26 = (bf16[128,1024]{1,0:T(8,128)(2,1)S(1)}, bf16[128,1024]{1,0:T(8,128)(2,1)S(1)}, u32[]{:S(2)}, u32[]{:S(2)}) collective-permute-start(bf16[128,1024]{1,0:T(8,128)(2,1)S(1)} %get-tuple-element.490), channel_id=1, source_target_pairs={{0,4},{1,5},{2,6},{3,7},{4,0},{5,1},{6,2},{7,3},{8,12},{9,13},{10,... | collective-permute-start | bytes 786440 | tf_op jit(solution)/shard_map/ppermute | solution.py:58
  113.7 15.6 %collective-permute-start.33 = (bf16[512,1024]{1,0:T(8,128)(2,1)S(1)}, bf16[512,1024]{1,0:T(8,128)(2,1)S(1)}, u32[]{:S(2)}, u32[]{:S(2)}) collective-permute-start(bf16[512,1024]{1,0:T(8,128)(2,1)S(1)} %get-tuple-element.527.refs_8_.refs_4_), channel_id=1, source_target_pairs={{0,1},{1,0},{2,3},{3,2},{4,5},{5,4},{6,7},{7,6},{8,9},{9,8},{10,11... | collective-permute-start | bytes 3145736 | tf_op jit(solution)/shard_map/ppermute | solution.py:61
  113.8 15.6 %collective-permute-start.32 = (bf16[512,768]{1,0:T(8,128)(2,1)S(1)}, bf16[512,768]{1,0:T(8,128)(2,1)S(1)}, u32[]{:S(2)}, u32[]{:S(2)}) collective-permute-start(bf16[512,768]{1,0:T(8,128)(2,1)S(1)} %get-tuple-element.506.refs_5_.refs_9_), channel_id=1, source_target_pairs={{0,1},{1,0},{2,3},{3,2},{4,5},{5,4},{6,7},{7,6},{8,9},{9,8},{10,11... | collective-permute-start | bytes 2359304 | tf_op jit(solution)/shard_map/ppermute | solution.py:61
  115.7 13.6 %collective-permute-start.30 = (bf16[128,1024]{1,0:T(8,128)(2,1)S(1)}, bf16[128,1024]{1,0:T(8,128)(2,1)S(1)}, u32[]{:S(2)}, u32[]{:S(2)}) collective-permute-start(bf16[128,1024]{1,0:T(8,128)(2,1)S(1)} %get-tuple-element.502.refs_0_), channel_id=1, source_target_pairs={{0,4},{1,5},{2,6},{3,7},{4,0},{5,1},{6,2},{7,3},{8,12},{9,13},{10,... | collective-permute-start | bytes 786440 | tf_op jit(solution)/shard_map/ppermute | solution.py:58
  116.3 13.0 %collective-permute-start.31 = (bf16[128,1024]{1,0:T(8,128)(2,1)S(1)}, bf16[128,1024]{1,0:T(8,128)(2,1)S(1)}, u32[]{:S(2)}, u32[]{:S(2)}) collective-permute-start(bf16[128,1024]{1,0:T(8,128)(2,1)S(1)} %get-tuple-element.502.refs_0_), channel_id=1, source_target_pairs={{0,6},{1,7},{2,4},{3,5},{4,2},{5,3},{6,0},{7,1},{8,14},{9,15},{10,... | collective-permute-start | bytes 786440 | tf_op jit(solution)/shard_map/ppermute | solution.py:58
  129.4 15.0 %collective-permute-start.37 = (bf16[128,1024]{1,0:T(8,128)(2,1)S(1)}, bf16[128,1024]{1,0:T(8,128)(2,1)S(1)}, u32[]{:S(2)}, u32[]{:S(2)}) collective-permute-start(bf16[128,1024]{1,0:T(8,128)(2,1)S(1)} %bitcast.13), channel_id=1, source_target_pairs={{0,0},{1,1},{2,2},{3,3},{4,4},{5,5},{6,6},{7,7},{12,8},{13,9},{14,... | collective-permute-start | bytes 786440 | tf_op jit(solution)/shard_map/ppermute | solution.py:43
  144.4 14.5 %collective-permute-start.41 = (bf16[192,1024]{1,0:T(8,128)(2,1)S(1)}, bf16[192,1024]{1,0:T(8,128)(2,1)S(1)}, u32[]{:S(2)}, u32[]{:S(2)}) collective-permute-start(bf16[192,1024]{1,0:T(8,128)(2,1)S(1)} %stack_halves.7.mine_ref), channel_id=1, source_target_pairs={{0,8},{8,0},{16,24},{24,16},{1,9},{9,1},{17,25},{25,17},{2,10},{10... | collective-permute-start | bytes 1179656 | tf_op jit(solution)/shard_map/ppermute | solution.py:64
  145.4 11.9 %collective-permute-start.39 = (bf16[512,256]{1,0:T(8,128)(2,1)S(1)}, bf16[512,256]{1,0:T(8,128)(2,1)S(1)}, u32[]{:S(2)}, u32[]{:S(2)}) collective-permute-start(bf16[512,256]{1,0:T(8,128)(2,1)S(1)} %get-tuple-element.523.refs_4_.refs_2_), channel_id=1, source_target_pairs={{0,4},{1,5},{2,6},{3,7},{4,0},{5,1},{6,2},{7,3},{8,12},{9,13},{10,... | collective-permute-start | bytes 786440 | tf_op jit(solution)/shard_map/ppermute | solution.py:58
  161.6 15.8 %collective-permute-start.46 = (bf16[128,1024]{1,0:T(8,128)(2,1)S(1)}, bf16[128,1024]{1,0:T(8,128)(2,1)S(1)}, u32[]{:S(2)}, u32[]{:S(2)}) collective-permute-start(bf16[128,1024]{1,0:T(8,128)(2,1)S(1)} %collective-permute-done.42.refs_0_.grad_ref.ref), channel_id=1, source_target_pairs={{0,4},{1,5},{2,6},{3,7},{4,0},{5,1},{6,2},{7,3},{8,12},{9,13},{10,... | collective-permute-start | bytes 786440 | tf_op jit(solution)/shard_map/ppermute | solution.py:58
  165.6 11.9 %collective-permute-start.47 = (bf16[128,1024]{1,0:T(8,128)(2,1)S(1)}, bf16[128,1024]{1,0:T(8,128)(2,1)S(1)}, u32[]{:S(2)}, u32[]{:S(2)}) collective-permute-start(bf16[128,1024]{1,0:T(8,128)(2,1)S(1)} %collective-permute-done.42.refs_0_.grad_ref.ref), channel_id=1, source_target_pairs={{0,6},{1,7},{2,4},{3,5},{4,2},{5,3},{6,0},{7,1},{8,14},{9,15},{10,... | collective-permute-start | bytes 786440 | tf_op jit(solution)/shard_map/ppermute | solution.py:58
  185.8 17.0 %collective-permute-start.52 = (bf16[512,512]{1,0:T(8,128)(2,1)S(1)}, bf16[512,512]{1,0:T(8,128)(2,1)S(1)}, u32[]{:S(2)}, u32[]{:S(2)}) collective-permute-start(bf16[512,512]{1,0:T(8,128)(2,1)S(1)} %get-tuple-element.570.refs_0_), channel_id=1, source_target_pairs={{0,8},{24,16},{1,9},{25,17},{2,10},{26,18},{3,11},{27,19},{4,12},{... | collective-permute-start | bytes 1572872 | tf_op jit(solution)/shard_map/ppermute | solution.py:909
  188.8 12.2 %collective-permute-start.50 = (bf16[128,1024]{1,0:T(8,128)(2,1)S(1)}, bf16[128,1024]{1,0:T(8,128)(2,1)S(1)}, u32[]{:S(2)}, u32[]{:S(2)}) collective-permute-start(bf16[128,1024]{1,0:T(8,128)(2,1)S(1)} %get-tuple-element.566), channel_id=1, source_target_pairs={{0,4},{1,5},{2,6},{3,7},{4,0},{5,1},{6,2},{7,3},{8,12},{9,13},{10,... | collective-permute-start | bytes 786440 | tf_op jit(solution)/shard_map/ppermute | solution.py:58
  189.3 13.5 %collective-permute-start.51 = (bf16[128,1024]{1,0:T(8,128)(2,1)S(1)}, bf16[128,1024]{1,0:T(8,128)(2,1)S(1)}, u32[]{:S(2)}, u32[]{:S(2)}) collective-permute-start(bf16[128,1024]{1,0:T(8,128)(2,1)S(1)} %get-tuple-element.567), channel_id=1, source_target_pairs={{0,6},{1,7},{2,4},{3,5},{4,2},{5,3},{6,0},{7,1},{8,14},{9,15},{10,... | collective-permute-start | bytes 786440 | tf_op jit(solution)/shard_map/ppermute | solution.py:58
  202.8 22.1 %collective-permute-start.56 = (bf16[512,512]{1,0:T(8,128)(2,1)}, bf16[512,512]{1,0:T(8,128)(2,1)}, u32[]{:S(2)}, u32[]{:S(2)}) collective-permute-start(bf16[512,512]{1,0:T(8,128)(2,1)} %get-tuple-element.579.refs_3_), channel_id=1, source_target_pairs={{0,8},{24,16},{1,9},{25,17},{2,10},{26,18},{3,11},{27,19},{4,12},{... | collective-permute-start | bytes 1572872 | tf_op jit(solution)/shard_map/ppermute | solution.py:909
  205.0 19.9 %collective-permute-start.57 = (bf16[512,512]{1,0:T(8,128)(2,1)}, bf16[512,512]{1,0:T(8,128)(2,1)}, u32[]{:S(2)}, u32[]{:S(2)}) collective-permute-start(bf16[512,512]{1,0:T(8,128)(2,1)} %turn.13.refs_1_), channel_id=1, source_target_pairs={{8,16},{16,8},{9,17},{17,9},{10,18},{18,10},{11,19},{19,11},{12,20... | collective-permute-start | bytes 1572872 | tf_op jit(solution)/shard_map/ppermute | solution.py:909
  211.6 13.3 %collective-permute-start.54 = (bf16[128,1024]{1,0:T(8,128)(2,1)}, bf16[128,1024]{1,0:T(8,128)(2,1)}, u32[]{:S(2)}, u32[]{:S(2)}) collective-permute-start(bf16[128,1024]{1,0:T(8,128)(2,1)} %get-tuple-element.581.refs_0_.refs_3_), channel_id=1, source_target_pairs={{0,4},{1,5},{2,6},{3,7},{4,0},{5,1},{6,2},{7,3},{8,12},{9,13},{10,... | collective-permute-start | bytes 786440 | tf_op jit(solution)/shard_map/ppermute | solution.py:58
  212.5 12.4 %collective-permute-start.55 = (bf16[128,1024]{1,0:T(8,128)(2,1)}, bf16[128,1024]{1,0:T(8,128)(2,1)}, u32[]{:S(2)}, u32[]{:S(2)}) collective-permute-start(bf16[128,1024]{1,0:T(8,128)(2,1)} %get-tuple-element.581.refs_0_.refs_3_), channel_id=1, source_target_pairs={{0,6},{1,7},{2,4},{3,5},{4,2},{5,3},{6,0},{7,1},{8,14},{9,15},{10,... | collective-permute-start | bytes 786440 | tf_op jit(solution)/shard_map/ppermute | solution.py:58
  226.7 14.6 %collective-permute-start.58 = (bf16[512,512]{1,0:T(8,128)(2,1)S(1)}, bf16[512,512]{1,0:T(8,128)(2,1)S(1)}, u32[]{:S(2)}, u32[]{:S(2)}) collective-permute-start(bf16[512,512]{1,0:T(8,128)(2,1)S(1)} %get-tuple-element.797.b_ref), channel_id=1, source_target_pairs={{0,8},{24,16},{8,0},{16,24},{1,9},{25,17},{9,1},{17,25},{2,10},{26... | collective-permute-start | bytes 1572872 | tf_op jit(solution)/shard_map/ppermute | solution.py:909
  228.3 13.9 %collective-permute-start.59 = (bf16[512,512]{1,0:T(8,128)(2,1)S(1)}, bf16[512,512]{1,0:T(8,128)(2,1)S(1)}, u32[]{:S(2)}, u32[]{:S(2)}) collective-permute-start(bf16[512,512]{1,0:T(8,128)(2,1)S(1)} %get-tuple-element.612.refs_1_), channel_id=1, source_target_pairs={{8,16},{16,8},{9,17},{17,9},{10,18},{18,10},{11,19},{19,11},{12,20... | collective-permute-start | bytes 1572872 | tf_op jit(solution)/shard_map/ppermute | solution.py:909
  243.0 16.1 %collective-permute-start.63 = (bf16[512,512]{1,0:T(8,128)(2,1)S(1)}, bf16[512,512]{1,0:T(8,128)(2,1)S(1)}, u32[]{:S(2)}, u32[]{:S(2)}) collective-permute-start(bf16[512,512]{1,0:T(8,128)(2,1)S(1)} %get-tuple-element.798.b_ref), channel_id=1, source_target_pairs={{0,8},{24,16},{8,0},{16,24},{1,9},{25,17},{9,1},{17,25},{2,10},{26... | collective-permute-start | bytes 1572872 | tf_op jit(solution)/shard_map/ppermute | solution.py:909
  243.1 16.1 %collective-permute-start.64 = (bf16[512,512]{1,0:T(8,128)(2,1)S(1)}, bf16[512,512]{1,0:T(8,128)(2,1)S(1)}, u32[]{:S(2)}, u32[]{:S(2)}) collective-permute-start(bf16[512,512]{1,0:T(8,128)(2,1)S(1)} %get-tuple-element.621.refs_1_), channel_id=1, source_target_pairs={{8,16},{16,8},{9,17},{17,9},{10,18},{18,10},{11,19},{19,11},{12,20... | collective-permute-start | bytes 1572872 | tf_op jit(solution)/shard_map/ppermute | solution.py:909
  245.4 11.5 %collective-permute-start.60 = (bf16[128,1024]{1,0:T(8,128)(2,1)S(1)}, bf16[128,1024]{1,0:T(8,128)(2,1)S(1)}, u32[]{:S(2)}, u32[]{:S(2)}) collective-permute-start(bf16[128,1024]{1,0:T(8,128)(2,1)S(1)} %get-tuple-element.599), channel_id=1, source_target_pairs={{0,2},{1,3},{2,0},{3,1},{4,6},{5,7},{6,4},{7,5},{8,10},{9,11},{10,... | collective-permute-start | bytes 786440 | tf_op jit(solution)/shard_map/ppermute | solution.py:58
  260.0 18.2 %collective-permute-start.68 = (bf16[512,512]{1,0:T(8,128)(2,1)S(1)}, bf16[512,512]{1,0:T(8,128)(2,1)S(1)}, u32[]{:S(2)}, u32[]{:S(2)}) collective-permute-start(bf16[512,512]{1,0:T(8,128)(2,1)S(1)} %get-tuple-element.736.b_ref), channel_id=1, source_target_pairs={{0,8},{24,16},{8,0},{16,24},{1,9},{25,17},{9,1},{17,25},{2,10},{26... | collective-permute-start | bytes 1572872 | tf_op jit(solution)/shard_map/ppermute | solution.py:909
  260.4 17.8 %collective-permute-start.69 = (bf16[512,512]{1,0:T(8,128)(2,1)S(1)}, bf16[512,512]{1,0:T(8,128)(2,1)S(1)}, u32[]{:S(2)}, u32[]{:S(2)}) collective-permute-start(bf16[512,512]{1,0:T(8,128)(2,1)S(1)} %get-tuple-element.648.refs_1_), channel_id=1, source_target_pairs={{8,16},{16,8},{9,17},{17,9},{10,18},{18,10},{11,19},{19,11},{12,20... | collective-permute-start | bytes 1572872 | tf_op jit(solution)/shard_map/ppermute | solution.py:909
  265.7 12.4 %collective-permute-start.67 = (bf16[128,1024]{1,0:T(8,128)(2,1)S(1)}, bf16[128,1024]{1,0:T(8,128)(2,1)S(1)}, u32[]{:S(2)}, u32[]{:S(2)}) collective-permute-start(bf16[128,1024]{1,0:T(8,128)(2,1)S(1)} %get-tuple-element.627.refs_0_), channel_id=1, source_target_pairs={{0,6},{1,7},{2,4},{3,5},{4,2},{5,3},{6,0},{7,1},{8,14},{9,15},{10,... | collective-permute-start | bytes 786440 | tf_op jit(solution)/shard_map/ppermute | solution.py:58
  281.0 14.4 %collective-permute-start.71 = (bf16[512,512]{1,0:T(8,128)(2,1)S(1)}, bf16[512,512]{1,0:T(8,128)(2,1)S(1)}, u32[]{:S(2)}, u32[]{:S(2)}) collective-permute-start(bf16[512,512]{1,0:T(8,128)(2,1)S(1)} %get-tuple-element.737.b_ref), channel_id=1, source_target_pairs={{0,8},{24,16},{8,0},{16,24},{1,9},{25,17},{9,1},{17,25},{2,10},{26... | collective-permute-start | bytes 1572872 | tf_op jit(solution)/shard_map/ppermute | solution.py:909
  281.0 16.2 %collective-permute-start.72 = (bf16[512,512]{1,0:T(8,128)(2,1)S(1)}, bf16[512,512]{1,0:T(8,128)(2,1)S(1)}, u32[]{:S(2)}, u32[]{:S(2)}) collective-permute-start(bf16[512,512]{1,0:T(8,128)(2,1)S(1)} %get-tuple-element.660.refs_1_), channel_id=1, source_target_pairs={{8,16},{16,8},{9,17},{17,9},{10,18},{18,10},{11,19},{19,11},{12,20... | collective-permute-start | bytes 1572872 | tf_op jit(solution)/shard_map/ppermute | solution.py:909
  298.0 17.1 %collective-permute-start.76 = (bf16[512,512]{1,0:T(8,128)(2,1)S(1)}, bf16[512,512]{1,0:T(8,128)(2,1)S(1)}, u32[]{:S(2)}, u32[]{:S(2)}) collective-permute-start(bf16[512,512]{1,0:T(8,128)(2,1)S(1)} %get-tuple-element.754.b_ref), channel_id=1, source_target_pairs={{0,8},{24,16},{8,0},{16,24},{1,9},{25,17},{9,1},{17,25},{2,10},{26... | collective-permute-start | bytes 1572872 | tf_op jit(solution)/shard_map/ppermute | solution.py:909
  298.1 17.0 %collective-permute-start.77 = (bf16[512,512]{1,0:T(8,128)(2,1)S(1)}, bf16[512,512]{1,0:T(8,128)(2,1)S(1)}, u32[]{:S(2)}, u32[]{:S(2)}) collective-permute-start(bf16[512,512]{1,0:T(8,128)(2,1)S(1)} %get-tuple-element.674.refs_1_), channel_id=1, source_target_pairs={{8,16},{16,8},{9,17},{17,9},{10,18},{18,10},{11,19},{19,11},{12,20... | collective-permute-start | bytes 1572872 | tf_op jit(solution)/shard_map/ppermute | solution.py:909
  303.1 12.0 %collective-permute-start.75 = (bf16[128,1024]{1,0:T(8,128)(2,1)S(1)}, bf16[128,1024]{1,0:T(8,128)(2,1)S(1)}, u32[]{:S(2)}, u32[]{:S(2)}) collective-permute-start(bf16[128,1024]{1,0:T(8,128)(2,1)S(1)} %get-tuple-element.656), channel_id=1, source_target_pairs={{0,6},{1,7},{2,4},{3,5},{4,2},{5,3},{6,0},{7,1},{8,14},{9,15},{10,... | collective-permute-start | bytes 786440 | tf_op jit(solution)/shard_map/ppermute | solution.py:58
  315.9 17.2 %collective-permute-start.81 = (bf16[512,512]{1,0:T(8,128)(2,1)S(1)}, bf16[512,512]{1,0:T(8,128)(2,1)S(1)}, u32[]{:S(2)}, u32[]{:S(2)}) collective-permute-start(bf16[512,512]{1,0:T(8,128)(2,1)S(1)} %get-tuple-element.755.b_ref), channel_id=1, source_target_pairs={{0,8},{24,16},{8,0},{16,24},{1,9},{25,17},{9,1},{17,25},{2,10},{26... | collective-permute-start | bytes 1572872 | tf_op jit(solution)/shard_map/ppermute | solution.py:909
  316.0 17.1 %collective-permute-start.82 = (bf16[512,512]{1,0:T(8,128)(2,1)S(1)}, bf16[512,512]{1,0:T(8,128)(2,1)S(1)}, u32[]{:S(2)}, u32[]{:S(2)}) collective-permute-start(bf16[512,512]{1,0:T(8,128)(2,1)S(1)} %get-tuple-element.691.refs_1_), channel_id=1, source_target_pairs={{8,16},{16,8},{9,17},{17,9},{10,18},{18,10},{11,19},{19,11},{12,20... | collective-permute-start | bytes 1572872 | tf_op jit(solution)/shard_map/ppermute | solution.py:909
  321.3 11.8 %collective-permute-start.79 = (bf16[128,1024]{1,0:T(8,128)(2,1)S(1)}, bf16[128,1024]{1,0:T(8,128)(2,1)S(1)}, u32[]{:S(2)}, u32[]{:S(2)}) collective-permute-start(bf16[128,1024]{1,0:T(8,128)(2,1)S(1)} %get-tuple-element.679.refs_0_.refs_3_), channel_id=1, source_target_pairs={{0,4},{1,5},{2,6},{3,7},{4,0},{5,1},{6,2},{7,3},{8,12},{9,13},{10,... | collective-permute-start | bytes 786440 | tf_op jit(solution)/shard_map/ppermute | solution.py:58
  333.9 12.6 %collective-permute-start.83 = (bf16[512,512]{1,0:T(8,128)(2,1)S(1)}, bf16[512,512]{1,0:T(8,128)(2,1)S(1)}, u32[]{:S(2)}, u32[]{:S(2)}) collective-permute-start(bf16[512,512]{1,0:T(8,128)(2,1)S(1)} %get-tuple-element.790.b_ref), channel_id=1, source_target_pairs={{0,8},{24,16},{8,0},{16,24},{1,9},{25,17},{9,1},{17,25},{2,10},{26... | collective-permute-start | bytes 1572872 | tf_op jit(solution)/shard_map/ppermute | solution.py:909
  334.0 12.5 %collective-permute-start.84 = (bf16[512,512]{1,0:T(8,128)(2,1)S(1)}, bf16[512,512]{1,0:T(8,128)(2,1)S(1)}, u32[]{:S(2)}, u32[]{:S(2)}) collective-permute-start(bf16[512,512]{1,0:T(8,128)(2,1)S(1)} %get-tuple-element.718.refs_1_), channel_id=1, source_target_pairs={{8,16},{16,8},{9,17},{17,9},{10,18},{18,10},{11,19},{19,11},{12,20... | collective-permute-start | bytes 1572872 | tf_op jit(solution)/shard_map/ppermute | solution.py:909
  347.4 16.3 %collective-permute-start.88 = (bf16[512,512]{1,0:T(8,128)(2,1)S(1)}, bf16[512,512]{1,0:T(8,128)(2,1)S(1)}, u32[]{:S(2)}, u32[]{:S(2)}) collective-permute-start(bf16[512,512]{1,0:T(8,128)(2,1)S(1)} %get-tuple-element.791.b_ref), channel_id=1, source_target_pairs={{0,8},{24,16},{8,0},{16,24},{1,9},{25,17},{9,1},{17,25},{2,10},{26... | collective-permute-start | bytes 1572872 | tf_op jit(solution)/shard_map/ppermute | solution.py:909
  347.4 16.3 %collective-permute-start.89 = (bf16[512,512]{1,0:T(8,128)(2,1)S(1)}, bf16[512,512]{1,0:T(8,128)(2,1)S(1)}, u32[]{:S(2)}, u32[]{:S(2)}) collective-permute-start(bf16[512,512]{1,0:T(8,128)(2,1)S(1)} %get-tuple-element.730.refs_1_), channel_id=1, source_target_pairs={{8,16},{16,8},{9,17},{17,9},{10,18},{18,10},{11,19},{19,11},{12,20... | collective-permute-start | bytes 1572872 | tf_op jit(solution)/shard_map/ppermute | solution.py:909
  364.5 17.5 %collective-permute-start.93 = (bf16[528,512]{1,0:T(8,128)(2,1)S(1)}, bf16[528,512]{1,0:T(8,128)(2,1)S(1)}, u32[]{:S(2)}, u32[]{:S(2)}) collective-permute-start(bf16[528,512]{1,0:T(8,128)(2,1)S(1)} %get-tuple-element.770.b_ref), channel_id=1, source_target_pairs={{0,8},{24,16},{8,0},{16,24},{1,9},{25,17},{9,1},{17,25},{2,10},{26... | collective-permute-start | bytes 1622024 | tf_op jit(solution)/shard_map/ppermute | solution.py:909
  364.6 17.4 %collective-permute-start.94 = (bf16[512,512]{1,0:T(8,128)(2,1)S(1)}, bf16[512,512]{1,0:T(8,128)(2,1)S(1)}, u32[]{:S(2)}, u32[]{:S(2)}) collective-permute-start(bf16[512,512]{1,0:T(8,128)(2,1)S(1)} %get-tuple-element.743.refs_1_), channel_id=1, source_target_pairs={{8,16},{16,8},{9,17},{17,9},{10,18},{18,10},{11,19},{19,11},{12,20... | collective-permute-start | bytes 1572872 | tf_op jit(solution)/shard_map/ppermute | solution.py:909
  368.6 13.4 %collective-permute-start.91 = (bf16[128,1024]{1,0:T(8,128)(2,1)S(1)}, bf16[128,1024]{1,0:T(8,128)(2,1)S(1)}, u32[]{:S(2)}, u32[]{:S(2)}) collective-permute-start(bf16[128,1024]{1,0:T(8,128)(2,1)S(1)} %copy-done.57), channel_id=1, source_target_pairs={{0,4},{1,5},{2,6},{3,7},{4,0},{5,1},{6,2},{7,3},{8,12},{9,13},{10,... | collective-permute-start | bytes 786440 | tf_op jit(solution)/shard_map/ppermute | solution.py:58
  369.8 12.2 %collective-permute-start.92 = (bf16[128,1024]{1,0:T(8,128)(2,1)S(1)}, bf16[128,1024]{1,0:T(8,128)(2,1)S(1)}, u32[]{:S(2)}, u32[]{:S(2)}) collective-permute-start(bf16[128,1024]{1,0:T(8,128)(2,1)S(1)} %copy-done.55), channel_id=1, source_target_pairs={{0,6},{1,7},{2,4},{3,5},{4,2},{5,3},{6,0},{7,1},{8,14},{9,15},{10,... | collective-permute-start | bytes 786440 | tf_op jit(solution)/shard_map/ppermute | solution.py:58
  382.8 16.9 %collective-permute-start.98 = (bf16[528,512]{1,0:T(8,128)(2,1)S(1)}, bf16[528,512]{1,0:T(8,128)(2,1)S(1)}, u32[]{:S(2)}, u32[]{:S(2)}) collective-permute-start(bf16[528,512]{1,0:T(8,128)(2,1)S(1)} %get-tuple-element.771.b_ref), channel_id=1, source_target_pairs={{0,8},{24,16},{8,0},{16,24},{1,9},{25,17},{9,1},{17,25},{2,10},{26... | collective-permute-start | bytes 1622024 | tf_op jit(solution)/shard_map/ppermute | solution.py:909
  382.9 16.9 %collective-permute-start.99 = (bf16[528,512]{1,0:T(8,128)(2,1)S(1)}, bf16[528,512]{1,0:T(8,128)(2,1)S(1)}, u32[]{:S(2)}, u32[]{:S(2)}) collective-permute-start(bf16[528,512]{1,0:T(8,128)(2,1)S(1)} %get-tuple-element.761.refs_0_), channel_id=1, source_target_pairs={{8,16},{16,8},{9,17},{17,9},{10,18},{18,10},{11,19},{19,11},{12,20... | collective-permute-start | bytes 1622024 | tf_op jit(solution)/shard_map/ppermute | solution.py:909
  387.7 12.1 %collective-permute-start.96 = (bf16[128,1024]{1,0:T(8,128)(2,1)S(1)}, bf16[128,1024]{1,0:T(8,128)(2,1)S(1)}, u32[]{:S(2)}, u32[]{:S(2)}) collective-permute-start(bf16[128,1024]{1,0:T(8,128)(2,1)S(1)} %get-tuple-element.740), channel_id=1, source_target_pairs={{0,4},{1,5},{2,6},{3,7},{4,0},{5,1},{6,2},{7,3},{8,12},{9,13},{10,... | collective-permute-start | bytes 786440 | tf_op jit(solution)/shard_map/ppermute | solution.py:58
  400.6 14.4 %collective-permute-start.103 = (bf16[528,512]{1,0:T(8,128)(2,1)S(1)}, bf16[528,512]{1,0:T(8,128)(2,1)S(1)}, u32[]{:S(2)}, u32[]{:S(2)}) collective-permute-start(bf16[528,512]{1,0:T(8,128)(2,1)S(1)} %get-tuple-element.767.b_ref), channel_id=1, source_target_pairs={{8,0},{16,24},{9,1},{17,25},{10,2},{18,26},{11,3},{19,27},{12,4},{... | collective-permute-start | bytes 1622024 | tf_op jit(solution)/shard_map/ppermute | solution.py:909
  402.4 12.8 %collective-permute-start.104 = (bf16[528,512]{1,0:T(8,128)(2,1)S(1)}, bf16[528,512]{1,0:T(8,128)(2,1)S(1)}, u32[]{:S(2)}, u32[]{:S(2)}) collective-permute-start(bf16[528,512]{1,0:T(8,128)(2,1)S(1)} %get-tuple-element.776.refs_0_), channel_id=1, source_target_pairs={{8,16},{16,8},{9,17},{17,9},{10,18},{18,10},{11,19},{19,11},{12,20... | collective-permute-start | bytes 1622024 | tf_op jit(solution)/shard_map/ppermute | solution.py:909
  415.3 13.7 %collective-permute-start.108 = (bf16[528,512]{1,0:T(8,128)(2,1)S(1)}, bf16[528,512]{1,0:T(8,128)(2,1)S(1)}, u32[]{:S(2)}, u32[]{:S(2)}) collective-permute-start(bf16[528,512]{1,0:T(8,128)(2,1)S(1)} %turn.25.b_ref), channel_id=1, source_target_pairs={{8,0},{16,24},{9,1},{17,25},{10,2},{18,26},{11,3},{19,27},{12,4},{... | collective-permute-start | bytes 1622024 | tf_op jit(solution)/shard_map/ppermute | solution.py:909
  429.7 21.6 %collective-permute-start.109 = (bf16[176,768]{1,0:T(8,128)(2,1)S(1)}, bf16[176,768]{1,0:T(8,128)(2,1)S(1)}, u32[]{:S(2)}, u32[]{:S(2)}) collective-permute-start(bf16[176,768]{1,0:T(8,128)(2,1)S(1)} %get-tuple-element.781), channel_id=1, source_target_pairs={{0,2},{1,3},{2,0},{3,1},{4,6},{5,7},{6,4},{7,5},{8,10},{9,11},{10,... | collective-permute-start | bytes 811016 | tf_op jit(solution)/shard_map/ppermute | solution.py:58
  431.5 19.8 %collective-permute-start.110 = (bf16[176,768]{1,0:T(8,128)(2,1)S(1)}, bf16[176,768]{1,0:T(8,128)(2,1)S(1)}, u32[]{:S(2)}, u32[]{:S(2)}) collective-permute-start(bf16[176,768]{1,0:T(8,128)(2,1)S(1)} %get-tuple-element.782), channel_id=1, source_target_pairs={{0,4},{1,5},{2,6},{3,7},{4,0},{5,1},{6,2},{7,3},{8,12},{9,13},{10,... | collective-permute-start | bytes 811016 | tf_op jit(solution)/shard_map/ppermute | solution.py:58
  431.9 19.4 %collective-permute-start.111 = (bf16[176,768]{1,0:T(8,128)(2,1)S(1)}, bf16[176,768]{1,0:T(8,128)(2,1)S(1)}, u32[]{:S(2)}, u32[]{:S(2)}) collective-permute-start(bf16[176,768]{1,0:T(8,128)(2,1)S(1)} %get-tuple-element.783), channel_id=1, source_target_pairs={{0,6},{1,7},{2,4},{3,5},{4,2},{5,3},{6,0},{7,1},{8,14},{9,15},{10,... | collective-permute-start | bytes 811016 | tf_op jit(solution)/shard_map/ppermute | solution.py:58
  433.2 15.2 %collective-permute-start.112 = (bf16[128,1024]{1,0:T(8,128)(2,1)S(1)}, bf16[128,1024]{1,0:T(8,128)(2,1)S(1)}, u32[]{:S(2)}, u32[]{:S(2)}) collective-permute-start(bf16[128,1024]{1,0:T(8,128)(2,1)S(1)} %get-tuple-element.784), channel_id=1, source_target_pairs={{0,0},{1,1},{10,2},{11,3},{20,4},{21,5},{30,6},{31,7},{16,12},{17,... | collective-permute-start | bytes 786440 | tf_op jit(solution)/shard_map/ppermute | solution.py:43
  435.1 16.1 %collective-permute-start.113 = (bf16[128,1024]{1,0:T(8,128)(2,1)S(1)}, bf16[128,1024]{1,0:T(8,128)(2,1)S(1)}, u32[]{:S(2)}, u32[]{:S(2)}) collective-permute-start(bf16[128,1024]{1,0:T(8,128)(2,1)S(1)} %get-tuple-element.785), channel_id=1, source_target_pairs={{0,0},{1,1},{10,2},{11,3},{20,4},{21,5},{30,6},{31,7},{16,12},{17,... | collective-permute-start | bytes 786440 | tf_op jit(solution)/shard_map/ppermute | solution.py:43
  (131 other events, 1801.1 us)

commit v8 on v7

--- a/solution.py
+++ b/solution.py
@@ -926,60 +926,68 @@
         return values
 
 
-def write_layer(net, layer, layers, before, down, proj, up, qkv):
+def write_layer(net, layer, layers, before, attention, feed):
     n_p = net.n_p
-    rows = up[0].shape[0]
     cw, fw = D // n_p, FF // n_p
-    split = isinstance(qkv[0], tuple)
+    proj, qkv = attention or (None, [])
+    up, down = feed or ([], [])
+    rows = (up[0] if feed else proj).shape[0]
+    split = len(qkv) > 0 and isinstance(qkv[0], tuple)
     flat = [v for pair in qkv for v in pair] if split else list(qkv)
-    n_in = 3 + n_p + len(flat)
-    skip = 0 if before is None else 4
     steps = min(4, rows // 16)
-    part = rows // steps
-    down_rows = down[0].shape[0]
-    down_part = down_rows // steps
+    which = [0, 1] * (attention is not None) + [2, 3] * (feed is not None)
+    ins = [proj] * (attention is not None) + [*flat, *up, *down]
+    n_in = len(ins)
+    skip = 0 if before is None else len(which)
 
     def body(place, *refs):
         p = place[0]
-        downs, proj_ref = refs[:2], refs[2]
-        ups, qkvs = refs[3 : 3 + n_p], refs[3 + n_p : n_in]
-        qkv_out, proj_out, up_out, down_out = refs[n_in + skip :]
-        proj_out[0] = proj_ref[...].astype(F32)
-        for k in range(2):
-            down_out[0, :, k * (D // 2) : (k + 1) * (D // 2)] = downs[k][...].astype(F32)
-        for j in range(n_p):
-            up_out[0, :, tile(p ^ j, fw)] = ups[j][...].astype(F32)
-            for i in range(3):
-                to = tile(i * n_p + (p ^ j), cw)
-                ref, at = (qkvs[2 * j + i // 2], i % 2) if split else (qkvs[j], i)
-                qkv_out[0, :, to] = ref[:, at * cw : (at + 1) * cw].astype(F32)
-
-    def of_rows(v, size):
-        return pl.BlockSpec((size, v.shape[1]), lambda i: (i, 0))
-
-    ins = [*down, proj, *up, *flat]
-    specs = [IN_SMEM] + [of_rows(v, down_part) for v in down] + [of_rows(v, part) for v in [proj, *up, *flat]]
+        outs = refs[n_in + skip :]
+        taken = 0
+        if attention is not None:
+            qkvs = refs[1 : 1 + len(flat)]
+            taken = 1 + len(flat)
+            qkv_out, proj_out, *outs = outs
+            proj_out[0] = refs[0][...].astype(F32)
+            for j in range(n_p):
+                for i in range(3):
+                    to = tile(i * n_p + (p ^ j), cw)
+                    ref, at = (qkvs[2 * j + i // 2], i % 2) if split else (qkvs[j], i)
+                    qkv_out[0, :, to] = ref[:, at * cw : (at + 1) * cw].astype(F32)
+        if feed is not None:
+            ups, downs = refs[taken : taken + n_p], refs[taken + n_p : n_in]
+            up_out, down_out = outs
+            for k in range(2):
+                down_out[0, :, k * (D // 2) : (k + 1) * (D // 2)] = downs[k][...].astype(F32)
+            for j in range(n_p):
+                up_out[0, :, tile(p ^ j, fw)] = ups[j][...].astype(F32)
+
+    down_rows = down[0].shape[0] if feed else 0
+    all_shapes = [(rows, 3 * D), (rows, D), (rows, FF), (down_rows, D)]
+    shapes = [all_shapes[k] for k in which]
+    specs = [IN_SMEM] + [pl.BlockSpec((rows // steps, v.shape[1]), lambda i: (i, 0)) for v in ins[: n_in - len(down)]]
+    specs += [pl.BlockSpec((down_rows // steps, v.shape[1]), lambda i: (i, 0)) for v in down]
     aliases = {}
     if before is not None:
-        aliases = {1 + n_in + k: k for k in range(4)}
-        specs += [IN_ANY] * 4
-        ins = ins + list(before)
-    shapes = [(rows, 3 * D), (rows, D), (rows, FF), (down_rows, D)]
-    sizes = [part, part, part, down_part]
+        aliases = {1 + n_in + k: k for k in range(skip)}
+        specs += [IN_ANY] * skip
+        ins = ins + [before[k] for k in which]
     moved = 6 * sum(a * b for a, b in shapes)
-    return pl.pallas_call(
+    new = pl.pallas_call(
         body,
         grid=(steps,),
         out_shape=[jax.ShapeDtypeStruct((layers, *shape), F32) for shape in shapes],
         in_specs=specs,
-        out_specs=[
-            pl.BlockSpec((1, size, shape[1]), lambda i: (layer, i, 0)) for size, shape in zip(sizes, shapes)
-        ],
+        out_specs=[pl.BlockSpec((1, shape[0] // steps, shape[1]), lambda i: (layer, i, 0)) for shape in shapes],
         input_output_aliases=aliases,
         compiler_params=pltpu.CompilerParams(vmem_limit_bytes=16 << 20),
         cost_estimate=pl.CostEstimate(flops=0, bytes_accessed=moved, transcendentals=0),
         name="write_layer",
     )(net.place, *ins)
+    out = [None] * 4 if before is None else list(before)
+    for k, v in zip(which, new):
+        out[k] = v
+    return out
 
 
 def on_device(
@@ -1145,9 +1153,11 @@
         dm = flow.collect(dm)
     pieces, proj_last = to_owners(sums[0][2], 2 * layers * n_p)
     dm, sent_out = net.from_place(dm), net.from_place(sent_out)
-    out = write_layer(net, 1, layers, None, [c.value for c in sums[1][0]], proj_g, up_pieces, qkv_pieces)
+    downs = [[c.value for c in sums[layer][0]] for layer in range(layers)]
+    out = write_layer(net, 1, layers, None, (proj_g, qkv_pieces), (up_pieces, downs[1]))
+    out = write_layer(net, 0, layers, out, None, (up_last, downs[0]))
     *small_out, input_grad, sent_out = sum_small(net, layers, pieces, sizes, D // net.n_f, [dm, sent_out])
-    out = write_layer(net, 0, layers, out, [c.value for c in sums[0][0]], proj_last, up_last, pieces)
+    out = write_layer(net, 0, layers, out, (proj_last, pieces), None)
     return (
         sent_out[None],
         input_grad[None],

time: 466 us -> 465 us (level)
  transfers between devices with their start and end apart: 114 -> 114, of which waited for: 48 -> 48; matrix products, arithmetic and copies ran while one was open for 0% -> 0% of each run, Pallas kernels for 18% -> 19%
where the time goes in v8:
time: 465 us; the launch traced here: 456 us
  waiting for transfers between devices  159 us (34%)
  starting transfers between devices  154 us (33%)
  Pallas kernels  112 us (24%)
  blocking collectives  21.7 us (5%)
  local copies, waits for them, and re-layouts  6.02 us (1%)
    ppermute x66, waiting for transfers between devices, chip(): return lax.ppermute(v, 'fsdp', xor_pairs(self.n_f, 2 * j))  136 us
    pallas_call x73, Pallas kernels, run(): pl.pallas_call(body, out_shape=[jax.ShapeDtypeStruct(shape, dtype) for sh...  103 us
    ppermute x66, starting transfers between devices, chip(): return lax.ppermute(v, 'fsdp', xor_pairs(self.n_f, 2 * j))  79.8 us
    ppermute x26, starting transfers between devices, start(): lax.ppermute(v, 'seq', m[3])  44.1 us
    ppermute x7, starting transfers between devices, send(): return lax.ppermute(v, ('seq', 'fsdp'), pairs)  22.2 us
    all_to_all x4, blocking collectives, swap_cores(): return lax.all_to_all(both, 'fsdp', 0, 0, axis_index_groups=pair_groups)  21.7 us
  transfers between devices with their start and end apart: 114, of which 48 were waited for; matrix products, arithmetic and copies ran while one was open for 0% of the time, Pallas kernels for 19%

profile of v8, /device:TPU:10, one launch (start us, length us, event | category | flops | bytes accessed | tf_op | source)
XLA Modules:
  0.0 455.7 jit_solution(2060992701287220170)
XLA Ops:
  1.8 3.4 collective-permute-start
  11.7 3.6 collective-permute-start.4
  15.3 3.4 collective-permute-start.1
  21.0 3.9 collective-permute-done.4.refs_1_
  33.0 5.4 %collective-permute-done.7.refs_1_.refs_12_ = bf16[144,1024]{1,0:T(8,128)(2,1)S(1)} collective-permute-done((bf16[144,1024]{1,0:T(8,128)(2,1)S(1)}, bf16[144,1024]{1,0:T(8,128)(2,1)S(1)}, u32[]{:S(2)}, u32[]{:S(2)}) %collective-permute-start.7) | collective-permute-done | bytes 294944 | tf_op jit(solution)/shard_map/ppermute | solution.py:58
  38.4 4.3 collective-permute-done.8.refs_2_.refs_13_
  45.7 3.3 collective-permute-done.11.refs_6_.refs_10_
  53.8 5.3 %attend.2 = (s32[1,512]{1,0:T(1,128)S(1)}, s32[512,1]{1,0:T(8,128)S(1)}, bf16[512,1024]{1,0:T(8,128)(2,1)S(1)}, bf16[512,768]{1,0:T(8,128)(2,1)S(1)}, bf16[512,256]{1,0:T(8,128)(2,1)S(1)}) custom-call(s32[3]{0:T(128)S(1)} %pad_add_fusion.2.place, bf16[144,1024]{1,0:T(8,128)(2,1)S(1)} %put_small.1.refs_0_.refs_11_.hidden_ref, ...), custom_call_target="tpu_custom_call" | custom-call | flops 805306368 | bytes 2785292 | tf_op jit(solution)/shard_map/attend/pallas_call | solution.py:93
  64.4 5.8 %collective-permute-done.16.refs_5_ = bf16[512,256]{1,0:T(8,128)(2,1)S(1)} collective-permute-done((bf16[512,256]{1,0:T(8,128)(2,1)S(1)}, bf16[512,256]{1,0:T(8,128)(2,1)S(1)}, u32[]{:S(2)}, u32[]{:S(2)}) %collective-permute-start.16) | collective-permute-done | bytes 262176 | tf_op jit(solution)/shard_map/ppermute | solution.py:58
  70.2 3.5 collective-permute-done.17.refs_6_
  77.4 2.7 close_attention.2
  85.4 4.1 feed_forward.2
  90.9 3.2 collective-permute-done.23.refs_1_
  101.2 5.8 %collective-permute-done.25.refs_1_ = bf16[128,1024]{1,0:T(8,128)(2,1)S(1)} collective-permute-done((bf16[128,1024]{1,0:T(8,128)(2,1)S(1)}, bf16[128,1024]{1,0:T(8,128)(2,1)S(1)}, u32[]{:S(2)}, u32[]{:S(2)}) %collective-permute-start.25) | collective-permute-done | bytes 262176 | tf_op jit(solution)/shard_map/ppermute | solution.py:58
  106.9 3.7 collective-permute-done.26.refs_2_
  118.0 5.7 %collective-permute-done.29.refs_1_ = bf16[128,1024]{1,0:T(8,128)(2,1)S(1)} collective-permute-done((bf16[128,1024]{1,0:T(8,128)(2,1)S(1)}, bf16[128,1024]{1,0:T(8,128)(2,1)S(1)}, u32[]{:S(2)}, u32[]{:S(2)}) %collective-permute-start.29) | collective-permute-done | bytes 262176 | tf_op jit(solution)/shard_map/ppermute | solution.py:58
  123.7 5.6 %collective-permute-done.30.refs_2_ = bf16[128,1024]{1,0:T(8,128)(2,1)S(1)} collective-permute-done((bf16[128,1024]{1,0:T(8,128)(2,1)S(1)}, bf16[128,1024]{1,0:T(8,128)(2,1)S(1)}, u32[]{:S(2)}, u32[]{:S(2)}) %collective-permute-start.30) | collective-permute-done | bytes 262176 | tf_op jit(solution)/shard_map/ppermute | solution.py:58
  129.4 3.0 collective-permute-start.37
  136.6 5.3 %attend.3 = (bf16[512,1024]{1,0:T(8,128)(2,1)S(1)}, bf16[512,768]{1,0:T(8,128)(2,1)S(1)}, bf16[512,256]{1,0:T(8,128)(2,1)S(1)}) custom-call(s32[3]{0:T(128)S(1)} %pad_add_fusion.2.place, bf16[128,1024]{1,0:T(8,128)(2,1)S(1)} %get-tuple-element.502.refs_0_, bf16[128,1024]{1,0:T(8,128)(2,1)S(1)} %collective-permute-done.29.refs_1_, ...), custom_call_target="tpu_custom_call" | custom-call | flops 805306368 | bytes 2658316 | tf_op jit(solution)/shard_map/attend/pallas_call | solution.py:93
  148.0 5.9 %collective-permute-start.42 = (bf16[128,1024]{1,0:T(8,128)(2,1)S(1)}, bf16[128,1024]{1,0:T(8,128)(2,1)S(1)}, u32[]{:S(2)}, u32[]{:S(2)}) collective-permute-start(bf16[128,1024]{1,0:T(8,128)(2,1)S(1)} %collective-permute-done.37), channel_id=1, source_target_pairs={{0,0},{1,1},{2,10},{3,11},{4,20},{5,21},{6,30},{7,31},{8,16},{9,17... | collective-permute-start | bytes 786440 | tf_op jit(solution)/shard_map/ppermute | solution.py:43
  153.9 3.4 collective-permute-done.39.refs_6_
  161.6 4.0 collective-permute-start.46
  165.6 2.7 close_attention.3
  168.4 4.1 feed_forward.3
  172.5 4.9 %collective-permute-done.46.refs_2_ = bf16[128,1024]{1,0:T(8,128)(2,1)S(1)} collective-permute-done((bf16[128,1024]{1,0:T(8,128)(2,1)S(1)}, bf16[128,1024]{1,0:T(8,128)(2,1)S(1)}, u32[]{:S(2)}, u32[]{:S(2)}) %collective-permute-start.46) | collective-permute-done | bytes 262176 | tf_op jit(solution)/shard_map/ppermute | solution.py:58
  179.4 5.4 %feed_back.2 = (bf16[128,1024]{1,0:T(8,128)(2,1)S(1)}, bf16[128,1024]{1,0:T(8,128)(2,1)S(1)}, bf16[128,1024]{1,0:T(8,128)(2,1)S(1)}, bf16[128,1024]{1,0:T(8,128)...) custom-call(s32[3]{0:T(128)S(1)} %pad_add_fusion.2.place, ...), custom_call_target="tpu_custom_call" | custom-call | flops 2147483648 | bytes 7340044 | tf_op jit(solution)/shard_map/feed_back/pallas_call | solution.py:93
  192.7 5.4 %all_to_all.20.ref = bf16[2,512,1024]{2,1,0:T(8,128)(2,1)S(1)} all-to-all(bf16[2,512,1024]{2,1,0:T(8,128)(2,1)S(1)} %up_weight_grad.2), channel_id=1, replica_groups={{0,1},{2,3},{4,5},{6,7},{8,9},{10,11},{12,13},{14,15},{16,17},{18,19},{..., dimensions={0} | all-to-all | bytes 4194304 | tf_op jit(solution)/shard_map/all_to_all | solution.py:1026
  198.1 2.9 collective-permute-done.50.refs_2_
  214.1 5.7 %collective-permute-done.53.refs_1_.refs_4_ = bf16[128,1024]{1,0:T(8,128)(2,1)} collective-permute-done((bf16[128,1024]{1,0:T(8,128)(2,1)}, bf16[128,1024]{1,0:T(8,128)(2,1)}, u32[]{:S(2)}, u32[]{:S(2)}) %collective-permute-start.53) | collective-permute-done | bytes 262176 | tf_op jit(solution)/shard_map/ppermute | solution.py:58
  219.8 5.1 %collective-permute-done.54.refs_2_.refs_5_ = bf16[128,1024]{1,0:T(8,128)(2,1)} collective-permute-done((bf16[128,1024]{1,0:T(8,128)(2,1)}, bf16[128,1024]{1,0:T(8,128)(2,1)}, u32[]{:S(2)}, u32[]{:S(2)}) %collective-permute-start.54) | collective-permute-done | bytes 262176 | tf_op jit(solution)/shard_map/ppermute | solution.py:58
  228.3 3.3 collective-permute-start.59
  231.6 9.6 %attend_back.2 = (bf16[128,1024]{1,0:T(8,128)(2,1)S(1)}, bf16[128,1024]{1,0:T(8,128)(2,1)S(1)}, bf16[128,1024]{1,0:T(8,128)(2,1)S(1)}, bf16[128,1024]{1,0:T(8,12...) custom-call(s32[3]{0:T(128)S(1)} %pad_add_fusion.2.place, ...), custom_call_target="tpu_custom_call" | custom-call | flops 2147483648 | bytes 5509132 | tf_op jit(solution)/shard_map/attend_back/pallas_call | solution.py:93
  249.0 2.6 attend_weight_grad.2
  251.5 5.4 %all_to_all.21.ref = bf16[2,512,1024]{2,1,0:T(8,128)(2,1)S(1)} all-to-all(bf16[2,512,1024]{2,1,0:T(8,128)(2,1)S(1)} %attend_weight_grad.2), channel_id=1, replica_groups={{0,1},{2,3},{4,5},{6,7},{8,9},{10,11},{12,13},{14,15},{16,17},{18,19},{..., dimensions={0} | all-to-all | bytes 4194304 | tf_op jit(solution)/shard_map/all_to_all | solution.py:1026
  260.4 3.5 collective-permute-start.69
  267.4 5.7 %collective-permute-done.65.refs_1_ = bf16[128,1024]{1,0:T(8,128)(2,1)S(1)} collective-permute-done((bf16[128,1024]{1,0:T(8,128)(2,1)S(1)}, bf16[128,1024]{1,0:T(8,128)(2,1)S(1)}, u32[]{:S(2)}, u32[]{:S(2)}) %collective-permute-start.65) | collective-permute-done | bytes 262176 | tf_op jit(solution)/shard_map/ppermute | solution.py:58
  273.1 5.0 %collective-permute-done.67.refs_3_ = bf16[128,1024]{1,0:T(8,128)(2,1)S(1)} collective-permute-done((bf16[128,1024]{1,0:T(8,128)(2,1)S(1)}, bf16[128,1024]{1,0:T(8,128)(2,1)S(1)}, u32[]{:S(2)}, u32[]{:S(2)}) %collective-permute-start.67) | collective-permute-done | bytes 262176 | tf_op jit(solution)/shard_map/ppermute | solution.py:58
  281.1 3.1 collective-permute-start.72
  284.2 5.4 %feed_back.3 = (bf16[128,1024]{1,0:T(8,128)(2,1)S(1)}, bf16[128,1024]{1,0:T(8,128)(2,1)S(1)}, bf16[128,1024]{1,0:T(8,128)(2,1)S(1)}, bf16[128,1024]{1,0:T(8,128)...) custom-call(s32[3]{0:T(128)S(1)} %pad_add_fusion.2.place, ...), custom_call_target="tpu_custom_call" | custom-call | flops 2147483648 | bytes 7340044 | tf_op jit(solution)/shard_map/feed_back/pallas_call | solution.py:93
  289.9 5.5 %collective-permute-done.71.refs_4_.a_ref = bf16[512,512]{1,0:T(8,128)(2,1)S(1)} collective-permute-done((bf16[512,512]{1,0:T(8,128)(2,1)S(1)}, bf16[512,512]{1,0:T(8,128)(2,1)S(1)}, u32[]{:S(2)}, u32[]{:S(2)}) %collective-permute-start.71) | collective-permute-done | bytes 524320 | tf_op jit(solution)/shard_map/ppermute | solution.py:909
  298.1 3.1 collective-permute-start.77
  306.7 5.4 %all_to_all.22.ref = bf16[2,512,1024]{2,1,0:T(8,128)(2,1)S(1)} all-to-all(bf16[2,512,1024]{2,1,0:T(8,128)(2,1)S(1)} %up_weight_grad.3), channel_id=1, replica_groups={{0,1},{2,3},{4,5},{6,7},{8,9},{10,11},{12,13},{14,15},{16,17},{18,19},{..., dimensions={0} | all-to-all | bytes 4194304 | tf_op jit(solution)/shard_map/all_to_all | solution.py:1026
  312.1 3.0 collective-permute-done.75.refs_3_
  316.0 3.1 collective-permute-start.82
  324.3 5.0 %collective-permute-done.78.refs_1_.refs_4_ = bf16[128,1024]{1,0:T(8,128)(2,1)S(1)} collective-permute-done((bf16[128,1024]{1,0:T(8,128)(2,1)S(1)}, bf16[128,1024]{1,0:T(8,128)(2,1)S(1)}, u32[]{:S(2)}, u32[]{:S(2)}) %collective-permute-start.78) | collective-permute-done | bytes 262176 | tf_op jit(solution)/shard_map/ppermute | solution.py:58
  329.3 3.8 collective-permute-done.79.refs_2_.refs_5_
  334.0 3.1 collective-permute-start.84
  337.4 9.2 %attend_back.3 = (bf16[128,1024]{1,0:T(8,128)(2,1)S(1)}, bf16[128,1024]{1,0:T(8,128)(2,1)S(1)}, bf16[128,1024]{1,0:T(8,128)(2,1)S(1)}, bf16[128,1024]{1,0:T(8,12...) custom-call(s32[3]{0:T(128)S(1)} %pad_add_fusion.2.place, ...), custom_call_target="tpu_custom_call" | custom-call | flops 2147483648 | bytes 6688780 | tf_op jit(solution)/shard_map/attend_back/pallas_call | solution.py:93
  347.5 2.9 collective-permute-start.89
  356.0 5.5 %all_to_all.23.ref = bf16[2,528,1024]{2,1,0:T(8,128)(2,1)S(1)} all-to-all(bf16[2,528,1024]{2,1,0:T(8,128)(2,1)S(1)} %attend_weight_grad.3), channel_id=1, replica_groups={{0,1},{2,3},{4,5},{6,7},{8,9},{10,11},{12,13},{14,15},{16,17},{18,19},{..., dimensions={0} | all-to-all | bytes 4325376 | tf_op jit(solution)/shard_map/all_to_all | solution.py:1026
  364.6 2.9 collective-permute-start.94
  371.1 5.7 %collective-permute-done.90.refs_1_ = bf16[128,1024]{1,0:T(8,128)(2,1)S(1)} collective-permute-done((bf16[128,1024]{1,0:T(8,128)(2,1)S(1)}, bf16[128,1024]{1,0:T(8,128)(2,1)S(1)}, u32[]{:S(2)}, u32[]{:S(2)}) %collective-permute-start.90) | collective-permute-done | bytes 262176 | tf_op jit(solution)/shard_map/ppermute | solution.py:58
  376.8 5.2 %collective-permute-done.91.refs_2_ = bf16[128,1024]{1,0:T(8,128)(2,1)S(1)} collective-permute-done((bf16[128,1024]{1,0:T(8,128)(2,1)S(1)}, bf16[128,1024]{1,0:T(8,128)(2,1)S(1)}, u32[]{:S(2)}, u32[]{:S(2)}) %collective-permute-start.91) | collective-permute-done | bytes 262176 | tf_op jit(solution)/shard_map/ppermute | solution.py:58
  382.9 2.9 collective-permute-start.99
  390.1 5.8 %collective-permute-done.95.refs_6_ = bf16[128,1024]{1,0:T(8,128)(2,1)S(1)} collective-permute-done((bf16[128,1024]{1,0:T(8,128)(2,1)S(1)}, bf16[128,1024]{1,0:T(8,128)(2,1)S(1)}, u32[]{:S(2)}, u32[]{:S(2)}) %collective-permute-start.95) | collective-permute-done | bytes 262176 | tf_op jit(solution)/shard_map/ppermute | solution.py:58
  395.9 3.9 collective-permute-done.96.refs_7_
  402.4 3.0 collective-permute-start.104
  411.9 3.2 collective-permute-done.101.refs_3_
  421.0 3.2 collective-permute-done.105.refs_1_
  424.2 4.2 collective-permute-done.106.refs_2_
  437.6 3.5 write_layer.3
  441.1 2.9 write_layer.5
  444.0 4.4 collective-permute-done.112.refs_4_
  448.4 2.8 collective-permute-done.113.refs_5_
  (416 shorter events, 175.0 us)
Async XLA Ops:
  1.8 13.5 %collective-permute-start = (bf16[64,1024]{1,0:T(8,128)(2,1)S(1)}, bf16[64,1024]{1,0:T(8,128)(2,1)S(1)}, u32[]{:S(2)}, u32[]{:S(2)}) collective-permute-start(bf16[64,1024]{1,0:T(8,128)(2,1)S(1)} %get-tuple-element.823), channel_id=1, source_target_pairs={{0,0},{1,1},{2,2},{3,3},{4,4},{5,5},{6,6},{7,7},{12,8},{13,9},{14,... | collective-permute-start | bytes 393224 | tf_op jit(solution)/shard_map/ppermute | solution.py:43
  8.6 12.4 %collective-permute-start.3 = (bf16[64,1792]{1,0:T(8,128)(2,1)S(1)}, bf16[64,1792]{1,0:T(8,128)(2,1)S(1)}, u32[]{:S(2)}, u32[]{:S(2)}) collective-permute-start(bf16[64,1792]{1,0:T(8,128)(2,1)S(1)} %get-tuple-element.418), channel_id=1, source_target_pairs={{0,2},{1,3},{2,0},{3,1},{4,6},{5,7},{6,4},{7,5},{8,10},{9,11},{10,... | collective-permute-start | bytes 688136 | tf_op jit(solution)/shard_map/ppermute | solution.py:58
  9.2 17.5 %collective-permute-start.2 = (bf16[80,1024]{1,0:T(8,128)(2,1)S(1)}, bf16[80,1024]{1,0:T(8,128)(2,1)S(1)}, u32[]{:S(2)}, u32[]{:S(2)}) collective-permute-start(bf16[80,1024]{1,0:T(8,128)(2,1)S(1)} %pad_add_fusion), channel_id=1, source_target_pairs={{0,0},{1,1},{2,10},{3,11},{4,20},{5,21},{6,30},{7,31},{12,16},{13,... | collective-permute-start | bytes 491528 | tf_op jit(solution)/shard_map/ppermute | solution.py:43
  11.7 13.3 %collective-permute-start.4 = (bf16[64,1792]{1,0:T(8,128)(2,1)S(1)}, bf16[64,1792]{1,0:T(8,128)(2,1)S(1)}, u32[]{:S(2)}, u32[]{:S(2)}) collective-permute-start(bf16[64,1792]{1,0:T(8,128)(2,1)S(1)} %get-tuple-element.419), channel_id=1, source_target_pairs={{0,4},{1,5},{2,6},{3,7},{4,0},{5,1},{6,2},{7,3},{8,12},{9,13},{10,... | collective-permute-start | bytes 688136 | tf_op jit(solution)/shard_map/ppermute | solution.py:58
  15.3 11.4 %collective-permute-start.1 = (bf16[64,1024]{1,0:T(8,128)(2,1)S(1)}, bf16[64,1024]{1,0:T(8,128)(2,1)S(1)}, u32[]{:S(2)}, u32[]{:S(2)}) collective-permute-start(bf16[64,1024]{1,0:T(8,128)(2,1)S(1)} %collective-permute-done), channel_id=1, source_target_pairs={{0,0},{1,1},{2,10},{3,11},{4,20},{5,21},{6,30},{7,31},{8,16},{9,17... | collective-permute-start | bytes 393224 | tf_op jit(solution)/shard_map/ppermute | solution.py:43
  26.7 17.3 %collective-permute-start.10 = (bf16[192,1792]{1,0:T(8,128)(2,1)S(1)}, bf16[192,1792]{1,0:T(8,128)(2,1)S(1)}, u32[]{:S(2)}, u32[]{:S(2)}) collective-permute-start(bf16[192,1792]{1,0:T(8,128)(2,1)S(1)} %stack_halves.4.mine_ref), channel_id=1, source_target_pairs={{0,8},{8,0},{16,24},{24,16},{1,9},{9,1},{17,25},{25,17},{2,10},{10... | collective-permute-start | bytes 2064392 | tf_op jit(solution)/shard_map/ppermute | solution.py:64
  29.1 13.6 %collective-permute-start.8 = (bf16[144,1024]{1,0:T(8,128)(2,1)S(1)}, bf16[144,1024]{1,0:T(8,128)(2,1)S(1)}, u32[]{:S(2)}, u32[]{:S(2)}) collective-permute-start(bf16[144,1024]{1,0:T(8,128)(2,1)S(1)} %put_small.1.refs_0_.refs_11_.hidden_ref), channel_id=1, source_target_pairs={{0,4},{1,5},{2,6},{3,7},{4,0},{5,1},{6,2},{7,3},{8,12},{9,13},{10,... | collective-permute-start | bytes 884744 | tf_op jit(solution)/shard_map/ppermute | solution.py:58
  31.6 12.4 %collective-permute-start.9 = (bf16[144,1024]{1,0:T(8,128)(2,1)S(1)}, bf16[144,1024]{1,0:T(8,128)(2,1)S(1)}, u32[]{:S(2)}, u32[]{:S(2)}) collective-permute-start(bf16[144,1024]{1,0:T(8,128)(2,1)S(1)} %put_small.1.refs_0_.refs_11_.hidden_ref), channel_id=1, source_target_pairs={{0,6},{1,7},{2,4},{3,5},{4,2},{5,3},{6,0},{7,1},{8,14},{9,15},{10,... | collective-permute-start | bytes 884744 | tf_op jit(solution)/shard_map/ppermute | solution.py:58
  59.9 15.0 %collective-permute-start.19 = (bf16[192,1024]{1,0:T(8,128)(2,1)S(1)}, bf16[192,1024]{1,0:T(8,128)(2,1)S(1)}, u32[]{:S(2)}, u32[]{:S(2)}) collective-permute-start(bf16[192,1024]{1,0:T(8,128)(2,1)S(1)} %stack_halves.5.mine_ref), channel_id=1, source_target_pairs={{0,8},{8,0},{16,24},{24,16},{1,9},{9,1},{17,25},{25,17},{2,10},{10... | collective-permute-start | bytes 1179656 | tf_op jit(solution)/shard_map/ppermute | solution.py:64
  63.5 11.5 %collective-permute-start.18 = (bf16[512,256]{1,0:T(8,128)(2,1)S(1)}, bf16[512,256]{1,0:T(8,128)(2,1)S(1)}, u32[]{:S(2)}, u32[]{:S(2)}) collective-permute-start(bf16[512,256]{1,0:T(8,128)(2,1)S(1)} %get-tuple-element.457.refs_4_.refs_2_), channel_id=1, source_target_pairs={{0,6},{1,7},{2,4},{3,5},{4,2},{5,3},{6,0},{7,1},{8,14},{9,15},{10,... | collective-permute-start | bytes 786440 | tf_op jit(solution)/shard_map/ppermute | solution.py:58
  82.8 11.3 %collective-permute-start.23 = (bf16[64,1792]{1,0:T(8,128)(2,1)S(1)}, bf16[64,1792]{1,0:T(8,128)(2,1)S(1)}, u32[]{:S(2)}, u32[]{:S(2)}) collective-permute-start(bf16[64,1792]{1,0:T(8,128)(2,1)S(1)} %get-tuple-element.486), channel_id=1, source_target_pairs={{0,4},{1,5},{2,6},{3,7},{4,0},{5,1},{6,2},{7,3},{8,12},{9,13},{10,... | collective-permute-start | bytes 688136 | tf_op jit(solution)/shard_map/ppermute | solution.py:58
  95.9 16.7 %collective-permute-start.28 = (bf16[192,1792]{1,0:T(8,128)(2,1)S(1)}, bf16[192,1792]{1,0:T(8,128)(2,1)S(1)}, u32[]{:S(2)}, u32[]{:S(2)}) collective-permute-start(bf16[192,1792]{1,0:T(8,128)(2,1)S(1)} %stack_halves.6.mine_ref), channel_id=1, source_target_pairs={{0,8},{8,0},{16,24},{24,16},{1,9},{9,1},{17,25},{25,17},{2,10},{10... | collective-permute-start | bytes 2064392 | tf_op jit(solution)/shard_map/ppermute | solution.py:64
  98.3 12.4 %collective-permute-start.26 = (bf16[128,1024]{1,0:T(8,128)(2,1)S(1)}, bf16[128,1024]{1,0:T(8,128)(2,1)S(1)}, u32[]{:S(2)}, u32[]{:S(2)}) collective-permute-start(bf16[128,1024]{1,0:T(8,128)(2,1)S(1)} %get-tuple-element.490), channel_id=1, source_target_pairs={{0,4},{1,5},{2,6},{3,7},{4,0},{5,1},{6,2},{7,3},{8,12},{9,13},{10,... | collective-permute-start | bytes 786440 | tf_op jit(solution)/shard_map/ppermute | solution.py:58
  113.7 15.6 %collective-permute-start.33 = (bf16[512,1024]{1,0:T(8,128)(2,1)S(1)}, bf16[512,1024]{1,0:T(8,128)(2,1)S(1)}, u32[]{:S(2)}, u32[]{:S(2)}) collective-permute-start(bf16[512,1024]{1,0:T(8,128)(2,1)S(1)} %get-tuple-element.527.refs_8_.refs_4_), channel_id=1, source_target_pairs={{0,1},{1,0},{2,3},{3,2},{4,5},{5,4},{6,7},{7,6},{8,9},{9,8},{10,11... | collective-permute-start | bytes 3145736 | tf_op jit(solution)/shard_map/ppermute | solution.py:61
  113.8 15.6 %collective-permute-start.32 = (bf16[512,768]{1,0:T(8,128)(2,1)S(1)}, bf16[512,768]{1,0:T(8,128)(2,1)S(1)}, u32[]{:S(2)}, u32[]{:S(2)}) collective-permute-start(bf16[512,768]{1,0:T(8,128)(2,1)S(1)} %get-tuple-element.506.refs_5_.refs_9_), channel_id=1, source_target_pairs={{0,1},{1,0},{2,3},{3,2},{4,5},{5,4},{6,7},{7,6},{8,9},{9,8},{10,11... | collective-permute-start | bytes 2359304 | tf_op jit(solution)/shard_map/ppermute | solution.py:61
  115.7 13.6 %collective-permute-start.30 = (bf16[128,1024]{1,0:T(8,128)(2,1)S(1)}, bf16[128,1024]{1,0:T(8,128)(2,1)S(1)}, u32[]{:S(2)}, u32[]{:S(2)}) collective-permute-start(bf16[128,1024]{1,0:T(8,128)(2,1)S(1)} %get-tuple-element.502.refs_0_), channel_id=1, source_target_pairs={{0,4},{1,5},{2,6},{3,7},{4,0},{5,1},{6,2},{7,3},{8,12},{9,13},{10,... | collective-permute-start | bytes 786440 | tf_op jit(solution)/shard_map/ppermute | solution.py:58
  116.3 13.0 %collective-permute-start.31 = (bf16[128,1024]{1,0:T(8,128)(2,1)S(1)}, bf16[128,1024]{1,0:T(8,128)(2,1)S(1)}, u32[]{:S(2)}, u32[]{:S(2)}) collective-permute-start(bf16[128,1024]{1,0:T(8,128)(2,1)S(1)} %get-tuple-element.502.refs_0_), channel_id=1, source_target_pairs={{0,6},{1,7},{2,4},{3,5},{4,2},{5,3},{6,0},{7,1},{8,14},{9,15},{10,... | collective-permute-start | bytes 786440 | tf_op jit(solution)/shard_map/ppermute | solution.py:58
  129.4 15.0 %collective-permute-start.37 = (bf16[128,1024]{1,0:T(8,128)(2,1)S(1)}, bf16[128,1024]{1,0:T(8,128)(2,1)S(1)}, u32[]{:S(2)}, u32[]{:S(2)}) collective-permute-start(bf16[128,1024]{1,0:T(8,128)(2,1)S(1)} %bitcast.13), channel_id=1, source_target_pairs={{0,0},{1,1},{2,2},{3,3},{4,4},{5,5},{6,6},{7,7},{12,8},{13,9},{14,... | collective-permute-start | bytes 786440 | tf_op jit(solution)/shard_map/ppermute | solution.py:43
  144.4 14.5 %collective-permute-start.41 = (bf16[192,1024]{1,0:T(8,128)(2,1)S(1)}, bf16[192,1024]{1,0:T(8,128)(2,1)S(1)}, u32[]{:S(2)}, u32[]{:S(2)}) collective-permute-start(bf16[192,1024]{1,0:T(8,128)(2,1)S(1)} %stack_halves.7.mine_ref), channel_id=1, source_target_pairs={{0,8},{8,0},{16,24},{24,16},{1,9},{9,1},{17,25},{25,17},{2,10},{10... | collective-permute-start | bytes 1179656 | tf_op jit(solution)/shard_map/ppermute | solution.py:64
  145.4 11.9 %collective-permute-start.39 = (bf16[512,256]{1,0:T(8,128)(2,1)S(1)}, bf16[512,256]{1,0:T(8,128)(2,1)S(1)}, u32[]{:S(2)}, u32[]{:S(2)}) collective-permute-start(bf16[512,256]{1,0:T(8,128)(2,1)S(1)} %get-tuple-element.523.refs_4_.refs_2_), channel_id=1, source_target_pairs={{0,4},{1,5},{2,6},{3,7},{4,0},{5,1},{6,2},{7,3},{8,12},{9,13},{10,... | collective-permute-start | bytes 786440 | tf_op jit(solution)/shard_map/ppermute | solution.py:58
  161.6 15.8 %collective-permute-start.46 = (bf16[128,1024]{1,0:T(8,128)(2,1)S(1)}, bf16[128,1024]{1,0:T(8,128)(2,1)S(1)}, u32[]{:S(2)}, u32[]{:S(2)}) collective-permute-start(bf16[128,1024]{1,0:T(8,128)(2,1)S(1)} %collective-permute-done.42.refs_0_.grad_ref.ref), channel_id=1, source_target_pairs={{0,4},{1,5},{2,6},{3,7},{4,0},{5,1},{6,2},{7,3},{8,12},{9,13},{10,... | collective-permute-start | bytes 786440 | tf_op jit(solution)/shard_map/ppermute | solution.py:58
  165.6 11.9 %collective-permute-start.47 = (bf16[128,1024]{1,0:T(8,128)(2,1)S(1)}, bf16[128,1024]{1,0:T(8,128)(2,1)S(1)}, u32[]{:S(2)}, u32[]{:S(2)}) collective-permute-start(bf16[128,1024]{1,0:T(8,128)(2,1)S(1)} %collective-permute-done.42.refs_0_.grad_ref.ref), channel_id=1, source_target_pairs={{0,6},{1,7},{2,4},{3,5},{4,2},{5,3},{6,0},{7,1},{8,14},{9,15},{10,... | collective-permute-start | bytes 786440 | tf_op jit(solution)/shard_map/ppermute | solution.py:58
  185.8 17.0 %collective-permute-start.52 = (bf16[512,512]{1,0:T(8,128)(2,1)S(1)}, bf16[512,512]{1,0:T(8,128)(2,1)S(1)}, u32[]{:S(2)}, u32[]{:S(2)}) collective-permute-start(bf16[512,512]{1,0:T(8,128)(2,1)S(1)} %get-tuple-element.570.refs_0_), channel_id=1, source_target_pairs={{0,8},{24,16},{1,9},{25,17},{2,10},{26,18},{3,11},{27,19},{4,12},{... | collective-permute-start | bytes 1572872 | tf_op jit(solution)/shard_map/ppermute | solution.py:909
  188.8 12.2 %collective-permute-start.50 = (bf16[128,1024]{1,0:T(8,128)(2,1)S(1)}, bf16[128,1024]{1,0:T(8,128)(2,1)S(1)}, u32[]{:S(2)}, u32[]{:S(2)}) collective-permute-start(bf16[128,1024]{1,0:T(8,128)(2,1)S(1)} %get-tuple-element.566), channel_id=1, source_target_pairs={{0,4},{1,5},{2,6},{3,7},{4,0},{5,1},{6,2},{7,3},{8,12},{9,13},{10,... | collective-permute-start | bytes 786440 | tf_op jit(solution)/shard_map/ppermute | solution.py:58
  189.3 13.5 %collective-permute-start.51 = (bf16[128,1024]{1,0:T(8,128)(2,1)S(1)}, bf16[128,1024]{1,0:T(8,128)(2,1)S(1)}, u32[]{:S(2)}, u32[]{:S(2)}) collective-permute-start(bf16[128,1024]{1,0:T(8,128)(2,1)S(1)} %get-tuple-element.567), channel_id=1, source_target_pairs={{0,6},{1,7},{2,4},{3,5},{4,2},{5,3},{6,0},{7,1},{8,14},{9,15},{10,... | collective-permute-start | bytes 786440 | tf_op jit(solution)/shard_map/ppermute | solution.py:58
  202.8 22.1 %collective-permute-start.56 = (bf16[512,512]{1,0:T(8,128)(2,1)}, bf16[512,512]{1,0:T(8,128)(2,1)}, u32[]{:S(2)}, u32[]{:S(2)}) collective-permute-start(bf16[512,512]{1,0:T(8,128)(2,1)} %get-tuple-element.579.refs_3_), channel_id=1, source_target_pairs={{0,8},{24,16},{1,9},{25,17},{2,10},{26,18},{3,11},{27,19},{4,12},{... | collective-permute-start | bytes 1572872 | tf_op jit(solution)/shard_map/ppermute | solution.py:909
  205.0 19.9 %collective-permute-start.57 = (bf16[512,512]{1,0:T(8,128)(2,1)}, bf16[512,512]{1,0:T(8,128)(2,1)}, u32[]{:S(2)}, u32[]{:S(2)}) collective-permute-start(bf16[512,512]{1,0:T(8,128)(2,1)} %turn.13.refs_1_), channel_id=1, source_target_pairs={{8,16},{16,8},{9,17},{17,9},{10,18},{18,10},{11,19},{19,11},{12,20... | collective-permute-start | bytes 1572872 | tf_op jit(solution)/shard_map/ppermute | solution.py:909
  211.6 13.3 %collective-permute-start.54 = (bf16[128,1024]{1,0:T(8,128)(2,1)}, bf16[128,1024]{1,0:T(8,128)(2,1)}, u32[]{:S(2)}, u32[]{:S(2)}) collective-permute-start(bf16[128,1024]{1,0:T(8,128)(2,1)} %get-tuple-element.581.refs_0_.refs_3_), channel_id=1, source_target_pairs={{0,4},{1,5},{2,6},{3,7},{4,0},{5,1},{6,2},{7,3},{8,12},{9,13},{10,... | collective-permute-start | bytes 786440 | tf_op jit(solution)/shard_map/ppermute | solution.py:58
  212.5 12.4 %collective-permute-start.55 = (bf16[128,1024]{1,0:T(8,128)(2,1)}, bf16[128,1024]{1,0:T(8,128)(2,1)}, u32[]{:S(2)}, u32[]{:S(2)}) collective-permute-start(bf16[128,1024]{1,0:T(8,128)(2,1)} %get-tuple-element.581.refs_0_.refs_3_), channel_id=1, source_target_pairs={{0,6},{1,7},{2,4},{3,5},{4,2},{5,3},{6,0},{7,1},{8,14},{9,15},{10,... | collective-permute-start | bytes 786440 | tf_op jit(solution)/shard_map/ppermute | solution.py:58
  226.7 14.6 %collective-permute-start.58 = (bf16[512,512]{1,0:T(8,128)(2,1)S(1)}, bf16[512,512]{1,0:T(8,128)(2,1)S(1)}, u32[]{:S(2)}, u32[]{:S(2)}) collective-permute-start(bf16[512,512]{1,0:T(8,128)(2,1)S(1)} %get-tuple-element.800.b_ref), channel_id=1, source_target_pairs={{0,8},{24,16},{8,0},{16,24},{1,9},{25,17},{9,1},{17,25},{2,10},{26... | collective-permute-start | bytes 1572872 | tf_op jit(solution)/shard_map/ppermute | solution.py:909
  228.3 13.9 %collective-permute-start.59 = (bf16[512,512]{1,0:T(8,128)(2,1)S(1)}, bf16[512,512]{1,0:T(8,128)(2,1)S(1)}, u32[]{:S(2)}, u32[]{:S(2)}) collective-permute-start(bf16[512,512]{1,0:T(8,128)(2,1)S(1)} %get-tuple-element.612.refs_1_), channel_id=1, source_target_pairs={{8,16},{16,8},{9,17},{17,9},{10,18},{18,10},{11,19},{19,11},{12,20... | collective-permute-start | bytes 1572872 | tf_op jit(solution)/shard_map/ppermute | solution.py:909
  243.0 16.1 %collective-permute-start.63 = (bf16[512,512]{1,0:T(8,128)(2,1)S(1)}, bf16[512,512]{1,0:T(8,128)(2,1)S(1)}, u32[]{:S(2)}, u32[]{:S(2)}) collective-permute-start(bf16[512,512]{1,0:T(8,128)(2,1)S(1)} %get-tuple-element.801.b_ref), channel_id=1, source_target_pairs={{0,8},{24,16},{8,0},{16,24},{1,9},{25,17},{9,1},{17,25},{2,10},{26... | collective-permute-start | bytes 1572872 | tf_op jit(solution)/shard_map/ppermute | solution.py:909
  243.1 16.1 %collective-permute-start.64 = (bf16[512,512]{1,0:T(8,128)(2,1)S(1)}, bf16[512,512]{1,0:T(8,128)(2,1)S(1)}, u32[]{:S(2)}, u32[]{:S(2)}) collective-permute-start(bf16[512,512]{1,0:T(8,128)(2,1)S(1)} %get-tuple-element.621.refs_1_), channel_id=1, source_target_pairs={{8,16},{16,8},{9,17},{17,9},{10,18},{18,10},{11,19},{19,11},{12,20... | collective-permute-start | bytes 1572872 | tf_op jit(solution)/shard_map/ppermute | solution.py:909
  245.4 11.5 %collective-permute-start.60 = (bf16[128,1024]{1,0:T(8,128)(2,1)S(1)}, bf16[128,1024]{1,0:T(8,128)(2,1)S(1)}, u32[]{:S(2)}, u32[]{:S(2)}) collective-permute-start(bf16[128,1024]{1,0:T(8,128)(2,1)S(1)} %get-tuple-element.599), channel_id=1, source_target_pairs={{0,2},{1,3},{2,0},{3,1},{4,6},{5,7},{6,4},{7,5},{8,10},{9,11},{10,... | collective-permute-start | bytes 786440 | tf_op jit(solution)/shard_map/ppermute | solution.py:58
  260.0 18.2 %collective-permute-start.68 = (bf16[512,512]{1,0:T(8,128)(2,1)S(1)}, bf16[512,512]{1,0:T(8,128)(2,1)S(1)}, u32[]{:S(2)}, u32[]{:S(2)}) collective-permute-start(bf16[512,512]{1,0:T(8,128)(2,1)S(1)} %get-tuple-element.736.b_ref), channel_id=1, source_target_pairs={{0,8},{24,16},{8,0},{16,24},{1,9},{25,17},{9,1},{17,25},{2,10},{26... | collective-permute-start | bytes 1572872 | tf_op jit(solution)/shard_map/ppermute | solution.py:909
  260.4 17.8 %collective-permute-start.69 = (bf16[512,512]{1,0:T(8,128)(2,1)S(1)}, bf16[512,512]{1,0:T(8,128)(2,1)S(1)}, u32[]{:S(2)}, u32[]{:S(2)}) collective-permute-start(bf16[512,512]{1,0:T(8,128)(2,1)S(1)} %get-tuple-element.648.refs_1_), channel_id=1, source_target_pairs={{8,16},{16,8},{9,17},{17,9},{10,18},{18,10},{11,19},{19,11},{12,20... | collective-permute-start | bytes 1572872 | tf_op jit(solution)/shard_map/ppermute | solution.py:909
  265.7 12.4 %collective-permute-start.67 = (bf16[128,1024]{1,0:T(8,128)(2,1)S(1)}, bf16[128,1024]{1,0:T(8,128)(2,1)S(1)}, u32[]{:S(2)}, u32[]{:S(2)}) collective-permute-start(bf16[128,1024]{1,0:T(8,128)(2,1)S(1)} %get-tuple-element.627.refs_0_), channel_id=1, source_target_pairs={{0,6},{1,7},{2,4},{3,5},{4,2},{5,3},{6,0},{7,1},{8,14},{9,15},{10,... | collective-permute-start | bytes 786440 | tf_op jit(solution)/shard_map/ppermute | solution.py:58
  281.0 14.4 %collective-permute-start.71 = (bf16[512,512]{1,0:T(8,128)(2,1)S(1)}, bf16[512,512]{1,0:T(8,128)(2,1)S(1)}, u32[]{:S(2)}, u32[]{:S(2)}) collective-permute-start(bf16[512,512]{1,0:T(8,128)(2,1)S(1)} %get-tuple-element.737.b_ref), channel_id=1, source_target_pairs={{0,8},{24,16},{8,0},{16,24},{1,9},{25,17},{9,1},{17,25},{2,10},{26... | collective-permute-start | bytes 1572872 | tf_op jit(solution)/shard_map/ppermute | solution.py:909
  281.1 16.2 %collective-permute-start.72 = (bf16[512,512]{1,0:T(8,128)(2,1)S(1)}, bf16[512,512]{1,0:T(8,128)(2,1)S(1)}, u32[]{:S(2)}, u32[]{:S(2)}) collective-permute-start(bf16[512,512]{1,0:T(8,128)(2,1)S(1)} %get-tuple-element.660.refs_1_), channel_id=1, source_target_pairs={{8,16},{16,8},{9,17},{17,9},{10,18},{18,10},{11,19},{19,11},{12,20... | collective-permute-start | bytes 1572872 | tf_op jit(solution)/shard_map/ppermute | solution.py:909
  298.1 17.1 %collective-permute-start.76 = (bf16[512,512]{1,0:T(8,128)(2,1)S(1)}, bf16[512,512]{1,0:T(8,128)(2,1)S(1)}, u32[]{:S(2)}, u32[]{:S(2)}) collective-permute-start(bf16[512,512]{1,0:T(8,128)(2,1)S(1)} %get-tuple-element.754.b_ref), channel_id=1, source_target_pairs={{0,8},{24,16},{8,0},{16,24},{1,9},{25,17},{9,1},{17,25},{2,10},{26... | collective-permute-start | bytes 1572872 | tf_op jit(solution)/shard_map/ppermute | solution.py:909
  298.1 17.0 %collective-permute-start.77 = (bf16[512,512]{1,0:T(8,128)(2,1)S(1)}, bf16[512,512]{1,0:T(8,128)(2,1)S(1)}, u32[]{:S(2)}, u32[]{:S(2)}) collective-permute-start(bf16[512,512]{1,0:T(8,128)(2,1)S(1)} %get-tuple-element.674.refs_1_), channel_id=1, source_target_pairs={{8,16},{16,8},{9,17},{17,9},{10,18},{18,10},{11,19},{19,11},{12,20... | collective-permute-start | bytes 1572872 | tf_op jit(solution)/shard_map/ppermute | solution.py:909
  303.1 12.0 %collective-permute-start.75 = (bf16[128,1024]{1,0:T(8,128)(2,1)S(1)}, bf16[128,1024]{1,0:T(8,128)(2,1)S(1)}, u32[]{:S(2)}, u32[]{:S(2)}) collective-permute-start(bf16[128,1024]{1,0:T(8,128)(2,1)S(1)} %get-tuple-element.656), channel_id=1, source_target_pairs={{0,6},{1,7},{2,4},{3,5},{4,2},{5,3},{6,0},{7,1},{8,14},{9,15},{10,... | collective-permute-start | bytes 786440 | tf_op jit(solution)/shard_map/ppermute | solution.py:58
  316.0 17.2 %collective-permute-start.81 = (bf16[512,512]{1,0:T(8,128)(2,1)S(1)}, bf16[512,512]{1,0:T(8,128)(2,1)S(1)}, u32[]{:S(2)}, u32[]{:S(2)}) collective-permute-start(bf16[512,512]{1,0:T(8,128)(2,1)S(1)} %get-tuple-element.755.b_ref), channel_id=1, source_target_pairs={{0,8},{24,16},{8,0},{16,24},{1,9},{25,17},{9,1},{17,25},{2,10},{26... | collective-permute-start | bytes 1572872 | tf_op jit(solution)/shard_map/ppermute | solution.py:909
  316.0 17.1 %collective-permute-start.82 = (bf16[512,512]{1,0:T(8,128)(2,1)S(1)}, bf16[512,512]{1,0:T(8,128)(2,1)S(1)}, u32[]{:S(2)}, u32[]{:S(2)}) collective-permute-start(bf16[512,512]{1,0:T(8,128)(2,1)S(1)} %get-tuple-element.691.refs_1_), channel_id=1, source_target_pairs={{8,16},{16,8},{9,17},{17,9},{10,18},{18,10},{11,19},{19,11},{12,20... | collective-permute-start | bytes 1572872 | tf_op jit(solution)/shard_map/ppermute | solution.py:909
  321.3 11.8 %collective-permute-start.79 = (bf16[128,1024]{1,0:T(8,128)(2,1)S(1)}, bf16[128,1024]{1,0:T(8,128)(2,1)S(1)}, u32[]{:S(2)}, u32[]{:S(2)}) collective-permute-start(bf16[128,1024]{1,0:T(8,128)(2,1)S(1)} %get-tuple-element.679.refs_0_.refs_3_), channel_id=1, source_target_pairs={{0,4},{1,5},{2,6},{3,7},{4,0},{5,1},{6,2},{7,3},{8,12},{9,13},{10,... | collective-permute-start | bytes 786440 | tf_op jit(solution)/shard_map/ppermute | solution.py:58
  333.9 12.6 %collective-permute-start.83 = (bf16[512,512]{1,0:T(8,128)(2,1)S(1)}, bf16[512,512]{1,0:T(8,128)(2,1)S(1)}, u32[]{:S(2)}, u32[]{:S(2)}) collective-permute-start(bf16[512,512]{1,0:T(8,128)(2,1)S(1)} %get-tuple-element.814.b_ref), channel_id=1, source_target_pairs={{0,8},{24,16},{8,0},{16,24},{1,9},{25,17},{9,1},{17,25},{2,10},{26... | collective-permute-start | bytes 1572872 | tf_op jit(solution)/shard_map/ppermute | solution.py:909
  334.0 12.5 %collective-permute-start.84 = (bf16[512,512]{1,0:T(8,128)(2,1)S(1)}, bf16[512,512]{1,0:T(8,128)(2,1)S(1)}, u32[]{:S(2)}, u32[]{:S(2)}) collective-permute-start(bf16[512,512]{1,0:T(8,128)(2,1)S(1)} %get-tuple-element.718.refs_1_), channel_id=1, source_target_pairs={{8,16},{16,8},{9,17},{17,9},{10,18},{18,10},{11,19},{19,11},{12,20... | collective-permute-start | bytes 1572872 | tf_op jit(solution)/shard_map/ppermute | solution.py:909
  347.4 16.3 %collective-permute-start.88 = (bf16[512,512]{1,0:T(8,128)(2,1)S(1)}, bf16[512,512]{1,0:T(8,128)(2,1)S(1)}, u32[]{:S(2)}, u32[]{:S(2)}) collective-permute-start(bf16[512,512]{1,0:T(8,128)(2,1)S(1)} %get-tuple-element.815.b_ref), channel_id=1, source_target_pairs={{0,8},{24,16},{8,0},{16,24},{1,9},{25,17},{9,1},{17,25},{2,10},{26... | collective-permute-start | bytes 1572872 | tf_op jit(solution)/shard_map/ppermute | solution.py:909
  347.5 16.2 %collective-permute-start.89 = (bf16[512,512]{1,0:T(8,128)(2,1)S(1)}, bf16[512,512]{1,0:T(8,128)(2,1)S(1)}, u32[]{:S(2)}, u32[]{:S(2)}) collective-permute-start(bf16[512,512]{1,0:T(8,128)(2,1)S(1)} %get-tuple-element.730.refs_1_), channel_id=1, source_target_pairs={{8,16},{16,8},{9,17},{17,9},{10,18},{18,10},{11,19},{19,11},{12,20... | collective-permute-start | bytes 1572872 | tf_op jit(solution)/shard_map/ppermute | solution.py:909
  364.5 17.5 %collective-permute-start.93 = (bf16[528,512]{1,0:T(8,128)(2,1)S(1)}, bf16[528,512]{1,0:T(8,128)(2,1)S(1)}, u32[]{:S(2)}, u32[]{:S(2)}) collective-permute-start(bf16[528,512]{1,0:T(8,128)(2,1)S(1)} %get-tuple-element.770.b_ref), channel_id=1, source_target_pairs={{0,8},{24,16},{8,0},{16,24},{1,9},{25,17},{9,1},{17,25},{2,10},{26... | collective-permute-start | bytes 1622024 | tf_op jit(solution)/shard_map/ppermute | solution.py:909
  364.6 17.4 %collective-permute-start.94 = (bf16[512,512]{1,0:T(8,128)(2,1)S(1)}, bf16[512,512]{1,0:T(8,128)(2,1)S(1)}, u32[]{:S(2)}, u32[]{:S(2)}) collective-permute-start(bf16[512,512]{1,0:T(8,128)(2,1)S(1)} %get-tuple-element.743.refs_1_), channel_id=1, source_target_pairs={{8,16},{16,8},{9,17},{17,9},{10,18},{18,10},{11,19},{19,11},{12,20... | collective-permute-start | bytes 1572872 | tf_op jit(solution)/shard_map/ppermute | solution.py:909
  368.6 13.4 %collective-permute-start.91 = (bf16[128,1024]{1,0:T(8,128)(2,1)S(1)}, bf16[128,1024]{1,0:T(8,128)(2,1)S(1)}, u32[]{:S(2)}, u32[]{:S(2)}) collective-permute-start(bf16[128,1024]{1,0:T(8,128)(2,1)S(1)} %copy-done.57), channel_id=1, source_target_pairs={{0,4},{1,5},{2,6},{3,7},{4,0},{5,1},{6,2},{7,3},{8,12},{9,13},{10,... | collective-permute-start | bytes 786440 | tf_op jit(solution)/shard_map/ppermute | solution.py:58
  369.8 12.2 %collective-permute-start.92 = (bf16[128,1024]{1,0:T(8,128)(2,1)S(1)}, bf16[128,1024]{1,0:T(8,128)(2,1)S(1)}, u32[]{:S(2)}, u32[]{:S(2)}) collective-permute-start(bf16[128,1024]{1,0:T(8,128)(2,1)S(1)} %copy-done.55), channel_id=1, source_target_pairs={{0,6},{1,7},{2,4},{3,5},{4,2},{5,3},{6,0},{7,1},{8,14},{9,15},{10,... | collective-permute-start | bytes 786440 | tf_op jit(solution)/shard_map/ppermute | solution.py:58
  382.9 17.0 %collective-permute-start.98 = (bf16[528,512]{1,0:T(8,128)(2,1)S(1)}, bf16[528,512]{1,0:T(8,128)(2,1)S(1)}, u32[]{:S(2)}, u32[]{:S(2)}) collective-permute-start(bf16[528,512]{1,0:T(8,128)(2,1)S(1)} %get-tuple-element.771.b_ref), channel_id=1, source_target_pairs={{0,8},{24,16},{8,0},{16,24},{1,9},{25,17},{9,1},{17,25},{2,10},{26... | collective-permute-start | bytes 1622024 | tf_op jit(solution)/shard_map/ppermute | solution.py:909
  382.9 16.9 %collective-permute-start.99 = (bf16[528,512]{1,0:T(8,128)(2,1)S(1)}, bf16[528,512]{1,0:T(8,128)(2,1)S(1)}, u32[]{:S(2)}, u32[]{:S(2)}) collective-permute-start(bf16[528,512]{1,0:T(8,128)(2,1)S(1)} %get-tuple-element.761.refs_0_), channel_id=1, source_target_pairs={{8,16},{16,8},{9,17},{17,9},{10,18},{18,10},{11,19},{19,11},{12,20... | collective-permute-start | bytes 1622024 | tf_op jit(solution)/shard_map/ppermute | solution.py:909
  387.7 12.1 %collective-permute-start.96 = (bf16[128,1024]{1,0:T(8,128)(2,1)S(1)}, bf16[128,1024]{1,0:T(8,128)(2,1)S(1)}, u32[]{:S(2)}, u32[]{:S(2)}) collective-permute-start(bf16[128,1024]{1,0:T(8,128)(2,1)S(1)} %get-tuple-element.740), channel_id=1, source_target_pairs={{0,4},{1,5},{2,6},{3,7},{4,0},{5,1},{6,2},{7,3},{8,12},{9,13},{10,... | collective-permute-start | bytes 786440 | tf_op jit(solution)/shard_map/ppermute | solution.py:58
  400.6 14.4 %collective-permute-start.103 = (bf16[528,512]{1,0:T(8,128)(2,1)S(1)}, bf16[528,512]{1,0:T(8,128)(2,1)S(1)}, u32[]{:S(2)}, u32[]{:S(2)}) collective-permute-start(bf16[528,512]{1,0:T(8,128)(2,1)S(1)} %get-tuple-element.767.b_ref), channel_id=1, source_target_pairs={{8,0},{16,24},{9,1},{17,25},{10,2},{18,26},{11,3},{19,27},{12,4},{... | collective-permute-start | bytes 1622024 | tf_op jit(solution)/shard_map/ppermute | solution.py:909
  402.4 12.8 %collective-permute-start.104 = (bf16[528,512]{1,0:T(8,128)(2,1)S(1)}, bf16[528,512]{1,0:T(8,128)(2,1)S(1)}, u32[]{:S(2)}, u32[]{:S(2)}) collective-permute-start(bf16[528,512]{1,0:T(8,128)(2,1)S(1)} %get-tuple-element.776.refs_0_), channel_id=1, source_target_pairs={{8,16},{16,8},{9,17},{17,9},{10,18},{18,10},{11,19},{19,11},{12,20... | collective-permute-start | bytes 1622024 | tf_op jit(solution)/shard_map/ppermute | solution.py:909
  415.3 13.7 %collective-permute-start.108 = (bf16[528,512]{1,0:T(8,128)(2,1)S(1)}, bf16[528,512]{1,0:T(8,128)(2,1)S(1)}, u32[]{:S(2)}, u32[]{:S(2)}) collective-permute-start(bf16[528,512]{1,0:T(8,128)(2,1)S(1)} %turn.25.b_ref), channel_id=1, source_target_pairs={{8,0},{16,24},{9,1},{17,25},{10,2},{18,26},{11,3},{19,27},{12,4},{... | collective-permute-start | bytes 1622024 | tf_op jit(solution)/shard_map/ppermute | solution.py:909
  429.7 21.6 %collective-permute-start.109 = (bf16[176,768]{1,0:T(8,128)(2,1)S(1)}, bf16[176,768]{1,0:T(8,128)(2,1)S(1)}, u32[]{:S(2)}, u32[]{:S(2)}) collective-permute-start(bf16[176,768]{1,0:T(8,128)(2,1)S(1)} %get-tuple-element.781), channel_id=1, source_target_pairs={{0,2},{1,3},{2,0},{3,1},{4,6},{5,7},{6,4},{7,5},{8,10},{9,11},{10,... | collective-permute-start | bytes 811016 | tf_op jit(solution)/shard_map/ppermute | solution.py:58
  431.5 19.8 %collective-permute-start.110 = (bf16[176,768]{1,0:T(8,128)(2,1)S(1)}, bf16[176,768]{1,0:T(8,128)(2,1)S(1)}, u32[]{:S(2)}, u32[]{:S(2)}) collective-permute-start(bf16[176,768]{1,0:T(8,128)(2,1)S(1)} %get-tuple-element.782), channel_id=1, source_target_pairs={{0,4},{1,5},{2,6},{3,7},{4,0},{5,1},{6,2},{7,3},{8,12},{9,13},{10,... | collective-permute-start | bytes 811016 | tf_op jit(solution)/shard_map/ppermute | solution.py:58
  431.9 19.3 %collective-permute-start.111 = (bf16[176,768]{1,0:T(8,128)(2,1)S(1)}, bf16[176,768]{1,0:T(8,128)(2,1)S(1)}, u32[]{:S(2)}, u32[]{:S(2)}) collective-permute-start(bf16[176,768]{1,0:T(8,128)(2,1)S(1)} %get-tuple-element.783), channel_id=1, source_target_pairs={{0,6},{1,7},{2,4},{3,5},{4,2},{5,3},{6,0},{7,1},{8,14},{9,15},{10,... | collective-permute-start | bytes 811016 | tf_op jit(solution)/shard_map/ppermute | solution.py:58
  433.2 15.2 %collective-permute-start.112 = (bf16[128,1024]{1,0:T(8,128)(2,1)S(1)}, bf16[128,1024]{1,0:T(8,128)(2,1)S(1)}, u32[]{:S(2)}, u32[]{:S(2)}) collective-permute-start(bf16[128,1024]{1,0:T(8,128)(2,1)S(1)} %get-tuple-element.784), channel_id=1, source_target_pairs={{0,0},{1,1},{10,2},{11,3},{20,4},{21,5},{30,6},{31,7},{16,12},{17,... | collective-permute-start | bytes 786440 | tf_op jit(solution)/shard_map/ppermute | solution.py:43
  435.1 16.1 %collective-permute-start.113 = (bf16[128,1024]{1,0:T(8,128)(2,1)S(1)}, bf16[128,1024]{1,0:T(8,128)(2,1)S(1)}, u32[]{:S(2)}, u32[]{:S(2)}) collective-permute-start(bf16[128,1024]{1,0:T(8,128)(2,1)S(1)} %get-tuple-element.785), channel_id=1, source_target_pairs={{0,0},{1,1},{10,2},{11,3},{20,4},{21,5},{30,6},{31,7},{16,12},{17,... | collective-permute-start | bytes 786440 | tf_op jit(solution)/shard_map/ppermute | solution.py:43
  (131 other events, 1801.3 us)

commit v9 on v8

--- a/solution.py
+++ b/solution.py
@@ -781,30 +781,44 @@
     return run("cut_rows", body, outs, [first, second], net.place)
 
 
-def sum_small(net, layers, pieces, sizes, rows, more):
+def sum_small(net, layers, pieces, sizes, rows):
     width = pieces[0].shape[1]
-    count = len(pieces)
     starts = [sum(sizes[:i]) for i in range(len(sizes))]
+    lines = 2 * layers * net.n_p
+    block = (lines, rows // lines) if rows % lines == 0 and lines % 16 == 0 else (pieces[0].shape[0], 0)
+    first = 0 if block[1] else rows
 
     def body(place, *refs):
-        lines = slice(rows, rows + 2 * layers * net.n_p)
-        every = refs[0][lines, :].astype(F32)
-        for ref in refs[1:count]:
-            every = every + ref[lines, :].astype(F32)
+        here = slice(first, first + lines)
+        every = refs[0][here, :].astype(F32)
+        for ref in refs[1 : len(pieces)]:
+            every = every + ref[here, :].astype(F32)
         total = jnp.zeros((2 * layers, width), F32)
         for i in range(net.n_p):
             total = jnp.where(place[0] == i, every[i * 2 * layers : (i + 1) * 2 * layers], total)
-        outs = refs[count + len(more) :]
-        for out, at, size in zip(outs, starts, sizes):
+        for out, at, size in zip(refs[len(pieces) :], starts, sizes):
             half = at // width
             for layer in range(layers):
                 row = 2 * layer + half
                 out[layer : layer + 1, :] = total[row : row + 1, at - half * width : at - half * width + size]
-        for ref, out in zip(refs[count : count + len(more)], outs[len(sizes) :]):
+
+    return pl.pallas_call(
+        body,
+        grid=(1,),
+        out_shape=[jax.ShapeDtypeStruct((layers, size), F32) for size in sizes],
+        in_specs=[IN_SMEM] + [pl.BlockSpec((block[0], width), lambda i: (block[1], 0))] * len(pieces),
+        out_specs=[pl.BlockSpec((layers, size), lambda i: (0, 0)) for size in sizes],
+        compiler_params=pltpu.CompilerParams(vmem_limit_bytes=16 << 20),
+        name="sum_small",
+    )(net.place, *pieces)
+
+
+def widen(net, values):
+    def body(place, *refs):
+        for ref, out in zip(refs, refs[len(values) :]):
             out[...] = ref[...].astype(F32)
 
-    outs = [((layers, size), F32) for size in sizes] + [(v.shape, F32) for v in more]
-    return run("sum_small", body, outs, [*pieces, *more], net.place)
+    return run("widen", body, [(v.shape, F32) for v in values], values, net.place)
 
 
 def take_if(here, a, b, rows):
@@ -1156,7 +1170,8 @@
     downs = [[c.value for c in sums[layer][0]] for layer in range(layers)]
     out = write_layer(net, 1, layers, None, (proj_g, qkv_pieces), (up_pieces, downs[1]))
     out = write_layer(net, 0, layers, out, None, (up_last, downs[0]))
-    *small_out, input_grad, sent_out = sum_small(net, layers, pieces, sizes, D // net.n_f, [dm, sent_out])
+    input_grad, sent_out = widen(net, [dm, sent_out])
+    small_out = sum_small(net, layers, pieces, sizes, D // net.n_f)
     out = write_layer(net, 0, layers, out, (proj_last, pieces), None)
     return (
         sent_out[None],

time: 465 us -> 466 us (level)
  no operation moved by 1% of the time
where the time goes in v9:
time: 466 us; the launch traced here: 457 us
  waiting for transfers between devices  160 us (34%)
  starting transfers between devices  153 us (33%)
  Pallas kernels  113 us (24%)
  blocking collectives  21.7 us (5%)
  local copies, waits for them, and re-layouts  5.99 us (1%)
    ppermute x66, waiting for transfers between devices, chip(): return lax.ppermute(v, 'fsdp', xor_pairs(self.n_f, 2 * j))  136 us
    pallas_call x73, Pallas kernels, run(): pl.pallas_call(body, out_shape=[jax.ShapeDtypeStruct(shape, dtype) for sh...  103 us
    ppermute x66, starting transfers between devices, chip(): return lax.ppermute(v, 'fsdp', xor_pairs(self.n_f, 2 * j))  79.8 us
    ppermute x26, starting transfers between devices, start(): lax.ppermute(v, 'seq', m[3])  44.2 us
    ppermute x7, starting transfers between devices, send(): return lax.ppermute(v, ('seq', 'fsdp'), pairs)  21.9 us
    all_to_all x4, blocking collectives, swap_cores(): return lax.all_to_all(both, 'fsdp', 0, 0, axis_index_groups=pair_groups)  21.7 us
  transfers between devices with their start and end apart: 114, of which 48 were waited for; matrix products, arithmetic and copies ran while one was open for 0% of the time, Pallas kernels for 19%

profile of v9, /device:TPU:10, one launch (start us, length us, event | category | flops | bytes accessed | tf_op | source)
XLA Modules:
  0.0 456.8 jit_solution(15471760846752295160)
XLA Ops:
  1.8 3.4 collective-permute-start
  11.7 3.6 collective-permute-start.4
  15.3 3.4 collective-permute-start.1
  21.0 3.9 collective-permute-done.4.refs_1_
  33.0 5.4 %collective-permute-done.7.refs_1_.refs_12_ = bf16[144,1024]{1,0:T(8,128)(2,1)S(1)} collective-permute-done((bf16[144,1024]{1,0:T(8,128)(2,1)S(1)}, bf16[144,1024]{1,0:T(8,128)(2,1)S(1)}, u32[]{:S(2)}, u32[]{:S(2)}) %collective-permute-start.7) | collective-permute-done | bytes 294944 | tf_op jit(solution)/shard_map/ppermute | solution.py:58
  38.4 4.3 collective-permute-done.8.refs_2_.refs_13_
  45.7 3.3 collective-permute-done.11.refs_6_.refs_10_
  53.8 5.3 %attend.2 = (s32[1,512]{1,0:T(1,128)S(1)}, s32[512,1]{1,0:T(8,128)S(1)}, bf16[512,1024]{1,0:T(8,128)(2,1)S(1)}, bf16[512,768]{1,0:T(8,128)(2,1)S(1)}, bf16[512,256]{1,0:T(8,128)(2,1)S(1)}) custom-call(s32[3]{0:T(128)S(1)} %pad_add_fusion.2.place, bf16[144,1024]{1,0:T(8,128)(2,1)S(1)} %put_small.1.refs_0_.refs_11_.hidden_ref, ...), custom_call_target="tpu_custom_call" | custom-call | flops 805306368 | bytes 2785292 | tf_op jit(solution)/shard_map/attend/pallas_call | solution.py:93
  64.4 5.8 %collective-permute-done.16.refs_5_ = bf16[512,256]{1,0:T(8,128)(2,1)S(1)} collective-permute-done((bf16[512,256]{1,0:T(8,128)(2,1)S(1)}, bf16[512,256]{1,0:T(8,128)(2,1)S(1)}, u32[]{:S(2)}, u32[]{:S(2)}) %collective-permute-start.16) | collective-permute-done | bytes 262176 | tf_op jit(solution)/shard_map/ppermute | solution.py:58
  70.2 3.5 collective-permute-done.17.refs_6_
  77.4 2.7 close_attention.2
  85.4 4.1 feed_forward.2
  90.9 3.2 collective-permute-done.23.refs_1_
  101.2 5.8 %collective-permute-done.25.refs_1_ = bf16[128,1024]{1,0:T(8,128)(2,1)S(1)} collective-permute-done((bf16[128,1024]{1,0:T(8,128)(2,1)S(1)}, bf16[128,1024]{1,0:T(8,128)(2,1)S(1)}, u32[]{:S(2)}, u32[]{:S(2)}) %collective-permute-start.25) | collective-permute-done | bytes 262176 | tf_op jit(solution)/shard_map/ppermute | solution.py:58
  106.9 3.7 collective-permute-done.26.refs_2_
  118.0 5.7 %collective-permute-done.29.refs_1_ = bf16[128,1024]{1,0:T(8,128)(2,1)S(1)} collective-permute-done((bf16[128,1024]{1,0:T(8,128)(2,1)S(1)}, bf16[128,1024]{1,0:T(8,128)(2,1)S(1)}, u32[]{:S(2)}, u32[]{:S(2)}) %collective-permute-start.29) | collective-permute-done | bytes 262176 | tf_op jit(solution)/shard_map/ppermute | solution.py:58
  123.7 5.6 %collective-permute-done.30.refs_2_ = bf16[128,1024]{1,0:T(8,128)(2,1)S(1)} collective-permute-done((bf16[128,1024]{1,0:T(8,128)(2,1)S(1)}, bf16[128,1024]{1,0:T(8,128)(2,1)S(1)}, u32[]{:S(2)}, u32[]{:S(2)}) %collective-permute-start.30) | collective-permute-done | bytes 262176 | tf_op jit(solution)/shard_map/ppermute | solution.py:58
  129.4 3.0 collective-permute-start.37
  136.6 5.3 %attend.3 = (bf16[512,1024]{1,0:T(8,128)(2,1)S(1)}, bf16[512,768]{1,0:T(8,128)(2,1)S(1)}, bf16[512,256]{1,0:T(8,128)(2,1)S(1)}) custom-call(s32[3]{0:T(128)S(1)} %pad_add_fusion.2.place, bf16[128,1024]{1,0:T(8,128)(2,1)S(1)} %get-tuple-element.502.refs_0_, bf16[128,1024]{1,0:T(8,128)(2,1)S(1)} %collective-permute-done.29.refs_1_, ...), custom_call_target="tpu_custom_call" | custom-call | flops 805306368 | bytes 2658316 | tf_op jit(solution)/shard_map/attend/pallas_call | solution.py:93
  148.0 5.9 %collective-permute-start.42 = (bf16[128,1024]{1,0:T(8,128)(2,1)S(1)}, bf16[128,1024]{1,0:T(8,128)(2,1)S(1)}, u32[]{:S(2)}, u32[]{:S(2)}) collective-permute-start(bf16[128,1024]{1,0:T(8,128)(2,1)S(1)} %collective-permute-done.37), channel_id=1, source_target_pairs={{0,0},{1,1},{2,10},{3,11},{4,20},{5,21},{6,30},{7,31},{8,16},{9,17... | collective-permute-start | bytes 786440 | tf_op jit(solution)/shard_map/ppermute | solution.py:43
  153.9 3.4 collective-permute-done.39.refs_6_
  161.6 4.0 collective-permute-start.46
  165.6 2.7 close_attention.3
  168.4 4.1 feed_forward.3
  172.5 5.0 %collective-permute-done.46.refs_2_ = bf16[128,1024]{1,0:T(8,128)(2,1)S(1)} collective-permute-done((bf16[128,1024]{1,0:T(8,128)(2,1)S(1)}, bf16[128,1024]{1,0:T(8,128)(2,1)S(1)}, u32[]{:S(2)}, u32[]{:S(2)}) %collective-permute-start.46) | collective-permute-done | bytes 262176 | tf_op jit(solution)/shard_map/ppermute | solution.py:58
  179.4 5.4 %feed_back.2 = (bf16[128,1024]{1,0:T(8,128)(2,1)S(1)}, bf16[128,1024]{1,0:T(8,128)(2,1)S(1)}, bf16[128,1024]{1,0:T(8,128)(2,1)S(1)}, bf16[128,1024]{1,0:T(8,128)...) custom-call(s32[3]{0:T(128)S(1)} %pad_add_fusion.2.place, ...), custom_call_target="tpu_custom_call" | custom-call | flops 2147483648 | bytes 7340044 | tf_op jit(solution)/shard_map/feed_back/pallas_call | solution.py:93
  192.7 5.4 %all_to_all.20.ref = bf16[2,512,1024]{2,1,0:T(8,128)(2,1)S(1)} all-to-all(bf16[2,512,1024]{2,1,0:T(8,128)(2,1)S(1)} %up_weight_grad.2), channel_id=1, replica_groups={{0,1},{2,3},{4,5},{6,7},{8,9},{10,11},{12,13},{14,15},{16,17},{18,19},{..., dimensions={0} | all-to-all | bytes 4194304 | tf_op jit(solution)/shard_map/all_to_all | solution.py:1040
  198.1 2.9 collective-permute-done.50.refs_2_
  214.1 5.7 %collective-permute-done.53.refs_1_.refs_4_ = bf16[128,1024]{1,0:T(8,128)(2,1)} collective-permute-done((bf16[128,1024]{1,0:T(8,128)(2,1)}, bf16[128,1024]{1,0:T(8,128)(2,1)}, u32[]{:S(2)}, u32[]{:S(2)}) %collective-permute-start.53) | collective-permute-done | bytes 262176 | tf_op jit(solution)/shard_map/ppermute | solution.py:58
  219.8 5.1 %collective-permute-done.54.refs_2_.refs_5_ = bf16[128,1024]{1,0:T(8,128)(2,1)} collective-permute-done((bf16[128,1024]{1,0:T(8,128)(2,1)}, bf16[128,1024]{1,0:T(8,128)(2,1)}, u32[]{:S(2)}, u32[]{:S(2)}) %collective-permute-start.54) | collective-permute-done | bytes 262176 | tf_op jit(solution)/shard_map/ppermute | solution.py:58
  228.3 3.3 collective-permute-start.59
  231.7 9.7 %attend_back.2 = (bf16[128,1024]{1,0:T(8,128)(2,1)S(1)}, bf16[128,1024]{1,0:T(8,128)(2,1)S(1)}, bf16[128,1024]{1,0:T(8,128)(2,1)S(1)}, bf16[128,1024]{1,0:T(8,12...) custom-call(s32[3]{0:T(128)S(1)} %pad_add_fusion.2.place, ...), custom_call_target="tpu_custom_call" | custom-call | flops 2147483648 | bytes 5509132 | tf_op jit(solution)/shard_map/attend_back/pallas_call | solution.py:93
  249.0 2.6 attend_weight_grad.2
  251.5 5.4 %all_to_all.21.ref = bf16[2,512,1024]{2,1,0:T(8,128)(2,1)S(1)} all-to-all(bf16[2,512,1024]{2,1,0:T(8,128)(2,1)S(1)} %attend_weight_grad.2), channel_id=1, replica_groups={{0,1},{2,3},{4,5},{6,7},{8,9},{10,11},{12,13},{14,15},{16,17},{18,19},{..., dimensions={0} | all-to-all | bytes 4194304 | tf_op jit(solution)/shard_map/all_to_all | solution.py:1040
  260.4 3.5 collective-permute-start.69
  267.4 5.7 %collective-permute-done.65.refs_1_ = bf16[128,1024]{1,0:T(8,128)(2,1)S(1)} collective-permute-done((bf16[128,1024]{1,0:T(8,128)(2,1)S(1)}, bf16[128,1024]{1,0:T(8,128)(2,1)S(1)}, u32[]{:S(2)}, u32[]{:S(2)}) %collective-permute-start.65) | collective-permute-done | bytes 262176 | tf_op jit(solution)/shard_map/ppermute | solution.py:58
  273.1 5.0 %collective-permute-done.67.refs_3_ = bf16[128,1024]{1,0:T(8,128)(2,1)S(1)} collective-permute-done((bf16[128,1024]{1,0:T(8,128)(2,1)S(1)}, bf16[128,1024]{1,0:T(8,128)(2,1)S(1)}, u32[]{:S(2)}, u32[]{:S(2)}) %collective-permute-start.67) | collective-permute-done | bytes 262176 | tf_op jit(solution)/shard_map/ppermute | solution.py:58
  281.1 3.1 collective-permute-start.72
  284.2 5.4 %feed_back.3 = (bf16[128,1024]{1,0:T(8,128)(2,1)S(1)}, bf16[128,1024]{1,0:T(8,128)(2,1)S(1)}, bf16[128,1024]{1,0:T(8,128)(2,1)S(1)}, bf16[128,1024]{1,0:T(8,128)...) custom-call(s32[3]{0:T(128)S(1)} %pad_add_fusion.2.place, ...), custom_call_target="tpu_custom_call" | custom-call | flops 2147483648 | bytes 7340044 | tf_op jit(solution)/shard_map/feed_back/pallas_call | solution.py:93
  289.9 5.4 %collective-permute-done.71.refs_4_.a_ref = bf16[512,512]{1,0:T(8,128)(2,1)S(1)} collective-permute-done((bf16[512,512]{1,0:T(8,128)(2,1)S(1)}, bf16[512,512]{1,0:T(8,128)(2,1)S(1)}, u32[]{:S(2)}, u32[]{:S(2)}) %collective-permute-start.71) | collective-permute-done | bytes 524320 | tf_op jit(solution)/shard_map/ppermute | solution.py:923
  298.1 3.1 collective-permute-start.77
  306.7 5.4 %all_to_all.22.ref = bf16[2,512,1024]{2,1,0:T(8,128)(2,1)S(1)} all-to-all(bf16[2,512,1024]{2,1,0:T(8,128)(2,1)S(1)} %up_weight_grad.3), channel_id=1, replica_groups={{0,1},{2,3},{4,5},{6,7},{8,9},{10,11},{12,13},{14,15},{16,17},{18,19},{..., dimensions={0} | all-to-all | bytes 4194304 | tf_op jit(solution)/shard_map/all_to_all | solution.py:1040
  312.1 3.0 collective-permute-done.75.refs_3_
  316.1 3.1 collective-permute-start.82
  324.2 5.0 %collective-permute-done.78.refs_1_.refs_4_ = bf16[128,1024]{1,0:T(8,128)(2,1)S(1)} collective-permute-done((bf16[128,1024]{1,0:T(8,128)(2,1)S(1)}, bf16[128,1024]{1,0:T(8,128)(2,1)S(1)}, u32[]{:S(2)}, u32[]{:S(2)}) %collective-permute-start.78) | collective-permute-done | bytes 262176 | tf_op jit(solution)/shard_map/ppermute | solution.py:58
  329.3 3.8 collective-permute-done.79.refs_2_.refs_5_
  334.0 3.2 collective-permute-start.84
  337.4 9.2 %attend_back.3 = (bf16[128,1024]{1,0:T(8,128)(2,1)S(1)}, bf16[128,1024]{1,0:T(8,128)(2,1)S(1)}, bf16[128,1024]{1,0:T(8,128)(2,1)S(1)}, bf16[128,1024]{1,0:T(8,12...) custom-call(s32[3]{0:T(128)S(1)} %pad_add_fusion.2.place, ...), custom_call_target="tpu_custom_call" | custom-call | flops 2147483648 | bytes 6688780 | tf_op jit(solution)/shard_map/attend_back/pallas_call | solution.py:93
  347.5 2.9 collective-permute-start.89
  356.0 5.5 %all_to_all.23.ref = bf16[2,528,1024]{2,1,0:T(8,128)(2,1)S(1)} all-to-all(bf16[2,528,1024]{2,1,0:T(8,128)(2,1)S(1)} %attend_weight_grad.3), channel_id=1, replica_groups={{0,1},{2,3},{4,5},{6,7},{8,9},{10,11},{12,13},{14,15},{16,17},{18,19},{..., dimensions={0} | all-to-all | bytes 4325376 | tf_op jit(solution)/shard_map/all_to_all | solution.py:1040
  364.6 3.0 collective-permute-start.94
  371.1 5.7 %collective-permute-done.90.refs_1_ = bf16[128,1024]{1,0:T(8,128)(2,1)S(1)} collective-permute-done((bf16[128,1024]{1,0:T(8,128)(2,1)S(1)}, bf16[128,1024]{1,0:T(8,128)(2,1)S(1)}, u32[]{:S(2)}, u32[]{:S(2)}) %collective-permute-start.90) | collective-permute-done | bytes 262176 | tf_op jit(solution)/shard_map/ppermute | solution.py:58
  376.8 5.2 %collective-permute-done.91.refs_2_ = bf16[128,1024]{1,0:T(8,128)(2,1)S(1)} collective-permute-done((bf16[128,1024]{1,0:T(8,128)(2,1)S(1)}, bf16[128,1024]{1,0:T(8,128)(2,1)S(1)}, u32[]{:S(2)}, u32[]{:S(2)}) %collective-permute-start.91) | collective-permute-done | bytes 262176 | tf_op jit(solution)/shard_map/ppermute | solution.py:58
  382.9 2.9 collective-permute-start.99
  390.1 5.8 %collective-permute-done.95.refs_6_ = bf16[128,1024]{1,0:T(8,128)(2,1)S(1)} collective-permute-done((bf16[128,1024]{1,0:T(8,128)(2,1)S(1)}, bf16[128,1024]{1,0:T(8,128)(2,1)S(1)}, u32[]{:S(2)}, u32[]{:S(2)}) %collective-permute-start.95) | collective-permute-done | bytes 262176 | tf_op jit(solution)/shard_map/ppermute | solution.py:58
  395.9 3.9 collective-permute-done.96.refs_7_
  402.4 3.0 collective-permute-start.104
  411.9 3.2 collective-permute-done.101.refs_3_
  421.1 3.3 collective-permute-done.105.refs_1_
  424.4 3.6 collective-permute-done.106.refs_2_
  437.5 3.5 write_layer.3
  441.1 2.9 write_layer.5
  444.0 4.5 collective-permute-done.109.refs_0_
  448.5 2.8 collective-permute-done.110.refs_1_
  (417 shorter events, 176.6 us)
Async XLA Ops:
  1.8 13.5 %collective-permute-start = (bf16[64,1024]{1,0:T(8,128)(2,1)S(1)}, bf16[64,1024]{1,0:T(8,128)(2,1)S(1)}, u32[]{:S(2)}, u32[]{:S(2)}) collective-permute-start(bf16[64,1024]{1,0:T(8,128)(2,1)S(1)} %get-tuple-element.823), channel_id=1, source_target_pairs={{0,0},{1,1},{2,2},{3,3},{4,4},{5,5},{6,6},{7,7},{12,8},{13,9},{14,... | collective-permute-start | bytes 393224 | tf_op jit(solution)/shard_map/ppermute | solution.py:43
  8.6 12.4 %collective-permute-start.3 = (bf16[64,1792]{1,0:T(8,128)(2,1)S(1)}, bf16[64,1792]{1,0:T(8,128)(2,1)S(1)}, u32[]{:S(2)}, u32[]{:S(2)}) collective-permute-start(bf16[64,1792]{1,0:T(8,128)(2,1)S(1)} %get-tuple-element.418), channel_id=1, source_target_pairs={{0,2},{1,3},{2,0},{3,1},{4,6},{5,7},{6,4},{7,5},{8,10},{9,11},{10,... | collective-permute-start | bytes 688136 | tf_op jit(solution)/shard_map/ppermute | solution.py:58
  9.2 17.5 %collective-permute-start.2 = (bf16[80,1024]{1,0:T(8,128)(2,1)S(1)}, bf16[80,1024]{1,0:T(8,128)(2,1)S(1)}, u32[]{:S(2)}, u32[]{:S(2)}) collective-permute-start(bf16[80,1024]{1,0:T(8,128)(2,1)S(1)} %pad_add_fusion), channel_id=1, source_target_pairs={{0,0},{1,1},{2,10},{3,11},{4,20},{5,21},{6,30},{7,31},{12,16},{13,... | collective-permute-start | bytes 491528 | tf_op jit(solution)/shard_map/ppermute | solution.py:43
  11.7 13.3 %collective-permute-start.4 = (bf16[64,1792]{1,0:T(8,128)(2,1)S(1)}, bf16[64,1792]{1,0:T(8,128)(2,1)S(1)}, u32[]{:S(2)}, u32[]{:S(2)}) collective-permute-start(bf16[64,1792]{1,0:T(8,128)(2,1)S(1)} %get-tuple-element.419), channel_id=1, source_target_pairs={{0,4},{1,5},{2,6},{3,7},{4,0},{5,1},{6,2},{7,3},{8,12},{9,13},{10,... | collective-permute-start | bytes 688136 | tf_op jit(solution)/shard_map/ppermute | solution.py:58
  15.3 11.4 %collective-permute-start.1 = (bf16[64,1024]{1,0:T(8,128)(2,1)S(1)}, bf16[64,1024]{1,0:T(8,128)(2,1)S(1)}, u32[]{:S(2)}, u32[]{:S(2)}) collective-permute-start(bf16[64,1024]{1,0:T(8,128)(2,1)S(1)} %collective-permute-done), channel_id=1, source_target_pairs={{0,0},{1,1},{2,10},{3,11},{4,20},{5,21},{6,30},{7,31},{8,16},{9,17... | collective-permute-start | bytes 393224 | tf_op jit(solution)/shard_map/ppermute | solution.py:43
  26.7 17.3 %collective-permute-start.10 = (bf16[192,1792]{1,0:T(8,128)(2,1)S(1)}, bf16[192,1792]{1,0:T(8,128)(2,1)S(1)}, u32[]{:S(2)}, u32[]{:S(2)}) collective-permute-start(bf16[192,1792]{1,0:T(8,128)(2,1)S(1)} %stack_halves.4.mine_ref), channel_id=1, source_target_pairs={{0,8},{8,0},{16,24},{24,16},{1,9},{9,1},{17,25},{25,17},{2,10},{10... | collective-permute-start | bytes 2064392 | tf_op jit(solution)/shard_map/ppermute | solution.py:64
  29.1 13.6 %collective-permute-start.8 = (bf16[144,1024]{1,0:T(8,128)(2,1)S(1)}, bf16[144,1024]{1,0:T(8,128)(2,1)S(1)}, u32[]{:S(2)}, u32[]{:S(2)}) collective-permute-start(bf16[144,1024]{1,0:T(8,128)(2,1)S(1)} %put_small.1.refs_0_.refs_11_.hidden_ref), channel_id=1, source_target_pairs={{0,4},{1,5},{2,6},{3,7},{4,0},{5,1},{6,2},{7,3},{8,12},{9,13},{10,... | collective-permute-start | bytes 884744 | tf_op jit(solution)/shard_map/ppermute | solution.py:58
  31.6 12.4 %collective-permute-start.9 = (bf16[144,1024]{1,0:T(8,128)(2,1)S(1)}, bf16[144,1024]{1,0:T(8,128)(2,1)S(1)}, u32[]{:S(2)}, u32[]{:S(2)}) collective-permute-start(bf16[144,1024]{1,0:T(8,128)(2,1)S(1)} %put_small.1.refs_0_.refs_11_.hidden_ref), channel_id=1, source_target_pairs={{0,6},{1,7},{2,4},{3,5},{4,2},{5,3},{6,0},{7,1},{8,14},{9,15},{10,... | collective-permute-start | bytes 884744 | tf_op jit(solution)/shard_map/ppermute | solution.py:58
  59.9 15.0 %collective-permute-start.19 = (bf16[192,1024]{1,0:T(8,128)(2,1)S(1)}, bf16[192,1024]{1,0:T(8,128)(2,1)S(1)}, u32[]{:S(2)}, u32[]{:S(2)}) collective-permute-start(bf16[192,1024]{1,0:T(8,128)(2,1)S(1)} %stack_halves.5.mine_ref), channel_id=1, source_target_pairs={{0,8},{8,0},{16,24},{24,16},{1,9},{9,1},{17,25},{25,17},{2,10},{10... | collective-permute-start | bytes 1179656 | tf_op jit(solution)/shard_map/ppermute | solution.py:64
  63.5 11.5 %collective-permute-start.18 = (bf16[512,256]{1,0:T(8,128)(2,1)S(1)}, bf16[512,256]{1,0:T(8,128)(2,1)S(1)}, u32[]{:S(2)}, u32[]{:S(2)}) collective-permute-start(bf16[512,256]{1,0:T(8,128)(2,1)S(1)} %get-tuple-element.457.refs_4_.refs_2_), channel_id=1, source_target_pairs={{0,6},{1,7},{2,4},{3,5},{4,2},{5,3},{6,0},{7,1},{8,14},{9,15},{10,... | collective-permute-start | bytes 786440 | tf_op jit(solution)/shard_map/ppermute | solution.py:58
  82.7 11.3 %collective-permute-start.23 = (bf16[64,1792]{1,0:T(8,128)(2,1)S(1)}, bf16[64,1792]{1,0:T(8,128)(2,1)S(1)}, u32[]{:S(2)}, u32[]{:S(2)}) collective-permute-start(bf16[64,1792]{1,0:T(8,128)(2,1)S(1)} %get-tuple-element.486), channel_id=1, source_target_pairs={{0,4},{1,5},{2,6},{3,7},{4,0},{5,1},{6,2},{7,3},{8,12},{9,13},{10,... | collective-permute-start | bytes 688136 | tf_op jit(solution)/shard_map/ppermute | solution.py:58
  95.9 16.7 %collective-permute-start.28 = (bf16[192,1792]{1,0:T(8,128)(2,1)S(1)}, bf16[192,1792]{1,0:T(8,128)(2,1)S(1)}, u32[]{:S(2)}, u32[]{:S(2)}) collective-permute-start(bf16[192,1792]{1,0:T(8,128)(2,1)S(1)} %stack_halves.6.mine_ref), channel_id=1, source_target_pairs={{0,8},{8,0},{16,24},{24,16},{1,9},{9,1},{17,25},{25,17},{2,10},{10... | collective-permute-start | bytes 2064392 | tf_op jit(solution)/shard_map/ppermute | solution.py:64
  98.3 12.4 %collective-permute-start.26 = (bf16[128,1024]{1,0:T(8,128)(2,1)S(1)}, bf16[128,1024]{1,0:T(8,128)(2,1)S(1)}, u32[]{:S(2)}, u32[]{:S(2)}) collective-permute-start(bf16[128,1024]{1,0:T(8,128)(2,1)S(1)} %get-tuple-element.490), channel_id=1, source_target_pairs={{0,4},{1,5},{2,6},{3,7},{4,0},{5,1},{6,2},{7,3},{8,12},{9,13},{10,... | collective-permute-start | bytes 786440 | tf_op jit(solution)/shard_map/ppermute | solution.py:58
  113.7 15.7 %collective-permute-start.33 = (bf16[512,1024]{1,0:T(8,128)(2,1)S(1)}, bf16[512,1024]{1,0:T(8,128)(2,1)S(1)}, u32[]{:S(2)}, u32[]{:S(2)}) collective-permute-start(bf16[512,1024]{1,0:T(8,128)(2,1)S(1)} %get-tuple-element.527.refs_8_.refs_4_), channel_id=1, source_target_pairs={{0,1},{1,0},{2,3},{3,2},{4,5},{5,4},{6,7},{7,6},{8,9},{9,8},{10,11... | collective-permute-start | bytes 3145736 | tf_op jit(solution)/shard_map/ppermute | solution.py:61
  113.8 15.6 %collective-permute-start.32 = (bf16[512,768]{1,0:T(8,128)(2,1)S(1)}, bf16[512,768]{1,0:T(8,128)(2,1)S(1)}, u32[]{:S(2)}, u32[]{:S(2)}) collective-permute-start(bf16[512,768]{1,0:T(8,128)(2,1)S(1)} %get-tuple-element.506.refs_5_.refs_9_), channel_id=1, source_target_pairs={{0,1},{1,0},{2,3},{3,2},{4,5},{5,4},{6,7},{7,6},{8,9},{9,8},{10,11... | collective-permute-start | bytes 2359304 | tf_op jit(solution)/shard_map/ppermute | solution.py:61
  115.7 13.6 %collective-permute-start.30 = (bf16[128,1024]{1,0:T(8,128)(2,1)S(1)}, bf16[128,1024]{1,0:T(8,128)(2,1)S(1)}, u32[]{:S(2)}, u32[]{:S(2)}) collective-permute-start(bf16[128,1024]{1,0:T(8,128)(2,1)S(1)} %get-tuple-element.502.refs_0_), channel_id=1, source_target_pairs={{0,4},{1,5},{2,6},{3,7},{4,0},{5,1},{6,2},{7,3},{8,12},{9,13},{10,... | collective-permute-start | bytes 786440 | tf_op jit(solution)/shard_map/ppermute | solution.py:58
  116.3 13.0 %collective-permute-start.31 = (bf16[128,1024]{1,0:T(8,128)(2,1)S(1)}, bf16[128,1024]{1,0:T(8,128)(2,1)S(1)}, u32[]{:S(2)}, u32[]{:S(2)}) collective-permute-start(bf16[128,1024]{1,0:T(8,128)(2,1)S(1)} %get-tuple-element.502.refs_0_), channel_id=1, source_target_pairs={{0,6},{1,7},{2,4},{3,5},{4,2},{5,3},{6,0},{7,1},{8,14},{9,15},{10,... | collective-permute-start | bytes 786440 | tf_op jit(solution)/shard_map/ppermute | solution.py:58
  129.4 15.0 %collective-permute-start.37 = (bf16[128,1024]{1,0:T(8,128)(2,1)S(1)}, bf16[128,1024]{1,0:T(8,128)(2,1)S(1)}, u32[]{:S(2)}, u32[]{:S(2)}) collective-permute-start(bf16[128,1024]{1,0:T(8,128)(2,1)S(1)} %bitcast.13), channel_id=1, source_target_pairs={{0,0},{1,1},{2,2},{3,3},{4,4},{5,5},{6,6},{7,7},{12,8},{13,9},{14,... | collective-permute-start | bytes 786440 | tf_op jit(solution)/shard_map/ppermute | solution.py:43
  144.4 14.5 %collective-permute-start.41 = (bf16[192,1024]{1,0:T(8,128)(2,1)S(1)}, bf16[192,1024]{1,0:T(8,128)(2,1)S(1)}, u32[]{:S(2)}, u32[]{:S(2)}) collective-permute-start(bf16[192,1024]{1,0:T(8,128)(2,1)S(1)} %stack_halves.7.mine_ref), channel_id=1, source_target_pairs={{0,8},{8,0},{16,24},{24,16},{1,9},{9,1},{17,25},{25,17},{2,10},{10... | collective-permute-start | bytes 1179656 | tf_op jit(solution)/shard_map/ppermute | solution.py:64
  145.4 11.9 %collective-permute-start.39 = (bf16[512,256]{1,0:T(8,128)(2,1)S(1)}, bf16[512,256]{1,0:T(8,128)(2,1)S(1)}, u32[]{:S(2)}, u32[]{:S(2)}) collective-permute-start(bf16[512,256]{1,0:T(8,128)(2,1)S(1)} %get-tuple-element.523.refs_4_.refs_2_), channel_id=1, source_target_pairs={{0,4},{1,5},{2,6},{3,7},{4,0},{5,1},{6,2},{7,3},{8,12},{9,13},{10,... | collective-permute-start | bytes 786440 | tf_op jit(solution)/shard_map/ppermute | solution.py:58
  161.6 15.8 %collective-permute-start.46 = (bf16[128,1024]{1,0:T(8,128)(2,1)S(1)}, bf16[128,1024]{1,0:T(8,128)(2,1)S(1)}, u32[]{:S(2)}, u32[]{:S(2)}) collective-permute-start(bf16[128,1024]{1,0:T(8,128)(2,1)S(1)} %collective-permute-done.42.refs_0_.grad_ref.ref), channel_id=1, source_target_pairs={{0,4},{1,5},{2,6},{3,7},{4,0},{5,1},{6,2},{7,3},{8,12},{9,13},{10,... | collective-permute-start | bytes 786440 | tf_op jit(solution)/shard_map/ppermute | solution.py:58
  165.6 11.9 %collective-permute-start.47 = (bf16[128,1024]{1,0:T(8,128)(2,1)S(1)}, bf16[128,1024]{1,0:T(8,128)(2,1)S(1)}, u32[]{:S(2)}, u32[]{:S(2)}) collective-permute-start(bf16[128,1024]{1,0:T(8,128)(2,1)S(1)} %collective-permute-done.42.refs_0_.grad_ref.ref), channel_id=1, source_target_pairs={{0,6},{1,7},{2,4},{3,5},{4,2},{5,3},{6,0},{7,1},{8,14},{9,15},{10,... | collective-permute-start | bytes 786440 | tf_op jit(solution)/shard_map/ppermute | solution.py:58
  185.8 17.0 %collective-permute-start.52 = (bf16[512,512]{1,0:T(8,128)(2,1)S(1)}, bf16[512,512]{1,0:T(8,128)(2,1)S(1)}, u32[]{:S(2)}, u32[]{:S(2)}) collective-permute-start(bf16[512,512]{1,0:T(8,128)(2,1)S(1)} %get-tuple-element.570.refs_0_), channel_id=1, source_target_pairs={{0,8},{24,16},{1,9},{25,17},{2,10},{26,18},{3,11},{27,19},{4,12},{... | collective-permute-start | bytes 1572872 | tf_op jit(solution)/shard_map/ppermute | solution.py:923
  188.8 12.2 %collective-permute-start.50 = (bf16[128,1024]{1,0:T(8,128)(2,1)S(1)}, bf16[128,1024]{1,0:T(8,128)(2,1)S(1)}, u32[]{:S(2)}, u32[]{:S(2)}) collective-permute-start(bf16[128,1024]{1,0:T(8,128)(2,1)S(1)} %get-tuple-element.566), channel_id=1, source_target_pairs={{0,4},{1,5},{2,6},{3,7},{4,0},{5,1},{6,2},{7,3},{8,12},{9,13},{10,... | collective-permute-start | bytes 786440 | tf_op jit(solution)/shard_map/ppermute | solution.py:58
  189.4 13.5 %collective-permute-start.51 = (bf16[128,1024]{1,0:T(8,128)(2,1)S(1)}, bf16[128,1024]{1,0:T(8,128)(2,1)S(1)}, u32[]{:S(2)}, u32[]{:S(2)}) collective-permute-start(bf16[128,1024]{1,0:T(8,128)(2,1)S(1)} %get-tuple-element.567), channel_id=1, source_target_pairs={{0,6},{1,7},{2,4},{3,5},{4,2},{5,3},{6,0},{7,1},{8,14},{9,15},{10,... | collective-permute-start | bytes 786440 | tf_op jit(solution)/shard_map/ppermute | solution.py:58
  202.8 22.1 %collective-permute-start.56 = (bf16[512,512]{1,0:T(8,128)(2,1)}, bf16[512,512]{1,0:T(8,128)(2,1)}, u32[]{:S(2)}, u32[]{:S(2)}) collective-permute-start(bf16[512,512]{1,0:T(8,128)(2,1)} %get-tuple-element.579.refs_3_), channel_id=1, source_target_pairs={{0,8},{24,16},{1,9},{25,17},{2,10},{26,18},{3,11},{27,19},{4,12},{... | collective-permute-start | bytes 1572872 | tf_op jit(solution)/shard_map/ppermute | solution.py:923
  205.0 19.9 %collective-permute-start.57 = (bf16[512,512]{1,0:T(8,128)(2,1)}, bf16[512,512]{1,0:T(8,128)(2,1)}, u32[]{:S(2)}, u32[]{:S(2)}) collective-permute-start(bf16[512,512]{1,0:T(8,128)(2,1)} %turn.13.refs_1_), channel_id=1, source_target_pairs={{8,16},{16,8},{9,17},{17,9},{10,18},{18,10},{11,19},{19,11},{12,20... | collective-permute-start | bytes 1572872 | tf_op jit(solution)/shard_map/ppermute | solution.py:923
  211.6 13.3 %collective-permute-start.54 = (bf16[128,1024]{1,0:T(8,128)(2,1)}, bf16[128,1024]{1,0:T(8,128)(2,1)}, u32[]{:S(2)}, u32[]{:S(2)}) collective-permute-start(bf16[128,1024]{1,0:T(8,128)(2,1)} %get-tuple-element.581.refs_0_.refs_3_), channel_id=1, source_target_pairs={{0,4},{1,5},{2,6},{3,7},{4,0},{5,1},{6,2},{7,3},{8,12},{9,13},{10,... | collective-permute-start | bytes 786440 | tf_op jit(solution)/shard_map/ppermute | solution.py:58
  212.6 12.4 %collective-permute-start.55 = (bf16[128,1024]{1,0:T(8,128)(2,1)}, bf16[128,1024]{1,0:T(8,128)(2,1)}, u32[]{:S(2)}, u32[]{:S(2)}) collective-permute-start(bf16[128,1024]{1,0:T(8,128)(2,1)} %get-tuple-element.581.refs_0_.refs_3_), channel_id=1, source_target_pairs={{0,6},{1,7},{2,4},{3,5},{4,2},{5,3},{6,0},{7,1},{8,14},{9,15},{10,... | collective-permute-start | bytes 786440 | tf_op jit(solution)/shard_map/ppermute | solution.py:58
  226.7 14.6 %collective-permute-start.58 = (bf16[512,512]{1,0:T(8,128)(2,1)S(1)}, bf16[512,512]{1,0:T(8,128)(2,1)S(1)}, u32[]{:S(2)}, u32[]{:S(2)}) collective-permute-start(bf16[512,512]{1,0:T(8,128)(2,1)S(1)} %get-tuple-element.800.b_ref), channel_id=1, source_target_pairs={{0,8},{24,16},{8,0},{16,24},{1,9},{25,17},{9,1},{17,25},{2,10},{26... | collective-permute-start | bytes 1572872 | tf_op jit(solution)/shard_map/ppermute | solution.py:923
  228.3 13.9 %collective-permute-start.59 = (bf16[512,512]{1,0:T(8,128)(2,1)S(1)}, bf16[512,512]{1,0:T(8,128)(2,1)S(1)}, u32[]{:S(2)}, u32[]{:S(2)}) collective-permute-start(bf16[512,512]{1,0:T(8,128)(2,1)S(1)} %get-tuple-element.612.refs_1_), channel_id=1, source_target_pairs={{8,16},{16,8},{9,17},{17,9},{10,18},{18,10},{11,19},{19,11},{12,20... | collective-permute-start | bytes 1572872 | tf_op jit(solution)/shard_map/ppermute | solution.py:923
  243.0 16.1 %collective-permute-start.63 = (bf16[512,512]{1,0:T(8,128)(2,1)S(1)}, bf16[512,512]{1,0:T(8,128)(2,1)S(1)}, u32[]{:S(2)}, u32[]{:S(2)}) collective-permute-start(bf16[512,512]{1,0:T(8,128)(2,1)S(1)} %get-tuple-element.801.b_ref), channel_id=1, source_target_pairs={{0,8},{24,16},{8,0},{16,24},{1,9},{25,17},{9,1},{17,25},{2,10},{26... | collective-permute-start | bytes 1572872 | tf_op jit(solution)/shard_map/ppermute | solution.py:923
  243.1 16.1 %collective-permute-start.64 = (bf16[512,512]{1,0:T(8,128)(2,1)S(1)}, bf16[512,512]{1,0:T(8,128)(2,1)S(1)}, u32[]{:S(2)}, u32[]{:S(2)}) collective-permute-start(bf16[512,512]{1,0:T(8,128)(2,1)S(1)} %get-tuple-element.621.refs_1_), channel_id=1, source_target_pairs={{8,16},{16,8},{9,17},{17,9},{10,18},{18,10},{11,19},{19,11},{12,20... | collective-permute-start | bytes 1572872 | tf_op jit(solution)/shard_map/ppermute | solution.py:923
  245.4 11.5 %collective-permute-start.60 = (bf16[128,1024]{1,0:T(8,128)(2,1)S(1)}, bf16[128,1024]{1,0:T(8,128)(2,1)S(1)}, u32[]{:S(2)}, u32[]{:S(2)}) collective-permute-start(bf16[128,1024]{1,0:T(8,128)(2,1)S(1)} %get-tuple-element.599), channel_id=1, source_target_pairs={{0,2},{1,3},{2,0},{3,1},{4,6},{5,7},{6,4},{7,5},{8,10},{9,11},{10,... | collective-permute-start | bytes 786440 | tf_op jit(solution)/shard_map/ppermute | solution.py:58
  260.0 18.2 %collective-permute-start.68 = (bf16[512,512]{1,0:T(8,128)(2,1)S(1)}, bf16[512,512]{1,0:T(8,128)(2,1)S(1)}, u32[]{:S(2)}, u32[]{:S(2)}) collective-permute-start(bf16[512,512]{1,0:T(8,128)(2,1)S(1)} %get-tuple-element.736.b_ref), channel_id=1, source_target_pairs={{0,8},{24,16},{8,0},{16,24},{1,9},{25,17},{9,1},{17,25},{2,10},{26... | collective-permute-start | bytes 1572872 | tf_op jit(solution)/shard_map/ppermute | solution.py:923
  260.4 17.8 %collective-permute-start.69 = (bf16[512,512]{1,0:T(8,128)(2,1)S(1)}, bf16[512,512]{1,0:T(8,128)(2,1)S(1)}, u32[]{:S(2)}, u32[]{:S(2)}) collective-permute-start(bf16[512,512]{1,0:T(8,128)(2,1)S(1)} %get-tuple-element.648.refs_1_), channel_id=1, source_target_pairs={{8,16},{16,8},{9,17},{17,9},{10,18},{18,10},{11,19},{19,11},{12,20... | collective-permute-start | bytes 1572872 | tf_op jit(solution)/shard_map/ppermute | solution.py:923
  265.7 12.4 %collective-permute-start.67 = (bf16[128,1024]{1,0:T(8,128)(2,1)S(1)}, bf16[128,1024]{1,0:T(8,128)(2,1)S(1)}, u32[]{:S(2)}, u32[]{:S(2)}) collective-permute-start(bf16[128,1024]{1,0:T(8,128)(2,1)S(1)} %get-tuple-element.627.refs_0_), channel_id=1, source_target_pairs={{0,6},{1,7},{2,4},{3,5},{4,2},{5,3},{6,0},{7,1},{8,14},{9,15},{10,... | collective-permute-start | bytes 786440 | tf_op jit(solution)/shard_map/ppermute | solution.py:58
  281.0 14.4 %collective-permute-start.71 = (bf16[512,512]{1,0:T(8,128)(2,1)S(1)}, bf16[512,512]{1,0:T(8,128)(2,1)S(1)}, u32[]{:S(2)}, u32[]{:S(2)}) collective-permute-start(bf16[512,512]{1,0:T(8,128)(2,1)S(1)} %get-tuple-element.737.b_ref), channel_id=1, source_target_pairs={{0,8},{24,16},{8,0},{16,24},{1,9},{25,17},{9,1},{17,25},{2,10},{26... | collective-permute-start | bytes 1572872 | tf_op jit(solution)/shard_map/ppermute | solution.py:923
  281.1 16.2 %collective-permute-start.72 = (bf16[512,512]{1,0:T(8,128)(2,1)S(1)}, bf16[512,512]{1,0:T(8,128)(2,1)S(1)}, u32[]{:S(2)}, u32[]{:S(2)}) collective-permute-start(bf16[512,512]{1,0:T(8,128)(2,1)S(1)} %get-tuple-element.660.refs_1_), channel_id=1, source_target_pairs={{8,16},{16,8},{9,17},{17,9},{10,18},{18,10},{11,19},{19,11},{12,20... | collective-permute-start | bytes 1572872 | tf_op jit(solution)/shard_map/ppermute | solution.py:923
  298.1 17.1 %collective-permute-start.76 = (bf16[512,512]{1,0:T(8,128)(2,1)S(1)}, bf16[512,512]{1,0:T(8,128)(2,1)S(1)}, u32[]{:S(2)}, u32[]{:S(2)}) collective-permute-start(bf16[512,512]{1,0:T(8,128)(2,1)S(1)} %get-tuple-element.754.b_ref), channel_id=1, source_target_pairs={{0,8},{24,16},{8,0},{16,24},{1,9},{25,17},{9,1},{17,25},{2,10},{26... | collective-permute-start | bytes 1572872 | tf_op jit(solution)/shard_map/ppermute | solution.py:923
  298.1 17.0 %collective-permute-start.77 = (bf16[512,512]{1,0:T(8,128)(2,1)S(1)}, bf16[512,512]{1,0:T(8,128)(2,1)S(1)}, u32[]{:S(2)}, u32[]{:S(2)}) collective-permute-start(bf16[512,512]{1,0:T(8,128)(2,1)S(1)} %get-tuple-element.674.refs_1_), channel_id=1, source_target_pairs={{8,16},{16,8},{9,17},{17,9},{10,18},{18,10},{11,19},{19,11},{12,20... | collective-permute-start | bytes 1572872 | tf_op jit(solution)/shard_map/ppermute | solution.py:923
  303.1 12.1 %collective-permute-start.75 = (bf16[128,1024]{1,0:T(8,128)(2,1)S(1)}, bf16[128,1024]{1,0:T(8,128)(2,1)S(1)}, u32[]{:S(2)}, u32[]{:S(2)}) collective-permute-start(bf16[128,1024]{1,0:T(8,128)(2,1)S(1)} %get-tuple-element.656), channel_id=1, source_target_pairs={{0,6},{1,7},{2,4},{3,5},{4,2},{5,3},{6,0},{7,1},{8,14},{9,15},{10,... | collective-permute-start | bytes 786440 | tf_op jit(solution)/shard_map/ppermute | solution.py:58
  316.0 17.1 %collective-permute-start.81 = (bf16[512,512]{1,0:T(8,128)(2,1)S(1)}, bf16[512,512]{1,0:T(8,128)(2,1)S(1)}, u32[]{:S(2)}, u32[]{:S(2)}) collective-permute-start(bf16[512,512]{1,0:T(8,128)(2,1)S(1)} %get-tuple-element.755.b_ref), channel_id=1, source_target_pairs={{0,8},{24,16},{8,0},{16,24},{1,9},{25,17},{9,1},{17,25},{2,10},{26... | collective-permute-start | bytes 1572872 | tf_op jit(solution)/shard_map/ppermute | solution.py:923
  316.1 17.1 %collective-permute-start.82 = (bf16[512,512]{1,0:T(8,128)(2,1)S(1)}, bf16[512,512]{1,0:T(8,128)(2,1)S(1)}, u32[]{:S(2)}, u32[]{:S(2)}) collective-permute-start(bf16[512,512]{1,0:T(8,128)(2,1)S(1)} %get-tuple-element.691.refs_1_), channel_id=1, source_target_pairs={{8,16},{16,8},{9,17},{17,9},{10,18},{18,10},{11,19},{19,11},{12,20... | collective-permute-start | bytes 1572872 | tf_op jit(solution)/shard_map/ppermute | solution.py:923
  321.3 11.8 %collective-permute-start.79 = (bf16[128,1024]{1,0:T(8,128)(2,1)S(1)}, bf16[128,1024]{1,0:T(8,128)(2,1)S(1)}, u32[]{:S(2)}, u32[]{:S(2)}) collective-permute-start(bf16[128,1024]{1,0:T(8,128)(2,1)S(1)} %get-tuple-element.679.refs_0_.refs_3_), channel_id=1, source_target_pairs={{0,4},{1,5},{2,6},{3,7},{4,0},{5,1},{6,2},{7,3},{8,12},{9,13},{10,... | collective-permute-start | bytes 786440 | tf_op jit(solution)/shard_map/ppermute | solution.py:58
  333.9 12.7 %collective-permute-start.83 = (bf16[512,512]{1,0:T(8,128)(2,1)S(1)}, bf16[512,512]{1,0:T(8,128)(2,1)S(1)}, u32[]{:S(2)}, u32[]{:S(2)}) collective-permute-start(bf16[512,512]{1,0:T(8,128)(2,1)S(1)} %get-tuple-element.814.b_ref), channel_id=1, source_target_pairs={{0,8},{24,16},{8,0},{16,24},{1,9},{25,17},{9,1},{17,25},{2,10},{26... | collective-permute-start | bytes 1572872 | tf_op jit(solution)/shard_map/ppermute | solution.py:923
  334.0 12.6 %collective-permute-start.84 = (bf16[512,512]{1,0:T(8,128)(2,1)S(1)}, bf16[512,512]{1,0:T(8,128)(2,1)S(1)}, u32[]{:S(2)}, u32[]{:S(2)}) collective-permute-start(bf16[512,512]{1,0:T(8,128)(2,1)S(1)} %get-tuple-element.718.refs_1_), channel_id=1, source_target_pairs={{8,16},{16,8},{9,17},{17,9},{10,18},{18,10},{11,19},{19,11},{12,20... | collective-permute-start | bytes 1572872 | tf_op jit(solution)/shard_map/ppermute | solution.py:923
  347.4 16.3 %collective-permute-start.88 = (bf16[512,512]{1,0:T(8,128)(2,1)S(1)}, bf16[512,512]{1,0:T(8,128)(2,1)S(1)}, u32[]{:S(2)}, u32[]{:S(2)}) collective-permute-start(bf16[512,512]{1,0:T(8,128)(2,1)S(1)} %get-tuple-element.815.b_ref), channel_id=1, source_target_pairs={{0,8},{24,16},{8,0},{16,24},{1,9},{25,17},{9,1},{17,25},{2,10},{26... | collective-permute-start | bytes 1572872 | tf_op jit(solution)/shard_map/ppermute | solution.py:923
  347.5 16.2 %collective-permute-start.89 = (bf16[512,512]{1,0:T(8,128)(2,1)S(1)}, bf16[512,512]{1,0:T(8,128)(2,1)S(1)}, u32[]{:S(2)}, u32[]{:S(2)}) collective-permute-start(bf16[512,512]{1,0:T(8,128)(2,1)S(1)} %get-tuple-element.730.refs_1_), channel_id=1, source_target_pairs={{8,16},{16,8},{9,17},{17,9},{10,18},{18,10},{11,19},{19,11},{12,20... | collective-permute-start | bytes 1572872 | tf_op jit(solution)/shard_map/ppermute | solution.py:923
  364.5 17.5 %collective-permute-start.93 = (bf16[528,512]{1,0:T(8,128)(2,1)S(1)}, bf16[528,512]{1,0:T(8,128)(2,1)S(1)}, u32[]{:S(2)}, u32[]{:S(2)}) collective-permute-start(bf16[528,512]{1,0:T(8,128)(2,1)S(1)} %get-tuple-element.768.b_ref), channel_id=1, source_target_pairs={{0,8},{24,16},{8,0},{16,24},{1,9},{25,17},{9,1},{17,25},{2,10},{26... | collective-permute-start | bytes 1622024 | tf_op jit(solution)/shard_map/ppermute | solution.py:923
  364.6 17.5 %collective-permute-start.94 = (bf16[512,512]{1,0:T(8,128)(2,1)S(1)}, bf16[512,512]{1,0:T(8,128)(2,1)S(1)}, u32[]{:S(2)}, u32[]{:S(2)}) collective-permute-start(bf16[512,512]{1,0:T(8,128)(2,1)S(1)} %get-tuple-element.743.refs_1_), channel_id=1, source_target_pairs={{8,16},{16,8},{9,17},{17,9},{10,18},{18,10},{11,19},{19,11},{12,20... | collective-permute-start | bytes 1572872 | tf_op jit(solution)/shard_map/ppermute | solution.py:923
  368.6 13.4 %collective-permute-start.91 = (bf16[128,1024]{1,0:T(8,128)(2,1)S(1)}, bf16[128,1024]{1,0:T(8,128)(2,1)S(1)}, u32[]{:S(2)}, u32[]{:S(2)}) collective-permute-start(bf16[128,1024]{1,0:T(8,128)(2,1)S(1)} %copy-done.57), channel_id=1, source_target_pairs={{0,4},{1,5},{2,6},{3,7},{4,0},{5,1},{6,2},{7,3},{8,12},{9,13},{10,... | collective-permute-start | bytes 786440 | tf_op jit(solution)/shard_map/ppermute | solution.py:58
  369.8 12.2 %collective-permute-start.92 = (bf16[128,1024]{1,0:T(8,128)(2,1)S(1)}, bf16[128,1024]{1,0:T(8,128)(2,1)S(1)}, u32[]{:S(2)}, u32[]{:S(2)}) collective-permute-start(bf16[128,1024]{1,0:T(8,128)(2,1)S(1)} %copy-done.55), channel_id=1, source_target_pairs={{0,6},{1,7},{2,4},{3,5},{4,2},{5,3},{6,0},{7,1},{8,14},{9,15},{10,... | collective-permute-start | bytes 786440 | tf_op jit(solution)/shard_map/ppermute | solution.py:58
  382.9 16.9 %collective-permute-start.98 = (bf16[528,512]{1,0:T(8,128)(2,1)S(1)}, bf16[528,512]{1,0:T(8,128)(2,1)S(1)}, u32[]{:S(2)}, u32[]{:S(2)}) collective-permute-start(bf16[528,512]{1,0:T(8,128)(2,1)S(1)} %get-tuple-element.769.b_ref), channel_id=1, source_target_pairs={{0,8},{24,16},{8,0},{16,24},{1,9},{25,17},{9,1},{17,25},{2,10},{26... | collective-permute-start | bytes 1622024 | tf_op jit(solution)/shard_map/ppermute | solution.py:923
  382.9 16.9 %collective-permute-start.99 = (bf16[528,512]{1,0:T(8,128)(2,1)S(1)}, bf16[528,512]{1,0:T(8,128)(2,1)S(1)}, u32[]{:S(2)}, u32[]{:S(2)}) collective-permute-start(bf16[528,512]{1,0:T(8,128)(2,1)S(1)} %get-tuple-element.761.refs_0_), channel_id=1, source_target_pairs={{8,16},{16,8},{9,17},{17,9},{10,18},{18,10},{11,19},{19,11},{12,20... | collective-permute-start | bytes 1622024 | tf_op jit(solution)/shard_map/ppermute | solution.py:923
  387.7 12.1 %collective-permute-start.96 = (bf16[128,1024]{1,0:T(8,128)(2,1)S(1)}, bf16[128,1024]{1,0:T(8,128)(2,1)S(1)}, u32[]{:S(2)}, u32[]{:S(2)}) collective-permute-start(bf16[128,1024]{1,0:T(8,128)(2,1)S(1)} %get-tuple-element.740), channel_id=1, source_target_pairs={{0,4},{1,5},{2,6},{3,7},{4,0},{5,1},{6,2},{7,3},{8,12},{9,13},{10,... | collective-permute-start | bytes 786440 | tf_op jit(solution)/shard_map/ppermute | solution.py:58
  400.6 14.5 %collective-permute-start.103 = (bf16[528,512]{1,0:T(8,128)(2,1)S(1)}, bf16[528,512]{1,0:T(8,128)(2,1)S(1)}, u32[]{:S(2)}, u32[]{:S(2)}) collective-permute-start(bf16[528,512]{1,0:T(8,128)(2,1)S(1)} %get-tuple-element.781.b_ref), channel_id=1, source_target_pairs={{8,0},{16,24},{9,1},{17,25},{10,2},{18,26},{11,3},{19,27},{12,4},{... | collective-permute-start | bytes 1622024 | tf_op jit(solution)/shard_map/ppermute | solution.py:923
  402.4 12.9 %collective-permute-start.104 = (bf16[528,512]{1,0:T(8,128)(2,1)S(1)}, bf16[528,512]{1,0:T(8,128)(2,1)S(1)}, u32[]{:S(2)}, u32[]{:S(2)}) collective-permute-start(bf16[528,512]{1,0:T(8,128)(2,1)S(1)} %get-tuple-element.774.refs_0_), channel_id=1, source_target_pairs={{8,16},{16,8},{9,17},{17,9},{10,18},{18,10},{11,19},{19,11},{12,20... | collective-permute-start | bytes 1622024 | tf_op jit(solution)/shard_map/ppermute | solution.py:923
  415.4 13.8 %collective-permute-start.108 = (bf16[528,512]{1,0:T(8,128)(2,1)S(1)}, bf16[528,512]{1,0:T(8,128)(2,1)S(1)}, u32[]{:S(2)}, u32[]{:S(2)}) collective-permute-start(bf16[528,512]{1,0:T(8,128)(2,1)S(1)} %turn.25.b_ref), channel_id=1, source_target_pairs={{8,0},{16,24},{9,1},{17,25},{10,2},{18,26},{11,3},{19,27},{12,4},{... | collective-permute-start | bytes 1622024 | tf_op jit(solution)/shard_map/ppermute | solution.py:923
  429.9 22.9 %collective-permute-start.111 = (bf16[176,768]{1,0:T(8,128)(2,1)S(1)}, bf16[176,768]{1,0:T(8,128)(2,1)S(1)}, u32[]{:S(2)}, u32[]{:S(2)}) collective-permute-start(bf16[176,768]{1,0:T(8,128)(2,1)S(1)} %get-tuple-element.785), channel_id=1, source_target_pairs={{0,2},{1,3},{2,0},{3,1},{4,6},{5,7},{6,4},{7,5},{8,10},{9,11},{10,... | collective-permute-start | bytes 811016 | tf_op jit(solution)/shard_map/ppermute | solution.py:58
  431.2 21.7 %collective-permute-start.112 = (bf16[176,768]{1,0:T(8,128)(2,1)S(1)}, bf16[176,768]{1,0:T(8,128)(2,1)S(1)}, u32[]{:S(2)}, u32[]{:S(2)}) collective-permute-start(bf16[176,768]{1,0:T(8,128)(2,1)S(1)} %get-tuple-element.786), channel_id=1, source_target_pairs={{0,4},{1,5},{2,6},{3,7},{4,0},{5,1},{6,2},{7,3},{8,12},{9,13},{10,... | collective-permute-start | bytes 811016 | tf_op jit(solution)/shard_map/ppermute | solution.py:58
  432.1 20.8 %collective-permute-start.113 = (bf16[176,768]{1,0:T(8,128)(2,1)S(1)}, bf16[176,768]{1,0:T(8,128)(2,1)S(1)}, u32[]{:S(2)}, u32[]{:S(2)}) collective-permute-start(bf16[176,768]{1,0:T(8,128)(2,1)S(1)} %get-tuple-element.787), channel_id=1, source_target_pairs={{0,6},{1,7},{2,4},{3,5},{4,2},{5,3},{6,0},{7,1},{8,14},{9,15},{10,... | collective-permute-start | bytes 811016 | tf_op jit(solution)/shard_map/ppermute | solution.py:58
  433.5 15.0 %collective-permute-start.109 = (bf16[128,1024]{1,0:T(8,128)(2,1)S(1)}, bf16[128,1024]{1,0:T(8,128)(2,1)S(1)}, u32[]{:S(2)}, u32[]{:S(2)}) collective-permute-start(bf16[128,1024]{1,0:T(8,128)(2,1)S(1)} %get-tuple-element.776), channel_id=1, source_target_pairs={{0,0},{1,1},{10,2},{11,3},{20,4},{21,5},{30,6},{31,7},{16,12},{17,... | collective-permute-start | bytes 786440 | tf_op jit(solution)/shard_map/ppermute | solution.py:43
  435.4 15.9 %collective-permute-start.110 = (bf16[128,1024]{1,0:T(8,128)(2,1)S(1)}, bf16[128,1024]{1,0:T(8,128)(2,1)S(1)}, u32[]{:S(2)}, u32[]{:S(2)}) collective-permute-start(bf16[128,1024]{1,0:T(8,128)(2,1)S(1)} %get-tuple-element.777), channel_id=1, source_target_pairs={{0,0},{1,1},{10,2},{11,3},{20,4},{21,5},{30,6},{31,7},{16,12},{17,... | collective-permute-start | bytes 786440 | tf_op jit(solution)/shard_map/ppermute | solution.py:43
  (131 other events, 1801.8 us)
